TPU v7x, 32 devices: a whole 2x2x4 slice. The times are simulated.
32 devices in a mesh: groups: 2 (over y), sec: 2 (over x), row: 4 (over z), col: 2 (over core).
Axes of the slice: x: 2, y: 2, z: 4, core: 2. Of those that a mesh axis runs over, the one named last changes fastest.
Arguments:
- factors: bfloat16 [4, 2048, 2048], P(('groups', 'sec'), 'row', 'col'), parts along dimension 0, may hold values from -0.125 to 0.125
- inverses: bfloat16 [4, 2048, 2048], P(('groups', 'sec'), 'row', 'col'), parts along dimension 0, may hold values from -1.4 to 1.4, as said below
- sigma_end: float32 [4096, 2048], P(('groups', 'row'), 'col'), parts along dimension 0, may hold values from -1 to 6, as said below
Outputs:
- variance: float32 [4, 2048, 2048], P(('groups', 'sec'), 'row', 'col'), parts along dimension 0
There are 2 independent parts, one for each index of `groups`. A program takes and returns all parts, laid end to end along the dimension named above; each array names one. Nothing has to cross between parts.
Inputs may be any that keep to these rules, and one draw needn't show every extreme that they name: inverses[t] is lower triangular; its diagonal entries lie in 0.6 to 1.4. sigma_end is symmetric with diagonal entries in 2.5 to 6.
All inputs are finite; a program needn't handle non-finite values.
Results may differ from a plain program's by a relative error of at most 0.011.
Values may be sent and summed in bfloat16 or wider, within the bound.
No kernel may reach another device: no remote copies, remote signals or barrier semaphores. Data moves between devices by JAX's collectives and lax.ppermute only.
A program may use at most 64 MiB of HBM per device.

v0:
```python
import jax
import jax.numpy as jnp
from jax import lax
from jax.sharding import PartitionSpec as P


def partner(shard, axis, stride):
    return lax.ppermute(shard, axis, [(i, i ^ 1 << stride) for i in range(lax.axis_size(axis))])


def passed_along(value, axis, steps):
    count = lax.axis_size(axis)
    first, last = (max(0, -steps), min(count, count - steps))
    return lax.ppermute(value, axis, [(source, source + steps) for source in range(first, last)])


def local(factors, inverses, sigma_end):
    row_size = lax.axis_size("row")
    col_size = lax.axis_size("col")
    sec_size = lax.axis_size("sec")
    row_index = lax.axis_index("row")
    col_index = lax.axis_index("col")
    sec_index = lax.axis_index("sec")
    step_count, tile_rows, tile_cols = factors.shape
    per_column = row_size // col_size
    offset = row_index % per_column * tile_rows
    owner = row_index // per_column
    owns_panel = col_index == owner

    def own_columns(full_panel):
        return lax.dynamic_slice_in_dim(full_panel, offset, tile_rows, 2)

    factor_full, inverse_full = (
        lax.all_gather(factors, "row", axis=1, tiled=True),
        lax.all_gather(inverses, "row", axis=1, tiled=True),
    )
    local_pair = (own_columns(factor_full), own_columns(inverse_full))
    partner_pair = partner((local_pair[0], local_pair[1]), "col", 0)
    factor_left = jnp.where(owns_panel, local_pair[0], partner_pair[0])
    inverse_left = jnp.where(owns_panel, local_pair[1], partner_pair[1])
    diagonal = jnp.einsum(
        "skr,skc->src", inverse_left, inverse_full, preferred_element_type=jnp.float32
    )
    end_low = sigma_end.astype(jnp.bfloat16)

    def run_segment(segment_number, carried):
        state_low, results = carried
        shifted = passed_along(state_low, "sec", -1)
        current = jnp.where(sec_index == sec_size - 1, end_low, shifted)
        active = sec_index == sec_size - 1 - segment_number
        produced = [None] * step_count
        state_full = lax.all_gather(current, "col", axis=1, tiled=True)
        image = jnp.dot(state_full, factor_full[0], preferred_element_type=jnp.float32).astype(
            jnp.bfloat16
        )
        left_panel = factor_left[0]

        def accumulate(running, incoming_rows, first_row, left_panel=left_panel):
            return running + lax.dot_general(
                left_panel,
                incoming_rows,
                (((0,), (0,)), ((), ())),
                preferred_element_type=jnp.float32,
            )

        variance_block = accumulate(
            diagonal[0], lax.all_gather(image, "row", axis=0, tiled=True), jnp.int32(0)
        )
        produced[0] = variance_block
        current = variance_block.astype(jnp.bfloat16)
        results = jnp.where(active, jnp.stack(produced), results)
        return (current, results)

    initial = (end_low, jnp.zeros((step_count, tile_rows, tile_cols), jnp.float32))
    finished = lax.fori_loop(0, sec_size, run_segment, initial)
    return finished[1]


def solution(mesh):
    in_specs = (
        P(("groups", "sec"), "row", "col"),
        P(("groups", "sec"), "row", "col"),
        P(("groups", "row"), "col"),
    )
    out_specs = P(("groups", "sec"), "row", "col")
    return jax.shard_map(local, mesh=mesh, in_specs=in_specs, out_specs=out_specs, check_vma=False)
```

profile of v0, /device:TPU:0, one launch (start us, length us, event | category | flops | bytes accessed | tf_op | source)
XLA Modules:
  0.0 459.4 jit_solution(6147883923048715536)
XLA Ops:
  8.0 84.4 %all-gather.5.cloned.1.call-done = bf16[1,2048,1024]{2,1,0:T(8,128)(2,1)} async-done(((bf16[1,512,1024]{2,1,0:T(8,128)(2,1)}), bf16[1,2048,1024]{2,1,0:T(8,128)(2,1)}) %all-gather.5.cloned.1.call-update) | async-done | bytes 4194320 | tf_op jit(solution)/shard_map/all_gather | solution.py:35
  92.4 3.0 constant_dynamic-slice_fusion.1
  95.5 77.8 %all-gather.7.cloned.1.call-done = bf16[1,2048,1024]{2,1,0:T(8,128)(2,1)} async-done(((bf16[1,512,1024]{2,1,0:T(8,128)(2,1)}), bf16[1,2048,1024]{2,1,0:T(8,128)(2,1)}) %all-gather.7.cloned.1.call-update) | async-done | bytes 4194320 | tf_op jit(solution)/shard_map/all_gather | solution.py:34
  173.3 3.1 constant_dynamic-slice_fusion
  176.4 1.8 copy.4
  178.2 7.0 %fusion.14 = f32[1,512,1024]{1,2,0:T(8,128)} fusion(bf16[1,2048,1024]{2,1,0:T(8,128)(2,1)} %all-gather.5.cloned.1.call-done, bf16[1,2048,512]{2,1,0:T(8,128)(2,1)} %constant_dynamic-slice_fusion.1, bf16[1,2048,512]{2,1,0:T(8,128)(2,1)} %collective-permute-done.1, pred[]{:T(512)S(6)} %eq.22), kind=kOutput, calls=%fused_computation.14 | convolution fusion | flops 2148532224 | bytes 10485761 | tf_op jit(solution)/shard_map/skr,skc->src/dot_general | solution.py:41
  185.2 2.2 broadcast_select_fusion.1
  187.4 263.4 %while.17 = (s32[]{:T(128)}, bf16[512,1024]{0,1:T(8,128)(2,1)S(1)}, f32[1,512,1024]{1,2,0:T(8,128)S(1)}, f32[1,512,1024]{1,2,0:T(8,128)}, pred[]{:T(512)}, /*ind...) while((s32[]{:T(128)}, bf16[512,1024]{0,1:T(8,128)(2,1)S(1)}, ...), condition=%wide.region_1.2_spmd.clone, body=%wide.region_0.1_spmd.clone.sunk | while | flops 4298113024 | bytes 57671944 | solution.py:75
  187.4 1.3 collective-permute-start
  188.7 25.4 %collective-permute-done = bf16[512,1024]{0,1:T(8,128)(2,1)S(1)} collective-permute-done((bf16[512,1024]{0,1:T(8,128)(2,1)S(1)}, bf16[512,1024]{0,1:T(8,128)(2,1)S(1)}, u32[]{:S(2)}, u32[]{:S(2)}) %collective-permute-start) | collective-permute-done | bytes 1048608 | tf_op jit(solution)/shard_map/while/body/eval_jaxpr/ppermute | solution.py:14
  214.1 1.1 broadcast_select_fusion.3
  215.3 9.3 %all-gather.9.cloned.1.call-done = bf16[512,2048]{0,1:T(8,128)(2,1)} async-done(((bf16[512,1024]{0,1:T(8,128)(2,1)}), bf16[512,2048]{0,1:T(8,128)(2,1)}) %all-gather.9.cloned.1.call-update) | async-done | bytes 2097168 | tf_op jit(solution)/shard_map/while/body/eval_jaxpr/all_gather | solution.py:52
  224.5 6.1 %fusion.30 = bf16[512,1024]{1,0:T(8,128)(2,1)} fusion(bf16[512,2048]{0,1:T(8,128)(2,1)} %all-gather.9.cloned.1.call-done, bf16[1,2048,1024]{2,1,0:T(8,128)(2,1)} %get-tuple-element.328), kind=kOutput, calls=%fused_computation.6.clone.1 | convolution fusion | flops 2148007936 | bytes 7340032 | tf_op jit(solution)/shard_map/while/body/eval_jaxpr/dot_general | solution.py:53
  230.7 82.1 %all-gather.11.cloned.1.call-done = bf16[2048,1024]{1,0:T(8,128)(2,1)} async-done(((bf16[512,1024]{1,0:T(8,128)(2,1)}), bf16[2048,1024]{1,0:T(8,128)(2,1)}) %all-gather.11.cloned.1.call-update) | async-done | bytes 4194320 | tf_op jit(solution)/shard_map/while/body/eval_jaxpr/all_gather | solution.py:67
  312.8 5.8 %fusion.31 = (bf16[512,1024]{0,1:T(8,128)(2,1)S(1)}, f32[512,1024]{0,1:T(8,128)S(1)}) fusion(bf16[2048,1024]{1,0:T(8,128)(2,1)} %all-gather.11.cloned.1.call-done, bf16[1,2048,512]{2,1,0:T(8,128)(2,1)} %get-tuple-element.329, f32[1,512,1024]{1,2,0:T(8,128)} %get-tuple-element.325), kind=kOutput, calls=%fused_computation.17.clone.1 | convolution fusion | flops 2148532224 | bytes 11534336 | tf_op jit(solution)/shard_map/while/body/eval_jaxpr/dot_general | solution.py:59
  318.6 0.7 bitcast_select_fusion.2
  319.4 1.3 collective-permute-start
  320.7 25.5 %collective-permute-done = bf16[512,1024]{0,1:T(8,128)(2,1)S(1)} collective-permute-done((bf16[512,1024]{0,1:T(8,128)(2,1)S(1)}, bf16[512,1024]{0,1:T(8,128)(2,1)S(1)}, u32[]{:S(2)}, u32[]{:S(2)}) %collective-permute-start) | collective-permute-done | bytes 1048608 | tf_op jit(solution)/shard_map/while/body/eval_jaxpr/ppermute | solution.py:14
  346.2 1.1 broadcast_select_fusion.3
  347.4 8.6 %all-gather.9.cloned.1.call-done = bf16[512,2048]{0,1:T(8,128)(2,1)} async-done(((bf16[512,1024]{0,1:T(8,128)(2,1)}), bf16[512,2048]{0,1:T(8,128)(2,1)}) %all-gather.9.cloned.1.call-update) | async-done | bytes 2097168 | tf_op jit(solution)/shard_map/while/body/eval_jaxpr/all_gather | solution.py:52
  356.0 6.1 %fusion.30 = bf16[512,1024]{1,0:T(8,128)(2,1)} fusion(bf16[512,2048]{0,1:T(8,128)(2,1)} %all-gather.9.cloned.1.call-done, bf16[1,2048,1024]{2,1,0:T(8,128)(2,1)} %get-tuple-element.328), kind=kOutput, calls=%fused_computation.6.clone.1 | convolution fusion | flops 2148007936 | bytes 7340032 | tf_op jit(solution)/shard_map/while/body/eval_jaxpr/dot_general | solution.py:53
  362.2 82.1 %all-gather.11.cloned.1.call-done = bf16[2048,1024]{1,0:T(8,128)(2,1)} async-done(((bf16[512,1024]{1,0:T(8,128)(2,1)}), bf16[2048,1024]{1,0:T(8,128)(2,1)}) %all-gather.11.cloned.1.call-update) | async-done | bytes 4194320 | tf_op jit(solution)/shard_map/while/body/eval_jaxpr/all_gather | solution.py:67
  444.2 5.8 %fusion.31 = (bf16[512,1024]{0,1:T(8,128)(2,1)S(1)}, f32[512,1024]{0,1:T(8,128)S(1)}) fusion(bf16[2048,1024]{1,0:T(8,128)(2,1)} %all-gather.11.cloned.1.call-done, bf16[1,2048,512]{2,1,0:T(8,128)(2,1)} %get-tuple-element.329, f32[1,512,1024]{1,2,0:T(8,128)} %get-tuple-element.325), kind=kOutput, calls=%fused_computation.17.clone.1 | convolution fusion | flops 2148532224 | bytes 11534336 | tf_op jit(solution)/shard_map/while/body/eval_jaxpr/dot_general | solution.py:59
  450.8 1.8 copy.6
  (24 shorter events, 2.4 us)
Async XLA Ops:
  6.5 85.9 %all-gather.5.cloned.1.call-start = ((), (), s32[]{:S(2)}) async-start(), calls=%async_computation | async-start | bytes 5242880 | tf_op jit(solution)/shard_map/all_gather | solution.py:35
  7.3 166.1 %all-gather.7.cloned.1.call-start = ((), (), s32[]{:S(2)}) async-start(), calls=%async_computation.1 | async-start | bytes 5242880 | tf_op jit(solution)/shard_map/all_gather | solution.py:34
  95.5 82.7 %collective-permute-start.1 = (bf16[1,2048,512]{2,1,0:T(8,128)(2,1)}, bf16[1,2048,512]{2,1,0:T(8,128)(2,1)}, u32[]{:S(2)}, u32[]{:S(2)}) collective-permute-start(bf16[1,2048,512]{2,1,0:T(8,128)(2,1)} %constant_dynamic-slice_fusion.1), channel_id=1, source_target_pairs={{0,1},{1,0},{2,3},{3,2},{4,5},{5,4},{6,7},{7,6},{8,9},{9,8},{10,11... | collective-permute-start | bytes 6291464 | tf_op jit(solution)/shard_map/ppermute | solution.py:8
  176.4 8.8 %collective-permute-start.2 = (bf16[1,2048,512]{2,1,0:T(8,128)(2,1)}, bf16[1,2048,512]{2,1,0:T(8,128)(2,1)}, u32[]{:S(2)}, u32[]{:S(2)}) collective-permute-start(bf16[1,2048,512]{2,1,0:T(8,128)(2,1)} %constant_dynamic-slice_fusion), channel_id=1, source_target_pairs={{0,1},{1,0},{2,3},{3,2},{4,5},{5,4},{6,7},{7,6},{8,9},{9,8},{10,11... | collective-permute-start | bytes 6291464 | tf_op jit(solution)/shard_map/ppermute | solution.py:8
  178.2 7.0 %copy-start = (bf16[512,1024]{0,1:T(8,128)(2,1)}, bf16[512,1024]{0,1:T(8,128)(2,1)S(1)}, u32[]{:S(2)}) copy-start(bf16[512,1024]{0,1:T(8,128)(2,1)S(1)} %copy.4) | copy-start | bytes 3145732
  178.2 7.0 %copy-start.2 = (bf16[1,2048,1024]{2,1,0:T(8,128)(2,1)S(1)}, bf16[1,2048,1024]{2,1,0:T(8,128)(2,1)}, u32[]{:S(2)}) copy-start(bf16[1,2048,1024]{2,1,0:T(8,128)(2,1)} %all-gather.7.cloned.1.call-done) | copy-start | bytes 12582916
  185.2 2.2 copy-start.1
  187.4 37.1 %all-gather.9.cloned.1.call-start = ((), (), s32[]{:S(2)}) async-start(), calls=%async_computation.2 | async-start | bytes 3145728 | tf_op jit(solution)/shard_map/while/body/eval_jaxpr/all_gather | solution.py:52
  187.4 26.7 %collective-permute-start = (bf16[512,1024]{0,1:T(8,128)(2,1)S(1)}, bf16[512,1024]{0,1:T(8,128)(2,1)S(1)}, u32[]{:S(2)}, u32[]{:S(2)}) collective-permute-start(bf16[512,1024]{0,1:T(8,128)(2,1)S(1)} %get-tuple-element.312), channel_id=1, source_target_pairs={{8,0},{9,1},{10,2},{11,3},{12,4},{13,5},{14,6},{15,7},{24,16},{25,... | collective-permute-start | bytes 3145736 | tf_op jit(solution)/shard_map/while/body/eval_jaxpr/ppermute | solution.py:14
  215.2 97.6 %all-gather.11.cloned.1.call-start = ((), (), s32[]{:S(2)}) async-start(), calls=%async_computation.3 | async-start | bytes 5242880 | tf_op jit(solution)/shard_map/while/body/eval_jaxpr/all_gather | solution.py:67
  319.4 36.6 %all-gather.9.cloned.1.call-start = ((), (), s32[]{:S(2)}) async-start(), calls=%async_computation.2 | async-start | bytes 3145728 | tf_op jit(solution)/shard_map/while/body/eval_jaxpr/all_gather | solution.py:52
  319.4 26.8 %collective-permute-start = (bf16[512,1024]{0,1:T(8,128)(2,1)S(1)}, bf16[512,1024]{0,1:T(8,128)(2,1)S(1)}, u32[]{:S(2)}, u32[]{:S(2)}) collective-permute-start(bf16[512,1024]{0,1:T(8,128)(2,1)S(1)} %get-tuple-element.312), channel_id=1, source_target_pairs={{8,0},{9,1},{10,2},{11,3},{12,4},{13,5},{14,6},{15,7},{24,16},{25,... | collective-permute-start | bytes 3145736 | tf_op jit(solution)/shard_map/while/body/eval_jaxpr/ppermute | solution.py:14
  347.3 96.9 %all-gather.11.cloned.1.call-start = ((), (), s32[]{:S(2)}) async-start(), calls=%async_computation.3 | async-start | bytes 5242880 | tf_op jit(solution)/shard_map/while/body/eval_jaxpr/all_gather | solution.py:67
Sparse Core Ops, SparseCore 0:
  8.9 83.4 all-gather.4
  94.0 79.2 all-gather.6
  215.3 9.1 all-gather.8
  230.8 81.9 all-gather.10
  347.4 8.4 all-gather.8
  362.3 81.9 all-gather.10
where the time goes:
time: 460 us; the launch traced here: 459 us
  waiting for transfers between devices  397 us (86%)
  matrix products  30.8 us (7%)
  between operations  13.5 us (3%)
  local copies, waits for them, and re-layouts  9.71 us (2%)
  other arithmetic  5.84 us (1%)
    all_gather x2, waiting for transfers between devices, run_segment(): lax.all_gather(image, 'row', axis=0, tiled=True)  164 us
    all_gather x1, waiting for transfers between devices, local(): lax.all_gather(inverses, 'row', axis=1, tiled=True)  84.4 us
    all_gather x1, waiting for transfers between devices, local(): lax.all_gather(factors, 'row', axis=1, tiled=True)  77.8 us
    ppermute x2, waiting for transfers between devices, passed_along(): lax.ppermute(value, axis, [(source, source + steps) for source in range(f...  50.9 us
    all_gather x2, waiting for transfers between devices, run_segment(): state_full = lax.all_gather(current, 'col', axis=1, tiled=True)  17.9 us
    dot_general x2, matrix products, run_segment(): jnp.dot(state_full, factor_full[0], preferred_element_type=jnp.float32)  12.3 us
    dot_general x2, matrix products, accumulate(): lax.dot_general(left_panel, incoming_rows, (((0,), (0,)), ((), ())), pref...  11.6 us
  transfers between devices with their start and end apart: 10, of which 8 were waited for; matrix products, arithmetic and copies ran while one was open for 3% of the time, Pallas kernels for 0%

commit v1 on v0

v1 whole, which is shorter than its diff:
```python
import jax
import jax.numpy as jnp
from jax import lax
from jax.sharding import PartitionSpec as P

CHUNKS = 2


def transposed_dot(left, right):
    return lax.dot_general(
        left, right, (((0,), (0,)), ((), ())), preferred_element_type=jnp.float32
    )


def dot(left, right):
    return jnp.dot(left, right, preferred_element_type=jnp.float32)


def exchanged(value, axis, steps):
    count = lax.axis_size(axis)
    return lax.ppermute(value, axis, [(i, (i + steps) % count) for i in range(count)])


def both_halves(own):
    col_size = lax.axis_size("col")
    col_index = lax.axis_index("col")
    pieces = [own] + [exchanged(own, "col", k) for k in range(1, col_size)]
    ordered = []
    for c in range(col_size):
        piece = pieces[0]
        for k in range(1, col_size):
            piece = jnp.where((col_index - k) % col_size == c, pieces[k], piece)
        ordered.append(piece)
    return jnp.concatenate(ordered, axis=-1)


def spread_over_sections(tile, width):
    sec_size = lax.axis_size("sec")
    sec_index = lax.axis_index("sec")

    def panel(array, offset):
        first = (sec_index + offset) % sec_size * width
        return lax.dynamic_slice_in_dim(array, first, width, 1)

    arrived = [(panel(tile, 0), tile)]
    for k in range(1, sec_size):
        pieces = [
            exchanged(panel(tile, (k + j) % sec_size), "sec", k) for j in range(sec_size)
        ]
        whole = jnp.zeros_like(tile)
        for j in range(sec_size):
            first = (sec_index + j) % sec_size * width
            whole = lax.dynamic_update_slice_in_dim(whole, pieces[j], first, 1)
        arrived.append((pieces[0], whole))

    panels, tiles = [], []
    for step in range(sec_size):
        chosen_panel, chosen_tile = arrived[0]
        for k in range(1, sec_size):
            here = (sec_index - k) % sec_size == step
            chosen_panel = jnp.where(here, arrived[k][0], chosen_panel)
            chosen_tile = jnp.where(here, arrived[k][1], chosen_tile)
        panels.append(chosen_panel)
        tiles.append(chosen_tile)
    return panels, tiles


def scattered_sum(partial, rows):
    row_size = lax.axis_size("row")
    row_index = lax.axis_index("row")

    def block(number):
        number = jnp.clip(number, 0, row_size - 1)
        return lax.dynamic_slice_in_dim(partial, number * rows, rows, 0)

    up = down = None
    for slot in range(row_size - 1):
        up_block = block(row_size - 1 - slot + row_index)
        down_block = block(row_index + slot - (row_size - 1))
        if slot:
            up_block = up_block + up
            down_block = down_block + down
        up = lax.ppermute(
            up_block.astype(jnp.bfloat16), "row", [(i, i + 1) for i in range(slot + 1)]
        ).astype(jnp.float32)
        down = lax.ppermute(
            down_block.astype(jnp.bfloat16),
            "row",
            [(i, i - 1) for i in range(row_size - 1 - slot, row_size)],
        ).astype(jnp.float32)
    return block(row_index) + up + down


def local(factors, inverses, sigma_end):
    row_size = lax.axis_size("row")
    sec_size = lax.axis_size("sec")
    sec_index = lax.axis_index("sec")
    step_count, rows, cols = factors.shape
    assert step_count == 1
    width = cols // sec_size
    chunk = width // CHUNKS

    factor_panels, factor_tiles = spread_over_sections(factors[0], width)
    gathered = {}
    for step in reversed(range(sec_size)):
        for part in range(CHUNKS):
            piece = factor_panels[step][:, part * chunk : (part + 1) * chunk]
            gathered[step, part] = lax.all_gather(piece, "row", axis=0, tiled=True)
    inverse_panels, inverse_tiles = spread_over_sections(inverses[0], width)

    state = both_halves(sigma_end.astype(jnp.bfloat16))
    output = jnp.zeros((rows, cols), jnp.float32)
    for step in reversed(range(sec_size)):
        factor_rows = both_halves(factor_tiles[step])
        inverse_rows = both_halves(inverse_tiles[step])
        summed = []
        for part in range(CHUNKS):
            inverse_piece = inverse_panels[step][:, part * chunk : (part + 1) * chunk]
            diagonal = transposed_dot(inverse_rows, inverse_piece)
            image = dot(state, gathered[step, part]).astype(jnp.bfloat16)
            partial = diagonal + transposed_dot(factor_rows, image)
            summed.append(scattered_sum(partial, rows).astype(jnp.bfloat16))
        panel = jnp.concatenate(summed, axis=1)
        tile = jnp.zeros((rows, cols), jnp.bfloat16)
        tile = lax.dynamic_update_slice_in_dim(tile, panel, sec_index * width, 1)
        for k in range(1, sec_size):
            other = exchanged(panel, "sec", k)
            first = (sec_index - k) % sec_size * width
            tile = lax.dynamic_update_slice_in_dim(tile, other, first, 1)
        output = jnp.where(sec_index == step, tile.astype(jnp.float32), output)
        if step:
            state = both_halves(tile)
    return output[None]


def solution(mesh):
    in_specs = (
        P(("groups", "sec"), "row", "col"),
        P(("groups", "sec"), "row", "col"),
        P(("groups", "row"), "col"),
    )
    out_specs = P(("groups", "sec"), "row", "col")
    return jax.shard_map(local, mesh=mesh, in_specs=in_specs, out_specs=out_specs, check_vma=False)
```

time: 460 us -> 281 us (0.61)
  waiting for transfers between devices: 397 us -> 101 us
  starting transfers between devices: 2.75 us -> 73.9 us
  other arithmetic: 5.84 us -> 42.7 us
    all_gather x6 -> x4, waiting for transfers between devices: 344 us -> 29.5 us  [local(): gathered[step, part] = lax.all_gather(piece, 'row', axis=0, tiled=True)]
    ppermute x4 -> x36, starting transfers between devices: 2.58 us -> 73.6 us  [the longest x12 49.1 us: scattered_sum(): lax.ppermute(up_block.astype(jnp.bfloat16), 'row', [(i, i + 1) for i in r...]
    ppermute x4 -> x36, waiting for transfers between devices: 50.9 us -> 71.6 us  [the longest x12 47.2 us: exchanged(): lax.ppermute(value, axis, [(i, (i + steps) % count) for i in range(count)])]
    select_n x5 -> x12, other arithmetic: 5.84 us -> 24.2 us  [the longest x6 16 us: both_halves(): piece = jnp.where((col_index - k) % col_size == c, pieces[k], piece)]
    convert_element_type x0 -> x17, other arithmetic: none -> 16.7 us  [the longest x8 7.61 us: scattered_sum(): up_block.astype(jnp.bfloat16)]
    dot_general x5 -> x8, matrix products: 30.8 us -> 35.1 us  [transposed_dot(): lax.dot_general(left, right, (((0,), (0,)), ((), ())), preferred_element_...]
  transfers between devices with their start and end apart: 10 -> 40, of which waited for: 8 -> 19; matrix products, arithmetic and copies ran while one was open for 3% -> 30% of each run, Pallas kernels for 0% -> 0%
where the time goes in v1:
time: 281 us; the launch traced here: 279 us
  waiting for transfers between devices  101 us (36%)
  starting transfers between devices  73.9 us (26%)
  other arithmetic  42.7 us (15%)
  matrix products  35.1 us (12%)
  between operations  13.8 us (5%)
  local copies, waits for them, and re-layouts  12.4 us (4%)
    ppermute x12, starting transfers between devices, scattered_sum(): lax.ppermute(up_block.astype(jnp.bfloat16), 'row', [(i, i + 1) for i in r...  49.1 us
    ppermute x12, waiting for transfers between devices, exchanged(): lax.ppermute(value, axis, [(i, (i + steps) % count) for i in range(count)])  47.2 us
    dot_general x8, matrix products, transposed_dot(): lax.dot_general(left, right, (((0,), (0,)), ((), ())), preferred_element_...  35.1 us
    all_gather x4, waiting for transfers between devices, local(): gathered[step, part] = lax.all_gather(piece, 'row', axis=0, tiled=True)  29.5 us
    select_n x6, other arithmetic, both_halves(): piece = jnp.where((col_index - k) % col_size == c, pieces[k], piece)  16 us
    ppermute x12, waiting for transfers between devices, scattered_sum(): lax.ppermute(down_block.astype(jnp.bfloat16), 'row', [(i, i - 1) for i in...  13.7 us
    ppermute x12, starting transfers between devices, scattered_sum(): lax.ppermute(down_block.astype(jnp.bfloat16), 'row', [(i, i - 1) for i in...  13.4 us
    ppermute x12, starting transfers between devices, exchanged(): lax.ppermute(value, axis, [(i, (i + steps) % count) for i in range(count)])  11.1 us
  transfers between devices with their start and end apart: 40, of which 19 were waited for; matrix products, arithmetic and copies ran while one was open for 30% of the time, Pallas kernels for 0%

profile of v1, /device:TPU:0, one launch (start us, length us, event | category | flops | bytes accessed | tf_op | source)
XLA Modules:
  0.0 279.0 jit_solution(14457117138462086276)
XLA Ops:
  14.4 9.1 %collective-permute-done.3 = bf16[512,512]{1,0:T(8,128)(2,1)S(1)} collective-permute-done((bf16[512,512]{1,0:T(8,128)(2,1)S(1)}, bf16[512,512]{1,0:T(8,128)(2,1)S(1)}, u32[]{:S(2)}, u32[]{:S(2)}) %collective-permute-start.3) | collective-permute-done | bytes 524320 | tf_op jit(solution)/shard_map/ppermute | solution.py:21
  29.1 5.8 %collective-permute-done = bf16[512,512]{1,0:T(8,128)(2,1)} collective-permute-done((bf16[512,512]{1,0:T(8,128)(2,1)}, bf16[512,512]{1,0:T(8,128)(2,1)}, u32[]{:S(2)}, u32[]{:S(2)}) %collective-permute-start) | collective-permute-done | bytes 524320 | tf_op jit(solution)/shard_map/ppermute | solution.py:21
  41.2 4.8 %collective-permute-done.4 = bf16[512,512]{1,0:T(8,128)(2,1)} collective-permute-done((bf16[512,512]{1,0:T(8,128)(2,1)}, bf16[512,512]{1,0:T(8,128)(2,1)}, u32[]{:S(2)}, u32[]{:S(2)}) %collective-permute-start.4) | collective-permute-done | bytes 524320 | tf_op jit(solution)/shard_map/ppermute | solution.py:21
  48.3 8.1 %collective-permute-done.1 = bf16[512,512]{1,0:T(8,128)(2,1)S(1)} collective-permute-done((bf16[512,512]{1,0:T(8,128)(2,1)S(1)}, bf16[512,512]{1,0:T(8,128)(2,1)S(1)}, u32[]{:S(2)}, u32[]{:S(2)}) %collective-permute-start.1) | collective-permute-done | bytes 524320 | tf_op jit(solution)/shard_map/ppermute | solution.py:21
  66.4 5.7 %fusion.5 = f32[2048,256]{0,1:T(8,128)} fusion(bf16[512,1024]{1,0:T(8,128)(2,1)S(1)} %get-tuple-element.40, bf16[512,1024]{1,0:T(8,128)(2,1)S(1)} %get-tuple-element.39, bf16[2048,256]{1,0:T(8,128)(2,1)} %all-gather.5.cloned.1.call-done, bf16[512,1024]{1,0:T(8,128)(2,1)} %get-tuple-element.38, bf16[512,1024]{1,0:T(8,128)(2,1)} %get-tuple-element.37), kind=kOutput, calls=%fused_computation.16 | convolution fusion | flops 1082261504 | bytes 7340032 | tf_op jit(solution)/shard_map/dot_general | solution.py:10
  75.6 4.4 %collective-permute-start.9 = (bf16[512,256]{0,1:T(8,128)(2,1)}, bf16[512,256]{0,1:T(8,128)(2,1)}, u32[]{:S(2)}, u32[]{:S(2)}) collective-permute-start(bf16[512,256]{0,1:T(8,128)(2,1)} %get-tuple-element.29), channel_id=1, source_target_pairs={{0,2},{1,3},{8,10},{9,11},{16,18},{17,19},{24,26},{25,27}} | collective-permute-start | bytes 786440 | tf_op jit(solution)/shard_map/ppermute | solution.py:83
  80.1 9.6 %all-gather.7.cloned.1.call-done = bf16[2048,256]{1,0:T(8,128)(2,1)} async-done(((bf16[512,256]{1,0:T(8,128)(2,1)}), bf16[2048,256]{1,0:T(8,128)(2,1)}) %all-gather.7.cloned.1.call-update) | async-done | bytes 1048592 | tf_op jit(solution)/shard_map/all_gather | solution.py:108
  89.7 6.2 %fusion.4 = f32[2048,256]{0,1:T(8,128)} fusion(bf16[512,1024]{1,0:T(8,128)(2,1)} %copy-done.13, bf16[512,1024]{1,0:T(8,128)(2,1)} %copy-done.12, bf16[2048,256]{1,0:T(8,128)(2,1)} %all-gather.7.cloned.1.call-done, bf16[512,1024]{1,0:T(8,128)(2,1)} %get-tuple-element.38, bf16[512,1024]{1,0:T(8,128)(2,1)} %get-tuple-element.37), kind=kOutput, calls=%fused_computation.15 | convolution fusion | flops 1082261504 | bytes 7340032 | tf_op jit(solution)/shard_map/dot_general | solution.py:10
  100.1 4.7 %collective-permute-start.15 = (bf16[512,256]{0,1:T(8,128)(2,1)S(1)}, bf16[512,256]{0,1:T(8,128)(2,1)S(1)}, u32[]{:S(2)}, u32[]{:S(2)}) collective-permute-start(bf16[512,256]{0,1:T(8,128)(2,1)S(1)} %get-tuple-element.33), channel_id=1, source_target_pairs={{0,2},{1,3},{8,10},{9,11},{16,18},{17,19},{24,26},{25,27}} | collective-permute-start | bytes 786440 | tf_op jit(solution)/shard_map/ppermute | solution.py:83
  112.5 4.4 %collective-permute-start.16 = (bf16[512,256]{0,1:T(8,128)(2,1)S(1)}, bf16[512,256]{0,1:T(8,128)(2,1)S(1)}, u32[]{:S(2)}, u32[]{:S(2)}) collective-permute-start(bf16[512,256]{0,1:T(8,128)(2,1)S(1)} %add_convert_fusion.14), channel_id=1, source_target_pairs={{0,2},{2,4},{1,3},{3,5},{8,10},{10,12},{9,11},{11,13},{16,18},{18,... | collective-permute-start | bytes 786440 | tf_op jit(solution)/shard_map/ppermute | solution.py:83
  124.9 5.2 %collective-permute-start.11 = (bf16[512,256]{0,1:T(8,128)(2,1)}, bf16[512,256]{0,1:T(8,128)(2,1)}, u32[]{:S(2)}, u32[]{:S(2)}) collective-permute-start(bf16[512,256]{0,1:T(8,128)(2,1)} %get-tuple-element.27), channel_id=1, source_target_pairs={{0,2},{2,4},{4,6},{1,3},{3,5},{5,7},{8,10},{10,12},{12,14},{9,11},... | collective-permute-start | bytes 786440 | tf_op jit(solution)/shard_map/ppermute | solution.py:83
  130.1 3.9 %collective-permute-start.17 = (bf16[512,256]{0,1:T(8,128)(2,1)}, bf16[512,256]{0,1:T(8,128)(2,1)S(1)}, u32[]{:S(2)}, u32[]{:S(2)}) collective-permute-start(bf16[512,256]{0,1:T(8,128)(2,1)} %get-tuple-element.31), channel_id=1, source_target_pairs={{0,2},{2,4},{4,6},{1,3},{3,5},{5,7},{8,10},{10,12},{12,14},{9,11},... | collective-permute-start | bytes 786440 | tf_op jit(solution)/shard_map/ppermute | solution.py:83
  141.4 5.7 %collective-permute-done.14 = bf16[512,256]{0,1:T(8,128)(2,1)} collective-permute-done((bf16[512,256]{0,1:T(8,128)(2,1)}, bf16[512,256]{0,1:T(8,128)(2,1)}, u32[]{:S(2)}, u32[]{:S(2)}) %collective-permute-start.14) | collective-permute-done | bytes 262176 | tf_op jit(solution)/shard_map/ppermute | solution.py:86
  152.9 9.7 %collective-permute-done.21 = bf16[512,512]{0,1:T(8,128)(2,1)} collective-permute-done((bf16[512,512]{0,1:T(8,128)(2,1)S(1)}, bf16[512,512]{0,1:T(8,128)(2,1)}, u32[]{:S(2)}, u32[]{:S(2)}) %collective-permute-start.21) | collective-permute-done | bytes 524320 | tf_op jit(solution)/shard_map/ppermute | solution.py:21
  174.3 5.9 %fusion.7 = f32[2048,256]{0,1:T(8,128)} fusion(bf16[512,1024]{1,0:T(8,128)(2,1)} %get-tuple-element.24, bf16[512,1024]{1,0:T(8,128)(2,1)S(1)} %get-tuple-element.23, bf16[2048,256]{1,0:T(8,128)(2,1)} %all-gather.9.cloned.1.call-done, bf16[512,1024]{1,0:T(8,128)(2,1)} %get-tuple-element.22, bf16[512,1024]{1,0:T(8,128)(2,1)} %get-tuple-element.21), kind=kOutput, calls=%fused_computation.18 | convolution fusion | flops 1082261504 | bytes 7340032 | tf_op jit(solution)/shard_map/dot_general | solution.py:10
  183.8 4.0 %collective-permute-start.23 = (bf16[512,256]{0,1:T(8,128)(2,1)}, bf16[512,256]{0,1:T(8,128)(2,1)}, u32[]{:S(2)}, u32[]{:S(2)}) collective-permute-start(bf16[512,256]{0,1:T(8,128)(2,1)} %get-tuple-element.11), channel_id=1, source_target_pairs={{0,2},{1,3},{8,10},{9,11},{16,18},{17,19},{24,26},{25,27}} | collective-permute-start | bytes 786440 | tf_op jit(solution)/shard_map/ppermute | solution.py:83
  187.8 18.1 %all-gather.11.cloned.1.call-done = bf16[2048,256]{1,0:T(8,128)(2,1)} async-done(((bf16[512,256]{1,0:T(8,128)(2,1)}), bf16[2048,256]{1,0:T(8,128)(2,1)}) %all-gather.11.cloned.1.call-update) | async-done | bytes 1048592 | tf_op jit(solution)/shard_map/all_gather | solution.py:108
  205.8 6.2 %fusion.6 = f32[2048,256]{0,1:T(8,128)} fusion(bf16[512,1024]{1,0:T(8,128)(2,1)} %get-tuple-element.24, bf16[512,1024]{1,0:T(8,128)(2,1)} %copy-done.11, bf16[2048,256]{1,0:T(8,128)(2,1)} %all-gather.11.cloned.1.call-done, bf16[512,1024]{1,0:T(8,128)(2,1)} %get-tuple-element.22, bf16[512,1024]{1,0:T(8,128)(2,1)} %get-tuple-element.21), kind=kOutput, calls=%fused_computation.17 | convolution fusion | flops 1082261504 | bytes 7340032 | tf_op jit(solution)/shard_map/dot_general | solution.py:10
  214.9 4.6 %collective-permute-start.29 = (bf16[512,256]{0,1:T(8,128)(2,1)S(1)}, bf16[512,256]{0,1:T(8,128)(2,1)S(1)}, u32[]{:S(2)}, u32[]{:S(2)}) collective-permute-start(bf16[512,256]{0,1:T(8,128)(2,1)S(1)} %get-tuple-element.15), channel_id=1, source_target_pairs={{0,2},{1,3},{8,10},{9,11},{16,18},{17,19},{24,26},{25,27}} | collective-permute-start | bytes 786440 | tf_op jit(solution)/shard_map/ppermute | solution.py:83
  226.3 4.4 %collective-permute-start.30 = (bf16[512,256]{0,1:T(8,128)(2,1)S(1)}, bf16[512,256]{0,1:T(8,128)(2,1)S(1)}, u32[]{:S(2)}, u32[]{:S(2)}) collective-permute-start(bf16[512,256]{0,1:T(8,128)(2,1)S(1)} %add_convert_fusion.4), channel_id=1, source_target_pairs={{0,2},{2,4},{1,3},{3,5},{8,10},{10,12},{9,11},{11,13},{16,18},{18,... | collective-permute-start | bytes 786440 | tf_op jit(solution)/shard_map/ppermute | solution.py:83
  237.3 5.0 %collective-permute-start.25 = (bf16[512,256]{0,1:T(8,128)(2,1)S(1)}, bf16[512,256]{0,1:T(8,128)(2,1)S(1)}, u32[]{:S(2)}, u32[]{:S(2)}) collective-permute-start(bf16[512,256]{0,1:T(8,128)(2,1)S(1)} %get-tuple-element.9), channel_id=1, source_target_pairs={{0,2},{2,4},{4,6},{1,3},{3,5},{5,7},{8,10},{10,12},{12,14},{9,11},... | collective-permute-start | bytes 786440 | tf_op jit(solution)/shard_map/ppermute | solution.py:83
  243.7 5.2 %collective-permute-start.31 = (bf16[512,256]{0,1:T(8,128)(2,1)S(1)}, bf16[512,256]{0,1:T(8,128)(2,1)S(1)}, u32[]{:S(2)}, u32[]{:S(2)}) collective-permute-start(bf16[512,256]{0,1:T(8,128)(2,1)S(1)} %get-tuple-element.13), channel_id=1, source_target_pairs={{0,2},{2,4},{4,6},{1,3},{3,5},{5,7},{8,10},{10,12},{12,14},{9,11},... | collective-permute-start | bytes 786440 | tf_op jit(solution)/shard_map/ppermute | solution.py:83
  253.2 4.4 %collective-permute-done.34 = bf16[512,256]{0,1:T(8,128)(2,1)S(1)} collective-permute-done((bf16[512,256]{0,1:T(8,128)(2,1)S(1)}, bf16[512,256]{0,1:T(8,128)(2,1)S(1)}, u32[]{:S(2)}, u32[]{:S(2)}) %collective-permute-start.34) | collective-permute-done | bytes 262176 | tf_op jit(solution)/shard_map/ppermute | solution.py:86
  259.7 9.7 %collective-permute-done.35 = bf16[512,512]{0,1:T(8,128)(2,1)} collective-permute-done((bf16[512,512]{0,1:T(8,128)(2,1)S(1)}, bf16[512,512]{0,1:T(8,128)(2,1)}, u32[]{:S(2)}, u32[]{:S(2)}) %collective-permute-start.35) | collective-permute-done | bytes 524320 | tf_op jit(solution)/shard_map/ppermute | solution.py:21
  (150 shorter events, 110.5 us)
Async XLA Ops:
  6.5 59.8 %all-gather.5.cloned.1.call-start = ((), (), s32[]{:S(2)}) async-start(), calls=%async_computation | async-start | bytes 1310720 | tf_op jit(solution)/shard_map/all_gather | solution.py:108
  7.7 15.8 %collective-permute-start.3 = (bf16[512,512]{1,0:T(8,128)(2,1)S(1)}, bf16[512,512]{1,0:T(8,128)(2,1)S(1)}, u32[]{:S(2)}, u32[]{:S(2)}) collective-permute-start(bf16[512,512]{1,0:T(8,128)(2,1)S(1)} %dynamic-slice_bitcast_fusion.1), channel_id=1, source_target_pairs={{0,8},{8,0},{1,9},{9,1},{2,10},{10,2},{3,11},{11,3},{4,12},{12,4},... | collective-permute-start | bytes 1572872 | tf_op jit(solution)/shard_map/ppermute | solution.py:21
  13.4 44.6 %collective-permute-start.8 = (bf16[512,1024]{1,0:T(8,128)(2,1)}, bf16[512,1024]{1,0:T(8,128)(2,1)}, u32[]{:S(2)}, u32[]{:S(2)}) collective-permute-start(bf16[512,1024]{1,0:T(8,128)(2,1)} %convert_element_type.177), channel_id=1, source_target_pairs={{0,1},{1,0},{2,3},{3,2},{4,5},{5,4},{6,7},{7,6},{8,9},{9,8},{10,11... | collective-permute-start | bytes 3145736 | tf_op jit(solution)/shard_map/ppermute | solution.py:21
  14.3 20.5 %collective-permute-start = (bf16[512,512]{1,0:T(8,128)(2,1)}, bf16[512,512]{1,0:T(8,128)(2,1)}, u32[]{:S(2)}, u32[]{:S(2)}) collective-permute-start(bf16[512,512]{1,0:T(8,128)(2,1)} %dynamic-slice_bitcast_fusion.3), channel_id=1, source_target_pairs={{0,8},{8,0},{1,9},{9,1},{2,10},{10,2},{3,11},{11,3},{4,12},{12,4},... | collective-permute-start | bytes 1572872 | tf_op jit(solution)/shard_map/ppermute | solution.py:21
  24.7 21.4 %collective-permute-start.4 = (bf16[512,512]{1,0:T(8,128)(2,1)}, bf16[512,512]{1,0:T(8,128)(2,1)}, u32[]{:S(2)}, u32[]{:S(2)}) collective-permute-start(bf16[512,512]{1,0:T(8,128)(2,1)} %get-tuple-element.8), channel_id=1, source_target_pairs={{0,8},{8,0},{1,9},{9,1},{2,10},{10,2},{3,11},{11,3},{4,12},{12,4},... | collective-permute-start | bytes 1572872 | tf_op jit(solution)/shard_map/ppermute | solution.py:21
  29.0 60.7 %all-gather.7.cloned.1.call-start = ((), (), s32[]{:S(2)}) async-start(), calls=%async_computation.1 | async-start | bytes 1310720 | tf_op jit(solution)/shard_map/all_gather | solution.py:108
  35.9 20.5 %collective-permute-start.1 = (bf16[512,512]{1,0:T(8,128)(2,1)S(1)}, bf16[512,512]{1,0:T(8,128)(2,1)S(1)}, u32[]{:S(2)}, u32[]{:S(2)}) collective-permute-start(bf16[512,512]{1,0:T(8,128)(2,1)S(1)} %get-tuple-element.6), channel_id=1, source_target_pairs={{0,8},{8,0},{1,9},{9,1},{2,10},{10,2},{3,11},{11,3},{4,12},{12,4},... | collective-permute-start | bytes 1572872 | tf_op jit(solution)/shard_map/ppermute | solution.py:21
  48.3 13.3 %collective-permute-start.7 = (bf16[512,1024]{1,0:T(8,128)(2,1)S(1)}, bf16[512,1024]{1,0:T(8,128)(2,1)}, u32[]{:S(2)}, u32[]{:S(2)}) collective-permute-start(bf16[512,1024]{1,0:T(8,128)(2,1)S(1)} %get-tuple-element.26), channel_id=1, source_target_pairs={{0,1},{1,0},{2,3},{3,2},{4,5},{5,4},{6,7},{7,6},{8,9},{9,8},{10,11... | collective-permute-start | bytes 3145736 | tf_op jit(solution)/shard_map/ppermute | solution.py:21
  58.0 116.3 %all-gather.9.cloned.1.call-start = ((), (), s32[]{:S(2)}) async-start(), calls=%async_computation.2 | async-start | bytes 1310720 | tf_op jit(solution)/shard_map/all_gather | solution.py:108
  75.6 30.5 %collective-permute-start.9 = (bf16[512,256]{0,1:T(8,128)(2,1)}, bf16[512,256]{0,1:T(8,128)(2,1)}, u32[]{:S(2)}, u32[]{:S(2)}) collective-permute-start(bf16[512,256]{0,1:T(8,128)(2,1)} %get-tuple-element.29), channel_id=1, source_target_pairs={{0,2},{1,3},{8,10},{9,11},{16,18},{17,19},{24,26},{25,27}} | collective-permute-start | bytes 786440 | tf_op jit(solution)/shard_map/ppermute | solution.py:83
  104.7 12.2 %collective-permute-start.12 = (bf16[512,256]{0,1:T(8,128)(2,1)S(1)}, bf16[512,256]{0,1:T(8,128)(2,1)}, u32[]{:S(2)}, u32[]{:S(2)}) collective-permute-start(bf16[512,256]{0,1:T(8,128)(2,1)S(1)} %get-tuple-element.30), channel_id=1, source_target_pairs={{6,4},{7,5},{14,12},{15,13},{22,20},{23,21},{30,28},{31,29}} | collective-permute-start | bytes 786440 | tf_op jit(solution)/shard_map/ppermute | solution.py:86
  109.1 11.4 %collective-permute-start.18 = (bf16[512,256]{0,1:T(8,128)(2,1)S(1)}, bf16[512,256]{0,1:T(8,128)(2,1)}, u32[]{:S(2)}, u32[]{:S(2)}) collective-permute-start(bf16[512,256]{0,1:T(8,128)(2,1)S(1)} %get-tuple-element.34), channel_id=1, source_target_pairs={{6,4},{7,5},{14,12},{15,13},{22,20},{23,21},{30,28},{31,29}} | collective-permute-start | bytes 786440 | tf_op jit(solution)/shard_map/ppermute | solution.py:86
  119.1 14.9 %collective-permute-start.13 = (bf16[512,256]{0,1:T(8,128)(2,1)}, bf16[512,256]{0,1:T(8,128)(2,1)}, u32[]{:S(2)}, u32[]{:S(2)}) collective-permute-start(bf16[512,256]{0,1:T(8,128)(2,1)} %get-tuple-element.28), channel_id=1, source_target_pairs={{4,2},{6,4},{5,3},{7,5},{12,10},{14,12},{13,11},{15,13},{20,18},{2... | collective-permute-start | bytes 786440 | tf_op jit(solution)/shard_map/ppermute | solution.py:86
  123.4 13.6 %collective-permute-start.19 = (bf16[512,256]{0,1:T(8,128)(2,1)}, bf16[512,256]{0,1:T(8,128)(2,1)}, u32[]{:S(2)}, u32[]{:S(2)}) collective-permute-start(bf16[512,256]{0,1:T(8,128)(2,1)} %get-tuple-element.32), channel_id=1, source_target_pairs={{4,2},{6,4},{5,3},{7,5},{12,10},{14,12},{13,11},{15,13},{20,18},{2... | collective-permute-start | bytes 786440 | tf_op jit(solution)/shard_map/ppermute | solution.py:86
  124.9 16.5 %collective-permute-start.11 = (bf16[512,256]{0,1:T(8,128)(2,1)}, bf16[512,256]{0,1:T(8,128)(2,1)}, u32[]{:S(2)}, u32[]{:S(2)}) collective-permute-start(bf16[512,256]{0,1:T(8,128)(2,1)} %get-tuple-element.27), channel_id=1, source_target_pairs={{0,2},{2,4},{4,6},{1,3},{3,5},{5,7},{8,10},{10,12},{12,14},{9,11},... | collective-permute-start | bytes 786440 | tf_op jit(solution)/shard_map/ppermute | solution.py:83
  130.1 18.1 %collective-permute-start.17 = (bf16[512,256]{0,1:T(8,128)(2,1)}, bf16[512,256]{0,1:T(8,128)(2,1)S(1)}, u32[]{:S(2)}, u32[]{:S(2)}) collective-permute-start(bf16[512,256]{0,1:T(8,128)(2,1)} %get-tuple-element.31), channel_id=1, source_target_pairs={{0,2},{2,4},{4,6},{1,3},{3,5},{5,7},{8,10},{10,12},{12,14},{9,11},... | collective-permute-start | bytes 786440 | tf_op jit(solution)/shard_map/ppermute | solution.py:83
  141.1 64.8 %all-gather.11.cloned.1.call-start = ((), (), s32[]{:S(2)}) async-start(), calls=%async_computation.3 | async-start | bytes 1310720 | tf_op jit(solution)/shard_map/all_gather | solution.py:108
  141.3 22.7 %collective-permute-start.5 = (bf16[512,1024]{1,0:T(8,128)(2,1)S(1)}, bf16[512,1024]{1,0:T(8,128)(2,1)}, u32[]{:S(2)}, u32[]{:S(2)}) collective-permute-start(bf16[512,1024]{1,0:T(8,128)(2,1)S(1)} %copy-done.5), channel_id=1, source_target_pairs={{0,1},{1,0},{2,3},{3,2},{4,5},{5,4},{6,7},{7,6},{8,9},{9,8},{10,11... | collective-permute-start | bytes 3145736 | tf_op jit(solution)/shard_map/ppermute | solution.py:21
  151.2 11.4 %collective-permute-start.21 = (bf16[512,512]{0,1:T(8,128)(2,1)S(1)}, bf16[512,512]{0,1:T(8,128)(2,1)}, u32[]{:S(2)}, u32[]{:S(2)}) collective-permute-start(bf16[512,512]{0,1:T(8,128)(2,1)S(1)} %pad_maximum_fusion.34), channel_id=1, source_target_pairs={{0,8},{8,0},{1,9},{9,1},{2,10},{10,2},{3,11},{11,3},{4,12},{12,4},... | collective-permute-start | bytes 1572872 | tf_op jit(solution)/shard_map/ppermute | solution.py:21
  152.5 14.2 %collective-permute-start.2 = (bf16[512,1024]{1,0:T(8,128)(2,1)}, bf16[512,1024]{1,0:T(8,128)(2,1)}, u32[]{:S(2)}, u32[]{:S(2)}) collective-permute-start(bf16[512,1024]{1,0:T(8,128)(2,1)} %get-tuple-element.19), channel_id=1, source_target_pairs={{0,1},{1,0},{2,3},{3,2},{4,5},{5,4},{6,7},{7,6},{8,9},{9,8},{10,11... | collective-permute-start | bytes 3145736 | tf_op jit(solution)/shard_map/ppermute | solution.py:21
  183.8 36.5 %collective-permute-start.23 = (bf16[512,256]{0,1:T(8,128)(2,1)}, bf16[512,256]{0,1:T(8,128)(2,1)}, u32[]{:S(2)}, u32[]{:S(2)}) collective-permute-start(bf16[512,256]{0,1:T(8,128)(2,1)} %get-tuple-element.11), channel_id=1, source_target_pairs={{0,2},{1,3},{8,10},{9,11},{16,18},{17,19},{24,26},{25,27}} | collective-permute-start | bytes 786440 | tf_op jit(solution)/shard_map/ppermute | solution.py:83
  236.6 12.3 %collective-permute-start.33 = (bf16[512,256]{0,1:T(8,128)(2,1)S(1)}, bf16[512,256]{0,1:T(8,128)(2,1)S(1)}, u32[]{:S(2)}, u32[]{:S(2)}) collective-permute-start(bf16[512,256]{0,1:T(8,128)(2,1)S(1)} %get-tuple-element.14), channel_id=1, source_target_pairs={{4,2},{6,4},{5,3},{7,5},{12,10},{14,12},{13,11},{15,13},{20,18},{2... | collective-permute-start | bytes 786440 | tf_op jit(solution)/shard_map/ppermute | solution.py:86
  237.3 13.0 %collective-permute-start.25 = (bf16[512,256]{0,1:T(8,128)(2,1)S(1)}, bf16[512,256]{0,1:T(8,128)(2,1)S(1)}, u32[]{:S(2)}, u32[]{:S(2)}) collective-permute-start(bf16[512,256]{0,1:T(8,128)(2,1)S(1)} %get-tuple-element.9), channel_id=1, source_target_pairs={{0,2},{2,4},{4,6},{1,3},{3,5},{5,7},{8,10},{10,12},{12,14},{9,11},... | collective-permute-start | bytes 786440 | tf_op jit(solution)/shard_map/ppermute | solution.py:83
  257.8 11.6 %collective-permute-start.35 = (bf16[512,512]{0,1:T(8,128)(2,1)S(1)}, bf16[512,512]{0,1:T(8,128)(2,1)}, u32[]{:S(2)}, u32[]{:S(2)}) collective-permute-start(bf16[512,512]{0,1:T(8,128)(2,1)S(1)} %pad_maximum_fusion.35), channel_id=1, source_target_pairs={{0,8},{8,0},{1,9},{9,1},{2,10},{10,2},{3,11},{11,3},{4,12},{12,4},... | collective-permute-start | bytes 1572872 | tf_op jit(solution)/shard_map/ppermute | solution.py:21
  (30 other events, 260.9 us)
Sparse Core Ops, SparseCore 0:
  29.1 28.3 all-gather.4
  59.1 30.5 all-gather.6
  141.2 33.0 all-gather.8
  175.7 30.1 all-gather.10

commit v2 on v0

v2 whole, which is shorter than its diff:
```python
import functools

import jax
import jax.numpy as jnp
from jax import lax
from jax.experimental import pallas as pl
from jax.experimental.pallas import tpu as pltpu
from jax.sharding import PartitionSpec as P

CHUNKS = 2
ANY = pl.BlockSpec(memory_space=pl.ANY)
VMEM = pl.BlockSpec(memory_space=pltpu.VMEM)
PARAMS = pltpu.CompilerParams(vmem_limit_bytes=32 * 1024 * 1024)


def exchanged(value, axis, steps):
    count = lax.axis_size(axis)
    return lax.ppermute(value, axis, [(i, (i + steps) % count) for i in range(count)])


class Sizes:
    def __init__(self, rows, cols):
        self.row = lax.axis_size("row")
        self.sec = lax.axis_size("sec")
        self.col = lax.axis_size("col")
        self.rows = rows
        self.cols = cols
        self.order = cols * self.col
        self.width = cols // self.sec
        self.chunk = self.width // CHUNKS
        self.per_tile = self.row // self.col


def chosen_copies(sizes, step, tiles, target, sems):
    sec_index, col_index = lax.axis_index("sec"), lax.axis_index("col")
    copies = []
    for kc in range(sizes.col):
        place = lax.rem(col_index - kc + sizes.col, sizes.col)
        for kx in range(sizes.sec):
            copy = pltpu.make_async_copy(tiles[kx][kc], target.at[place], sems.at[kc])
            wanted = lax.rem(sec_index - kx + sizes.sec, sizes.sec) == step
            copies.append((wanted, copy))
    return copies


def start_all(copies):
    for wanted, copy in copies:
        pl.when(wanted)(copy.start)


def wait_all(copies):
    for wanted, copy in copies:
        pl.when(wanted)(copy.wait)


def nested(refs, sizes):
    return [refs[kx * sizes.col : (kx + 1) * sizes.col] for kx in range(sizes.sec)]


def diagonal_kernel(sizes, step, *refs):
    count = sizes.sec * sizes.col
    tiles, (out, held, sems) = nested(refs[:count], sizes), refs[count:]
    copies = chosen_copies(sizes, step, tiles, held, sems)
    start_all(copies)
    wait_all(copies)
    first = lax.axis_index("sec") * sizes.width
    for k in range(CHUNKS):
        begin = pl.multiple_of(first + k * sizes.chunk, sizes.chunk)
        left = held[lax.axis_index("col"), :, pl.ds(begin, sizes.chunk)].T
        for d in range(sizes.row):
            h, i = divmod(d, sizes.per_tile)
            right = held[h, :, i * sizes.rows : (i + 1) * sizes.rows]
            out[k, d] = jnp.dot(left, right, preferred_element_type=jnp.float32)


def diagonal(sizes, step, tiles):
    flat = [tile for per_section in tiles for tile in per_section]
    shape = (CHUNKS, sizes.row, sizes.chunk, sizes.rows)
    return pl.pallas_call(
        functools.partial(diagonal_kernel, sizes, step),
        out_shape=jax.ShapeDtypeStruct(shape, jnp.float32),
        in_specs=[ANY] * len(flat),
        out_specs=VMEM,
        scratch_shapes=[
            pltpu.VMEM((sizes.col, sizes.rows, sizes.cols), jnp.bfloat16),
            pltpu.SemaphoreType.DMA((sizes.col,)),
        ],
        compiler_params=PARAMS,
        cost_estimate=pl.CostEstimate(
            flops=2 * sizes.rows * sizes.width * sizes.order,
            bytes_accessed=2 * sizes.rows * sizes.order + 4 * sizes.width * sizes.order,
            transcendentals=0,
        ),
        name="diagonal",
    )(*flat)


def panel_kernel(sizes, step, offset, own, *refs):
    *sent, out, held, sem = refs
    sec_index = lax.axis_index("sec")
    count = out.shape[0]
    begin = pl.multiple_of(sec_index * sizes.width + offset, sizes.chunk)
    copies = [(sec_index == step, pltpu.make_async_copy(own.at[:, pl.ds(begin, count)], held, sem))]
    per_section = len(sent) // (sizes.sec - 1)
    for kx in range(1, sizes.sec):
        wanted = lax.rem(sec_index - kx + sizes.sec, sizes.sec) == step
        pieces = sent[(kx - 1) * per_section : kx * per_section]
        height = count // per_section
        for k, piece in enumerate(pieces):
            target = held.at[:, k * height : (k + 1) * height]
            copies.append((wanted, pltpu.make_async_copy(piece, target, sem)))
    start_all(copies)
    wait_all(copies)
    out[...] = held[...].T


def transposed_panel(sizes, step, own, sent, part=None):
    count = sizes.width if part is None else sizes.chunk
    offset = 0 if part is None else part * sizes.chunk
    flat = [piece for pieces in sent for piece in pieces]
    return pl.pallas_call(
        functools.partial(panel_kernel, sizes, step, offset),
        out_shape=jax.ShapeDtypeStruct((count, sizes.rows), jnp.bfloat16),
        in_specs=[ANY] * (1 + len(flat)),
        out_specs=VMEM,
        scratch_shapes=[
            pltpu.VMEM((sizes.rows, count), jnp.bfloat16),
            pltpu.SemaphoreType.DMA,
        ],
        compiler_params=PARAMS,
        name="panel",
    )(own, *flat)


def products_kernel(sizes, step, part, block_shifts, state_places, *refs):
    n_blocks, n_states, n_tiles = len(block_shifts), len(state_places), sizes.sec * sizes.col
    blocks, refs = refs[:n_blocks], refs[n_blocks:]
    states, refs = refs[:n_states], refs[n_states:]
    tiles, refs = nested(refs[:n_tiles], sizes), refs[n_tiles:]
    diagonals, out, state, rows, added, tile_sems, state_sems, added_sem = refs
    row_index, sec_index, col_index = (lax.axis_index(a) for a in ("row", "sec", "col"))

    state_copies = []
    for number, (kx, kc, offset) in enumerate(state_places):
        first = lax.rem(col_index - kc + sizes.col, sizes.col) * sizes.cols + offset
        if kx is not None:
            first = first + lax.rem(sec_index - kx + sizes.sec, sizes.sec) * sizes.width
        height = states[number].shape[0]
        place = state.at[pl.ds(pl.multiple_of(first, height), height)]
        state_copies.append(pltpu.make_async_copy(states[number], place, state_sems.at[number]))
    for copy in state_copies:
        copy.start()
    tile_copies = chosen_copies(sizes, step, tiles, rows, tile_sems)
    start_all(tile_copies)
    added_copy = pltpu.make_async_copy(diagonals.at[part], added, added_sem)
    added_copy.start()
    for copy in state_copies:
        copy.wait()

    out[0] = jnp.zeros((sizes.chunk, sizes.rows), jnp.float32)
    for number, shift in enumerate(block_shifts):
        def accumulate(block, q):
            first = pl.multiple_of(q * sizes.rows, sizes.rows)
            out[0] += jnp.dot(
                block, state[pl.ds(first, sizes.rows)], preferred_element_type=jnp.float32
            )

        if shift is None:
            for q in range(sizes.row):
                accumulate(blocks[number][q, part * sizes.chunk : (part + 1) * sizes.chunk], q)
        else:
            q = row_index + shift
            pl.when((q >= 0) & (q < sizes.row))(
                functools.partial(lambda ref, q: accumulate(ref[...], q), blocks[number], q)
            )
    image = out[0].astype(jnp.bfloat16)
    wait_all(tile_copies)
    added_copy.wait()
    for d in range(sizes.row):
        h, i = divmod(d, sizes.per_tile)
        right = rows[h, :, i * sizes.rows : (i + 1) * sizes.rows]
        out[d] = jnp.dot(image, right, preferred_element_type=jnp.float32) + added[d]


def products(sizes, step, part, blocks, states, tiles, diagonals):
    flat = [tile for per_section in tiles for tile in per_section]
    shape = (sizes.row, sizes.chunk, sizes.rows)
    return pl.pallas_call(
        functools.partial(
            products_kernel, sizes, step, part, [b[0] for b in blocks], [s[0] for s in states]
        ),
        out_shape=jax.ShapeDtypeStruct(shape, jnp.float32),
        in_specs=[VMEM] * len(blocks) + [ANY] * (len(states) + len(flat) + 1),
        out_specs=VMEM,
        scratch_shapes=[
            pltpu.VMEM((sizes.order, sizes.rows), jnp.bfloat16),
            pltpu.VMEM((sizes.col, sizes.rows, sizes.cols), jnp.bfloat16),
            pltpu.VMEM(shape, jnp.float32),
            pltpu.SemaphoreType.DMA((sizes.col,)),
            pltpu.SemaphoreType.DMA((len(states),)),
            pltpu.SemaphoreType.DMA,
        ],
        compiler_params=PARAMS,
        cost_estimate=pl.CostEstimate(
            flops=4 * sizes.rows * sizes.chunk * sizes.order,
            bytes_accessed=4 * sizes.rows * sizes.order + 10 * sizes.chunk * sizes.order,
            transcendentals=0,
        ),
        name="products",
    )(*[b[1] for b in blocks], *[s[1] for s in states], *flat, diagonals)


def output_kernel(sizes, *refs):
    per_step = sizes.sec * CHUNKS
    out = refs[-1]
    sec_index = lax.axis_index("sec")
    for step in range(sizes.sec):

        @pl.when(sec_index == step)
        def _():
            for kx in range(sizes.sec):
                for k in range(CHUNKS):
                    piece = refs[step * per_step + kx * CHUNKS + k][...]
                    first = lax.rem(sec_index - kx + sizes.sec, sizes.sec) * sizes.width
                    begin = pl.multiple_of(first + k * sizes.chunk, sizes.chunk)
                    out[:, pl.ds(begin, sizes.chunk)] = piece.astype(jnp.float32).T


def output(sizes, pieces):
    return pl.pallas_call(
        functools.partial(output_kernel, sizes),
        out_shape=jax.ShapeDtypeStruct((sizes.rows, sizes.cols), jnp.float32),
        in_specs=[VMEM] * len(pieces),
        out_specs=VMEM,
        compiler_params=PARAMS,
        name="output",
    )(*pieces)


def neighbours_gathered(sizes, block):
    up = down = block
    found = [(0, block)]
    for slot in range(sizes.row - 1):
        up = lax.ppermute(up, "row", [(i, i + 1) for i in range(slot, sizes.row - 1)])
        down = lax.ppermute(down, "row", [(i, i - 1) for i in range(1, sizes.row - slot)])
        found += [(-1 - slot, up), (1 + slot, down)]
    return found


def scattered_sum(sizes, partial):
    row_index = lax.axis_index("row")

    def block(number):
        number = jnp.clip(number, 0, sizes.row - 1)
        return lax.dynamic_index_in_dim(partial, number, 0, keepdims=False)

    up = down = None
    last = sizes.row - 1
    for slot in range(last):
        up_block = block(last - slot + row_index)
        down_block = block(row_index + slot - last)
        if slot:
            up_block = up_block + up.astype(jnp.float32)
            down_block = down_block + down.astype(jnp.float32)
        up = lax.ppermute(
            up_block.astype(jnp.bfloat16), "row", [(i, i + 1) for i in range(slot + 1)]
        )
        down = lax.ppermute(
            down_block.astype(jnp.bfloat16), "row", [(i, i - 1) for i in range(last - slot, last + 1)]
        )
    total = block(row_index) + up.astype(jnp.float32) + down.astype(jnp.float32)
    return total.astype(jnp.bfloat16)


def local(factors, inverses, sigma_end):
    step_count, rows, cols = factors.shape
    assert step_count == 1
    sizes = Sizes(rows, cols)
    sec_size, col_size, width, chunk = sizes.sec, sizes.col, sizes.width, sizes.chunk
    sec_index = lax.axis_index("sec")

    def panel(tile, offset, part=None):
        first = (sec_index + offset) % sec_size * width
        if part is None:
            return lax.dynamic_slice_in_dim(tile, first, width, 1)
        return lax.dynamic_slice_in_dim(tile, first + part * chunk, chunk, 1)

    factor, inverse = factors[0], inverses[0]

    arrived_chunks = [None]
    for kx in range(1, sec_size):
        arrived_chunks.append(
            [exchanged(panel(factor, kx, part), "sec", kx) for part in range(CHUNKS)]
        )

    factor_blocks = {}
    last = sec_size - 1
    for part in range(CHUNKS):
        sent = [[chunks[part]] for chunks in arrived_chunks[1:]]
        block = transposed_panel(sizes, last, factor, sent, part)
        factor_blocks[last, part] = neighbours_gathered(sizes, block)
    for step in reversed(range(last)):
        block = transposed_panel(sizes, step, factor, arrived_chunks[1:])
        whole = lax.all_gather(block, "row", axis=0)
        for part in range(CHUNKS):
            factor_blocks[step, part] = [(None, whole)]

    def tiles_over_sections(tile, first_chunks):
        found = [tile]
        for kx in range(1, sec_size):
            whole = jnp.zeros_like(tile)
            for j in range(sec_size):
                if j == 0 and first_chunks is not None:
                    piece = jnp.concatenate(first_chunks[kx], axis=1)
                else:
                    piece = exchanged(panel(tile, kx + j), "sec", kx)
                first = (sec_index + j) % sec_size * width
                whole = lax.dynamic_update_slice_in_dim(whole, piece, first, 1)
            found.append(whole)
        return found

    def over_columns(value):
        return [value] + [exchanged(value, "col", kc) for kc in range(1, col_size)]

    state_pieces = [
        ((None, kc, 0), piece)
        for kc, piece in enumerate(over_columns(sigma_end.astype(jnp.bfloat16).T))
    ]
    factor_tiles = [over_columns(tile) for tile in tiles_over_sections(factor, arrived_chunks)]
    inverse_tiles = [
        over_columns(tile)
        for tile in [inverse] + [exchanged(inverse, "sec", kx) for kx in range(1, sec_size)]
    ]

    results = {}
    for step in reversed(range(sec_size)):
        diagonals = diagonal(sizes, step, inverse_tiles)
        next_pieces = []
        for part in range(CHUNKS):
            partial = products(
                sizes, step, part, factor_blocks[step, part], state_pieces, factor_tiles, diagonals
            )
            total = scattered_sum(sizes, partial)
            for kx in range(sec_size):
                piece = exchanged(total, "sec", kx) if kx else total
                results[step, kx, part] = piece
                if step:
                    for kc, moved in enumerate(over_columns(piece)):
                        next_pieces.append(((kx, kc, part * chunk), moved))
        state_pieces = next_pieces

    return output(
        sizes,
        [
            results[step, kx, part]
            for step in range(sec_size)
            for kx in range(sec_size)
            for part in range(CHUNKS)
        ],
    )[None]


def solution(mesh):
    in_specs = (
        P(("groups", "sec"), "row", "col"),
        P(("groups", "sec"), "row", "col"),
        P(("groups", "row"), "col"),
    )
    out_specs = P(("groups", "sec"), "row", "col")
    return jax.shard_map(local, mesh=mesh, in_specs=in_specs, out_specs=out_specs, check_vma=False)
```

time: 460 us -> 271 us (0.59)
  waiting for transfers between devices: 397 us -> 94.1 us
  starting transfers between devices: 2.75 us -> 97.4 us
  matrix products: 30.8 us -> 0 us
  Pallas kernels: 0 us -> 24.3 us
  local copies, waits for them, and re-layouts: 9.71 us -> 24.4 us
  other arithmetic: 5.84 us -> 15.4 us
    all_gather x6 -> x1, waiting for transfers between devices: 344 us -> 0.01 us  [local(): whole = lax.all_gather(block, 'row', axis=0)]
    ppermute x4 -> x53, starting transfers between devices: 2.58 us -> 97.4 us  [the longest x12 50.7 us: scattered_sum(): lax.ppermute(up_block.astype(jnp.bfloat16), 'row', [(i, i + 1) for i in r...]
    ppermute x4 -> x53, waiting for transfers between devices: 50.9 us -> 94 us  [the longest x17 46.6 us: exchanged(): lax.ppermute(value, axis, [(i, (i + steps) % count) for i in range(count)])]
    dot_general x5 -> x0, matrix products: 30.8 us -> none  [the longest x2 12.3 us: run_segment(): jnp.dot(state_full, factor_full[0], preferred_element_type=jnp.float32)]
    pallas_call x0 -> x10, Pallas kernels: none -> 24.3 us  [the longest x4 15.3 us: products(): pl.pallas_call(functools.partial(products_kernel, sizes, step, part, [b[0...]
    unnamed x7 -> x61, local copies, waits for them, and re-layouts: 1.78 us -> 19.2 us
    convert_element_type x0 -> x16, other arithmetic: none -> 15.4 us  [the longest x8 8.57 us: scattered_sum(): up_block.astype(jnp.bfloat16)]
    select_n x5 -> x0, other arithmetic: 5.84 us -> none  [the longest x1 2.2 us: local(): factor_left = jnp.where(owns_panel, local_pair[0], partner_pair[0])]
  transfers between devices with their start and end apart: 10 -> 54, of which waited for: 8 -> 19; matrix products, arithmetic and copies ran while one was open for 3% -> 8% of each run, Pallas kernels for 0% -> 7%
where the time goes in v2:
time: 271 us; the launch traced here: 270 us
  starting transfers between devices  97.4 us (36%)
  waiting for transfers between devices  94.1 us (35%)
  local copies, waits for them, and re-layouts  24.4 us (9%)
  Pallas kernels  24.3 us (9%)
  other arithmetic  15.4 us (6%)
  between operations  14.2 us (5%)
    ppermute x12, starting transfers between devices, scattered_sum(): lax.ppermute(up_block.astype(jnp.bfloat16), 'row', [(i, i + 1) for i in r...  50.7 us
    ppermute x17, waiting for transfers between devices, exchanged(): lax.ppermute(value, axis, [(i, (i + steps) % count) for i in range(count)])  46.6 us
    ppermute x12, waiting for transfers between devices, scattered_sum(): lax.ppermute(up_block.astype(jnp.bfloat16), 'row', [(i, i + 1) for i in r...  22.1 us
    unnamed x61, local copies, waits for them, and re-layouts  19.2 us
    pallas_call x4, Pallas kernels, products(): pl.pallas_call(functools.partial(products_kernel, sizes, step, part, [b[0...  15.3 us
    ppermute x6, waiting for transfers between devices, neighbours_gathered(): lax.ppermute(down, 'row', [(i, i - 1) for i in range(1, sizes.row - slot)])  14.9 us
    ppermute x12, starting transfers between devices, scattered_sum(): lax.ppermute(down_block.astype(jnp.bfloat16), 'row', [(i, i - 1) for i in...  13.3 us
    ppermute x17, starting transfers between devices, exchanged(): lax.ppermute(value, axis, [(i, (i + steps) % count) for i in range(count)])  12.9 us
  transfers between devices with their start and end apart: 54, of which 19 were waited for; matrix products, arithmetic and copies ran while one was open for 8% of the time, Pallas kernels for 7%

profile of v2, /device:TPU:0, one launch (start us, length us, event | category | flops | bytes accessed | tf_op | source)
XLA Modules:
  0.0 269.8 jit_solution(5492594791726204693)
XLA Ops:
  14.0 3.9 %collective-permute-done.1.refs_1_.refs_0_ = bf16[512,256]{1,0:T(8,128)(2,1)S(1)} collective-permute-done((bf16[512,256]{1,0:T(8,128)(2,1)S(1)}, bf16[512,256]{1,0:T(8,128)(2,1)S(1)}, u32[]{:S(2)}, u32[]{:S(2)}) %collective-permute-start.1) | collective-permute-done | bytes 262176 | tf_op jit(solution)/shard_map/ppermute | solution.py:18
  18.0 4.1 %collective-permute-start.24 = (bf16[256,512]{1,0:T(8,128)(2,1)S(1)}, bf16[256,512]{1,0:T(8,128)(2,1)S(1)}, u32[]{:S(2)}, u32[]{:S(2)}) collective-permute-start(bf16[256,512]{1,0:T(8,128)(2,1)S(1)} %panel.5.refs_0_), channel_id=1, source_target_pairs={{0,2},{2,4},{4,6},{1,3},{3,5},{5,7},{8,10},{10,12},{12,14},{9,11},... | collective-permute-start | bytes 786440 | tf_op jit(solution)/shard_map/ppermute | solution.py:244
  23.4 33.0 %collective-permute-done.refs_0_ = bf16[512,256]{1,0:T(8,128)(2,1)S(1)} collective-permute-done((bf16[512,256]{1,0:T(8,128)(2,1)S(1)}, bf16[512,256]{1,0:T(8,128)(2,1)S(1)}, u32[]{:S(2)}, u32[]{:S(2)}) %collective-permute-start) | collective-permute-done | bytes 262176 | tf_op jit(solution)/shard_map/ppermute | solution.py:18
  56.5 3.7 %collective-permute-start.2 = (bf16[256,512]{1,0:T(8,128)(2,1)S(1)}, bf16[256,512]{1,0:T(8,128)(2,1)S(1)}, u32[]{:S(2)}, u32[]{:S(2)}) collective-permute-start(bf16[256,512]{1,0:T(8,128)(2,1)S(1)} %panel.4.refs_0_), channel_id=1, source_target_pairs={{0,2},{2,4},{4,6},{1,3},{3,5},{5,7},{8,10},{10,12},{12,14},{9,11},... | collective-permute-start | bytes 786440 | tf_op jit(solution)/shard_map/ppermute | solution.py:244
  71.8 3.9 %collective-permute-done.27.refs_4_ = bf16[256,512]{1,0:T(8,128)(2,1)} collective-permute-done((bf16[256,512]{1,0:T(8,128)(2,1)S(1)}, bf16[256,512]{1,0:T(8,128)(2,1)}, u32[]{:S(2)}, u32[]{:S(2)}) %collective-permute-start.27) | collective-permute-done | bytes 262176 | tf_op jit(solution)/shard_map/ppermute | solution.py:245
  81.5 4.6 %collective-permute-done.5.refs_4_ = bf16[256,512]{1,0:T(8,128)(2,1)} collective-permute-done((bf16[256,512]{1,0:T(8,128)(2,1)}, bf16[256,512]{1,0:T(8,128)(2,1)}, u32[]{:S(2)}, u32[]{:S(2)}) %collective-permute-start.5) | collective-permute-done | bytes 262176 | tf_op jit(solution)/shard_map/ppermute | solution.py:245
  96.2 5.1 %products.5 = f32[4,256,512]{2,1,0:T(8,128)S(1)} custom-call(bf16[256,512]{1,0:T(8,128)(2,1)S(1)} %copy-done.21, bf16[256,512]{1,0:T(8,128)(2,1)S(1)} %copy-done.25, bf16[256,512]{1,0:T(8,128)(2,1)S(1)} %copy-done.27, bf16[256,512]{1,0:T(8,128)(2,1)} %collective-permute-done.26.refs_3_, bf16[256,512]{1,0:T(8,128)(2,1)} %collective-permute-done.27.refs_4_, ...), custom_call_target="tpu_custom_call" | custom-call | flops 1073741824 | bytes 9437184 | tf_op jit(solution)/shard_map/products/pallas_call | solution.py:188
  103.3 5.0 %collective-permute-start.30 = (bf16[256,512]{1,0:T(8,128)(2,1)}, bf16[256,512]{1,0:T(8,128)(2,1)}, u32[]{:S(2)}, u32[]{:S(2)}) collective-permute-start(bf16[256,512]{1,0:T(8,128)(2,1)} %get-tuple-element.15), channel_id=1, source_target_pairs={{0,2},{1,3},{8,10},{9,11},{16,18},{17,19},{24,26},{25,27}} | collective-permute-start | bytes 786440 | tf_op jit(solution)/shard_map/ppermute | solution.py:265
  110.4 4.7 %products.4 = f32[4,256,512]{2,1,0:T(8,128)S(1)} custom-call(bf16[256,512]{1,0:T(8,128)(2,1)S(1)} %copy-done.19, bf16[256,512]{1,0:T(8,128)(2,1)S(1)} %copy-done.23, bf16[256,512]{1,0:T(8,128)(2,1)} %collective-permute-done.3.refs_2_, bf16[256,512]{1,0:T(8,128)(2,1)} %collective-permute-done.4.refs_3_, bf16[256,512]{1,0:T(8,128)(2,1)} %collective-permute-done.5.refs_4_, ...), custom_call_target="tpu_custom_call" | custom-call | flops 1073741824 | bytes 9437184 | tf_op jit(solution)/shard_map/products/pallas_call | solution.py:188
  122.5 4.7 %collective-permute-start.31 = (bf16[256,512]{1,0:T(8,128)(2,1)}, bf16[256,512]{1,0:T(8,128)(2,1)}, u32[]{:S(2)}, u32[]{:S(2)}) collective-permute-start(bf16[256,512]{1,0:T(8,128)(2,1)} %fusion.14), channel_id=1, source_target_pairs={{0,2},{2,4},{1,3},{3,5},{8,10},{10,12},{9,11},{11,13},{16,18},{18,... | collective-permute-start | bytes 786440 | tf_op jit(solution)/shard_map/ppermute | solution.py:265
  133.3 5.1 %collective-permute-start.16 = (bf16[256,512]{1,0:T(8,128)(2,1)}, bf16[256,512]{1,0:T(8,128)(2,1)}, u32[]{:S(2)}, u32[]{:S(2)}) collective-permute-start(bf16[256,512]{1,0:T(8,128)(2,1)} %fusion.20), channel_id=1, source_target_pairs={{0,2},{2,4},{1,3},{3,5},{8,10},{10,12},{9,11},{11,13},{16,18},{18,... | collective-permute-start | bytes 786440 | tf_op jit(solution)/shard_map/ppermute | solution.py:265
  138.4 4.3 %collective-permute-done.31 = bf16[256,512]{1,0:T(8,128)(2,1)} collective-permute-done((bf16[256,512]{1,0:T(8,128)(2,1)}, bf16[256,512]{1,0:T(8,128)(2,1)}, u32[]{:S(2)}, u32[]{:S(2)}) %collective-permute-start.31) | collective-permute-done | bytes 262176 | tf_op jit(solution)/shard_map/ppermute | solution.py:265
  146.3 7.3 %collective-permute-done.16 = bf16[256,512]{1,0:T(8,128)(2,1)} collective-permute-done((bf16[256,512]{1,0:T(8,128)(2,1)}, bf16[256,512]{1,0:T(8,128)(2,1)}, u32[]{:S(2)}, u32[]{:S(2)}) %collective-permute-start.16) | collective-permute-done | bytes 262176 | tf_op jit(solution)/shard_map/ppermute | solution.py:265
  157.0 4.3 %collective-permute-start.32 = (bf16[256,512]{1,0:T(8,128)(2,1)}, bf16[256,512]{1,0:T(8,128)(2,1)S(1)}, u32[]{:S(2)}, u32[]{:S(2)}) collective-permute-start(bf16[256,512]{1,0:T(8,128)(2,1)} %get-tuple-element.13), channel_id=1, source_target_pairs={{0,2},{2,4},{4,6},{1,3},{3,5},{5,7},{8,10},{10,12},{12,14},{9,11},... | collective-permute-start | bytes 786440 | tf_op jit(solution)/shard_map/ppermute | solution.py:265
  164.6 5.9 %collective-permute-start.17 = (bf16[256,512]{1,0:T(8,128)(2,1)}, bf16[256,512]{1,0:T(8,128)(2,1)}, u32[]{:S(2)}, u32[]{:S(2)}) collective-permute-start(bf16[256,512]{1,0:T(8,128)(2,1)} %get-tuple-element.17), channel_id=1, source_target_pairs={{0,2},{2,4},{4,6},{1,3},{3,5},{5,7},{8,10},{10,12},{12,14},{9,11},... | collective-permute-start | bytes 786440 | tf_op jit(solution)/shard_map/ppermute | solution.py:265
  177.3 4.1 %collective-permute-done.20 = bf16[256,512]{1,0:T(8,128)(2,1)} collective-permute-done((bf16[256,512]{1,0:T(8,128)(2,1)}, bf16[256,512]{1,0:T(8,128)(2,1)}, u32[]{:S(2)}, u32[]{:S(2)}) %collective-permute-start.20) | collective-permute-done | bytes 262176 | tf_op jit(solution)/shard_map/ppermute | solution.py:268
  184.7 4.5 %collective-permute-done.22.refs_3_.refs_6_ = bf16[256,512]{1,0:T(8,128)(2,1)} collective-permute-done((bf16[256,512]{1,0:T(8,128)(2,1)S(1)}, bf16[256,512]{1,0:T(8,128)(2,1)}, u32[]{:S(2)}, u32[]{:S(2)}) %collective-permute-start.22) | collective-permute-done | bytes 262176 | tf_op jit(solution)/shard_map/ppermute | solution.py:18
  215.1 4.4 %collective-permute-start.46 = (bf16[256,512]{1,0:T(8,128)(2,1)S(1)}, bf16[256,512]{1,0:T(8,128)(2,1)S(1)}, u32[]{:S(2)}, u32[]{:S(2)}) collective-permute-start(bf16[256,512]{1,0:T(8,128)(2,1)S(1)} %fusion.2), channel_id=1, source_target_pairs={{0,2},{2,4},{1,3},{3,5},{8,10},{10,12},{9,11},{11,13},{16,18},{18,... | collective-permute-start | bytes 786440 | tf_op jit(solution)/shard_map/ppermute | solution.py:265
  220.7 4.4 %collective-permute-start.40 = (bf16[256,512]{1,0:T(8,128)(2,1)S(1)}, bf16[256,512]{1,0:T(8,128)(2,1)S(1)}, u32[]{:S(2)}, u32[]{:S(2)}) collective-permute-start(bf16[256,512]{1,0:T(8,128)(2,1)S(1)} %fusion.8), channel_id=1, source_target_pairs={{0,2},{2,4},{1,3},{3,5},{8,10},{10,12},{9,11},{11,13},{16,18},{18,... | collective-permute-start | bytes 786440 | tf_op jit(solution)/shard_map/ppermute | solution.py:265
  227.1 4.4 %collective-permute-done.40 = bf16[256,512]{1,0:T(8,128)(2,1)S(1)} collective-permute-done((bf16[256,512]{1,0:T(8,128)(2,1)S(1)}, bf16[256,512]{1,0:T(8,128)(2,1)S(1)}, u32[]{:S(2)}, u32[]{:S(2)}) %collective-permute-start.40) | collective-permute-done | bytes 262176 | tf_op jit(solution)/shard_map/ppermute | solution.py:265
  232.4 5.0 %collective-permute-start.47 = (bf16[256,512]{1,0:T(8,128)(2,1)S(1)}, bf16[256,512]{1,0:T(8,128)(2,1)S(1)}, u32[]{:S(2)}, u32[]{:S(2)}) collective-permute-start(bf16[256,512]{1,0:T(8,128)(2,1)S(1)} %get-tuple-element.5), channel_id=1, source_target_pairs={{0,2},{2,4},{4,6},{1,3},{3,5},{5,7},{8,10},{10,12},{12,14},{9,11},... | collective-permute-start | bytes 786440 | tf_op jit(solution)/shard_map/ppermute | solution.py:265
  238.8 5.2 %collective-permute-start.41 = (bf16[256,512]{1,0:T(8,128)(2,1)S(1)}, bf16[256,512]{1,0:T(8,128)(2,1)S(1)}, u32[]{:S(2)}, u32[]{:S(2)}) collective-permute-start(bf16[256,512]{1,0:T(8,128)(2,1)S(1)} %get-tuple-element.9), channel_id=1, source_target_pairs={{0,2},{2,4},{4,6},{1,3},{3,5},{5,7},{8,10},{10,12},{12,14},{9,11},... | collective-permute-start | bytes 786440 | tf_op jit(solution)/shard_map/ppermute | solution.py:265
  249.4 3.8 %collective-permute-done.44 = bf16[256,512]{1,0:T(8,128)(2,1)S(1)} collective-permute-done((bf16[256,512]{1,0:T(8,128)(2,1)S(1)}, bf16[256,512]{1,0:T(8,128)(2,1)S(1)}, u32[]{:S(2)}, u32[]{:S(2)}) %collective-permute-start.44) | collective-permute-done | bytes 262176 | tf_op jit(solution)/shard_map/ppermute | solution.py:268
  254.9 5.3 %collective-permute-done.51.refs_2_ = bf16[256,512]{1,0:T(8,128)(2,1)S(1)} collective-permute-done((bf16[256,512]{1,0:T(8,128)(2,1)S(1)}, bf16[256,512]{1,0:T(8,128)(2,1)S(1)}, u32[]{:S(2)}, u32[]{:S(2)}) %collective-permute-start.51) | collective-permute-done | bytes 262176 | tf_op jit(solution)/shard_map/ppermute | solution.py:18
  (181 shorter events, 115.0 us)
Async XLA Ops:
  6.5 189.0 %all-gather.3.cloned.1.call-start = ((), (), s32[]{:S(2)}) async-start(), calls=%async_computation | async-start | bytes 2621440 | tf_op jit(solution)/shard_map/all_gather | solution.py:304
  10.7 69.2 %collective-permute-start.13 = (bf16[512,1024]{1,0:T(8,128)(2,1)}, bf16[512,1024]{1,0:T(8,128)(2,1)}, u32[]{:S(2)}, u32[]{:S(2)}) collective-permute-start(bf16[512,1024]{1,0:T(8,128)(2,1)} %bitcast.6.refs_0_), channel_id=1, source_target_pairs={{0,8},{8,0},{1,9},{9,1},{2,10},{10,2},{3,11},{11,3},{4,12},{12,4},... | collective-permute-start | bytes 3145736 | tf_op jit(solution)/shard_map/ppermute | solution.py:18
  11.9 48.4 %collective-permute-start.10 = (bf16[512,512]{1,0:T(8,128)(2,1)S(1)}, bf16[512,512]{1,0:T(8,128)(2,1)S(1)}, u32[]{:S(2)}, u32[]{:S(2)}) collective-permute-start(bf16[512,512]{1,0:T(8,128)(2,1)S(1)} %dynamic-slice_bitcast_fusion), channel_id=1, source_target_pairs={{0,8},{8,0},{1,9},{9,1},{2,10},{10,2},{3,11},{11,3},{4,12},{12,4},... | collective-permute-start | bytes 1572872 | tf_op jit(solution)/shard_map/ppermute | solution.py:18
  13.9 42.5 %collective-permute-start = (bf16[512,256]{1,0:T(8,128)(2,1)S(1)}, bf16[512,256]{1,0:T(8,128)(2,1)S(1)}, u32[]{:S(2)}, u32[]{:S(2)}) collective-permute-start(bf16[512,256]{1,0:T(8,128)(2,1)S(1)} %get-tuple-element.22), channel_id=1, source_target_pairs={{0,8},{8,0},{1,9},{9,1},{2,10},{10,2},{3,11},{11,3},{4,12},{12,4},... | collective-permute-start | bytes 786440 | tf_op jit(solution)/shard_map/ppermute | solution.py:18
  18.0 43.6 %collective-permute-start.24 = (bf16[256,512]{1,0:T(8,128)(2,1)S(1)}, bf16[256,512]{1,0:T(8,128)(2,1)S(1)}, u32[]{:S(2)}, u32[]{:S(2)}) collective-permute-start(bf16[256,512]{1,0:T(8,128)(2,1)S(1)} %panel.5.refs_0_), channel_id=1, source_target_pairs={{0,2},{2,4},{4,6},{1,3},{3,5},{5,7},{8,10},{10,12},{12,14},{9,11},... | collective-permute-start | bytes 786440 | tf_op jit(solution)/shard_map/ppermute | solution.py:244
  22.1 41.6 %collective-permute-start.25 = (bf16[256,512]{1,0:T(8,128)(2,1)S(1)}, bf16[256,512]{1,0:T(8,128)(2,1)S(1)}, u32[]{:S(2)}, u32[]{:S(2)}) collective-permute-start(bf16[256,512]{1,0:T(8,128)(2,1)S(1)} %panel.5.refs_0_), channel_id=1, source_target_pairs={{2,0},{4,2},{6,4},{3,1},{5,3},{7,5},{10,8},{12,10},{14,12},{11,9},... | collective-permute-start | bytes 786440 | tf_op jit(solution)/shard_map/ppermute | solution.py:245
  65.7 14.1 %collective-permute-start.4 = (bf16[256,512]{1,0:T(8,128)(2,1)S(1)}, bf16[256,512]{1,0:T(8,128)(2,1)}, u32[]{:S(2)}, u32[]{:S(2)}) collective-permute-start(bf16[256,512]{1,0:T(8,128)(2,1)S(1)} %collective-permute-done.2.refs_1_), channel_id=1, source_target_pairs={{2,4},{4,6},{3,5},{5,7},{10,12},{12,14},{11,13},{13,15},{18,20},{2... | collective-permute-start | bytes 786440 | tf_op jit(solution)/shard_map/ppermute | solution.py:244
  69.2 17.0 %collective-permute-start.5 = (bf16[256,512]{1,0:T(8,128)(2,1)}, bf16[256,512]{1,0:T(8,128)(2,1)}, u32[]{:S(2)}, u32[]{:S(2)}) collective-permute-start(bf16[256,512]{1,0:T(8,128)(2,1)} %collective-permute-done.3.refs_2_), channel_id=1, source_target_pairs={{2,0},{4,2},{3,1},{5,3},{10,8},{12,10},{11,9},{13,11},{18,16},{20,... | collective-permute-start | bytes 786440 | tf_op jit(solution)/shard_map/ppermute | solution.py:245
  70.5 15.7 %collective-permute-start.28 = (bf16[256,512]{1,0:T(8,128)(2,1)}, bf16[256,512]{1,0:T(8,128)(2,1)}, u32[]{:S(2)}, u32[]{:S(2)}) collective-permute-start(bf16[256,512]{1,0:T(8,128)(2,1)} %collective-permute-done.26.refs_3_), channel_id=1, source_target_pairs={{4,6},{5,7},{12,14},{13,15},{20,22},{21,23},{28,30},{29,31}} | collective-permute-start | bytes 786440 | tf_op jit(solution)/shard_map/ppermute | solution.py:244
  75.7 13.2 %collective-permute-start.29 = (bf16[256,512]{1,0:T(8,128)(2,1)}, bf16[256,512]{1,0:T(8,128)(2,1)}, u32[]{:S(2)}, u32[]{:S(2)}) collective-permute-start(bf16[256,512]{1,0:T(8,128)(2,1)} %collective-permute-done.27.refs_4_), channel_id=1, source_target_pairs={{2,0},{3,1},{10,8},{11,9},{18,16},{19,17},{26,24},{27,25}} | collective-permute-start | bytes 786440 | tf_op jit(solution)/shard_map/ppermute | solution.py:245
  91.1 17.3 %collective-permute-start.6 = (bf16[256,512]{1,0:T(8,128)(2,1)}, bf16[256,512]{1,0:T(8,128)(2,1)S(1)}, u32[]{:S(2)}, u32[]{:S(2)}) collective-permute-start(bf16[256,512]{1,0:T(8,128)(2,1)} %collective-permute-done.4.refs_3_), channel_id=1, source_target_pairs={{4,6},{5,7},{12,14},{13,15},{20,22},{21,23},{28,30},{29,31}} | collective-permute-start | bytes 786440 | tf_op jit(solution)/shard_map/ppermute | solution.py:244
  91.9 18.4 %collective-permute-start.7 = (bf16[256,512]{1,0:T(8,128)(2,1)}, bf16[256,512]{1,0:T(8,128)(2,1)S(1)}, u32[]{:S(2)}, u32[]{:S(2)}) collective-permute-start(bf16[256,512]{1,0:T(8,128)(2,1)} %collective-permute-done.5.refs_4_), channel_id=1, source_target_pairs={{2,0},{3,1},{10,8},{11,9},{18,16},{19,17},{26,24},{27,25}} | collective-permute-start | bytes 786440 | tf_op jit(solution)/shard_map/ppermute | solution.py:245
  103.3 17.3 %collective-permute-start.30 = (bf16[256,512]{1,0:T(8,128)(2,1)}, bf16[256,512]{1,0:T(8,128)(2,1)}, u32[]{:S(2)}, u32[]{:S(2)}) collective-permute-start(bf16[256,512]{1,0:T(8,128)(2,1)} %get-tuple-element.15), channel_id=1, source_target_pairs={{0,2},{1,3},{8,10},{9,11},{16,18},{17,19},{24,26},{25,27}} | collective-permute-start | bytes 786440 | tf_op jit(solution)/shard_map/ppermute | solution.py:265
  117.2 14.2 %collective-permute-start.15 = (bf16[256,512]{1,0:T(8,128)(2,1)}, bf16[256,512]{1,0:T(8,128)(2,1)}, u32[]{:S(2)}, u32[]{:S(2)}) collective-permute-start(bf16[256,512]{1,0:T(8,128)(2,1)} %get-tuple-element.19), channel_id=1, source_target_pairs={{0,2},{1,3},{8,10},{9,11},{16,18},{17,19},{24,26},{25,27}} | collective-permute-start | bytes 786440 | tf_op jit(solution)/shard_map/ppermute | solution.py:265
  119.2 19.2 %collective-permute-start.33 = (bf16[256,512]{1,0:T(8,128)(2,1)S(1)}, bf16[256,512]{1,0:T(8,128)(2,1)}, u32[]{:S(2)}, u32[]{:S(2)}) collective-permute-start(bf16[256,512]{1,0:T(8,128)(2,1)S(1)} %get-tuple-element.16), channel_id=1, source_target_pairs={{6,4},{7,5},{14,12},{15,13},{22,20},{23,21},{30,28},{31,29}} | collective-permute-start | bytes 786440 | tf_op jit(solution)/shard_map/ppermute | solution.py:268
  122.5 20.2 %collective-permute-start.31 = (bf16[256,512]{1,0:T(8,128)(2,1)}, bf16[256,512]{1,0:T(8,128)(2,1)}, u32[]{:S(2)}, u32[]{:S(2)}) collective-permute-start(bf16[256,512]{1,0:T(8,128)(2,1)} %fusion.14), channel_id=1, source_target_pairs={{0,2},{2,4},{1,3},{3,5},{8,10},{10,12},{9,11},{11,13},{16,18},{18,... | collective-permute-start | bytes 786440 | tf_op jit(solution)/shard_map/ppermute | solution.py:265
  127.2 19.2 %collective-permute-start.18 = (bf16[256,512]{1,0:T(8,128)(2,1)}, bf16[256,512]{1,0:T(8,128)(2,1)}, u32[]{:S(2)}, u32[]{:S(2)}) collective-permute-start(bf16[256,512]{1,0:T(8,128)(2,1)} %get-tuple-element.20), channel_id=1, source_target_pairs={{6,4},{7,5},{14,12},{15,13},{22,20},{23,21},{30,28},{31,29}} | collective-permute-start | bytes 786440 | tf_op jit(solution)/shard_map/ppermute | solution.py:268
  133.3 20.3 %collective-permute-start.16 = (bf16[256,512]{1,0:T(8,128)(2,1)}, bf16[256,512]{1,0:T(8,128)(2,1)}, u32[]{:S(2)}, u32[]{:S(2)}) collective-permute-start(bf16[256,512]{1,0:T(8,128)(2,1)} %fusion.20), channel_id=1, source_target_pairs={{0,2},{2,4},{1,3},{3,5},{8,10},{10,12},{9,11},{11,13},{16,18},{18,... | collective-permute-start | bytes 786440 | tf_op jit(solution)/shard_map/ppermute | solution.py:265
  145.0 16.4 %collective-permute-start.34 = (bf16[256,512]{1,0:T(8,128)(2,1)}, bf16[256,512]{1,0:T(8,128)(2,1)}, u32[]{:S(2)}, u32[]{:S(2)}) collective-permute-start(bf16[256,512]{1,0:T(8,128)(2,1)} %get-tuple-element.14), channel_id=1, source_target_pairs={{4,2},{6,4},{5,3},{7,5},{12,10},{14,12},{13,11},{15,13},{20,18},{2... | collective-permute-start | bytes 786440 | tf_op jit(solution)/shard_map/ppermute | solution.py:268
  155.7 14.8 %collective-permute-start.19 = (bf16[256,512]{1,0:T(8,128)(2,1)}, bf16[256,512]{1,0:T(8,128)(2,1)}, u32[]{:S(2)}, u32[]{:S(2)}) collective-permute-start(bf16[256,512]{1,0:T(8,128)(2,1)} %get-tuple-element.18), channel_id=1, source_target_pairs={{4,2},{6,4},{5,3},{7,5},{12,10},{14,12},{13,11},{15,13},{20,18},{2... | collective-permute-start | bytes 786440 | tf_op jit(solution)/shard_map/ppermute | solution.py:268
  157.0 16.6 %collective-permute-start.32 = (bf16[256,512]{1,0:T(8,128)(2,1)}, bf16[256,512]{1,0:T(8,128)(2,1)S(1)}, u32[]{:S(2)}, u32[]{:S(2)}) collective-permute-start(bf16[256,512]{1,0:T(8,128)(2,1)} %get-tuple-element.13), channel_id=1, source_target_pairs={{0,2},{2,4},{4,6},{1,3},{3,5},{5,7},{8,10},{10,12},{12,14},{9,11},... | collective-permute-start | bytes 786440 | tf_op jit(solution)/shard_map/ppermute | solution.py:265
  164.6 12.7 %collective-permute-start.17 = (bf16[256,512]{1,0:T(8,128)(2,1)}, bf16[256,512]{1,0:T(8,128)(2,1)}, u32[]{:S(2)}, u32[]{:S(2)}) collective-permute-start(bf16[256,512]{1,0:T(8,128)(2,1)} %get-tuple-element.17), channel_id=1, source_target_pairs={{0,2},{2,4},{4,6},{1,3},{3,5},{5,7},{8,10},{10,12},{12,14},{9,11},... | collective-permute-start | bytes 786440 | tf_op jit(solution)/shard_map/ppermute | solution.py:265
  212.7 12.5 %collective-permute-start.48 = (bf16[256,512]{1,0:T(8,128)(2,1)S(1)}, bf16[256,512]{1,0:T(8,128)(2,1)S(1)}, u32[]{:S(2)}, u32[]{:S(2)}) collective-permute-start(bf16[256,512]{1,0:T(8,128)(2,1)S(1)} %get-tuple-element.8), channel_id=1, source_target_pairs={{6,4},{7,5},{14,12},{15,13},{22,20},{23,21},{30,28},{31,29}} | collective-permute-start | bytes 786440 | tf_op jit(solution)/shard_map/ppermute | solution.py:268
  232.4 13.0 %collective-permute-start.47 = (bf16[256,512]{1,0:T(8,128)(2,1)S(1)}, bf16[256,512]{1,0:T(8,128)(2,1)S(1)}, u32[]{:S(2)}, u32[]{:S(2)}) collective-permute-start(bf16[256,512]{1,0:T(8,128)(2,1)S(1)} %get-tuple-element.5), channel_id=1, source_target_pairs={{0,2},{2,4},{4,6},{1,3},{3,5},{5,7},{8,10},{10,12},{12,14},{9,11},... | collective-permute-start | bytes 786440 | tf_op jit(solution)/shard_map/ppermute | solution.py:265
  (60 other events, 535.4 us)
Sparse Core Ops, SparseCore 0:
  91.2 63.1 all-gather.2

commit v3 on v2

--- a/solution.py
+++ b/solution.py
@@ -10,7 +10,7 @@
 CHUNKS = 2
 ANY = pl.BlockSpec(memory_space=pl.ANY)
 VMEM = pl.BlockSpec(memory_space=pltpu.VMEM)
-PARAMS = pltpu.CompilerParams(vmem_limit_bytes=32 * 1024 * 1024)
+PARAMS = pltpu.CompilerParams(vmem_limit_bytes=20 * 1024 * 1024)
 
 
 def exchanged(value, axis, steps):
@@ -132,12 +132,14 @@
     )(own, *flat)
 
 
-def products_kernel(sizes, step, part, block_shifts, state_places, *refs):
-    n_blocks, n_states, n_tiles = len(block_shifts), len(state_places), sizes.sec * sizes.col
+def products_kernel(sizes, step, part, block_rows, state_places, *refs):
+    n_blocks, n_states, n_tiles = len(block_rows), len(state_places), sizes.sec * sizes.col
     blocks, refs = refs[:n_blocks], refs[n_blocks:]
     states, refs = refs[:n_states], refs[n_states:]
     tiles, refs = nested(refs[:n_tiles], sizes), refs[n_tiles:]
-    diagonals, out, state, rows, added, tile_sems, state_sems, added_sem = refs
+    diagonals, refs = refs[0], refs[1:]
+    out, up_first, down_first, *refs = refs
+    state, rows, added, product, tile_sems, state_sems, added_sem = refs
     row_index, sec_index, col_index = (lax.axis_index(a) for a in ("row", "sec", "col"))
 
     state_copies = []
@@ -157,29 +159,29 @@
     for copy in state_copies:
         copy.wait()
 
-    out[0] = jnp.zeros((sizes.chunk, sizes.rows), jnp.float32)
-    for number, shift in enumerate(block_shifts):
-        def accumulate(block, q):
-            first = pl.multiple_of(q * sizes.rows, sizes.rows)
-            out[0] += jnp.dot(
-                block, state[pl.ds(first, sizes.rows)], preferred_element_type=jnp.float32
-            )
-
-        if shift is None:
-            for q in range(sizes.row):
-                accumulate(blocks[number][q, part * sizes.chunk : (part + 1) * sizes.chunk], q)
-        else:
-            q = row_index + shift
-            pl.when((q >= 0) & (q < sizes.row))(
-                functools.partial(lambda ref, q: accumulate(ref[...], q), blocks[number], q)
-            )
-    image = out[0].astype(jnp.bfloat16)
+    product[...] = jnp.zeros((sizes.chunk, sizes.rows), jnp.float32)
+
+    def accumulate(ref, q):
+        first = pl.multiple_of(q * sizes.rows, sizes.rows)
+        count = sizes.chunk
+        block = ref[...] if ref.shape[0] == count else ref[part * count : (part + 1) * count]
+        product[...] += jnp.dot(
+            block, state[pl.ds(first, sizes.rows)], preferred_element_type=jnp.float32
+        )
+
+    for ref, row_of in zip(blocks, block_rows):
+        q, low, high = row_of(row_index)
+        pl.when((q >= low) & (q <= high))(functools.partial(accumulate, ref, q))
+    image = product[...].astype(jnp.bfloat16)
     wait_all(tile_copies)
     added_copy.wait()
     for d in range(sizes.row):
         h, i = divmod(d, sizes.per_tile)
         right = rows[h, :, i * sizes.rows : (i + 1) * sizes.rows]
-        out[d] = jnp.dot(image, right, preferred_element_type=jnp.float32) + added[d]
+        place = lax.rem(d - row_index + sizes.row, sizes.row)
+        out[place] = jnp.dot(image, right, preferred_element_type=jnp.float32) + added[d]
+    up_first[...] = out[sizes.row - 1].astype(jnp.bfloat16)
+    down_first[...] = out[1].astype(jnp.bfloat16)
 
 
 def products(sizes, step, part, blocks, states, tiles, diagonals):
@@ -189,13 +191,15 @@
         functools.partial(
             products_kernel, sizes, step, part, [b[0] for b in blocks], [s[0] for s in states]
         ),
-        out_shape=jax.ShapeDtypeStruct(shape, jnp.float32),
+        out_shape=[jax.ShapeDtypeStruct(shape, jnp.float32)]
+        + [jax.ShapeDtypeStruct(shape[1:], jnp.bfloat16)] * 2,
         in_specs=[VMEM] * len(blocks) + [ANY] * (len(states) + len(flat) + 1),
-        out_specs=VMEM,
+        out_specs=[VMEM] * 3,
         scratch_shapes=[
             pltpu.VMEM((sizes.order, sizes.rows), jnp.bfloat16),
             pltpu.VMEM((sizes.col, sizes.rows, sizes.cols), jnp.bfloat16),
             pltpu.VMEM(shape, jnp.float32),
+            pltpu.VMEM(shape[1:], jnp.float32),
             pltpu.SemaphoreType.DMA((sizes.col,)),
             pltpu.SemaphoreType.DMA((len(states),)),
             pltpu.SemaphoreType.DMA,
@@ -237,38 +241,63 @@
     )(*pieces)
 
 
+def after(value, *others):
+    return lax.optimization_barrier((value, *others))[0]
+
+
 def neighbours_gathered(sizes, block):
+    last = sizes.row - 1
     up = down = block
-    found = [(0, block)]
-    for slot in range(sizes.row - 1):
-        up = lax.ppermute(up, "row", [(i, i + 1) for i in range(slot, sizes.row - 1)])
+    found = [(lambda row: (row, 0, last), block)]
+    for slot in range(last):
+        up = lax.ppermute(up, "row", [(i, i + 1) for i in range(slot, last)])
         down = lax.ppermute(down, "row", [(i, i - 1) for i in range(1, sizes.row - slot)])
-        found += [(-1 - slot, up), (1 + slot, down)]
+        found.append((lambda row, slot=slot: (row - 1 - slot, 0, last), up))
+        found.append((lambda row, slot=slot: (row + 1 + slot, 0, last), down))
     return found
 
 
-def scattered_sum(sizes, partial):
+def trailing_gather(sizes, block):
     row_index = lax.axis_index("row")
-
-    def block(number):
-        number = jnp.clip(number, 0, sizes.row - 1)
-        return lax.dynamic_index_in_dim(partial, number, 0, keepdims=False)
-
+    last = sizes.row - 1
+    ups, downs = [], []
+    found = [(lambda row: (row, 0, last), block)]
+    for time in range(1, 2 * last):
+        up = down = block
+        if time > 2:
+            up = jnp.where(row_index == time - 1, block, ups[-2])
+            down = jnp.where(last - row_index == time - 1, block, downs[-2])
+        senders = [i for i in range(last) if time // 2 <= i <= time - 1]
+        ups.append(lax.ppermute(up, "row", [(i, i + 1) for i in senders]))
+        downs.append(lax.ppermute(down, "row", [(last - i, last - i - 1) for i in senders]))
+
+        def from_below(row, time=time):
+            q = 2 * row - 1 - time
+            return q, 0, row - 1
+
+        def from_above(row, time=time):
+            q = 2 * row - last + 1 + time
+            return q, row + 1, last
+
+        found += [(from_below, ups[-1]), (from_above, downs[-1])]
+    return found
+
+
+def scattered_sum(sizes, partials):
+    blocks, up_first, down_first = partials
+    last = sizes.row - 1
     up = down = None
-    last = sizes.row - 1
     for slot in range(last):
-        up_block = block(last - slot + row_index)
-        down_block = block(row_index + slot - last)
         if slot:
-            up_block = up_block + up.astype(jnp.float32)
-            down_block = down_block + down.astype(jnp.float32)
-        up = lax.ppermute(
-            up_block.astype(jnp.bfloat16), "row", [(i, i + 1) for i in range(slot + 1)]
+            up_block = (blocks[last - slot] + up.astype(jnp.float32)).astype(jnp.bfloat16)
+            down_block = (blocks[slot + 1] + down.astype(jnp.float32)).astype(jnp.bfloat16)
+        else:
+            up_block, down_block = up_first, down_first
+        up = lax.ppermute(up_block, "row", [(i, i + 1) for i in range(slot + 1)])
+        down = lax.ppermute(
+            down_block, "row", [(i, i - 1) for i in range(last - slot, last + 1)]
         )
-        down = lax.ppermute(
-            down_block.astype(jnp.bfloat16), "row", [(i, i - 1) for i in range(last - slot, last + 1)]
-        )
-    total = block(row_index) + up.astype(jnp.float32) + down.astype(jnp.float32)
+    total = blocks[0] + up.astype(jnp.float32) + down.astype(jnp.float32)
     return total.astype(jnp.bfloat16)
 
 
@@ -301,9 +330,12 @@
         factor_blocks[last, part] = neighbours_gathered(sizes, block)
     for step in reversed(range(last)):
         block = transposed_panel(sizes, step, factor, arrived_chunks[1:])
-        whole = lax.all_gather(block, "row", axis=0)
+        block = after(block, *[array for _, array in factor_blocks[step + 1, CHUNKS - 1][:3]])
+        blocks = trailing_gather(sizes, block)
         for part in range(CHUNKS):
-            factor_blocks[step, part] = [(None, whole)]
+            factor_blocks[step, part] = blocks
+
+    swapped = [chunks[-1] for chunks in arrived_chunks[1:]]
 
     def tiles_over_sections(tile, first_chunks):
         found = [tile]
@@ -313,7 +345,7 @@
                 if j == 0 and first_chunks is not None:
                     piece = jnp.concatenate(first_chunks[kx], axis=1)
                 else:
-                    piece = exchanged(panel(tile, kx + j), "sec", kx)
+                    piece = exchanged(after(panel(tile, kx + j), *swapped), "sec", kx)
                 first = (sec_index + j) % sec_size * width
                 whole = lax.dynamic_update_slice_in_dim(whole, piece, first, 1)
             found.append(whole)
@@ -329,7 +361,8 @@
     factor_tiles = [over_columns(tile) for tile in tiles_over_sections(factor, arrived_chunks)]
     inverse_tiles = [
         over_columns(tile)
-        for tile in [inverse] + [exchanged(inverse, "sec", kx) for kx in range(1, sec_size)]
+        for tile in [inverse]
+        + [exchanged(after(inverse, *swapped), "sec", kx) for kx in range(1, sec_size)]
     ]
 
     results = {}

time: 271 us -> 253 us (0.934)
  starting transfers between devices: 97.4 us -> 118 us
  between operations: 14.2 us -> 1.02 us
  other arithmetic: 15.4 us -> 5.3 us
  local copies, waits for them, and re-layouts: 24.4 us -> 14.7 us
  waiting for transfers between devices: 94.1 us -> 84.7 us
    ppermute x30 -> x40, starting transfers between devices: 76.7 us -> 96.7 us  [the longest x12 59.3 us: scattered_sum(): up = lax.ppermute(up_block, 'row', [(i, i + 1) for i in range(slot + 1)])]
    ppermute x17, waiting for transfers between devices: 46.6 us -> 33.3 us  [exchanged(): lax.ppermute(value, axis, [(i, (i + steps) % count) for i in range(count)])]
    convert_element_type x12, other arithmetic: 12.5 us -> 2.15 us  [the longest x8 1.87 us: scattered_sum(): (blocks[last - slot] + up.astype(jnp.float32)).astype(jnp.bfloat16)]
    ppermute x30 -> x40, waiting for transfers between devices: 32.5 us -> 39.9 us  [the longest x12 14.4 us: scattered_sum(): lax.ppermute(down_block, 'row', [(i, i - 1) for i in range(last - slot, l...]
    unnamed x61 -> x51, local copies, waits for them, and re-layouts: 19.2 us -> 12.3 us
    ppermute x6, waiting for transfers between devices: 14.9 us -> 11.5 us  [neighbours_gathered(): lax.ppermute(down, 'row', [(i, i - 1) for i in range(1, sizes.row - slot)])]
  transfers between devices with their start and end apart: 54 -> 63, of which waited for: 19 -> 20; matrix products, arithmetic and copies ran while one was open for 8% -> 4% of each run, Pallas kernels for 7% -> 8%
where the time goes in v3:
time: 253 us; the launch traced here: 250 us
  starting transfers between devices  118 us (47%)
  waiting for transfers between devices  84.7 us (33%)
  Pallas kernels  25.9 us (10%)
  local copies, waits for them, and re-layouts  14.7 us (6%)
  other arithmetic  5.3 us (2%)
    ppermute x12, starting transfers between devices, scattered_sum(): up = lax.ppermute(up_block, 'row', [(i, i + 1) for i in range(slot + 1)])  59.3 us
    ppermute x17, waiting for transfers between devices, exchanged(): lax.ppermute(value, axis, [(i, (i + steps) % count) for i in range(count)])  33.3 us
    pallas_call x4, Pallas kernels, products(): pl.pallas_call(functools.partial(products_kernel, sizes, step, part, [b[0...  17.1 us
    ppermute x12, waiting for transfers between devices, scattered_sum(): lax.ppermute(down_block, 'row', [(i, i - 1) for i in range(last - slot, l...  14.4 us
    ppermute x12, waiting for transfers between devices, scattered_sum(): up = lax.ppermute(up_block, 'row', [(i, i + 1) for i in range(slot + 1)])  13.7 us
    ppermute x17, starting transfers between devices, exchanged(): lax.ppermute(value, axis, [(i, (i + steps) % count) for i in range(count)])  13.6 us
    ppermute x6, starting transfers between devices, neighbours_gathered(): up = lax.ppermute(up, 'row', [(i, i + 1) for i in range(slot, last)])  12.3 us
    unnamed x51, local copies, waits for them, and re-layouts  12.3 us
  transfers between devices with their start and end apart: 63, of which 20 were waited for; matrix products, arithmetic and copies ran while one was open for 4% of the time, Pallas kernels for 8%

profile of v3, /device:TPU:0, one launch (start us, length us, event | category | flops | bytes accessed | tf_op | source)
XLA Modules:
  0.0 249.6 jit_solution(1530102758516825749)
XLA Ops:
  1.2 3.0 %collective-permute-start.1 = (bf16[512,256]{1,0:T(8,128)(2,1)S(1)}, bf16[512,256]{1,0:T(8,128)(2,1)S(1)}, u32[]{:S(2)}, u32[]{:S(2)}) collective-permute-start(bf16[512,256]{1,0:T(8,128)(2,1)S(1)} %get-tuple-element.43), channel_id=1, source_target_pairs={{0,8},{8,0},{1,9},{9,1},{2,10},{10,2},{3,11},{11,3},{4,12},{12,4},... | collective-permute-start | bytes 786440 | tf_op jit(solution)/shard_map/ppermute | solution.py:18
  4.2 6.3 %collective-permute-done.1.refs_1_.refs_0_ = bf16[512,256]{1,0:T(8,128)(2,1)S(1)} collective-permute-done((bf16[512,256]{1,0:T(8,128)(2,1)S(1)}, bf16[512,256]{1,0:T(8,128)(2,1)S(1)}, u32[]{:S(2)}, u32[]{:S(2)}) %collective-permute-start.1) | collective-permute-done | bytes 262176 | tf_op jit(solution)/shard_map/ppermute | solution.py:18
  13.8 3.7 %collective-permute-start.2 = (bf16[256,512]{1,0:T(8,128)(2,1)S(1)}, bf16[256,512]{1,0:T(8,128)(2,1)S(1)}, u32[]{:S(2)}, u32[]{:S(2)}) collective-permute-start(bf16[256,512]{1,0:T(8,128)(2,1)S(1)} %panel.4.refs_0_), channel_id=1, source_target_pairs={{0,2},{2,4},{4,6},{1,3},{3,5},{5,7},{8,10},{10,12},{12,14},{9,11},... | collective-permute-start | bytes 786440 | tf_op jit(solution)/shard_map/ppermute | solution.py:253
  20.4 22.0 %collective-permute-done.refs_0_ = bf16[512,256]{1,0:T(8,128)(2,1)S(1)} collective-permute-done((bf16[512,256]{1,0:T(8,128)(2,1)S(1)}, bf16[512,256]{1,0:T(8,128)(2,1)S(1)}, u32[]{:S(2)}, u32[]{:S(2)}) %collective-permute-start) | collective-permute-done | bytes 262176 | tf_op jit(solution)/shard_map/ppermute | solution.py:18
  42.6 4.4 %collective-permute-start.14 = (bf16[256,512]{1,0:T(8,128)(2,1)S(1)}, bf16[256,512]{1,0:T(8,128)(2,1)}, u32[]{:S(2)}, u32[]{:S(2)}) collective-permute-start(bf16[256,512]{1,0:T(8,128)(2,1)S(1)} %panel.5.refs_0_), channel_id=1, source_target_pairs={{0,2},{2,4},{4,6},{1,3},{3,5},{5,7},{8,10},{10,12},{12,14},{9,11},... | collective-permute-start | bytes 786440 | tf_op jit(solution)/shard_map/ppermute | solution.py:253
  50.7 4.7 %collective-permute-done.15.refs_2_ = bf16[256,512]{1,0:T(8,128)(2,1)} collective-permute-done((bf16[256,512]{1,0:T(8,128)(2,1)S(1)}, bf16[256,512]{1,0:T(8,128)(2,1)}, u32[]{:S(2)}, u32[]{:S(2)}) %collective-permute-start.15) | collective-permute-done | bytes 262176 | tf_op jit(solution)/shard_map/ppermute | solution.py:254
  64.5 5.9 %collective-permute-done.17.refs_4_ = bf16[256,512]{1,0:T(8,128)(2,1)} collective-permute-done((bf16[256,512]{1,0:T(8,128)(2,1)}, bf16[256,512]{1,0:T(8,128)(2,1)}, u32[]{:S(2)}, u32[]{:S(2)}) %collective-permute-start.17) | collective-permute-done | bytes 262176 | tf_op jit(solution)/shard_map/ppermute | solution.py:254
  77.4 5.5 %collective-permute-start.4 = (bf16[512,512]{1,0:T(8,128)(2,1)}, bf16[512,512]{1,0:T(8,128)(2,1)}, u32[]{:S(2)}, u32[]{:S(2)}) collective-permute-start(bf16[512,512]{1,0:T(8,128)(2,1)} %panel.3.refs_0_), channel_id=1, source_target_pairs={{0,2},{1,3},{8,10},{9,11},{16,18},{17,19},{24,26},{25,27}} | collective-permute-start | bytes 1572872 | tf_op jit(solution)/shard_map/ppermute | solution.py:271
  87.1 4.7 %products.5 = (f32[4,256,512]{2,1,0:T(8,128)S(1)}, bf16[256,512]{1,0:T(8,128)(2,1)}, bf16[256,512]{1,0:T(8,128)(2,1)S(1)}) custom-call(bf16[256,512]{1,0:T(8,128)(2,1)S(1)} %copy-done.17, bf16[256,512]{1,0:T(8,128)(2,1)S(1)} %copy-done.19, bf16[256,512]{1,0:T(8,128)(2,1)} %collective-permute-done.3.refs_2_, bf16[256,512]{1,0:T(8,128)(2,1)S(1)} %copy-done.21, ...), custom_call_target="tpu_custom_call" | custom-call | flops 1073741824 | bytes 9437184 | tf_op jit(solution)/shard_map/products/pallas_call | solution.py:190
  93.9 5.9 %collective-permute-start.40 = (bf16[256,512]{1,0:T(8,128)(2,1)}, bf16[256,512]{1,0:T(8,128)(2,1)}, u32[]{:S(2)}, u32[]{:S(2)}) collective-permute-start(bf16[256,512]{1,0:T(8,128)(2,1)} %get-tuple-element.27), channel_id=1, source_target_pairs={{0,2},{1,3},{8,10},{9,11},{16,18},{17,19},{24,26},{25,27}} | collective-permute-start | bytes 786440 | tf_op jit(solution)/shard_map/ppermute | solution.py:296
  107.1 4.1 %products.4 = (f32[4,256,512]{2,1,0:T(8,128)S(1)}, bf16[256,512]{1,0:T(8,128)(2,1)S(1)}, bf16[256,512]{1,0:T(8,128)(2,1)S(1)}) custom-call(bf16[256,512]{1,0:T(8,128)(2,1)S(1)} %copy-done.15, bf16[256,512]{1,0:T(8,128)(2,1)} %collective-permute-done.14.refs_1_, bf16[256,512]{1,0:T(8,128)(2,1)} %collective-permute-done.15.refs_2_, ...), custom_call_target="tpu_custom_call" | custom-call | flops 1073741824 | bytes 9437184 | tf_op jit(solution)/shard_map/products/pallas_call | solution.py:190
  124.1 8.3 %collective-permute-start.28 = (bf16[256,512]{1,0:T(8,128)(2,1)S(1)}, bf16[256,512]{1,0:T(8,128)(2,1)S(1)}, u32[]{:S(2)}, u32[]{:S(2)}) collective-permute-start(bf16[256,512]{1,0:T(8,128)(2,1)S(1)} %fusion.19), channel_id=1, source_target_pairs={{0,2},{2,4},{1,3},{3,5},{8,10},{10,12},{9,11},{11,13},{16,18},{18,... | collective-permute-start | bytes 786440 | tf_op jit(solution)/shard_map/ppermute | solution.py:296
  132.5 3.7 %collective-permute-done.28 = bf16[256,512]{1,0:T(8,128)(2,1)S(1)} collective-permute-done((bf16[256,512]{1,0:T(8,128)(2,1)S(1)}, bf16[256,512]{1,0:T(8,128)(2,1)S(1)}, u32[]{:S(2)}, u32[]{:S(2)}) %collective-permute-start.28) | collective-permute-done | bytes 262176 | tf_op jit(solution)/shard_map/ppermute | solution.py:296
  137.1 17.1 %collective-permute-start.42 = (bf16[256,512]{1,0:T(8,128)(2,1)S(1)}, bf16[256,512]{1,0:T(8,128)(2,1)S(1)}, u32[]{:S(2)}, u32[]{:S(2)}) collective-permute-start(bf16[256,512]{1,0:T(8,128)(2,1)S(1)} %get-tuple-element.39), channel_id=1, source_target_pairs={{0,2},{2,4},{4,6},{1,3},{3,5},{5,7},{8,10},{10,12},{12,14},{9,11},... | collective-permute-start | bytes 786440 | tf_op jit(solution)/shard_map/ppermute | solution.py:296
  158.2 4.6 %collective-permute-start.29 = (bf16[256,512]{1,0:T(8,128)(2,1)S(1)}, bf16[256,512]{1,0:T(8,128)(2,1)S(1)}, u32[]{:S(2)}, u32[]{:S(2)}) collective-permute-start(bf16[256,512]{1,0:T(8,128)(2,1)S(1)} %get-tuple-element.41), channel_id=1, source_target_pairs={{0,2},{2,4},{4,6},{1,3},{3,5},{5,7},{8,10},{10,12},{12,14},{9,11},... | collective-permute-start | bytes 786440 | tf_op jit(solution)/shard_map/ppermute | solution.py:296
  168.1 9.0 %collective-permute-done.32 = bf16[256,512]{1,0:T(8,128)(2,1)S(1)} collective-permute-done((bf16[256,512]{1,0:T(8,128)(2,1)S(1)}, bf16[256,512]{1,0:T(8,128)(2,1)S(1)}, u32[]{:S(2)}, u32[]{:S(2)}) %collective-permute-start.32) | collective-permute-done | bytes 262176 | tf_op jit(solution)/shard_map/ppermute | solution.py:297
  179.2 8.9 %collective-permute-done.11.refs_8_ = bf16[512,512]{1,0:T(8,128)(2,1)S(1)} collective-permute-done((bf16[512,512]{1,0:T(8,128)(2,1)S(1)}, bf16[512,512]{1,0:T(8,128)(2,1)S(1)}, u32[]{:S(2)}, u32[]{:S(2)}) %collective-permute-start.11) | collective-permute-done | bytes 524320 | tf_op jit(solution)/shard_map/ppermute | solution.py:272
  193.8 4.1 %products.7 = (f32[4,256,512]{2,1,0:T(8,128)S(1)}, bf16[256,512]{1,0:T(8,128)(2,1)S(1)}, bf16[256,512]{1,0:T(8,128)(2,1)S(1)}) custom-call(bf16[512,512]{1,0:T(8,128)(2,1)} %panel.3.refs_0_, bf16[512,512]{1,0:T(8,128)(2,1)} %collective-permute-done.4.refs_1_, bf16[512,512]{1,0:T(8,128)(2,1)} %collective-permute-done.5.refs_2_, ...), custom_call_target="tpu_custom_call" | custom-call | flops 1073741824 | bytes 9437184 | tf_op jit(solution)/shard_map/products/pallas_call | solution.py:190
  199.3 4.1 %products.6 = (f32[4,256,512]{2,1,0:T(8,128)S(1)}, bf16[256,512]{1,0:T(8,128)(2,1)S(1)}, bf16[256,512]{1,0:T(8,128)(2,1)S(1)}) custom-call(bf16[512,512]{1,0:T(8,128)(2,1)} %panel.3.refs_0_, bf16[512,512]{1,0:T(8,128)(2,1)} %collective-permute-done.4.refs_1_, bf16[512,512]{1,0:T(8,128)(2,1)} %collective-permute-done.5.refs_2_, ...), custom_call_target="tpu_custom_call" | custom-call | flops 1073741824 | bytes 9437184 | tf_op jit(solution)/shard_map/products/pallas_call | solution.py:190
  211.6 4.4 %collective-permute-start.50 = (bf16[256,512]{1,0:T(8,128)(2,1)S(1)}, bf16[256,512]{1,0:T(8,128)(2,1)S(1)}, u32[]{:S(2)}, u32[]{:S(2)}) collective-permute-start(bf16[256,512]{1,0:T(8,128)(2,1)S(1)} %fusion.7), channel_id=1, source_target_pairs={{0,2},{2,4},{1,3},{3,5},{8,10},{10,12},{9,11},{11,13},{16,18},{18,... | collective-permute-start | bytes 786440 | tf_op jit(solution)/shard_map/ppermute | solution.py:296
  221.2 5.0 %collective-permute-start.57 = (bf16[256,512]{1,0:T(8,128)(2,1)S(1)}, bf16[256,512]{1,0:T(8,128)(2,1)S(1)}, u32[]{:S(2)}, u32[]{:S(2)}) collective-permute-start(bf16[256,512]{1,0:T(8,128)(2,1)S(1)} %get-tuple-element.35), channel_id=1, source_target_pairs={{0,2},{2,4},{4,6},{1,3},{3,5},{5,7},{8,10},{10,12},{12,14},{9,11},... | collective-permute-start | bytes 786440 | tf_op jit(solution)/shard_map/ppermute | solution.py:296
  227.7 5.4 %collective-permute-start.51 = (bf16[256,512]{1,0:T(8,128)(2,1)S(1)}, bf16[256,512]{1,0:T(8,128)(2,1)S(1)}, u32[]{:S(2)}, u32[]{:S(2)}) collective-permute-start(bf16[256,512]{1,0:T(8,128)(2,1)S(1)} %get-tuple-element.37), channel_id=1, source_target_pairs={{0,2},{2,4},{4,6},{1,3},{3,5},{5,7},{8,10},{10,12},{12,14},{9,11},... | collective-permute-start | bytes 786440 | tf_op jit(solution)/shard_map/ppermute | solution.py:296
  237.2 4.2 %collective-permute-done.54 = bf16[256,512]{1,0:T(8,128)(2,1)S(1)} collective-permute-done((bf16[256,512]{1,0:T(8,128)(2,1)S(1)}, bf16[256,512]{1,0:T(8,128)(2,1)S(1)}, u32[]{:S(2)}, u32[]{:S(2)}) %collective-permute-start.54) | collective-permute-done | bytes 262176 | tf_op jit(solution)/shard_map/ppermute | solution.py:297
  243.6 4.4 %collective-permute-done.61.refs_2_ = bf16[256,512]{1,0:T(8,128)(2,1)S(1)} collective-permute-done((bf16[256,512]{1,0:T(8,128)(2,1)S(1)}, bf16[256,512]{1,0:T(8,128)(2,1)S(1)}, u32[]{:S(2)}, u32[]{:S(2)}) %collective-permute-start.61) | collective-permute-done | bytes 262176 | tf_op jit(solution)/shard_map/ppermute | solution.py:18
  (186 shorter events, 95.3 us)
Async XLA Ops:
  10.5 39.7 %collective-permute-start.25 = (bf16[512,1024]{1,0:T(8,128)(2,1)}, bf16[512,1024]{1,0:T(8,128)(2,1)}, u32[]{:S(2)}, u32[]{:S(2)}) collective-permute-start(bf16[512,1024]{1,0:T(8,128)(2,1)} %bitcast.5.refs_0_), channel_id=1, source_target_pairs={{0,8},{8,0},{1,9},{9,1},{2,10},{10,2},{3,11},{11,3},{4,12},{12,4},... | collective-permute-start | bytes 3145736 | tf_op jit(solution)/shard_map/ppermute | solution.py:18
  12.2 30.2 %collective-permute-start = (bf16[512,256]{1,0:T(8,128)(2,1)S(1)}, bf16[512,256]{1,0:T(8,128)(2,1)S(1)}, u32[]{:S(2)}, u32[]{:S(2)}) collective-permute-start(bf16[512,256]{1,0:T(8,128)(2,1)S(1)} %get-tuple-element.44), channel_id=1, source_target_pairs={{0,8},{8,0},{1,9},{9,1},{2,10},{10,2},{3,11},{11,3},{4,12},{12,4},... | collective-permute-start | bytes 786440 | tf_op jit(solution)/shard_map/ppermute | solution.py:18
  13.8 33.2 %collective-permute-start.2 = (bf16[256,512]{1,0:T(8,128)(2,1)S(1)}, bf16[256,512]{1,0:T(8,128)(2,1)S(1)}, u32[]{:S(2)}, u32[]{:S(2)}) collective-permute-start(bf16[256,512]{1,0:T(8,128)(2,1)S(1)} %panel.4.refs_0_), channel_id=1, source_target_pairs={{0,2},{2,4},{4,6},{1,3},{3,5},{5,7},{8,10},{10,12},{12,14},{9,11},... | collective-permute-start | bytes 786440 | tf_op jit(solution)/shard_map/ppermute | solution.py:253
  17.5 39.1 %collective-permute-start.22 = (bf16[512,512]{1,0:T(8,128)(2,1)S(1)}, bf16[512,512]{1,0:T(8,128)(2,1)S(1)}, u32[]{:S(2)}, u32[]{:S(2)}) collective-permute-start(bf16[512,512]{1,0:T(8,128)(2,1)S(1)} %dynamic-slice_bitcast_fusion), channel_id=1, source_target_pairs={{0,8},{8,0},{1,9},{9,1},{2,10},{10,2},{3,11},{11,3},{4,12},{12,4},... | collective-permute-start | bytes 1572872 | tf_op jit(solution)/shard_map/ppermute | solution.py:18
  19.1 29.2 %collective-permute-start.3 = (bf16[256,512]{1,0:T(8,128)(2,1)S(1)}, bf16[256,512]{1,0:T(8,128)(2,1)}, u32[]{:S(2)}, u32[]{:S(2)}) collective-permute-start(bf16[256,512]{1,0:T(8,128)(2,1)S(1)} %panel.4.refs_0_), channel_id=1, source_target_pairs={{2,0},{4,2},{6,4},{3,1},{5,3},{7,5},{10,8},{12,10},{14,12},{11,9},... | collective-permute-start | bytes 786440 | tf_op jit(solution)/shard_map/ppermute | solution.py:254
  50.2 20.2 %collective-permute-start.24 = (bf16[512,1024]{1,0:T(8,128)(2,1)}, bf16[512,1024]{1,0:T(8,128)(2,1)}, u32[]{:S(2)}, u32[]{:S(2)}) collective-permute-start(bf16[512,1024]{1,0:T(8,128)(2,1)} %bitcast.5.refs_0_), channel_id=1, source_target_pairs={{0,1},{1,0},{2,3},{3,2},{4,5},{5,4},{6,7},{7,6},{8,9},{9,8},{10,11... | collective-permute-start | bytes 3145736 | tf_op jit(solution)/shard_map/ppermute | solution.py:18
  50.2 20.9 %collective-permute-start.26 = (bf16[512,1024]{1,0:T(8,128)(2,1)}, bf16[512,1024]{1,0:T(8,128)(2,1)}, u32[]{:S(2)}, u32[]{:S(2)}) collective-permute-start(bf16[512,1024]{1,0:T(8,128)(2,1)} %collective-permute-done.25.refs_2_), channel_id=1, source_target_pairs={{0,1},{1,0},{2,3},{3,2},{4,5},{5,4},{6,7},{7,6},{8,9},{9,8},{10,11... | collective-permute-start | bytes 3145736 | tf_op jit(solution)/shard_map/ppermute | solution.py:18
  63.9 20.4 %collective-permute-start.21 = (bf16[512,1024]{1,0:T(8,128)(2,1)S(1)}, bf16[512,1024]{1,0:T(8,128)(2,1)S(1)}, u32[]{:S(2)}, u32[]{:S(2)}) collective-permute-start(bf16[512,1024]{1,0:T(8,128)(2,1)S(1)} %bitcast.98), channel_id=1, source_target_pairs={{0,1},{1,0},{2,3},{3,2},{4,5},{5,4},{6,7},{7,6},{8,9},{9,8},{10,11... | collective-permute-start | bytes 3145736 | tf_op jit(solution)/shard_map/ppermute | solution.py:18
  64.0 21.8 %collective-permute-start.20 = (bf16[1024,512]{1,0:T(8,128)(2,1)S(1)}, bf16[1024,512]{1,0:T(8,128)(2,1)S(1)}, u32[]{:S(2)}, u32[]{:S(2)}) collective-permute-start(bf16[1024,512]{1,0:T(8,128)(2,1)S(1)} %bitcast.104), channel_id=1, source_target_pairs={{0,1},{1,0},{2,3},{3,2},{4,5},{5,4},{6,7},{7,6},{8,9},{9,8},{10,11... | collective-permute-start | bytes 3145736 | tf_op jit(solution)/shard_map/ppermute | solution.py:18
  70.4 16.7 %collective-permute-start.23 = (bf16[512,1024]{1,0:T(8,128)(2,1)S(1)}, bf16[512,1024]{1,0:T(8,128)(2,1)S(1)}, u32[]{:S(2)}, u32[]{:S(2)}) collective-permute-start(bf16[512,1024]{1,0:T(8,128)(2,1)S(1)} %constant_dynamic-update-slice_fusion.refs_11_.refs_21_), channel_id=1, source_target_pairs={{0,1},{1,0},{2,3},{3,2},{4,5},{5,4},{6,7},{7,6},{8,9},{9,8},{10,11... | collective-permute-start | bytes 3145736 | tf_op jit(solution)/shard_map/ppermute | solution.py:18
  77.4 36.9 %collective-permute-start.4 = (bf16[512,512]{1,0:T(8,128)(2,1)}, bf16[512,512]{1,0:T(8,128)(2,1)}, u32[]{:S(2)}, u32[]{:S(2)}) collective-permute-start(bf16[512,512]{1,0:T(8,128)(2,1)} %panel.3.refs_0_), channel_id=1, source_target_pairs={{0,2},{1,3},{8,10},{9,11},{16,18},{17,19},{24,26},{25,27}} | collective-permute-start | bytes 1572872 | tf_op jit(solution)/shard_map/ppermute | solution.py:271
  82.9 32.1 %collective-permute-start.5 = (bf16[512,512]{1,0:T(8,128)(2,1)}, bf16[512,512]{1,0:T(8,128)(2,1)}, u32[]{:S(2)}, u32[]{:S(2)}) collective-permute-start(bf16[512,512]{1,0:T(8,128)(2,1)} %panel.3.refs_0_), channel_id=1, source_target_pairs={{6,4},{7,5},{14,12},{15,13},{22,20},{23,21},{30,28},{31,29}} | collective-permute-start | bytes 1572872 | tf_op jit(solution)/shard_map/ppermute | solution.py:272
  84.4 15.4 %collective-permute-start.18 = (bf16[256,512]{1,0:T(8,128)(2,1)}, bf16[256,512]{1,0:T(8,128)(2,1)}, u32[]{:S(2)}, u32[]{:S(2)}) collective-permute-start(bf16[256,512]{1,0:T(8,128)(2,1)} %collective-permute-done.16.refs_3_), channel_id=1, source_target_pairs={{4,6},{5,7},{12,14},{13,15},{20,22},{21,23},{28,30},{29,31}} | collective-permute-start | bytes 786440 | tf_op jit(solution)/shard_map/ppermute | solution.py:253
  93.9 17.3 %collective-permute-start.40 = (bf16[256,512]{1,0:T(8,128)(2,1)}, bf16[256,512]{1,0:T(8,128)(2,1)}, u32[]{:S(2)}, u32[]{:S(2)}) collective-permute-start(bf16[256,512]{1,0:T(8,128)(2,1)} %get-tuple-element.27), channel_id=1, source_target_pairs={{0,2},{1,3},{8,10},{9,11},{16,18},{17,19},{24,26},{25,27}} | collective-permute-start | bytes 786440 | tf_op jit(solution)/shard_map/ppermute | solution.py:296
  99.8 54.4 %collective-permute-start.6 = (bf16[512,512]{1,0:T(8,128)(2,1)}, bf16[512,512]{1,0:T(8,128)(2,1)S(1)}, u32[]{:S(2)}, u32[]{:S(2)}) collective-permute-start(bf16[512,512]{1,0:T(8,128)(2,1)} %panel.3.refs_0_), channel_id=1, source_target_pairs={{2,4},{3,5},{10,12},{11,13},{18,20},{19,21},{26,28},{27,29}} | collective-permute-start | bytes 1572872 | tf_op jit(solution)/shard_map/ppermute | solution.py:271
  100.5 20.2 %collective-permute-start.43 = (bf16[256,512]{1,0:T(8,128)(2,1)}, bf16[256,512]{1,0:T(8,128)(2,1)S(1)}, u32[]{:S(2)}, u32[]{:S(2)}) collective-permute-start(bf16[256,512]{1,0:T(8,128)(2,1)} %copy-done.22), channel_id=1, source_target_pairs={{6,4},{7,5},{14,12},{15,13},{22,20},{23,21},{30,28},{31,29}} | collective-permute-start | bytes 786440 | tf_op jit(solution)/shard_map/ppermute | solution.py:297
  120.0 34.9 %collective-permute-start.7 = (bf16[512,512]{1,0:T(8,128)(2,1)}, bf16[512,512]{1,0:T(8,128)(2,1)S(1)}, u32[]{:S(2)}, u32[]{:S(2)}) collective-permute-start(bf16[512,512]{1,0:T(8,128)(2,1)} %panel.3.refs_0_), channel_id=1, source_target_pairs={{4,2},{5,3},{12,10},{13,11},{20,18},{21,19},{28,26},{29,27}} | collective-permute-start | bytes 1572872 | tf_op jit(solution)/shard_map/ppermute | solution.py:272
  120.8 35.5 %collective-permute-start.8 = (bf16[512,512]{1,0:T(8,128)(2,1)S(1)}, bf16[512,512]{1,0:T(8,128)(2,1)S(1)}, u32[]{:S(2)}, u32[]{:S(2)}) collective-permute-start(bf16[512,512]{1,0:T(8,128)(2,1)S(1)} %get-tuple-element.50), channel_id=1, source_target_pairs={{2,4},{4,6},{3,5},{5,7},{10,12},{12,14},{11,13},{13,15},{18,20},{2... | collective-permute-start | bytes 1572872 | tf_op jit(solution)/shard_map/ppermute | solution.py:271
  121.5 34.8 %collective-permute-start.9 = (bf16[512,512]{1,0:T(8,128)(2,1)S(1)}, bf16[512,512]{1,0:T(8,128)(2,1)S(1)}, u32[]{:S(2)}, u32[]{:S(2)}) collective-permute-start(bf16[512,512]{1,0:T(8,128)(2,1)S(1)} %get-tuple-element.49), channel_id=1, source_target_pairs={{4,2},{2,0},{5,3},{3,1},{12,10},{10,8},{13,11},{11,9},{20,18},{18,... | collective-permute-start | bytes 1572872 | tf_op jit(solution)/shard_map/ppermute | solution.py:272
  137.1 27.1 %collective-permute-start.42 = (bf16[256,512]{1,0:T(8,128)(2,1)S(1)}, bf16[256,512]{1,0:T(8,128)(2,1)S(1)}, u32[]{:S(2)}, u32[]{:S(2)}) collective-permute-start(bf16[256,512]{1,0:T(8,128)(2,1)S(1)} %get-tuple-element.39), channel_id=1, source_target_pairs={{0,2},{2,4},{4,6},{1,3},{3,5},{5,7},{8,10},{10,12},{12,14},{9,11},... | collective-permute-start | bytes 786440 | tf_op jit(solution)/shard_map/ppermute | solution.py:296
  157.5 21.1 %collective-permute-start.10 = (bf16[512,512]{1,0:T(8,128)(2,1)S(1)}, bf16[512,512]{1,0:T(8,128)(2,1)S(1)}, u32[]{:S(2)}, u32[]{:S(2)}) collective-permute-start(bf16[512,512]{1,0:T(8,128)(2,1)S(1)} %get-tuple-element.48), channel_id=1, source_target_pairs={{4,6},{5,7},{12,14},{13,15},{20,22},{21,23},{28,30},{29,31}} | collective-permute-start | bytes 1572872 | tf_op jit(solution)/shard_map/ppermute | solution.py:271
  164.1 24.0 %collective-permute-start.11 = (bf16[512,512]{1,0:T(8,128)(2,1)S(1)}, bf16[512,512]{1,0:T(8,128)(2,1)S(1)}, u32[]{:S(2)}, u32[]{:S(2)}) collective-permute-start(bf16[512,512]{1,0:T(8,128)(2,1)S(1)} %get-tuple-element.47), channel_id=1, source_target_pairs={{2,0},{3,1},{10,8},{11,9},{18,16},{19,17},{26,24},{27,25}} | collective-permute-start | bytes 1572872 | tf_op jit(solution)/shard_map/ppermute | solution.py:272
  165.5 22.7 %collective-permute-start.12 = (bf16[512,512]{1,0:T(8,128)(2,1)S(1)}, bf16[512,512]{1,0:T(8,128)(2,1)S(1)}, u32[]{:S(2)}, u32[]{:S(2)}) collective-permute-start(bf16[512,512]{1,0:T(8,128)(2,1)S(1)} %get-tuple-element.46), channel_id=1, source_target_pairs={{4,6},{5,7},{12,14},{13,15},{20,22},{21,23},{28,30},{29,31}} | collective-permute-start | bytes 1572872 | tf_op jit(solution)/shard_map/ppermute | solution.py:271
  166.6 27.1 %collective-permute-start.13 = (bf16[512,512]{1,0:T(8,128)(2,1)S(1)}, bf16[512,512]{1,0:T(8,128)(2,1)S(1)}, u32[]{:S(2)}, u32[]{:S(2)}) collective-permute-start(bf16[512,512]{1,0:T(8,128)(2,1)S(1)} %get-tuple-element.45), channel_id=1, source_target_pairs={{2,0},{3,1},{10,8},{11,9},{18,16},{19,17},{26,24},{27,25}} | collective-permute-start | bytes 1572872 | tf_op jit(solution)/shard_map/ppermute | solution.py:272
  (64 other events, 593.4 us)

commit v4 on v3

--- a/solution.py
+++ b/solution.py
@@ -10,7 +10,7 @@
 CHUNKS = 2
 ANY = pl.BlockSpec(memory_space=pl.ANY)
 VMEM = pl.BlockSpec(memory_space=pltpu.VMEM)
-PARAMS = pltpu.CompilerParams(vmem_limit_bytes=20 * 1024 * 1024)
+PARAMS = pltpu.CompilerParams(vmem_limit_bytes=16 * 1024 * 1024)
 
 
 def exchanged(value, axis, steps):
@@ -55,44 +55,6 @@
 
 def nested(refs, sizes):
     return [refs[kx * sizes.col : (kx + 1) * sizes.col] for kx in range(sizes.sec)]
-
-
-def diagonal_kernel(sizes, step, *refs):
-    count = sizes.sec * sizes.col
-    tiles, (out, held, sems) = nested(refs[:count], sizes), refs[count:]
-    copies = chosen_copies(sizes, step, tiles, held, sems)
-    start_all(copies)
-    wait_all(copies)
-    first = lax.axis_index("sec") * sizes.width
-    for k in range(CHUNKS):
-        begin = pl.multiple_of(first + k * sizes.chunk, sizes.chunk)
-        left = held[lax.axis_index("col"), :, pl.ds(begin, sizes.chunk)].T
-        for d in range(sizes.row):
-            h, i = divmod(d, sizes.per_tile)
-            right = held[h, :, i * sizes.rows : (i + 1) * sizes.rows]
-            out[k, d] = jnp.dot(left, right, preferred_element_type=jnp.float32)
-
-
-def diagonal(sizes, step, tiles):
-    flat = [tile for per_section in tiles for tile in per_section]
-    shape = (CHUNKS, sizes.row, sizes.chunk, sizes.rows)
-    return pl.pallas_call(
-        functools.partial(diagonal_kernel, sizes, step),
-        out_shape=jax.ShapeDtypeStruct(shape, jnp.float32),
-        in_specs=[ANY] * len(flat),
-        out_specs=VMEM,
-        scratch_shapes=[
-            pltpu.VMEM((sizes.col, sizes.rows, sizes.cols), jnp.bfloat16),
-            pltpu.SemaphoreType.DMA((sizes.col,)),
-        ],
-        compiler_params=PARAMS,
-        cost_estimate=pl.CostEstimate(
-            flops=2 * sizes.rows * sizes.width * sizes.order,
-            bytes_accessed=2 * sizes.rows * sizes.order + 4 * sizes.width * sizes.order,
-            transcendentals=0,
-        ),
-        name="diagonal",
-    )(*flat)
 
 
 def panel_kernel(sizes, step, offset, own, *refs):
@@ -137,9 +99,9 @@
     blocks, refs = refs[:n_blocks], refs[n_blocks:]
     states, refs = refs[:n_states], refs[n_states:]
     tiles, refs = nested(refs[:n_tiles], sizes), refs[n_tiles:]
-    diagonals, refs = refs[0], refs[1:]
+    inverse_tiles, refs = nested(refs[:n_tiles], sizes), refs[n_tiles:]
     out, up_first, down_first, *refs = refs
-    state, rows, added, product, tile_sems, state_sems, added_sem = refs
+    state, rows, inverses, product, tile_sems, inverse_sems, state_sems = refs
     row_index, sec_index, col_index = (lax.axis_index(a) for a in ("row", "sec", "col"))
 
     state_copies = []
@@ -154,8 +116,8 @@
         copy.start()
     tile_copies = chosen_copies(sizes, step, tiles, rows, tile_sems)
     start_all(tile_copies)
-    added_copy = pltpu.make_async_copy(diagonals.at[part], added, added_sem)
-    added_copy.start()
+    inverse_copies = chosen_copies(sizes, step, inverse_tiles, inverses, inverse_sems)
+    start_all(inverse_copies)
     for copy in state_copies:
         copy.wait()
 
@@ -174,18 +136,22 @@
         pl.when((q >= low) & (q <= high))(functools.partial(accumulate, ref, q))
     image = product[...].astype(jnp.bfloat16)
     wait_all(tile_copies)
-    added_copy.wait()
+    wait_all(inverse_copies)
+    begin = pl.multiple_of(sec_index * sizes.width + part * sizes.chunk, sizes.chunk)
+    left = inverses[col_index, :, pl.ds(begin, sizes.chunk)].T
     for d in range(sizes.row):
         h, i = divmod(d, sizes.per_tile)
-        right = rows[h, :, i * sizes.rows : (i + 1) * sizes.rows]
+        block = slice(i * sizes.rows, (i + 1) * sizes.rows)
         place = lax.rem(d - row_index + sizes.row, sizes.row)
-        out[place] = jnp.dot(image, right, preferred_element_type=jnp.float32) + added[d]
+        out[place] = jnp.dot(
+            image, rows[h, :, block], preferred_element_type=jnp.float32
+        ) + jnp.dot(left, inverses[h, :, block], preferred_element_type=jnp.float32)
     up_first[...] = out[sizes.row - 1].astype(jnp.bfloat16)
     down_first[...] = out[1].astype(jnp.bfloat16)
 
 
-def products(sizes, step, part, blocks, states, tiles, diagonals):
-    flat = [tile for per_section in tiles for tile in per_section]
+def products(sizes, step, part, blocks, states, tiles, inverse_tiles):
+    flat = [tile for per_section in tiles + inverse_tiles for tile in per_section]
     shape = (sizes.row, sizes.chunk, sizes.rows)
     return pl.pallas_call(
         functools.partial(
@@ -193,25 +159,25 @@
         ),
         out_shape=[jax.ShapeDtypeStruct(shape, jnp.float32)]
         + [jax.ShapeDtypeStruct(shape[1:], jnp.bfloat16)] * 2,
-        in_specs=[VMEM] * len(blocks) + [ANY] * (len(states) + len(flat) + 1),
+        in_specs=[VMEM] * len(blocks) + [ANY] * (len(states) + len(flat)),
         out_specs=[VMEM] * 3,
         scratch_shapes=[
             pltpu.VMEM((sizes.order, sizes.rows), jnp.bfloat16),
             pltpu.VMEM((sizes.col, sizes.rows, sizes.cols), jnp.bfloat16),
-            pltpu.VMEM(shape, jnp.float32),
+            pltpu.VMEM((sizes.col, sizes.rows, sizes.cols), jnp.bfloat16),
             pltpu.VMEM(shape[1:], jnp.float32),
             pltpu.SemaphoreType.DMA((sizes.col,)),
+            pltpu.SemaphoreType.DMA((sizes.col,)),
             pltpu.SemaphoreType.DMA((len(states),)),
-            pltpu.SemaphoreType.DMA,
         ],
         compiler_params=PARAMS,
         cost_estimate=pl.CostEstimate(
-            flops=4 * sizes.rows * sizes.chunk * sizes.order,
+            flops=6 * sizes.rows * sizes.chunk * sizes.order,
             bytes_accessed=4 * sizes.rows * sizes.order + 10 * sizes.chunk * sizes.order,
             transcendentals=0,
         ),
         name="products",
-    )(*[b[1] for b in blocks], *[s[1] for s in states], *flat, diagonals)
+    )(*[b[1] for b in blocks], *[s[1] for s in states], *flat)
 
 
 def output_kernel(sizes, *refs):
@@ -257,48 +223,42 @@
     return found
 
 
-def trailing_gather(sizes, block):
+def first_slot(sizes, block):
+    last = sizes.row - 1
+    up = lax.ppermute(block, "row", [(i, i + 1) for i in range(last)])
+    down = lax.ppermute(block, "row", [(i, i - 1) for i in range(1, sizes.row)])
+    return up, down
+
+
+def scattered_sum(sizes, partials, gather=None):
+    blocks, up_first, down_first = partials
     row_index = lax.axis_index("row")
     last = sizes.row - 1
-    ups, downs = [], []
-    found = [(lambda row: (row, 0, last), block)]
-    for time in range(1, 2 * last):
-        up = down = block
-        if time > 2:
-            up = jnp.where(row_index == time - 1, block, ups[-2])
-            down = jnp.where(last - row_index == time - 1, block, downs[-2])
-        senders = [i for i in range(last) if time // 2 <= i <= time - 1]
-        ups.append(lax.ppermute(up, "row", [(i, i + 1) for i in senders]))
-        downs.append(lax.ppermute(down, "row", [(last - i, last - i - 1) for i in senders]))
-
-        def from_below(row, time=time):
-            q = 2 * row - 1 - time
-            return q, 0, row - 1
-
-        def from_above(row, time=time):
-            q = 2 * row - last + 1 + time
-            return q, row + 1, last
-
-        found += [(from_below, ups[-1]), (from_above, downs[-1])]
-    return found
-
-
-def scattered_sum(sizes, partials):
-    blocks, up_first, down_first = partials
-    last = sizes.row - 1
     up = down = None
+    found = []
     for slot in range(last):
         if slot:
             up_block = (blocks[last - slot] + up.astype(jnp.float32)).astype(jnp.bfloat16)
             down_block = (blocks[slot + 1] + down.astype(jnp.float32)).astype(jnp.bfloat16)
         else:
             up_block, down_block = up_first, down_first
-        up = lax.ppermute(up_block, "row", [(i, i + 1) for i in range(slot + 1)])
+        low = slot
+        if gather is not None:
+            if slot == 0:
+                up, down = gather
+            if slot < last - 1:
+                up_block = jnp.where(row_index <= slot, up_block, up)
+                down_block = jnp.where(last - row_index <= slot, down_block, down)
+                low = last - 1
+        up = lax.ppermute(up_block, "row", [(i, i + 1) for i in range(low + 1)])
         down = lax.ppermute(
-            down_block, "row", [(i, i - 1) for i in range(last - slot, last + 1)]
+            down_block, "row", [(i, i - 1) for i in range(last - low, last + 1)]
         )
+        if gather is not None and slot < last - 1:
+            found.append((lambda row, slot=slot: (row - 2 - slot, 0, last), up))
+            found.append((lambda row, slot=slot: (row + 2 + slot, 0, last), down))
     total = blocks[0] + up.astype(jnp.float32) + down.astype(jnp.float32)
-    return total.astype(jnp.bfloat16)
+    return total.astype(jnp.bfloat16), found
 
 
 def local(factors, inverses, sigma_end):
@@ -328,14 +288,7 @@
         sent = [[chunks[part]] for chunks in arrived_chunks[1:]]
         block = transposed_panel(sizes, last, factor, sent, part)
         factor_blocks[last, part] = neighbours_gathered(sizes, block)
-    for step in reversed(range(last)):
-        block = transposed_panel(sizes, step, factor, arrived_chunks[1:])
-        block = after(block, *[array for _, array in factor_blocks[step + 1, CHUNKS - 1][:3]])
-        blocks = trailing_gather(sizes, block)
-        for part in range(CHUNKS):
-            factor_blocks[step, part] = blocks
-
-    swapped = [chunks[-1] for chunks in arrived_chunks[1:]]
+    swapped = [chunk for chunks in arrived_chunks[1:] for chunk in chunks]
 
     def tiles_over_sections(tile, first_chunks):
         found = [tile]
@@ -367,13 +320,30 @@
 
     results = {}
     for step in reversed(range(sec_size)):
-        diagonals = diagonal(sizes, step, inverse_tiles)
+        trailing = []
+        if step:
+            earlier = [array for k in range(CHUNKS) for _, array in factor_blocks[step, k][-2:]]
+            for part in range(CHUNKS):
+                sent = [[chunks[part]] for chunks in arrived_chunks[1:]]
+                block = after(transposed_panel(sizes, step - 1, factor, sent, part), *earlier)
+                trailing.append((block, first_slot(sizes, block)))
         next_pieces = []
         for part in range(CHUNKS):
-            partial = products(
-                sizes, step, part, factor_blocks[step, part], state_pieces, factor_tiles, diagonals
+            partials = products(
+                sizes, step, part, factor_blocks[step, part], state_pieces, factor_tiles, inverse_tiles
             )
-            total = scattered_sum(sizes, partial)
+            if step:
+                block, (up, down) = trailing[part]
+                total, found = scattered_sum(sizes, partials, (up, down))
+                edge = sizes.row - 1
+                factor_blocks[step - 1, part] = [
+                    (lambda row: (row, 0, edge), block),
+                    (lambda row: (row - 1, 0, edge), up),
+                    (lambda row: (row + 1, 0, edge), down),
+                    *found,
+                ]
+            else:
+                total, _ = scattered_sum(sizes, partials)
             for kx in range(sec_size):
                 piece = exchanged(total, "sec", kx) if kx else total
                 results[step, kx, part] = piece

time: 253 us -> 205 us (0.81)
  waiting for transfers between devices: 84.7 us -> 56.3 us
  starting transfers between devices: 118 us -> 108 us
  Pallas kernels: 25.9 us -> 21.7 us
    ppermute x34 -> x28, waiting for transfers between devices: 38.8 us -> 22.8 us  [the longest x12 14.9 us: scattered_sum(): lax.ppermute(down_block, 'row', [(i, i - 1) for i in range(last - low, la...]
    ppermute x17, waiting for transfers between devices: 33.3 us -> 17.7 us  [exchanged(): lax.ppermute(value, axis, [(i, (i + steps) % count) for i in range(count)])]
    ppermute x34 -> x28, starting transfers between devices: 84.4 us -> 72.2 us  [the longest x12 47.3 us: scattered_sum(): up = lax.ppermute(up_block, 'row', [(i, i + 1) for i in range(low + 1)])]
    pallas_call x2 -> x0, Pallas kernels: 5.76 us -> none  [diagonal(): pl.pallas_call(functools.partial(diagonal_kernel, sizes, step), out_shape...]
    ppermute x6, waiting for transfers between devices: 11.5 us -> 15.8 us  [neighbours_gathered(): lax.ppermute(down, 'row', [(i, i - 1) for i in range(1, sizes.row - slot)])]
    unnamed x51 -> x43, local copies, waits for them, and re-layouts: 12.3 us -> 11.3 us
  transfers between devices with their start and end apart: 63 -> 57, of which waited for: 20 -> 21; matrix products, arithmetic and copies ran while one was open for 4% -> 3% of each run, Pallas kernels for 8% -> 8%
where the time goes in v4:
time: 205 us; the launch traced here: 203 us
  starting transfers between devices  108 us (53%)
  waiting for transfers between devices  56.3 us (27%)
  Pallas kernels  21.7 us (11%)
  local copies, waits for them, and re-layouts  12.7 us (6%)
  other arithmetic  3.77 us (2%)
    ppermute x12, starting transfers between devices, scattered_sum(): up = lax.ppermute(up_block, 'row', [(i, i + 1) for i in range(low + 1)])  47.3 us
    pallas_call x4, Pallas kernels, products(): pl.pallas_call(functools.partial(products_kernel, sizes, step, part, [b[0...  18.6 us
    ppermute x17, waiting for transfers between devices, exchanged(): lax.ppermute(value, axis, [(i, (i + steps) % count) for i in range(count)])  17.7 us
    ppermute x6, waiting for transfers between devices, neighbours_gathered(): lax.ppermute(down, 'row', [(i, i - 1) for i in range(1, sizes.row - slot)])  15.8 us
    ppermute x12, waiting for transfers between devices, scattered_sum(): lax.ppermute(down_block, 'row', [(i, i - 1) for i in range(last - low, la...  14.9 us
    ppermute x6, starting transfers between devices, neighbours_gathered(): up = lax.ppermute(up, 'row', [(i, i + 1) for i in range(slot, last)])  14.1 us
    ppermute x17, starting transfers between devices, exchanged(): lax.ppermute(value, axis, [(i, (i + steps) % count) for i in range(count)])  13.9 us
    ppermute x12, starting transfers between devices, scattered_sum(): lax.ppermute(down_block, 'row', [(i, i - 1) for i in range(last - low, la...  13 us
  transfers between devices with their start and end apart: 57, of which 21 were waited for; matrix products, arithmetic and copies ran while one was open for 3% of the time, Pallas kernels for 8%

profile of v4, /device:TPU:0, one launch (start us, length us, event | category | flops | bytes accessed | tf_op | source)
XLA Modules:
  0.0 203.2 jit_solution(14864671100158367094)
XLA Ops:
  4.2 7.1 %collective-permute-done.7.refs_0_ = bf16[512,256]{1,0:T(8,128)(2,1)S(1)} collective-permute-done((bf16[512,256]{1,0:T(8,128)(2,1)S(1)}, bf16[512,256]{1,0:T(8,128)(2,1)S(1)}, u32[]{:S(2)}, u32[]{:S(2)}) %collective-permute-start.7) | collective-permute-done | bytes 262176 | tf_op jit(solution)/shard_map/ppermute | solution.py:18
  12.8 4.1 %collective-permute-start.8 = (bf16[256,512]{1,0:T(8,128)(2,1)S(1)}, bf16[256,512]{1,0:T(8,128)(2,1)S(1)}, u32[]{:S(2)}, u32[]{:S(2)}) collective-permute-start(bf16[256,512]{1,0:T(8,128)(2,1)S(1)} %panel.6.refs_0_), channel_id=1, source_target_pairs={{0,2},{2,4},{4,6},{1,3},{3,5},{5,7},{8,10},{10,12},{12,14},{9,11},... | collective-permute-start | bytes 786440 | tf_op jit(solution)/shard_map/ppermute | solution.py:219
  20.5 4.6 %collective-permute-start.1 = (bf16[256,512]{1,0:T(8,128)(2,1)S(1)}, bf16[256,512]{1,0:T(8,128)(2,1)S(1)}, u32[]{:S(2)}, u32[]{:S(2)}) collective-permute-start(bf16[256,512]{1,0:T(8,128)(2,1)S(1)} %panel.5.refs_0_), channel_id=1, source_target_pairs={{0,2},{2,4},{4,6},{1,3},{3,5},{5,7},{8,10},{10,12},{12,14},{9,11},... | collective-permute-start | bytes 786440 | tf_op jit(solution)/shard_map/ppermute | solution.py:219
  43.6 8.8 %collective-permute-done.5.refs_4_ = bf16[256,512]{1,0:T(8,128)(2,1)} collective-permute-done((bf16[256,512]{1,0:T(8,128)(2,1)S(1)}, bf16[256,512]{1,0:T(8,128)(2,1)}, u32[]{:S(2)}, u32[]{:S(2)}) %collective-permute-start.5) | collective-permute-done | bytes 262176 | tf_op jit(solution)/shard_map/ppermute | solution.py:220
  64.9 4.7 %collective-permute-start.32 = (bf16[256,512]{1,0:T(8,128)(2,1)}, bf16[256,512]{1,0:T(8,128)(2,1)S(1)}, u32[]{:S(2)}, u32[]{:S(2)}) collective-permute-start(bf16[256,512]{1,0:T(8,128)(2,1)} %panel.7.refs_0_), channel_id=1, source_target_pairs={{0,2},{2,4},{4,6},{1,3},{3,5},{5,7},{8,10},{10,12},{12,14},{9,11},... | collective-permute-start | bytes 786440 | tf_op jit(solution)/shard_map/ppermute | solution.py:228
  71.0 4.6 %collective-permute-start.14 = (bf16[256,512]{1,0:T(8,128)(2,1)S(1)}, bf16[256,512]{1,0:T(8,128)(2,1)S(1)}, u32[]{:S(2)}, u32[]{:S(2)}) collective-permute-start(bf16[256,512]{1,0:T(8,128)(2,1)S(1)} %panel.4.refs_0_), channel_id=1, source_target_pairs={{0,2},{2,4},{4,6},{1,3},{3,5},{5,7},{8,10},{10,12},{12,14},{9,11},... | collective-permute-start | bytes 786440 | tf_op jit(solution)/shard_map/ppermute | solution.py:228
  78.4 5.5 %products.5 = (f32[4,256,512]{2,1,0:T(8,128)S(1)}, bf16[256,512]{1,0:T(8,128)(2,1)S(1)}, bf16[256,512]{1,0:T(8,128)(2,1)S(1)}) custom-call(bf16[256,512]{1,0:T(8,128)(2,1)S(1)} %copy-done.10, bf16[256,512]{1,0:T(8,128)(2,1)S(1)} %copy-done.14, bf16[256,512]{1,0:T(8,128)(2,1)S(1)} %copy-done.18, bf16[256,512]{1,0:T(8,128)(2,1)} %collective-permute-done.9.refs_3_, ...), custom_call_target="tpu_custom_call" | custom-call | flops 1610612736 | bytes 9437184 | tf_op jit(solution)/shard_map/products/pallas_call | solution.py:156
  86.3 4.6 %collective-permute-start.33 = (bf16[256,512]{1,0:T(8,128)(2,1)S(1)}, bf16[256,512]{1,0:T(8,128)(2,1)S(1)}, u32[]{:S(2)}, u32[]{:S(2)}) collective-permute-start(bf16[256,512]{1,0:T(8,128)(2,1)S(1)} %broadcast_select_fusion.2), channel_id=1, source_target_pairs={{0,2},{2,4},{4,6},{1,3},{3,5},{5,7},{8,10},{10,12},{12,14},{9,11},... | collective-permute-start | bytes 786440 | tf_op jit(solution)/shard_map/ppermute | solution.py:253
  90.9 5.5 %products.4 = (f32[4,256,512]{2,1,0:T(8,128)S(1)}, bf16[256,512]{1,0:T(8,128)(2,1)S(1)}, bf16[256,512]{1,0:T(8,128)(2,1)S(1)}) custom-call(bf16[256,512]{1,0:T(8,128)(2,1)S(1)} %copy-done.8, bf16[256,512]{1,0:T(8,128)(2,1)S(1)} %copy-done.12, bf16[256,512]{1,0:T(8,128)(2,1)S(1)} %copy-done.16, bf16[256,512]{1,0:T(8,128)(2,1)} %collective-permute-done.2.refs_3_, ...), custom_call_target="tpu_custom_call" | custom-call | flops 1610612736 | bytes 9437184 | tf_op jit(solution)/shard_map/products/pallas_call | solution.py:156
  97.7 4.6 %collective-permute-start.23 = (bf16[256,512]{1,0:T(8,128)(2,1)S(1)}, bf16[256,512]{1,0:T(8,128)(2,1)S(1)}, u32[]{:S(2)}, u32[]{:S(2)}) collective-permute-start(bf16[256,512]{1,0:T(8,128)(2,1)S(1)} %broadcast_select_fusion.3), channel_id=1, source_target_pairs={{0,2},{2,4},{4,6},{1,3},{3,5},{5,7},{8,10},{10,12},{12,14},{9,11},... | collective-permute-start | bytes 786440 | tf_op jit(solution)/shard_map/ppermute | solution.py:253
  102.5 3.7 %collective-permute-start.34 = (bf16[256,512]{1,0:T(8,128)(2,1)S(1)}, bf16[256,512]{1,0:T(8,128)(2,1)S(1)}, u32[]{:S(2)}, u32[]{:S(2)}) collective-permute-start(bf16[256,512]{1,0:T(8,128)(2,1)S(1)} %get-tuple-element.43), channel_id=1, source_target_pairs={{0,2},{2,4},{4,6},{1,3},{3,5},{5,7},{8,10},{10,12},{12,14},{9,11},... | collective-permute-start | bytes 786440 | tf_op jit(solution)/shard_map/ppermute | solution.py:253
  108.6 4.4 %collective-permute-start.25 = (bf16[256,512]{1,0:T(8,128)(2,1)S(1)}, bf16[256,512]{1,0:T(8,128)(2,1)S(1)}, u32[]{:S(2)}, u32[]{:S(2)}) collective-permute-start(bf16[256,512]{1,0:T(8,128)(2,1)S(1)} %get-tuple-element.48), channel_id=1, source_target_pairs={{0,2},{2,4},{4,6},{1,3},{3,5},{5,7},{8,10},{10,12},{12,14},{9,11},... | collective-permute-start | bytes 786440 | tf_op jit(solution)/shard_map/ppermute | solution.py:253
  115.3 4.2 %collective-permute-start.35 = (bf16[256,512]{1,0:T(8,128)(2,1)S(1)}, bf16[256,512]{1,0:T(8,128)(2,1)S(1)}, u32[]{:S(2)}, u32[]{:S(2)}) collective-permute-start(bf16[256,512]{1,0:T(8,128)(2,1)S(1)} %get-tuple-element.41), channel_id=1, source_target_pairs={{0,2},{2,4},{4,6},{1,3},{3,5},{5,7},{8,10},{10,12},{12,14},{9,11},... | collective-permute-start | bytes 786440 | tf_op jit(solution)/shard_map/ppermute | solution.py:253
  120.8 3.3 %collective-permute-done.26.refs_6_ = bf16[256,512]{1,0:T(8,128)(2,1)S(1)} collective-permute-done((bf16[256,512]{1,0:T(8,128)(2,1)S(1)}, bf16[256,512]{1,0:T(8,128)(2,1)S(1)}, u32[]{:S(2)}, u32[]{:S(2)}) %collective-permute-start.26) | collective-permute-done | bytes 262176 | tf_op jit(solution)/shard_map/ppermute | solution.py:254
  132.1 3.5 %collective-permute-done.28 = bf16[256,512]{1,0:T(8,128)(2,1)S(1)} collective-permute-done((bf16[256,512]{1,0:T(8,128)(2,1)S(1)}, bf16[256,512]{1,0:T(8,128)(2,1)S(1)}, u32[]{:S(2)}, u32[]{:S(2)}) %collective-permute-start.28) | collective-permute-done | bytes 262176 | tf_op jit(solution)/shard_map/ppermute | solution.py:254
  138.8 3.4 %collective-permute-done.30.refs_9_.refs_6_ = bf16[256,512]{1,0:T(8,128)(2,1)S(1)} collective-permute-done((bf16[256,512]{1,0:T(8,128)(2,1)S(1)}, bf16[256,512]{1,0:T(8,128)(2,1)S(1)}, u32[]{:S(2)}, u32[]{:S(2)}) %collective-permute-start.30) | collective-permute-done | bytes 262176 | tf_op jit(solution)/shard_map/ppermute | solution.py:18
  143.7 4.4 %products.7 = (f32[4,256,512]{2,1,0:T(8,128)S(1)}, bf16[256,512]{1,0:T(8,128)(2,1)S(1)}, bf16[256,512]{1,0:T(8,128)(2,1)S(1)}) custom-call(bf16[256,512]{1,0:T(8,128)(2,1)} %panel.7.refs_0_, bf16[256,512]{1,0:T(8,128)(2,1)S(1)} %collective-permute-done.32.refs_1_, bf16[256,512]{1,0:T(8,128)(2,1)} %collective-permute-done.36.refs_2_, ...), custom_call_target="tpu_custom_call" | custom-call | flops 1610612736 | bytes 9437184 | tf_op jit(solution)/shard_map/products/pallas_call | solution.py:156
  157.4 4.4 %collective-permute-start.50 = (bf16[256,512]{1,0:T(8,128)(2,1)S(1)}, bf16[256,512]{1,0:T(8,128)(2,1)S(1)}, u32[]{:S(2)}, u32[]{:S(2)}) collective-permute-start(bf16[256,512]{1,0:T(8,128)(2,1)S(1)} %fusion.1), channel_id=1, source_target_pairs={{0,2},{2,4},{1,3},{3,5},{8,10},{10,12},{9,11},{11,13},{16,18},{18,... | collective-permute-start | bytes 786440 | tf_op jit(solution)/shard_map/ppermute | solution.py:253
  163.0 4.4 %collective-permute-start.44 = (bf16[256,512]{1,0:T(8,128)(2,1)S(1)}, bf16[256,512]{1,0:T(8,128)(2,1)S(1)}, u32[]{:S(2)}, u32[]{:S(2)}) collective-permute-start(bf16[256,512]{1,0:T(8,128)(2,1)S(1)} %fusion.7), channel_id=1, source_target_pairs={{0,2},{2,4},{1,3},{3,5},{8,10},{10,12},{9,11},{11,13},{16,18},{18,... | collective-permute-start | bytes 786440 | tf_op jit(solution)/shard_map/ppermute | solution.py:253
  169.4 4.0 %collective-permute-done.44 = bf16[256,512]{1,0:T(8,128)(2,1)S(1)} collective-permute-done((bf16[256,512]{1,0:T(8,128)(2,1)S(1)}, bf16[256,512]{1,0:T(8,128)(2,1)S(1)}, u32[]{:S(2)}, u32[]{:S(2)}) %collective-permute-start.44) | collective-permute-done | bytes 262176 | tf_op jit(solution)/shard_map/ppermute | solution.py:253
  174.2 5.0 %collective-permute-start.51 = (bf16[256,512]{1,0:T(8,128)(2,1)S(1)}, bf16[256,512]{1,0:T(8,128)(2,1)S(1)}, u32[]{:S(2)}, u32[]{:S(2)}) collective-permute-start(bf16[256,512]{1,0:T(8,128)(2,1)S(1)} %get-tuple-element.37), channel_id=1, source_target_pairs={{0,2},{2,4},{4,6},{1,3},{3,5},{5,7},{8,10},{10,12},{12,14},{9,11},... | collective-permute-start | bytes 786440 | tf_op jit(solution)/shard_map/ppermute | solution.py:253
  180.6 5.2 %collective-permute-start.45 = (bf16[256,512]{1,0:T(8,128)(2,1)S(1)}, bf16[256,512]{1,0:T(8,128)(2,1)S(1)}, u32[]{:S(2)}, u32[]{:S(2)}) collective-permute-start(bf16[256,512]{1,0:T(8,128)(2,1)S(1)} %get-tuple-element.39), channel_id=1, source_target_pairs={{0,2},{2,4},{4,6},{1,3},{3,5},{5,7},{8,10},{10,12},{12,14},{9,11},... | collective-permute-start | bytes 786440 | tf_op jit(solution)/shard_map/ppermute | solution.py:253
  191.3 3.4 %collective-permute-done.48 = bf16[256,512]{1,0:T(8,128)(2,1)S(1)} collective-permute-done((bf16[256,512]{1,0:T(8,128)(2,1)S(1)}, bf16[256,512]{1,0:T(8,128)(2,1)S(1)}, u32[]{:S(2)}, u32[]{:S(2)}) %collective-permute-start.48) | collective-permute-done | bytes 262176 | tf_op jit(solution)/shard_map/ppermute | solution.py:254
  196.7 4.8 %collective-permute-done.55.refs_2_ = bf16[256,512]{1,0:T(8,128)(2,1)S(1)} collective-permute-done((bf16[256,512]{1,0:T(8,128)(2,1)S(1)}, bf16[256,512]{1,0:T(8,128)(2,1)S(1)}, u32[]{:S(2)}, u32[]{:S(2)}) %collective-permute-start.55) | collective-permute-done | bytes 262176 | tf_op jit(solution)/shard_map/ppermute | solution.py:18
  (165 shorter events, 90.3 us)
Async XLA Ops:
  4.2 12.8 %collective-permute-start = (bf16[512,256]{1,0:T(8,128)(2,1)S(1)}, bf16[512,256]{1,0:T(8,128)(2,1)S(1)}, u32[]{:S(2)}, u32[]{:S(2)}) collective-permute-start(bf16[512,256]{1,0:T(8,128)(2,1)S(1)} %get-tuple-element.50), channel_id=1, source_target_pairs={{0,8},{8,0},{1,9},{9,1},{2,10},{10,2},{3,11},{11,3},{4,12},{12,4},... | collective-permute-start | bytes 786440 | tf_op jit(solution)/shard_map/ppermute | solution.py:18
  12.8 12.3 %collective-permute-start.8 = (bf16[256,512]{1,0:T(8,128)(2,1)S(1)}, bf16[256,512]{1,0:T(8,128)(2,1)S(1)}, u32[]{:S(2)}, u32[]{:S(2)}) collective-permute-start(bf16[256,512]{1,0:T(8,128)(2,1)S(1)} %panel.6.refs_0_), channel_id=1, source_target_pairs={{0,2},{2,4},{4,6},{1,3},{3,5},{5,7},{8,10},{10,12},{12,14},{9,11},... | collective-permute-start | bytes 786440 | tf_op jit(solution)/shard_map/ppermute | solution.py:219
  16.9 18.5 %collective-permute-start.18 = (bf16[512,512]{1,0:T(8,128)(2,1)S(1)}, bf16[512,512]{1,0:T(8,128)(2,1)S(1)}, u32[]{:S(2)}, u32[]{:S(2)}) collective-permute-start(bf16[512,512]{1,0:T(8,128)(2,1)S(1)} %dynamic-slice_bitcast_fusion), channel_id=1, source_target_pairs={{0,8},{8,0},{1,9},{9,1},{2,10},{10,2},{3,11},{11,3},{4,12},{12,4},... | collective-permute-start | bytes 1572872 | tf_op jit(solution)/shard_map/ppermute | solution.py:18
  18.5 42.5 %collective-permute-start.21 = (bf16[512,1024]{1,0:T(8,128)(2,1)S(1)}, bf16[512,1024]{1,0:T(8,128)(2,1)}, u32[]{:S(2)}, u32[]{:S(2)}) collective-permute-start(bf16[512,1024]{1,0:T(8,128)(2,1)S(1)} %bitcast.113), channel_id=1, source_target_pairs={{0,8},{8,0},{1,9},{9,1},{2,10},{10,2},{3,11},{11,3},{4,12},{12,4},... | collective-permute-start | bytes 3145736 | tf_op jit(solution)/shard_map/ppermute | solution.py:18
  29.7 11.2 %collective-permute-start.12 = (bf16[256,512]{1,0:T(8,128)(2,1)S(1)}, bf16[256,512]{1,0:T(8,128)(2,1)}, u32[]{:S(2)}, u32[]{:S(2)}) collective-permute-start(bf16[256,512]{1,0:T(8,128)(2,1)S(1)} %collective-permute-done.11.refs_2_), channel_id=1, source_target_pairs={{2,0},{4,2},{3,1},{5,3},{10,8},{12,10},{11,9},{13,11},{18,16},{20,... | collective-permute-start | bytes 786440 | tf_op jit(solution)/shard_map/ppermute | solution.py:220
  35.4 17.0 %collective-permute-start.5 = (bf16[256,512]{1,0:T(8,128)(2,1)S(1)}, bf16[256,512]{1,0:T(8,128)(2,1)}, u32[]{:S(2)}, u32[]{:S(2)}) collective-permute-start(bf16[256,512]{1,0:T(8,128)(2,1)S(1)} %collective-permute-done.4.refs_2_), channel_id=1, source_target_pairs={{2,0},{4,2},{3,1},{5,3},{10,8},{12,10},{11,9},{13,11},{18,16},{20,... | collective-permute-start | bytes 786440 | tf_op jit(solution)/shard_map/ppermute | solution.py:220
  37.4 20.2 %collective-permute-start.10 = (bf16[256,512]{1,0:T(8,128)(2,1)}, bf16[256,512]{1,0:T(8,128)(2,1)}, u32[]{:S(2)}, u32[]{:S(2)}) collective-permute-start(bf16[256,512]{1,0:T(8,128)(2,1)} %collective-permute-done.9.refs_3_), channel_id=1, source_target_pairs={{4,6},{5,7},{12,14},{13,15},{20,22},{21,23},{28,30},{29,31}} | collective-permute-start | bytes 786440 | tf_op jit(solution)/shard_map/ppermute | solution.py:219
  40.9 16.8 %collective-permute-start.13 = (bf16[256,512]{1,0:T(8,128)(2,1)}, bf16[256,512]{1,0:T(8,128)(2,1)}, u32[]{:S(2)}, u32[]{:S(2)}) collective-permute-start(bf16[256,512]{1,0:T(8,128)(2,1)} %collective-permute-done.12.refs_4_), channel_id=1, source_target_pairs={{2,0},{3,1},{10,8},{11,9},{18,16},{19,17},{26,24},{27,25}} | collective-permute-start | bytes 786440 | tf_op jit(solution)/shard_map/ppermute | solution.py:220
  42.2 16.0 %collective-permute-start.3 = (bf16[256,512]{1,0:T(8,128)(2,1)}, bf16[256,512]{1,0:T(8,128)(2,1)}, u32[]{:S(2)}, u32[]{:S(2)}) collective-permute-start(bf16[256,512]{1,0:T(8,128)(2,1)} %collective-permute-done.2.refs_3_), channel_id=1, source_target_pairs={{4,6},{5,7},{12,14},{13,15},{20,22},{21,23},{28,30},{29,31}} | collective-permute-start | bytes 786440 | tf_op jit(solution)/shard_map/ppermute | solution.py:219
  58.2 11.4 %collective-permute-start.16 = (bf16[1024,512]{1,0:T(8,128)(2,1)}, bf16[1024,512]{1,0:T(8,128)(2,1)}, u32[]{:S(2)}, u32[]{:S(2)}) collective-permute-start(bf16[1024,512]{1,0:T(8,128)(2,1)} %bitcast.103.refs_7_), channel_id=1, source_target_pairs={{0,1},{1,0},{2,3},{3,2},{4,5},{5,4},{6,7},{7,6},{8,9},{9,8},{10,11... | collective-permute-start | bytes 3145736 | tf_op jit(solution)/shard_map/ppermute | solution.py:18
  61.0 14.5 %collective-permute-start.22 = (bf16[512,1024]{1,0:T(8,128)(2,1)}, bf16[512,1024]{1,0:T(8,128)(2,1)}, u32[]{:S(2)}, u32[]{:S(2)}) collective-permute-start(bf16[512,1024]{1,0:T(8,128)(2,1)} %collective-permute-done.21.refs_15_.refs_21_), channel_id=1, source_target_pairs={{0,1},{1,0},{2,3},{3,2},{4,5},{5,4},{6,7},{7,6},{8,9},{9,8},{10,11... | collective-permute-start | bytes 3145736 | tf_op jit(solution)/shard_map/ppermute | solution.py:18
  63.4 20.5 %collective-permute-start.36 = (bf16[256,512]{1,0:T(8,128)(2,1)}, bf16[256,512]{1,0:T(8,128)(2,1)}, u32[]{:S(2)}, u32[]{:S(2)}) collective-permute-start(bf16[256,512]{1,0:T(8,128)(2,1)} %panel.7.refs_0_), channel_id=1, source_target_pairs={{2,0},{4,2},{6,4},{3,1},{5,3},{7,5},{10,8},{12,10},{14,12},{11,9},... | collective-permute-start | bytes 786440 | tf_op jit(solution)/shard_map/ppermute | solution.py:229
  64.9 21.3 %collective-permute-start.32 = (bf16[256,512]{1,0:T(8,128)(2,1)}, bf16[256,512]{1,0:T(8,128)(2,1)S(1)}, u32[]{:S(2)}, u32[]{:S(2)}) collective-permute-start(bf16[256,512]{1,0:T(8,128)(2,1)} %panel.7.refs_0_), channel_id=1, source_target_pairs={{0,2},{2,4},{4,6},{1,3},{3,5},{5,7},{8,10},{10,12},{12,14},{9,11},... | collective-permute-start | bytes 786440 | tf_op jit(solution)/shard_map/ppermute | solution.py:228
  69.7 26.7 %collective-permute-start.15 = (bf16[256,512]{1,0:T(8,128)(2,1)S(1)}, bf16[256,512]{1,0:T(8,128)(2,1)S(1)}, u32[]{:S(2)}, u32[]{:S(2)}) collective-permute-start(bf16[256,512]{1,0:T(8,128)(2,1)S(1)} %panel.4.refs_0_), channel_id=1, source_target_pairs={{2,0},{4,2},{6,4},{3,1},{5,3},{7,5},{10,8},{12,10},{14,12},{11,9},... | collective-permute-start | bytes 786440 | tf_op jit(solution)/shard_map/ppermute | solution.py:229
  71.0 26.7 %collective-permute-start.14 = (bf16[256,512]{1,0:T(8,128)(2,1)S(1)}, bf16[256,512]{1,0:T(8,128)(2,1)S(1)}, u32[]{:S(2)}, u32[]{:S(2)}) collective-permute-start(bf16[256,512]{1,0:T(8,128)(2,1)S(1)} %panel.4.refs_0_), channel_id=1, source_target_pairs={{0,2},{2,4},{4,6},{1,3},{3,5},{5,7},{8,10},{10,12},{12,14},{9,11},... | collective-permute-start | bytes 786440 | tf_op jit(solution)/shard_map/ppermute | solution.py:228
  84.9 17.4 %collective-permute-start.37 = (bf16[256,512]{1,0:T(8,128)(2,1)S(1)}, bf16[256,512]{1,0:T(8,128)(2,1)S(1)}, u32[]{:S(2)}, u32[]{:S(2)}) collective-permute-start(bf16[256,512]{1,0:T(8,128)(2,1)S(1)} %broadcast_select_fusion), channel_id=1, source_target_pairs={{2,0},{4,2},{6,4},{3,1},{5,3},{7,5},{10,8},{12,10},{14,12},{11,9},... | collective-permute-start | bytes 786440 | tf_op jit(solution)/shard_map/ppermute | solution.py:254
  86.3 16.1 %collective-permute-start.33 = (bf16[256,512]{1,0:T(8,128)(2,1)S(1)}, bf16[256,512]{1,0:T(8,128)(2,1)S(1)}, u32[]{:S(2)}, u32[]{:S(2)}) collective-permute-start(bf16[256,512]{1,0:T(8,128)(2,1)S(1)} %broadcast_select_fusion.2), channel_id=1, source_target_pairs={{0,2},{2,4},{4,6},{1,3},{3,5},{5,7},{8,10},{10,12},{12,14},{9,11},... | collective-permute-start | bytes 786440 | tf_op jit(solution)/shard_map/ppermute | solution.py:253
  102.5 11.8 %collective-permute-start.34 = (bf16[256,512]{1,0:T(8,128)(2,1)S(1)}, bf16[256,512]{1,0:T(8,128)(2,1)S(1)}, u32[]{:S(2)}, u32[]{:S(2)}) collective-permute-start(bf16[256,512]{1,0:T(8,128)(2,1)S(1)} %get-tuple-element.43), channel_id=1, source_target_pairs={{0,2},{2,4},{4,6},{1,3},{3,5},{5,7},{8,10},{10,12},{12,14},{9,11},... | collective-permute-start | bytes 786440 | tf_op jit(solution)/shard_map/ppermute | solution.py:253
  108.6 12.1 %collective-permute-start.25 = (bf16[256,512]{1,0:T(8,128)(2,1)S(1)}, bf16[256,512]{1,0:T(8,128)(2,1)S(1)}, u32[]{:S(2)}, u32[]{:S(2)}) collective-permute-start(bf16[256,512]{1,0:T(8,128)(2,1)S(1)} %get-tuple-element.48), channel_id=1, source_target_pairs={{0,2},{2,4},{4,6},{1,3},{3,5},{5,7},{8,10},{10,12},{12,14},{9,11},... | collective-permute-start | bytes 786440 | tf_op jit(solution)/shard_map/ppermute | solution.py:253
  115.3 13.4 %collective-permute-start.35 = (bf16[256,512]{1,0:T(8,128)(2,1)S(1)}, bf16[256,512]{1,0:T(8,128)(2,1)S(1)}, u32[]{:S(2)}, u32[]{:S(2)}) collective-permute-start(bf16[256,512]{1,0:T(8,128)(2,1)S(1)} %get-tuple-element.41), channel_id=1, source_target_pairs={{0,2},{2,4},{4,6},{1,3},{3,5},{5,7},{8,10},{10,12},{12,14},{9,11},... | collective-permute-start | bytes 786440 | tf_op jit(solution)/shard_map/ppermute | solution.py:253
  155.2 12.2 %collective-permute-start.52 = (bf16[256,512]{1,0:T(8,128)(2,1)S(1)}, bf16[256,512]{1,0:T(8,128)(2,1)S(1)}, u32[]{:S(2)}, u32[]{:S(2)}) collective-permute-start(bf16[256,512]{1,0:T(8,128)(2,1)S(1)} %get-tuple-element.36), channel_id=1, source_target_pairs={{6,4},{7,5},{14,12},{15,13},{22,20},{23,21},{30,28},{31,29}} | collective-permute-start | bytes 786440 | tf_op jit(solution)/shard_map/ppermute | solution.py:254
  157.4 11.2 %collective-permute-start.50 = (bf16[256,512]{1,0:T(8,128)(2,1)S(1)}, bf16[256,512]{1,0:T(8,128)(2,1)S(1)}, u32[]{:S(2)}, u32[]{:S(2)}) collective-permute-start(bf16[256,512]{1,0:T(8,128)(2,1)S(1)} %fusion.1), channel_id=1, source_target_pairs={{0,2},{2,4},{1,3},{3,5},{8,10},{10,12},{9,11},{11,13},{16,18},{18,... | collective-permute-start | bytes 786440 | tf_op jit(solution)/shard_map/ppermute | solution.py:253
  173.5 12.3 %collective-permute-start.47 = (bf16[256,512]{1,0:T(8,128)(2,1)S(1)}, bf16[256,512]{1,0:T(8,128)(2,1)S(1)}, u32[]{:S(2)}, u32[]{:S(2)}) collective-permute-start(bf16[256,512]{1,0:T(8,128)(2,1)S(1)} %get-tuple-element.40), channel_id=1, source_target_pairs={{4,2},{6,4},{5,3},{7,5},{12,10},{14,12},{13,11},{15,13},{20,18},{2... | collective-permute-start | bytes 786440 | tf_op jit(solution)/shard_map/ppermute | solution.py:254
  174.2 13.0 %collective-permute-start.51 = (bf16[256,512]{1,0:T(8,128)(2,1)S(1)}, bf16[256,512]{1,0:T(8,128)(2,1)S(1)}, u32[]{:S(2)}, u32[]{:S(2)}) collective-permute-start(bf16[256,512]{1,0:T(8,128)(2,1)S(1)} %get-tuple-element.37), channel_id=1, source_target_pairs={{0,2},{2,4},{4,6},{1,3},{3,5},{5,7},{8,10},{10,12},{12,14},{9,11},... | collective-permute-start | bytes 786440 | tf_op jit(solution)/shard_map/ppermute | solution.py:253
  (54 other events, 472.2 us)

commit v5 on v4

--- a/solution.py
+++ b/solution.py
@@ -31,13 +31,14 @@
         self.per_tile = self.row // self.col
 
 
-def chosen_copies(sizes, step, tiles, target, sems):
+def chosen_copies(sizes, step, tiles, target, top, sems):
     sec_index, col_index = lax.axis_index("sec"), lax.axis_index("col")
     copies = []
     for kc in range(sizes.col):
-        place = lax.rem(col_index - kc + sizes.col, sizes.col)
+        begin = lax.rem(col_index - kc + sizes.col, sizes.col) * sizes.cols
+        place = target.at[top : top + sizes.rows, pl.ds(pl.multiple_of(begin, sizes.cols), sizes.cols)]
         for kx in range(sizes.sec):
-            copy = pltpu.make_async_copy(tiles[kx][kc], target.at[place], sems.at[kc])
+            copy = pltpu.make_async_copy(tiles[kx][kc], place, sems.at[kc])
             wanted = lax.rem(sec_index - kx + sizes.sec, sizes.sec) == step
             copies.append((wanted, copy))
     return copies
@@ -45,12 +46,12 @@
 
 def start_all(copies):
     for wanted, copy in copies:
-        pl.when(wanted)(copy.start)
+        copy.start() if wanted is True else pl.when(wanted)(copy.start)
 
 
 def wait_all(copies):
     for wanted, copy in copies:
-        pl.when(wanted)(copy.wait)
+        copy.wait() if wanted is True else pl.when(wanted)(copy.wait)
 
 
 def nested(refs, sizes):
@@ -101,51 +102,46 @@
     tiles, refs = nested(refs[:n_tiles], sizes), refs[n_tiles:]
     inverse_tiles, refs = nested(refs[:n_tiles], sizes), refs[n_tiles:]
     out, up_first, down_first, *refs = refs
-    state, rows, inverses, product, tile_sems, inverse_sems, state_sems = refs
+    panel, state, rows, left, block_sems, state_sems, tile_sems = refs
     row_index, sec_index, col_index = (lax.axis_index(a) for a in ("row", "sec", "col"))
-
-    state_copies = []
+    count = sizes.chunk
+
+    first_copies = []
     for number, (kx, kc, offset) in enumerate(state_places):
         first = lax.rem(col_index - kc + sizes.col, sizes.col) * sizes.cols + offset
         if kx is not None:
             first = first + lax.rem(sec_index - kx + sizes.sec, sizes.sec) * sizes.width
         height = states[number].shape[0]
         place = state.at[pl.ds(pl.multiple_of(first, height), height)]
-        state_copies.append(pltpu.make_async_copy(states[number], place, state_sems.at[number]))
-    for copy in state_copies:
-        copy.start()
-    tile_copies = chosen_copies(sizes, step, tiles, rows, tile_sems)
+        copy = pltpu.make_async_copy(states[number], place, state_sems.at[number])
+        first_copies.append((True, copy))
+    for number, (ref, row_of) in enumerate(zip(blocks, block_rows)):
+        q, low, high = row_of(row_index)
+        wanted = (q >= low) & (q <= high)
+        source = ref if ref.shape[0] == count else ref.at[part * count : (part + 1) * count]
+        begin = pl.multiple_of(jnp.clip(q, 0, sizes.row - 1) * sizes.rows, sizes.rows)
+        place = panel.at[:, pl.ds(begin, sizes.rows)]
+        first_copies.append((wanted, pltpu.make_async_copy(source, place, block_sems.at[number])))
+    start_all(first_copies)
+    tile_copies = []
+    for number, array in enumerate((tiles, inverse_tiles)):
+        tile_copies += chosen_copies(sizes, step, array, rows, number * sizes.rows, tile_sems.at[number])
     start_all(tile_copies)
-    inverse_copies = chosen_copies(sizes, step, inverse_tiles, inverses, inverse_sems)
-    start_all(inverse_copies)
-    for copy in state_copies:
-        copy.wait()
-
-    product[...] = jnp.zeros((sizes.chunk, sizes.rows), jnp.float32)
-
-    def accumulate(ref, q):
-        first = pl.multiple_of(q * sizes.rows, sizes.rows)
-        count = sizes.chunk
-        block = ref[...] if ref.shape[0] == count else ref[part * count : (part + 1) * count]
-        product[...] += jnp.dot(
-            block, state[pl.ds(first, sizes.rows)], preferred_element_type=jnp.float32
-        )
-
-    for ref, row_of in zip(blocks, block_rows):
-        q, low, high = row_of(row_index)
-        pl.when((q >= low) & (q <= high))(functools.partial(accumulate, ref, q))
-    image = product[...].astype(jnp.bfloat16)
+
+    wait_all(first_copies)
+    image = jnp.dot(panel[...], state[...], preferred_element_type=jnp.float32)
+    left[:, : sizes.rows] = image.astype(jnp.bfloat16)
     wait_all(tile_copies)
-    wait_all(inverse_copies)
-    begin = pl.multiple_of(sec_index * sizes.width + part * sizes.chunk, sizes.chunk)
-    left = inverses[col_index, :, pl.ds(begin, sizes.chunk)].T
+    begin = col_index * sizes.cols + sec_index * sizes.width + part * count
+    inverse_panel = rows[sizes.rows :, pl.ds(pl.multiple_of(begin, count), count)]
+    left[:, sizes.rows :] = inverse_panel.T
     for d in range(sizes.row):
-        h, i = divmod(d, sizes.per_tile)
-        block = slice(i * sizes.rows, (i + 1) * sizes.rows)
         place = lax.rem(d - row_index + sizes.row, sizes.row)
         out[place] = jnp.dot(
-            image, rows[h, :, block], preferred_element_type=jnp.float32
-        ) + jnp.dot(left, inverses[h, :, block], preferred_element_type=jnp.float32)
+            left[...],
+            rows[:, d * sizes.rows : (d + 1) * sizes.rows],
+            preferred_element_type=jnp.float32,
+        )
     up_first[...] = out[sizes.row - 1].astype(jnp.bfloat16)
     down_first[...] = out[1].astype(jnp.bfloat16)
 
@@ -159,21 +155,21 @@
         ),
         out_shape=[jax.ShapeDtypeStruct(shape, jnp.float32)]
         + [jax.ShapeDtypeStruct(shape[1:], jnp.bfloat16)] * 2,
-        in_specs=[VMEM] * len(blocks) + [ANY] * (len(states) + len(flat)),
+        in_specs=[ANY] * (len(blocks) + len(states) + len(flat)),
         out_specs=[VMEM] * 3,
         scratch_shapes=[
+            pltpu.VMEM((sizes.chunk, sizes.order), jnp.bfloat16),
             pltpu.VMEM((sizes.order, sizes.rows), jnp.bfloat16),
-            pltpu.VMEM((sizes.col, sizes.rows, sizes.cols), jnp.bfloat16),
-            pltpu.VMEM((sizes.col, sizes.rows, sizes.cols), jnp.bfloat16),
-            pltpu.VMEM(shape[1:], jnp.float32),
-            pltpu.SemaphoreType.DMA((sizes.col,)),
-            pltpu.SemaphoreType.DMA((sizes.col,)),
+            pltpu.VMEM((2 * sizes.rows, sizes.order), jnp.bfloat16),
+            pltpu.VMEM((sizes.chunk, 2 * sizes.rows), jnp.bfloat16),
+            pltpu.SemaphoreType.DMA((len(blocks),)),
             pltpu.SemaphoreType.DMA((len(states),)),
+            pltpu.SemaphoreType.DMA((2, sizes.col)),
         ],
         compiler_params=PARAMS,
         cost_estimate=pl.CostEstimate(
             flops=6 * sizes.rows * sizes.chunk * sizes.order,
-            bytes_accessed=4 * sizes.rows * sizes.order + 10 * sizes.chunk * sizes.order,
+            bytes_accessed=6 * sizes.rows * sizes.order + 6 * sizes.chunk * sizes.order,
             transcendentals=0,
         ),
         name="products",
@@ -223,42 +219,86 @@
     return found
 
 
-def first_slot(sizes, block):
+class TrailingGather:
+    def __init__(self, sizes, panel):
+        self.sizes = sizes
+        self.panel = panel
+        self.last = sizes.row - 1
+        row_index = lax.axis_index("row")
+        self.places = (row_index, self.last - row_index)
+        self.got = {}
+
+    def own(self, part):
+        if part is None:
+            return self.panel
+        return self.panel[part * self.sizes.chunk : (part + 1) * self.sizes.chunk]
+
+    def received(self, time, part, way):
+        if (time, None) in self.got:
+            array = self.got[time, None][way]
+            if part is None:
+                return array
+            return array[part * self.sizes.chunk : (part + 1) * self.sizes.chunk]
+        return self.got[time, part][way]
+
+    def payload(self, time, part, way):
+        if time <= 2:
+            return self.own(part)
+        earlier = self.received(time - 2, part, way)
+        if time > self.last:
+            return earlier
+        return jnp.where(self.places[way] == time - 1, self.own(part), earlier)
+
+    def send(self, time, part, others=()):
+        senders = range(time // 2, min(time, self.last))
+        self.got[time, part] = [
+            lax.ppermute(
+                after(self.payload(time, part, way), *others), "row", pairs(self.sizes, senders, way)
+            )
+            for way in range(2)
+        ]
+
+    def blocks(self, part):
+        last = self.last
+        found = [(lambda row: (row, 0, last), self.panel)]
+        for (time, piece), (up, down) in self.got.items():
+            if piece in (None, part):
+                found.append((lambda row, time=time: (2 * row - 1 - time, 0, row - 1), up))
+                found.append((lambda row, time=time: (2 * row - last + 1 + time, row + 1, last), down))
+        return found
+
+
+def pairs(sizes, senders, way):
     last = sizes.row - 1
-    up = lax.ppermute(block, "row", [(i, i + 1) for i in range(last)])
-    down = lax.ppermute(block, "row", [(i, i - 1) for i in range(1, sizes.row)])
-    return up, down
-
-
-def scattered_sum(sizes, partials, gather=None):
-    blocks, up_first, down_first = partials
+    return [(last - i, last - i - 1) if way else (i, i + 1) for i in senders]
+
+
+def scattered_sum(sizes, partials, part, gather=None):
+    blocks, *first = partials
     row_index = lax.axis_index("row")
     last = sizes.row - 1
-    up = down = None
-    found = []
+    places = (row_index, last - row_index)
+    arrived = None
     for slot in range(last):
-        if slot:
-            up_block = (blocks[last - slot] + up.astype(jnp.float32)).astype(jnp.bfloat16)
-            down_block = (blocks[slot + 1] + down.astype(jnp.float32)).astype(jnp.bfloat16)
-        else:
-            up_block, down_block = up_first, down_first
-        low = slot
-        if gather is not None:
-            if slot == 0:
-                up, down = gather
-            if slot < last - 1:
-                up_block = jnp.where(row_index <= slot, up_block, up)
-                down_block = jnp.where(last - row_index <= slot, down_block, down)
-                low = last - 1
-        up = lax.ppermute(up_block, "row", [(i, i + 1) for i in range(low + 1)])
-        down = lax.ppermute(
-            down_block, "row", [(i, i - 1) for i in range(last - low, last + 1)]
-        )
-        if gather is not None and slot < last - 1:
-            found.append((lambda row, slot=slot: (row - 2 - slot, 0, last), up))
-            found.append((lambda row, slot=slot: (row + 2 + slot, 0, last), down))
-    total = blocks[0] + up.astype(jnp.float32) + down.astype(jnp.float32)
-    return total.astype(jnp.bfloat16), found
+        passed = []
+        riding = gather is not None and slot < last - 1
+        for way in range(2):
+            block = first[way]
+            if slot:
+                own = blocks[slot + 1 if way else last - slot]
+                block = (own + arrived[way].astype(jnp.float32)).astype(jnp.bfloat16)
+            senders = range(slot + 1)
+            if riding:
+                block = jnp.where(
+                    places[way] <= slot, block, gather.payload(last + slot, part, way)
+                )
+                senders = range(last)
+            passed.append(lax.ppermute(block, "row", pairs(sizes, senders, way)))
+        arrived = passed
+        if riding:
+            gather.got[last + slot, part] = passed
+    total = blocks[0] + arrived[0].astype(jnp.float32) + arrived[1].astype(jnp.float32)
+    return total.astype(jnp.bfloat16)
 
 
 def local(factors, inverses, sigma_end):
@@ -276,11 +316,12 @@
 
     factor, inverse = factors[0], inverses[0]
 
-    arrived_chunks = [None]
-    for kx in range(1, sec_size):
-        arrived_chunks.append(
-            [exchanged(panel(factor, kx, part), "sec", kx) for part in range(CHUNKS)]
-        )
+    arrived_chunks = [[] for _ in range(sec_size)]
+    for part in range(CHUNKS):
+        earlier = [chunks[-1] for chunks in arrived_chunks[1:] if chunks]
+        for kx in range(1, sec_size):
+            piece = after(panel(factor, kx, part), *earlier)
+            arrived_chunks[kx].append(exchanged(piece, "sec", kx))
 
     factor_blocks = {}
     last = sec_size - 1
@@ -320,30 +361,25 @@
 
     results = {}
     for step in reversed(range(sec_size)):
-        trailing = []
+        gather = None
         if step:
-            earlier = [array for k in range(CHUNKS) for _, array in factor_blocks[step, k][-2:]]
-            for part in range(CHUNKS):
-                sent = [[chunks[part]] for chunks in arrived_chunks[1:]]
-                block = after(transposed_panel(sizes, step - 1, factor, sent, part), *earlier)
-                trailing.append((block, first_slot(sizes, block)))
+            gather = TrailingGather(
+                sizes, transposed_panel(sizes, step - 1, factor, arrived_chunks[1:])
+            )
+            for time in range(1, sizes.row - 1):
+                others = []
+                if step == last:
+                    others = [a for _, a in factor_blocks[step, CHUNKS - 1][2 * time - 1 : 2 * time + 1]]
+                gather.send(time, None, others)
         next_pieces = []
         for part in range(CHUNKS):
             partials = products(
                 sizes, step, part, factor_blocks[step, part], state_pieces, factor_tiles, inverse_tiles
             )
+            total = scattered_sum(sizes, partials, part, gather)
             if step:
-                block, (up, down) = trailing[part]
-                total, found = scattered_sum(sizes, partials, (up, down))
-                edge = sizes.row - 1
-                factor_blocks[step - 1, part] = [
-                    (lambda row: (row, 0, edge), block),
-                    (lambda row: (row - 1, 0, edge), up),
-                    (lambda row: (row + 1, 0, edge), down),
-                    *found,
-                ]
-            else:
-                total, _ = scattered_sum(sizes, partials)
+                gather.send(2 * sizes.row - 3, part, [total])
+                factor_blocks[step - 1, part] = gather.blocks(part)
             for kx in range(sec_size):
                 piece = exchanged(total, "sec", kx) if kx else total
                 results[step, kx, part] = piece

time: 205 us -> 231 us (1.13)
  waiting for transfers between devices: 56.3 us -> 69.2 us
  starting transfers between devices: 108 us -> 115 us
  local copies, waits for them, and re-layouts: 12.7 us -> 19.6 us
  Pallas kernels: 21.7 us -> 18.1 us
  other arithmetic: 3.77 us -> 7.23 us
    ppermute x28 -> x32, waiting for transfers between devices: 22.8 us -> 32.3 us  [the longest x24 29.8 us: scattered_sum(): passed.append(lax.ppermute(block, 'row', pairs(sizes, senders, way)))]
    ppermute x28 -> x32, starting transfers between devices: 72.2 us -> 80.5 us  [the longest x24 66.8 us: scattered_sum(): passed.append(lax.ppermute(block, 'row', pairs(sizes, senders, way)))]
    ppermute x17, waiting for transfers between devices: 17.7 us -> 24 us  [exchanged(): lax.ppermute(value, axis, [(i, (i + steps) % count) for i in range(count)])]
    unnamed x43 -> x67, local copies, waits for them, and re-layouts: 11.3 us -> 17.1 us
    pallas_call x4, Pallas kernels: 18.6 us -> 14.9 us  [products(): pl.pallas_call(functools.partial(products_kernel, sizes, step, part, [b[0...]
    select_n x6 -> x2, other arithmetic: 1.34 us -> 4.72 us  [scattered_sum(): jnp.where(places[way] <= slot, block, gather.payload(last + slot, part, w...]
    ppermute x6, waiting for transfers between devices: 15.8 us -> 12.7 us  [neighbours_gathered(): lax.ppermute(down, 'row', [(i, i - 1) for i in range(1, sizes.row - slot)])]
  transfers between devices with their start and end apart: 57 -> 61, of which waited for: 21 -> 25; matrix products, arithmetic and copies ran while one was open for 3% -> 4% of each run, Pallas kernels for 8% -> 7%
where the time goes in v5:
time: 231 us; the launch traced here: 230 us
  starting transfers between devices  115 us (50%)
  waiting for transfers between devices  69.2 us (30%)
  local copies, waits for them, and re-layouts  19.6 us (8%)
  Pallas kernels  18.1 us (8%)
  other arithmetic  7.23 us (3%)
    ppermute x24, starting transfers between devices, scattered_sum(): passed.append(lax.ppermute(block, 'row', pairs(sizes, senders, way)))  66.8 us
    ppermute x24, waiting for transfers between devices, scattered_sum(): passed.append(lax.ppermute(block, 'row', pairs(sizes, senders, way)))  29.8 us
    ppermute x17, waiting for transfers between devices, exchanged(): lax.ppermute(value, axis, [(i, (i + steps) % count) for i in range(count)])  24 us
    unnamed x67, local copies, waits for them, and re-layouts  17.1 us
    pallas_call x4, Pallas kernels, products(): pl.pallas_call(functools.partial(products_kernel, sizes, step, part, [b[0...  14.9 us
    ppermute x8, starting transfers between devices, send(): lax.ppermute(after(self.payload(time, part, way), *others), 'row', pairs(...  13.7 us
    ppermute x17, starting transfers between devices, exchanged(): lax.ppermute(value, axis, [(i, (i + steps) % count) for i in range(count)])  13.6 us
    ppermute x6, starting transfers between devices, neighbours_gathered(): up = lax.ppermute(up, 'row', [(i, i + 1) for i in range(slot, last)])  13 us
  transfers between devices with their start and end apart: 61, of which 25 were waited for; matrix products, arithmetic and copies ran while one was open for 4% of the time, Pallas kernels for 7%

profile of v5, /device:TPU:0, one launch (start us, length us, event | category | flops | bytes accessed | tf_op | source)
XLA Modules:
  0.0 229.7 jit_solution(3570483081476437577)
XLA Ops:
  4.2 6.3 %collective-permute-done.refs_0_ = bf16[512,256]{1,0:T(8,128)(2,1)S(1)} collective-permute-done((bf16[512,256]{1,0:T(8,128)(2,1)S(1)}, bf16[512,256]{1,0:T(8,128)(2,1)S(1)}, u32[]{:S(2)}, u32[]{:S(2)}) %collective-permute-start) | collective-permute-done | bytes 262176 | tf_op jit(solution)/shard_map/ppermute | solution.py:18
  13.6 3.6 %collective-permute-start.10 = (bf16[256,512]{1,0:T(8,128)(2,1)S(1)}, bf16[256,512]{1,0:T(8,128)(2,1)S(1)}, u32[]{:S(2)}, u32[]{:S(2)}) collective-permute-start(bf16[256,512]{1,0:T(8,128)(2,1)S(1)} %panel.5.refs_0_), channel_id=1, source_target_pairs={{0,2},{2,4},{4,6},{1,3},{3,5},{5,7},{8,10},{10,12},{12,14},{9,11},... | collective-permute-start | bytes 786440 | tf_op jit(solution)/shard_map/ppermute | solution.py:215
  23.5 4.1 %collective-permute-done.11.refs_2_ = bf16[256,512]{1,0:T(8,128)(2,1)S(1)} collective-permute-done((bf16[256,512]{1,0:T(8,128)(2,1)S(1)}, bf16[256,512]{1,0:T(8,128)(2,1)S(1)}, u32[]{:S(2)}, u32[]{:S(2)}) %collective-permute-start.11) | collective-permute-done | bytes 262176 | tf_op jit(solution)/shard_map/ppermute | solution.py:216
  29.1 4.6 %collective-permute-start.2 = (bf16[256,512]{1,0:T(8,128)(2,1)S(1)}, bf16[256,512]{1,0:T(8,128)(2,1)S(1)}, u32[]{:S(2)}, u32[]{:S(2)}) collective-permute-start(bf16[256,512]{1,0:T(8,128)(2,1)S(1)} %panel.4.refs_0_), channel_id=1, source_target_pairs={{0,2},{2,4},{4,6},{1,3},{3,5},{5,7},{8,10},{10,12},{12,14},{9,11},... | collective-permute-start | bytes 786440 | tf_op jit(solution)/shard_map/ppermute | solution.py:215
  38.0 4.2 %collective-permute-done.3.refs_2_ = bf16[256,512]{1,0:T(8,128)(2,1)S(1)} collective-permute-done((bf16[256,512]{1,0:T(8,128)(2,1)S(1)}, bf16[256,512]{1,0:T(8,128)(2,1)S(1)}, u32[]{:S(2)}, u32[]{:S(2)}) %collective-permute-start.3) | collective-permute-done | bytes 262176 | tf_op jit(solution)/shard_map/ppermute | solution.py:216
  42.9 9.9 %collective-permute-done.18 = bf16[512,512]{1,0:T(8,128)(2,1)S(1)} collective-permute-done((bf16[512,512]{1,0:T(8,128)(2,1)S(1)}, bf16[512,512]{1,0:T(8,128)(2,1)S(1)}, u32[]{:S(2)}, u32[]{:S(2)}) %collective-permute-start.18) | collective-permute-done | bytes 524320 | tf_op jit(solution)/shard_map/ppermute | solution.py:18
  67.5 5.4 %collective-permute-start.4 = (bf16[512,512]{1,0:T(8,128)(2,1)}, bf16[512,512]{1,0:T(8,128)(2,1)}, u32[]{:S(2)}, u32[]{:S(2)}) collective-permute-start(bf16[512,512]{1,0:T(8,128)(2,1)} %panel.3.refs_0_), channel_id=1, source_target_pairs={{0,2},{1,3},{8,10},{9,11},{16,18},{17,19},{24,26},{25,27}} | collective-permute-start | bytes 1572872 | tf_op jit(solution)/shard_map/ppermute | solution.py:255
  86.0 3.9 %products.4 = (f32[4,256,512]{2,1,0:T(8,128)S(1)}, bf16[256,512]{1,0:T(8,128)(2,1)S(1)}, bf16[256,512]{1,0:T(8,128)(2,1)S(1)}) custom-call(bf16[256,512]{1,0:T(8,128)(2,1)S(1)} %copy-done.19, bf16[256,512]{1,0:T(8,128)(2,1)S(1)} %copy-done.23, bf16[256,512]{1,0:T(8,128)(2,1)S(1)} %copy-done.25, bf16[256,512]{1,0:T(8,128)(2,1)} %collective-permute-done.12.refs_3_, ...), custom_call_target="tpu_custom_call" | custom-call | flops 1610612736 | bytes 9437184 | tf_op jit(solution)/shard_map/products/pallas_call | solution.py:152
  92.8 3.7 %products.5 = (f32[4,256,512]{2,1,0:T(8,128)S(1)}, bf16[256,512]{1,0:T(8,128)(2,1)S(1)}, bf16[256,512]{1,0:T(8,128)(2,1)S(1)}) custom-call(bf16[256,512]{1,0:T(8,128)(2,1)S(1)} %copy-done.21, bf16[256,512]{1,0:T(8,128)(2,1)S(1)} %copy-done.28, bf16[256,512]{1,0:T(8,128)(2,1)S(1)} %copy-done.31, bf16[256,512]{1,0:T(8,128)(2,1)} %collective-permute-done.6.refs_3_, ...), custom_call_target="tpu_custom_call" | custom-call | flops 1610612736 | bytes 9437184 | tf_op jit(solution)/shard_map/products/pallas_call | solution.py:152
  100.2 8.5 %collective-permute-start.23 = (bf16[256,512]{1,0:T(8,128)(2,1)}, bf16[256,512]{1,0:T(8,128)(2,1)S(1)}, u32[]{:S(2)}, u32[]{:S(2)}) collective-permute-start(bf16[256,512]{1,0:T(8,128)(2,1)} %get-tuple-element.62), channel_id=1, source_target_pairs={{0,2},{2,4},{4,6},{1,3},{3,5},{5,7},{8,10},{10,12},{12,14},{9,11},... | collective-permute-start | bytes 786440 | tf_op jit(solution)/shard_map/ppermute | solution.py:296
  110.0 6.6 %collective-permute-start.36 = (bf16[256,512]{1,0:T(8,128)(2,1)}, bf16[256,512]{1,0:T(8,128)(2,1)}, u32[]{:S(2)}, u32[]{:S(2)}) collective-permute-start(bf16[256,512]{1,0:T(8,128)(2,1)} %get-tuple-element.61), channel_id=1, source_target_pairs={{0,2},{2,4},{4,6},{1,3},{3,5},{5,7},{8,10},{10,12},{12,14},{9,11},... | collective-permute-start | bytes 786440 | tf_op jit(solution)/shard_map/ppermute | solution.py:296
  120.6 4.8 %collective-permute-done.39.refs_6_ = bf16[256,512]{1,0:T(8,128)(2,1)} collective-permute-done((bf16[256,512]{1,0:T(8,128)(2,1)}, bf16[256,512]{1,0:T(8,128)(2,1)}, u32[]{:S(2)}, u32[]{:S(2)}) %collective-permute-start.39) | collective-permute-done | bytes 262176 | tf_op jit(solution)/shard_map/ppermute | solution.py:296
  132.4 4.6 %collective-permute-start.25 = (bf16[256,512]{1,0:T(8,128)(2,1)S(1)}, bf16[256,512]{1,0:T(8,128)(2,1)S(1)}, u32[]{:S(2)}, u32[]{:S(2)}) collective-permute-start(bf16[256,512]{1,0:T(8,128)(2,1)S(1)} %get-tuple-element.58), channel_id=1, source_target_pairs={{0,2},{2,4},{4,6},{1,3},{3,5},{5,7},{8,10},{10,12},{12,14},{9,11},... | collective-permute-start | bytes 786440 | tf_op jit(solution)/shard_map/ppermute | solution.py:296
  150.9 3.4 %collective-permute-done.41 = bf16[256,512]{1,0:T(8,128)(2,1)S(1)} collective-permute-done((bf16[256,512]{1,0:T(8,128)(2,1)S(1)}, bf16[256,512]{1,0:T(8,128)(2,1)S(1)}, u32[]{:S(2)}, u32[]{:S(2)}) %collective-permute-start.41) | collective-permute-done | bytes 262176 | tf_op jit(solution)/shard_map/ppermute | solution.py:296
  168.8 3.8 %products.7 = (f32[4,256,512]{2,1,0:T(8,128)S(1)}, bf16[256,512]{1,0:T(8,128)(2,1)S(1)}, bf16[256,512]{1,0:T(8,128)(2,1)S(1)}) custom-call(bf16[512,512]{1,0:T(8,128)(2,1)} %panel.3.refs_0_, bf16[512,512]{1,0:T(8,128)(2,1)} %collective-permute-done.4.refs_1_, bf16[512,512]{1,0:T(8,128)(2,1)} %collective-permute-done.5.refs_2_, ...), custom_call_target="tpu_custom_call" | custom-call | flops 1610612736 | bytes 9437184 | tf_op jit(solution)/shard_map/products/pallas_call | solution.py:152
  172.6 4.6 %collective-permute-start.53 = (bf16[256,512]{1,0:T(8,128)(2,1)S(1)}, bf16[256,512]{1,0:T(8,128)(2,1)S(1)}, u32[]{:S(2)}, u32[]{:S(2)}) collective-permute-start(bf16[256,512]{1,0:T(8,128)(2,1)S(1)} %get-tuple-element.45), channel_id=1, source_target_pairs={{0,2},{1,3},{8,10},{9,11},{16,18},{17,19},{24,26},{25,27}} | collective-permute-start | bytes 786440 | tf_op jit(solution)/shard_map/ppermute | solution.py:296
  177.6 3.6 %products.6 = (f32[4,256,512]{2,1,0:T(8,128)S(1)}, bf16[256,512]{1,0:T(8,128)(2,1)S(1)}, bf16[256,512]{1,0:T(8,128)(2,1)S(1)}) custom-call(bf16[512,512]{1,0:T(8,128)(2,1)} %panel.3.refs_0_, bf16[512,512]{1,0:T(8,128)(2,1)} %collective-permute-done.4.refs_1_, bf16[512,512]{1,0:T(8,128)(2,1)} %collective-permute-done.5.refs_2_, ...), custom_call_target="tpu_custom_call" | custom-call | flops 1610612736 | bytes 9437184 | tf_op jit(solution)/shard_map/products/pallas_call | solution.py:152
  183.6 4.4 %collective-permute-start.54 = (bf16[256,512]{1,0:T(8,128)(2,1)S(1)}, bf16[256,512]{1,0:T(8,128)(2,1)S(1)}, u32[]{:S(2)}, u32[]{:S(2)}) collective-permute-start(bf16[256,512]{1,0:T(8,128)(2,1)S(1)} %fusion.1), channel_id=1, source_target_pairs={{0,2},{2,4},{1,3},{3,5},{8,10},{10,12},{9,11},{11,13},{16,18},{18,... | collective-permute-start | bytes 786440 | tf_op jit(solution)/shard_map/ppermute | solution.py:296
  189.6 4.4 %collective-permute-start.46 = (bf16[256,512]{1,0:T(8,128)(2,1)S(1)}, bf16[256,512]{1,0:T(8,128)(2,1)S(1)}, u32[]{:S(2)}, u32[]{:S(2)}) collective-permute-start(bf16[256,512]{1,0:T(8,128)(2,1)S(1)} %fusion.7), channel_id=1, source_target_pairs={{0,2},{2,4},{1,3},{3,5},{8,10},{10,12},{9,11},{11,13},{16,18},{18,... | collective-permute-start | bytes 786440 | tf_op jit(solution)/shard_map/ppermute | solution.py:296
  196.0 4.0 %collective-permute-done.46 = bf16[256,512]{1,0:T(8,128)(2,1)S(1)} collective-permute-done((bf16[256,512]{1,0:T(8,128)(2,1)S(1)}, bf16[256,512]{1,0:T(8,128)(2,1)S(1)}, u32[]{:S(2)}, u32[]{:S(2)}) %collective-permute-start.46) | collective-permute-done | bytes 262176 | tf_op jit(solution)/shard_map/ppermute | solution.py:296
  200.8 5.0 %collective-permute-start.55 = (bf16[256,512]{1,0:T(8,128)(2,1)S(1)}, bf16[256,512]{1,0:T(8,128)(2,1)S(1)}, u32[]{:S(2)}, u32[]{:S(2)}) collective-permute-start(bf16[256,512]{1,0:T(8,128)(2,1)S(1)} %get-tuple-element.47), channel_id=1, source_target_pairs={{0,2},{2,4},{4,6},{1,3},{3,5},{5,7},{8,10},{10,12},{12,14},{9,11},... | collective-permute-start | bytes 786440 | tf_op jit(solution)/shard_map/ppermute | solution.py:296
  207.2 5.2 %collective-permute-start.47 = (bf16[256,512]{1,0:T(8,128)(2,1)S(1)}, bf16[256,512]{1,0:T(8,128)(2,1)S(1)}, u32[]{:S(2)}, u32[]{:S(2)}) collective-permute-start(bf16[256,512]{1,0:T(8,128)(2,1)S(1)} %get-tuple-element.49), channel_id=1, source_target_pairs={{0,2},{2,4},{4,6},{1,3},{3,5},{5,7},{8,10},{10,12},{12,14},{9,11},... | collective-permute-start | bytes 786440 | tf_op jit(solution)/shard_map/ppermute | solution.py:296
  217.5 3.8 %collective-permute-done.50 = bf16[256,512]{1,0:T(8,128)(2,1)S(1)} collective-permute-done((bf16[256,512]{1,0:T(8,128)(2,1)S(1)}, bf16[256,512]{1,0:T(8,128)(2,1)S(1)}, u32[]{:S(2)}, u32[]{:S(2)}) %collective-permute-start.50) | collective-permute-done | bytes 262176 | tf_op jit(solution)/shard_map/ppermute | solution.py:296
  223.0 5.0 %collective-permute-done.59.refs_2_ = bf16[256,512]{1,0:T(8,128)(2,1)S(1)} collective-permute-done((bf16[256,512]{1,0:T(8,128)(2,1)S(1)}, bf16[256,512]{1,0:T(8,128)(2,1)S(1)}, u32[]{:S(2)}, u32[]{:S(2)}) %collective-permute-start.59) | collective-permute-done | bytes 262176 | tf_op jit(solution)/shard_map/ppermute | solution.py:18
  (192 shorter events, 111.6 us)
Async XLA Ops:
  18.0 44.2 %collective-permute-start.21 = (bf16[512,1024]{1,0:T(8,128)(2,1)}, bf16[512,1024]{1,0:T(8,128)(2,1)}, u32[]{:S(2)}, u32[]{:S(2)}) collective-permute-start(bf16[512,1024]{1,0:T(8,128)(2,1)} %bitcast.112), channel_id=1, source_target_pairs={{0,8},{8,0},{1,9},{9,1},{2,10},{10,2},{3,11},{11,3},{4,12},{12,4},... | collective-permute-start | bytes 3145736 | tf_op jit(solution)/shard_map/ppermute | solution.py:18
  21.6 12.1 %collective-permute-start.12 = (bf16[256,512]{1,0:T(8,128)(2,1)S(1)}, bf16[256,512]{1,0:T(8,128)(2,1)}, u32[]{:S(2)}, u32[]{:S(2)}) collective-permute-start(bf16[256,512]{1,0:T(8,128)(2,1)S(1)} %collective-permute-done.10.refs_1_), channel_id=1, source_target_pairs={{2,4},{4,6},{3,5},{5,7},{10,12},{12,14},{11,13},{13,15},{18,20},{2... | collective-permute-start | bytes 786440 | tf_op jit(solution)/shard_map/ppermute | solution.py:215
  23.0 29.9 %collective-permute-start.18 = (bf16[512,512]{1,0:T(8,128)(2,1)S(1)}, bf16[512,512]{1,0:T(8,128)(2,1)S(1)}, u32[]{:S(2)}, u32[]{:S(2)}) collective-permute-start(bf16[512,512]{1,0:T(8,128)(2,1)S(1)} %dynamic-slice_bitcast_fusion), channel_id=1, source_target_pairs={{0,8},{8,0},{1,9},{9,1},{2,10},{10,2},{3,11},{11,3},{4,12},{12,4},... | collective-permute-start | bytes 1572872 | tf_op jit(solution)/shard_map/ppermute | solution.py:18
  36.7 22.1 %collective-permute-start.14 = (bf16[256,512]{1,0:T(8,128)(2,1)}, bf16[256,512]{1,0:T(8,128)(2,1)}, u32[]{:S(2)}, u32[]{:S(2)}) collective-permute-start(bf16[256,512]{1,0:T(8,128)(2,1)} %collective-permute-done.12.refs_3_), channel_id=1, source_target_pairs={{4,6},{5,7},{12,14},{13,15},{20,22},{21,23},{28,30},{29,31}} | collective-permute-start | bytes 786440 | tf_op jit(solution)/shard_map/ppermute | solution.py:215
  38.0 24.7 %collective-permute-start.17 = (bf16[512,1024]{1,0:T(8,128)(2,1)S(1)}, bf16[512,1024]{1,0:T(8,128)(2,1)}, u32[]{:S(2)}, u32[]{:S(2)}) collective-permute-start(bf16[512,1024]{1,0:T(8,128)(2,1)S(1)} %bitcast.106), channel_id=1, source_target_pairs={{0,1},{1,0},{2,3},{3,2},{4,5},{5,4},{6,7},{7,6},{8,9},{9,8},{10,11... | collective-permute-start | bytes 3145736 | tf_op jit(solution)/shard_map/ppermute | solution.py:18
  42.2 21.9 %collective-permute-start.20 = (bf16[512,1024]{1,0:T(8,128)(2,1)S(1)}, bf16[512,1024]{1,0:T(8,128)(2,1)}, u32[]{:S(2)}, u32[]{:S(2)}) collective-permute-start(bf16[512,1024]{1,0:T(8,128)(2,1)S(1)} %bitcast.113), channel_id=1, source_target_pairs={{0,1},{1,0},{2,3},{3,2},{4,5},{5,4},{6,7},{7,6},{8,9},{9,8},{10,11... | collective-permute-start | bytes 3145736 | tf_op jit(solution)/shard_map/ppermute | solution.py:18
  62.2 13.4 %collective-permute-start.19 = (bf16[512,1024]{1,0:T(8,128)(2,1)S(1)}, bf16[512,1024]{1,0:T(8,128)(2,1)S(1)}, u32[]{:S(2)}, u32[]{:S(2)}) collective-permute-start(bf16[512,1024]{1,0:T(8,128)(2,1)S(1)} %constant_dynamic-update-slice_fusion.refs_11_.refs_21_), channel_id=1, source_target_pairs={{0,1},{1,0},{2,3},{3,2},{4,5},{5,4},{6,7},{7,6},{8,9},{9,8},{10,11... | collective-permute-start | bytes 3145736 | tf_op jit(solution)/shard_map/ppermute | solution.py:18
  62.2 15.8 %collective-permute-start.22 = (bf16[512,1024]{1,0:T(8,128)(2,1)}, bf16[512,1024]{1,0:T(8,128)(2,1)}, u32[]{:S(2)}, u32[]{:S(2)}) collective-permute-start(bf16[512,1024]{1,0:T(8,128)(2,1)} %collective-permute-done.21.refs_15_.refs_25_), channel_id=1, source_target_pairs={{0,1},{1,0},{2,3},{3,2},{4,5},{5,4},{6,7},{7,6},{8,9},{9,8},{10,11... | collective-permute-start | bytes 3145736 | tf_op jit(solution)/shard_map/ppermute | solution.py:18
  64.1 10.8 %collective-permute-start.7 = (bf16[256,512]{1,0:T(8,128)(2,1)S(1)}, bf16[256,512]{1,0:T(8,128)(2,1)}, u32[]{:S(2)}, u32[]{:S(2)}) collective-permute-start(bf16[256,512]{1,0:T(8,128)(2,1)S(1)} %copy-done.30), channel_id=1, source_target_pairs={{2,0},{4,2},{3,1},{5,3},{10,8},{12,10},{11,9},{13,11},{18,16},{20,... | collective-permute-start | bytes 786440 | tf_op jit(solution)/shard_map/ppermute | solution.py:216
  67.5 30.2 %collective-permute-start.4 = (bf16[512,512]{1,0:T(8,128)(2,1)}, bf16[512,512]{1,0:T(8,128)(2,1)}, u32[]{:S(2)}, u32[]{:S(2)}) collective-permute-start(bf16[512,512]{1,0:T(8,128)(2,1)} %panel.3.refs_0_), channel_id=1, source_target_pairs={{0,2},{1,3},{8,10},{9,11},{16,18},{17,19},{24,26},{25,27}} | collective-permute-start | bytes 1572872 | tf_op jit(solution)/shard_map/ppermute | solution.py:255
  72.9 24.9 %collective-permute-start.5 = (bf16[512,512]{1,0:T(8,128)(2,1)}, bf16[512,512]{1,0:T(8,128)(2,1)}, u32[]{:S(2)}, u32[]{:S(2)}) collective-permute-start(bf16[512,512]{1,0:T(8,128)(2,1)} %panel.3.refs_0_), channel_id=1, source_target_pairs={{6,4},{7,5},{14,12},{15,13},{22,20},{23,21},{30,28},{31,29}} | collective-permute-start | bytes 1572872 | tf_op jit(solution)/shard_map/ppermute | solution.py:255
  74.9 16.4 %collective-permute-start.34 = (bf16[256,512]{1,0:T(8,128)(2,1)}, bf16[256,512]{1,0:T(8,128)(2,1)S(1)}, u32[]{:S(2)}, u32[]{:S(2)}) collective-permute-start(bf16[256,512]{1,0:T(8,128)(2,1)} %collective-permute-done.6.refs_3_), channel_id=1, source_target_pairs={{4,6},{5,7},{12,14},{13,15},{20,22},{21,23},{28,30},{29,31}} | collective-permute-start | bytes 786440 | tf_op jit(solution)/shard_map/ppermute | solution.py:215
  76.7 16.1 %collective-permute-start.35 = (bf16[256,512]{1,0:T(8,128)(2,1)}, bf16[256,512]{1,0:T(8,128)(2,1)}, u32[]{:S(2)}, u32[]{:S(2)}) collective-permute-start(bf16[256,512]{1,0:T(8,128)(2,1)} %collective-permute-done.7.refs_4_), channel_id=1, source_target_pairs={{2,0},{3,1},{10,8},{11,9},{18,16},{19,17},{26,24},{27,25}} | collective-permute-start | bytes 786440 | tf_op jit(solution)/shard_map/ppermute | solution.py:216
  78.0 38.6 %collective-permute-start.8 = (bf16[512,512]{1,0:T(8,128)(2,1)}, bf16[512,512]{1,0:T(8,128)(2,1)}, u32[]{:S(2)}, u32[]{:S(2)}) collective-permute-start(bf16[512,512]{1,0:T(8,128)(2,1)} %panel.3.refs_0_), channel_id=1, source_target_pairs={{2,4},{3,5},{10,12},{11,13},{18,20},{19,21},{26,28},{27,29}} | collective-permute-start | bytes 1572872 | tf_op jit(solution)/shard_map/ppermute | solution.py:255
  91.3 26.6 %collective-permute-start.9 = (bf16[512,512]{1,0:T(8,128)(2,1)}, bf16[512,512]{1,0:T(8,128)(2,1)}, u32[]{:S(2)}, u32[]{:S(2)}) collective-permute-start(bf16[512,512]{1,0:T(8,128)(2,1)} %panel.3.refs_0_), channel_id=1, source_target_pairs={{4,2},{5,3},{12,10},{13,11},{20,18},{21,19},{28,26},{29,27}} | collective-permute-start | bytes 1572872 | tf_op jit(solution)/shard_map/ppermute | solution.py:255
  100.2 17.7 %collective-permute-start.23 = (bf16[256,512]{1,0:T(8,128)(2,1)}, bf16[256,512]{1,0:T(8,128)(2,1)S(1)}, u32[]{:S(2)}, u32[]{:S(2)}) collective-permute-start(bf16[256,512]{1,0:T(8,128)(2,1)} %get-tuple-element.62), channel_id=1, source_target_pairs={{0,2},{2,4},{4,6},{1,3},{3,5},{5,7},{8,10},{10,12},{12,14},{9,11},... | collective-permute-start | bytes 786440 | tf_op jit(solution)/shard_map/ppermute | solution.py:296
  132.4 12.5 %collective-permute-start.25 = (bf16[256,512]{1,0:T(8,128)(2,1)S(1)}, bf16[256,512]{1,0:T(8,128)(2,1)S(1)}, u32[]{:S(2)}, u32[]{:S(2)}) collective-permute-start(bf16[256,512]{1,0:T(8,128)(2,1)S(1)} %get-tuple-element.58), channel_id=1, source_target_pairs={{0,2},{2,4},{4,6},{1,3},{3,5},{5,7},{8,10},{10,12},{12,14},{9,11},... | collective-permute-start | bytes 786440 | tf_op jit(solution)/shard_map/ppermute | solution.py:296
  143.4 10.9 %collective-permute-start.41 = (bf16[256,512]{1,0:T(8,128)(2,1)S(1)}, bf16[256,512]{1,0:T(8,128)(2,1)S(1)}, u32[]{:S(2)}, u32[]{:S(2)}) collective-permute-start(bf16[256,512]{1,0:T(8,128)(2,1)S(1)} %get-tuple-element.52), channel_id=1, source_target_pairs={{6,4},{4,2},{2,0},{7,5},{5,3},{3,1},{14,12},{12,10},{10,8},{15,13}... | collective-permute-start | bytes 786440 | tf_op jit(solution)/shard_map/ppermute | solution.py:296
  166.8 10.8 %collective-permute-start.30 = (bf16[256,512]{1,0:T(8,128)(2,1)}, bf16[256,512]{1,0:T(8,128)(2,1)S(1)}, u32[]{:S(2)}, u32[]{:S(2)}) collective-permute-start(bf16[256,512]{1,0:T(8,128)(2,1)} %collective-permute-done.24.refs_6_), channel_id=1, source_target_pairs={{2,0},{3,1},{10,8},{11,9},{18,16},{19,17},{26,24},{27,25}} | collective-permute-start | bytes 786440 | tf_op jit(solution)/shard_map/ppermute | solution.py:255
  172.6 10.9 %collective-permute-start.53 = (bf16[256,512]{1,0:T(8,128)(2,1)S(1)}, bf16[256,512]{1,0:T(8,128)(2,1)S(1)}, u32[]{:S(2)}, u32[]{:S(2)}) collective-permute-start(bf16[256,512]{1,0:T(8,128)(2,1)S(1)} %get-tuple-element.45), channel_id=1, source_target_pairs={{0,2},{1,3},{8,10},{9,11},{16,18},{17,19},{24,26},{25,27}} | collective-permute-start | bytes 786440 | tf_op jit(solution)/shard_map/ppermute | solution.py:296
  182.8 11.2 %collective-permute-start.56 = (bf16[256,512]{1,0:T(8,128)(2,1)S(1)}, bf16[256,512]{1,0:T(8,128)(2,1)S(1)}, u32[]{:S(2)}, u32[]{:S(2)}) collective-permute-start(bf16[256,512]{1,0:T(8,128)(2,1)S(1)} %get-tuple-element.46), channel_id=1, source_target_pairs={{6,4},{7,5},{14,12},{15,13},{22,20},{23,21},{30,28},{31,29}} | collective-permute-start | bytes 786440 | tf_op jit(solution)/shard_map/ppermute | solution.py:296
  183.6 11.5 %collective-permute-start.54 = (bf16[256,512]{1,0:T(8,128)(2,1)S(1)}, bf16[256,512]{1,0:T(8,128)(2,1)S(1)}, u32[]{:S(2)}, u32[]{:S(2)}) collective-permute-start(bf16[256,512]{1,0:T(8,128)(2,1)S(1)} %fusion.1), channel_id=1, source_target_pairs={{0,2},{2,4},{1,3},{3,5},{8,10},{10,12},{9,11},{11,13},{16,18},{18,... | collective-permute-start | bytes 786440 | tf_op jit(solution)/shard_map/ppermute | solution.py:296
  200.1 12.3 %collective-permute-start.49 = (bf16[256,512]{1,0:T(8,128)(2,1)S(1)}, bf16[256,512]{1,0:T(8,128)(2,1)S(1)}, u32[]{:S(2)}, u32[]{:S(2)}) collective-permute-start(bf16[256,512]{1,0:T(8,128)(2,1)S(1)} %get-tuple-element.50), channel_id=1, source_target_pairs={{6,4},{4,2},{7,5},{5,3},{14,12},{12,10},{15,13},{13,11},{22,20},{2... | collective-permute-start | bytes 786440 | tf_op jit(solution)/shard_map/ppermute | solution.py:296
  200.8 13.0 %collective-permute-start.55 = (bf16[256,512]{1,0:T(8,128)(2,1)S(1)}, bf16[256,512]{1,0:T(8,128)(2,1)S(1)}, u32[]{:S(2)}, u32[]{:S(2)}) collective-permute-start(bf16[256,512]{1,0:T(8,128)(2,1)S(1)} %get-tuple-element.47), channel_id=1, source_target_pairs={{0,2},{2,4},{4,6},{1,3},{3,5},{5,7},{8,10},{10,12},{12,14},{9,11},... | collective-permute-start | bytes 786440 | tf_op jit(solution)/shard_map/ppermute | solution.py:296
  (70 other events, 630.0 us)

commit v6 on v4

v6 whole, which is shorter than its diff:
```python
import functools

import jax
import jax.numpy as jnp
from jax import lax
from jax.experimental import pallas as pl
from jax.experimental.pallas import tpu as pltpu
from jax.sharding import PartitionSpec as P

CHUNKS = 2
HBM = pl.BlockSpec(memory_space=pltpu.HBM)
VMEM = pl.BlockSpec(memory_space=pltpu.VMEM)
PARAMS = pltpu.CompilerParams(vmem_limit_bytes=16 * 1024 * 1024)


def exchanged(value, axis, steps):
    count = lax.axis_size(axis)
    return lax.ppermute(value, axis, [(i, (i + steps) % count) for i in range(count)])


class Sizes:
    def __init__(self, rows, cols):
        self.row = lax.axis_size("row")
        self.sec = lax.axis_size("sec")
        self.col = lax.axis_size("col")
        self.rows = rows
        self.cols = cols
        self.order = cols * self.col
        self.width = cols // self.sec
        self.chunk = self.width // CHUNKS
        self.per_tile = self.row // self.col


def chosen_copies(sizes, step, tiles, target, top, sems):
    sec_index, col_index = lax.axis_index("sec"), lax.axis_index("col")
    copies = []
    for kx in range(sizes.sec):
        wanted = lax.rem(sec_index - kx + sizes.sec, sizes.sec) == step
        for kc in range(sizes.col):
            tile = lax.rem(col_index - kc + sizes.col, sizes.col) * sizes.cols
            for number, (array, source, panel, offset) in enumerate(tiles[kx][kc]):
                begin = tile + offset
                if panel is not None:
                    begin = begin + lax.rem(sec_index + panel, sizes.sec) * sizes.width
                first, count = source
                place = target.at[
                    top : top + sizes.rows, pl.ds(pl.multiple_of(begin, sizes.chunk), count)
                ]
                columns = array.at[:, first : first + count]
                copies.append((wanted, pltpu.make_async_copy(columns, place, sems.at[kc, number])))
    return copies


def start_all(copies):
    for wanted, copy in copies:
        copy.start() if wanted is True else pl.when(wanted)(copy.start)


def wait_all(copies):
    for wanted, copy in copies:
        copy.wait() if wanted is True else pl.when(wanted)(copy.wait)


def with_arrays(tiles, arrays):
    arrays = iter(arrays)
    return [
        [[(next(arrays), *piece[1:]) for piece in pieces] for pieces in per_section]
        for per_section in tiles
    ]


def arrays_of(tiles):
    return [piece[0] for per_section in tiles for pieces in per_section for piece in pieces]


def own_panel_kernel(sizes, own, out, held, sem):
    begin = pl.multiple_of(lax.axis_index("sec") * sizes.width, sizes.width)
    copy = pltpu.make_async_copy(own.at[:, pl.ds(begin, sizes.width)], held, sem)
    copy.start()
    copy.wait()
    out[...] = held[...].T


def own_panel(sizes, own):
    return pl.pallas_call(
        functools.partial(own_panel_kernel, sizes),
        out_shape=jax.ShapeDtypeStruct((sizes.width, sizes.rows), jnp.bfloat16),
        in_specs=[HBM],
        out_specs=VMEM,
        scratch_shapes=[
            pltpu.VMEM((sizes.rows, sizes.width), jnp.bfloat16),
            pltpu.SemaphoreType.DMA,
        ],
        compiler_params=PARAMS,
        name="own_panel",
    )(own)


def sent_chunk_kernel(sizes, step, *refs):
    *sent, out, held, sem = refs
    distance = lax.rem(lax.axis_index("sec") - step + sizes.sec, sizes.sec)
    distance = jnp.where(distance == 0, 1, distance)
    copies = [
        (distance == kx, pltpu.make_async_copy(piece, held, sem))
        for kx, piece in enumerate(sent, start=1)
    ]
    start_all(copies)
    wait_all(copies)
    out[...] = held[...].T


def sent_chunk(sizes, step, sent):
    shape = (sizes.rows, sizes.chunk)
    return pl.pallas_call(
        functools.partial(sent_chunk_kernel, sizes, step),
        out_shape=jax.ShapeDtypeStruct(shape[::-1], jnp.bfloat16),
        in_specs=[HBM] * len(sent),
        out_specs=VMEM,
        scratch_shapes=[pltpu.VMEM(shape, jnp.bfloat16), pltpu.SemaphoreType.DMA],
        compiler_params=PARAMS,
        name="sent_chunk",
    )(*sent)


def products_kernel(sizes, step, part, block_rows, state_places, tiles, inverse_tiles, *refs):
    n_blocks, n_states = len(block_rows), len(state_places)
    n_tiles, n_inverse_tiles = len(arrays_of(tiles)), len(arrays_of(inverse_tiles))
    blocks, refs = refs[:n_blocks], refs[n_blocks:]
    states, refs = refs[:n_states], refs[n_states:]
    tiles, refs = with_arrays(tiles, refs[:n_tiles]), refs[n_tiles:]
    inverse_tiles, refs = with_arrays(inverse_tiles, refs[:n_inverse_tiles]), refs[n_inverse_tiles:]
    out, up_first, down_first, *refs = refs
    panel, state, rows, left, block_sems, state_sems, tile_sems = refs
    row_index, sec_index, col_index = (lax.axis_index(a) for a in ("row", "sec", "col"))
    count = sizes.chunk

    first_copies = []
    for number, (kx, kc, offset) in enumerate(state_places):
        first = lax.rem(col_index - kc + sizes.col, sizes.col) * sizes.cols + offset
        if kx is not None:
            first = first + lax.rem(sec_index - kx + sizes.sec, sizes.sec) * sizes.width
        height = states[number].shape[0]
        place = state.at[pl.ds(pl.multiple_of(first, height), height)]
        copy = pltpu.make_async_copy(states[number], place, state_sems.at[number])
        first_copies.append((True, copy))
    for number, (ref, row_of) in enumerate(zip(blocks, block_rows)):
        q, wanted = row_of(row_index, sec_index)
        wanted = wanted & (q >= 0) & (q < sizes.row)
        source = ref if ref.shape[0] == count else ref.at[part * count : (part + 1) * count]
        begin = pl.multiple_of(jnp.clip(q, 0, sizes.row - 1) * sizes.rows, sizes.rows)
        place = panel.at[:, pl.ds(begin, sizes.rows)]
        first_copies.append((wanted, pltpu.make_async_copy(source, place, block_sems.at[number])))
    start_all(first_copies)
    tile_copies = []
    for number, array in enumerate((tiles, inverse_tiles)):
        tile_copies += chosen_copies(sizes, step, array, rows, number * sizes.rows, tile_sems.at[number])
    start_all(tile_copies)

    wait_all(first_copies)
    image = jnp.dot(panel[...], state[...], preferred_element_type=jnp.float32)
    left[:, : sizes.rows] = image.astype(jnp.bfloat16)
    wait_all(tile_copies)
    begin = col_index * sizes.cols + sec_index * sizes.width + part * count
    inverse_panel = rows[sizes.rows :, pl.ds(pl.multiple_of(begin, count), count)]
    left[:, sizes.rows :] = inverse_panel.T
    for d in range(sizes.row):
        place = lax.rem(d - row_index + sizes.row, sizes.row)
        out[place] = jnp.dot(
            left[...],
            rows[:, d * sizes.rows : (d + 1) * sizes.rows],
            preferred_element_type=jnp.float32,
        )
    up_first[...] = out[sizes.row - 1].astype(jnp.bfloat16)
    down_first[...] = out[1].astype(jnp.bfloat16)


def products(sizes, step, part, blocks, states, tiles, inverse_tiles):
    flat = arrays_of(tiles) + arrays_of(inverse_tiles)
    most = max(len(p) for per_section in tiles + inverse_tiles for p in per_section)
    shape = (sizes.row, sizes.chunk, sizes.rows)
    return pl.pallas_call(
        functools.partial(
            products_kernel,
            sizes,
            step,
            part,
            [b[0] for b in blocks],
            [s[0] for s in states],
            with_arrays(tiles, [None] * len(flat)),
            with_arrays(inverse_tiles, [None] * len(flat)),
        ),
        out_shape=[jax.ShapeDtypeStruct(shape, jnp.float32)]
        + [jax.ShapeDtypeStruct(shape[1:], jnp.bfloat16)] * 2,
        in_specs=[HBM] * (len(blocks) + len(states) + len(flat)),
        out_specs=[VMEM] * 3,
        scratch_shapes=[
            pltpu.VMEM((sizes.chunk, sizes.order), jnp.bfloat16),
            pltpu.VMEM((sizes.order, sizes.rows), jnp.bfloat16),
            pltpu.VMEM((2 * sizes.rows, sizes.order), jnp.bfloat16),
            pltpu.VMEM((sizes.chunk, 2 * sizes.rows), jnp.bfloat16),
            pltpu.SemaphoreType.DMA((len(blocks),)),
            pltpu.SemaphoreType.DMA((len(states),)),
            pltpu.SemaphoreType.DMA((2, sizes.col, most)),
        ],
        compiler_params=PARAMS,
        cost_estimate=pl.CostEstimate(
            flops=6 * sizes.rows * sizes.chunk * sizes.order,
            bytes_accessed=6 * sizes.rows * sizes.order + 6 * sizes.chunk * sizes.order,
            transcendentals=0,
        ),
        name="products",
    )(*[b[1] for b in blocks], *[s[1] for s in states], *flat)


def output_kernel(sizes, *refs):
    per_step = sizes.sec * CHUNKS
    out = refs[-1]
    sec_index = lax.axis_index("sec")
    for step in range(sizes.sec):

        @pl.when(sec_index == step)
        def _():
            for kx in range(sizes.sec):
                for k in range(CHUNKS):
                    piece = refs[step * per_step + kx * CHUNKS + k][...]
                    first = lax.rem(sec_index - kx + sizes.sec, sizes.sec) * sizes.width
                    begin = pl.multiple_of(first + k * sizes.chunk, sizes.chunk)
                    out[:, pl.ds(begin, sizes.chunk)] = piece.astype(jnp.float32).T


def output(sizes, pieces):
    return pl.pallas_call(
        functools.partial(output_kernel, sizes),
        out_shape=jax.ShapeDtypeStruct((sizes.rows, sizes.cols), jnp.float32),
        in_specs=[VMEM] * len(pieces),
        out_specs=VMEM,
        compiler_params=PARAMS,
        name="output",
    )(*pieces)


def after(value, *others):
    return lax.optimization_barrier((value, *others))[0]


def always(shift):
    return lambda row, sec: (row + shift, True)


def owning(shift, step, owns):
    return lambda row, sec: (row + shift, (sec == step) == owns)


def further_slots(sizes, up, down, others=()):
    last = sizes.row - 1
    found = []
    for slot in range(1, last):
        if slot == 2:
            up, down = after(up, *others), after(down, *others)
        up = lax.ppermute(up, "row", [(i, i + 1) for i in range(slot, last)])
        down = lax.ppermute(down, "row", [(i, i - 1) for i in range(1, sizes.row - slot)])
        found += [(always(-1 - slot), up), (always(1 + slot), down)]
    return found


def first_slot(sizes, block):
    last = sizes.row - 1
    up = lax.ppermute(block, "row", [(i, i + 1) for i in range(last)])
    down = lax.ppermute(block, "row", [(i, i - 1) for i in range(1, sizes.row)])
    return up, down


def scattered_sum(sizes, partials, gather=None):
    blocks, up_first, down_first = partials
    row_index = lax.axis_index("row")
    last = sizes.row - 1
    up = down = None
    found = []
    for slot in range(last):
        if slot:
            up_block = (blocks[last - slot] + up.astype(jnp.float32)).astype(jnp.bfloat16)
            down_block = (blocks[slot + 1] + down.astype(jnp.float32)).astype(jnp.bfloat16)
        else:
            up_block, down_block = up_first, down_first
        low = slot
        if gather is not None:
            if slot == 0:
                up, down = gather
            if slot < last - 1:
                up_block = jnp.where(row_index <= slot, up_block, up)
                down_block = jnp.where(last - row_index <= slot, down_block, down)
                low = last - 1
        up = lax.ppermute(up_block, "row", [(i, i + 1) for i in range(low + 1)])
        down = lax.ppermute(
            down_block, "row", [(i, i - 1) for i in range(last - low, last + 1)]
        )
        if gather is not None and slot < last - 1:
            found += [(always(-2 - slot), up), (always(2 + slot), down)]
    total = blocks[0] + up.astype(jnp.float32) + down.astype(jnp.float32)
    return total.astype(jnp.bfloat16), found


def local(factors, inverses, sigma_end):
    step_count, rows, cols = factors.shape
    assert step_count == 1
    sizes = Sizes(rows, cols)
    sec_size, col_size, width, chunk_width = sizes.sec, sizes.col, sizes.width, sizes.chunk
    sec_index = lax.axis_index("sec")

    def panel(tile, offset, part=None):
        first = (sec_index + offset) % sec_size * width
        if part is None:
            return lax.dynamic_slice_in_dim(tile, first, width, 1)
        return lax.dynamic_slice_in_dim(tile, first + part * chunk_width, chunk_width, 1)

    factor, inverse = factors[0], inverses[0]

    def over_columns(value):
        return [value] + [exchanged(value, "col", kc) for kc in range(1, col_size)]

    def over_columns(value):
        return [value] + [exchanged(value, "col", kc) for kc in range(1, col_size)]

    def part_of(array, part):
        return array[part * chunk_width : (part + 1) * chunk_width]

    def over_columns(value):
        return [value] + [exchanged(value, "col", kc) for kc in range(1, col_size)]

    def part_of(array, part):
        return array[part * chunk_width : (part + 1) * chunk_width]

    last = sec_size - 1
    is_last = sec_index == last
    sent = [[] for _ in range(sec_size)]
    for part in range(CHUNKS):
        for kx in range(1, sec_size):
            sent[kx].append(exchanged(panel(factor, kx, part), "sec", kx))
    own = own_panel(sizes, factor)
    own_first = first_slot(sizes, own)
    own_factors = [factor] + over_columns(after(factor, *own_first))[1:]
    own_inverses = [inverse] + over_columns(after(inverse, *own_first))[1:]
    states = over_columns(after(sigma_end, own).astype(jnp.bfloat16).T)
    state_pieces = [((None, kc, 0), piece) for kc, piece in enumerate(states)]

    sent = [[after(chunk, *own_first) for chunk in chunks] for chunks in sent]
    other, other_first = [], []
    for part in range(CHUNKS):
        block = sent_chunk(sizes, last, [chunks[part] for chunks in sent[1:]])
        if part:
            block = after(block, *states[1:])
        other.append(block)
        other_first.append(first_slot(sizes, block))
    swapped = [chunk for chunks in sent[1:] for chunk in chunks]
    messages = []
    for kx in range(1, sec_size):
        rest = [panel(factor, kx + j) for j in range(1, sec_size)]
        message = jnp.concatenate([*rest, after(inverse, own)], axis=1)
        messages.append(exchanged(after(message, *swapped), "sec", kx))
    sent_columns = [[over_columns(chunk) for chunk in chunks] for chunks in sent]
    moved = [array for chunks in sent_columns for pieces in chunks for array in pieces[1:]]

    factor_blocks = {}
    for part in range(CHUNKS):
        first = other_first[part]
        up, down = (
            jnp.where(is_last, part_of(mine, part), theirs)
            for mine, theirs in zip(own_first, first)
        )
        factor_blocks[last, part] = [
            (owning(0, last, True), own),
            (owning(-1, last, True), own_first[0]),
            (owning(1, last, True), own_first[1]),
            (owning(0, last, False), other[part]),
            (owning(-1, last, False), first[0]),
            (owning(1, last, False), first[1]),
            *further_slots(
                sizes,
                after(up, *moved),
                after(down, *moved),
                [] if part else [*own_factors[1:], *own_inverses[1:], *other_first[CHUNKS - 1]],
            ),
        ]

    late = [array for part in range(CHUNKS) for _, array in factor_blocks[last, part][-2:]]
    factor_tiles = [[[(tile, (0, cols), None, 0)] for tile in own_factors]]
    inverse_tiles = [[[(tile, (0, cols), None, 0)] for tile in own_inverses]]
    for kx in range(1, sec_size):
        arrived = over_columns(after(messages[kx - 1], *late))
        factor_tiles.append(
            [
                [
                    (sent_columns[kx][part][kc], (0, chunk_width), 0, part * chunk_width)
                    for part in range(CHUNKS)
                ]
                + [
                    (arrived[kc], ((j - 1) * width, width), j, 0)
                    for j in range(1, sec_size)
                ]
                for kc in range(col_size)
            ]
        )
        inverse_tiles.append([[(tile, (last * width, cols), None, 0)] for tile in arrived])

    results = {}
    for step in reversed(range(sec_size)):
        next_pieces = []
        for part in range(CHUNKS):
            if step == last and sec_size == 2:
                ahead = tuple(
                    jnp.where(is_last, theirs, part_of(mine, part))
                    for mine, theirs in zip(own_first, other_first[part])
                )
                started = [
                    (owning(0, last, True), other[part]),
                    (owning(-1, last, True), other_first[part][0]),
                    (owning(1, last, True), other_first[part][1]),
                    (owning(0, last, False), own),
                    (owning(-1, last, False), own_first[0]),
                    (owning(1, last, False), own_first[1]),
                ]
            elif step:
                earlier = [array for _, array in factor_blocks[step, part][-2:]]
                mine = sent_chunk(sizes, step - 1, [chunks[part] for chunks in sent[1:]])
                block = after(jnp.where(sec_index == step - 1, part_of(own, part), mine), *earlier)
                ahead = first_slot(sizes, block)
                started = [(always(0), block), (always(-1), ahead[0]), (always(1), ahead[1])]
            partials = products(
                sizes, step, part, factor_blocks[step, part], state_pieces, factor_tiles, inverse_tiles
            )
            if step:
                total, found = scattered_sum(sizes, partials, ahead)
                factor_blocks[step - 1, part] = started + found
            else:
                total, _ = scattered_sum(sizes, partials)
            for kx in range(sec_size):
                piece = exchanged(total, "sec", kx) if kx else total
                results[step, kx, part] = piece
                if step:
                    for kc, moved in enumerate(over_columns(piece)):
                        next_pieces.append(((kx, kc, part * chunk_width), moved))
        state_pieces = next_pieces

    return output(
        sizes,
        [
            results[step, kx, part]
            for step in range(sec_size)
            for kx in range(sec_size)
            for part in range(CHUNKS)
        ],
    )[None]


def solution(mesh):
    in_specs = (
        P(("groups", "sec"), "row", "col"),
        P(("groups", "sec"), "row", "col"),
        P(("groups", "row"), "col"),
    )
    out_specs = P(("groups", "sec"), "row", "col")
    return jax.shard_map(local, mesh=mesh, in_specs=in_specs, out_specs=out_specs, check_vma=False)
```

time: 205 us -> 232 us (1.13)
  local copies, waits for them, and re-layouts: 12.7 us -> 26.8 us
  waiting for transfers between devices: 56.3 us -> 70.2 us
  other arithmetic: 3.77 us -> 10.7 us
  starting transfers between devices: 108 us -> 102 us
    ppermute x2 -> x3, waiting for transfers between devices: 0.01 us -> 16.1 us  [first_slot(): down = lax.ppermute(block, 'row', [(i, i - 1) for i in range(1, sizes.row)])]
    ppermute x12 -> x8, starting transfers between devices: 21.8 us -> 7.83 us  [the longest x4 5.15 us: further_slots(): lax.ppermute(down, 'row', [(i, i - 1) for i in range(1, sizes.row - slot)])]
    unnamed x43 -> x104, local copies, waits for them, and re-layouts: 11.3 us -> 23.3 us
    ppermute x2 -> x3, starting transfers between devices: 9.26 us -> 14.1 us  [first_slot(): up = lax.ppermute(block, 'row', [(i, i + 1) for i in range(last)])]
    ppermute x12, starting transfers between devices: 47.3 us -> 50.2 us  [scattered_sum(): up = lax.ppermute(up_block, 'row', [(i, i + 1) for i in range(low + 1)])]
    ppermute x2 -> x3, waiting for transfers between devices: 0.01 us -> 2.79 us  [first_slot(): up = lax.ppermute(block, 'row', [(i, i + 1) for i in range(last)])]
    optimization_barrier x0 -> x1, local copies, waits for them, and re-layouts: none -> 2.75 us  [after(): return lax.optimization_barrier((value, *others))[0]]
    ppermute x12 -> x8, waiting for transfers between devices: 15.8 us -> 13.3 us  [the longest x4 13.2 us: further_slots(): lax.ppermute(down, 'row', [(i, i - 1) for i in range(1, sizes.row - slot)])]
  transfers between devices with their start and end apart: 57 -> 55, of which waited for: 21 -> 24; matrix products, arithmetic and copies ran while one was open for 3% -> 5% of each run, Pallas kernels for 8% -> 2%
where the time goes in v6:
time: 232 us; the launch traced here: 230 us
  starting transfers between devices  102 us (44%)
  waiting for transfers between devices  70.2 us (30%)
  local copies, waits for them, and re-layouts  26.8 us (12%)
  Pallas kernels  19.8 us (9%)
  other arithmetic  10.7 us (5%)
    ppermute x12, starting transfers between devices, scattered_sum(): up = lax.ppermute(up_block, 'row', [(i, i + 1) for i in range(low + 1)])  50.2 us
    unnamed x104, local copies, waits for them, and re-layouts  23.3 us
    ppermute x17, waiting for transfers between devices, exchanged(): lax.ppermute(value, axis, [(i, (i + steps) % count) for i in range(count)])  19.1 us
    ppermute x3, waiting for transfers between devices, first_slot(): down = lax.ppermute(block, 'row', [(i, i - 1) for i in range(1, sizes.row)])  16.1 us
    pallas_call x4, Pallas kernels, products(): pl.pallas_call(functools.partial(products_kernel, sizes, step, part, [b[0...  16.1 us
    ppermute x3, starting transfers between devices, first_slot(): up = lax.ppermute(block, 'row', [(i, i + 1) for i in range(last)])  14.1 us
    ppermute x12, starting transfers between devices, scattered_sum(): lax.ppermute(down_block, 'row', [(i, i - 1) for i in range(last - low, la...  13.4 us
    ppermute x4, waiting for transfers between devices, further_slots(): lax.ppermute(down, 'row', [(i, i - 1) for i in range(1, sizes.row - slot)])  13.2 us
  transfers between devices with their start and end apart: 55, of which 24 were waited for; matrix products, arithmetic and copies ran while one was open for 5% of the time, Pallas kernels for 2%

profile of v6, /device:TPU:0, one launch (start us, length us, event | category | flops | bytes accessed | tf_op | source)
XLA Modules:
  0.0 230.3 jit_solution(5412758680898749750)
XLA Ops:
  4.7 4.5 %collective-permute-start.1 = (bf16[512,512]{1,0:T(8,128)(2,1)S(1)}, bf16[512,512]{1,0:T(8,128)(2,1)S(1)}, u32[]{:S(2)}, u32[]{:S(2)}) collective-permute-start(bf16[512,512]{1,0:T(8,128)(2,1)S(1)} %own_panel.1.refs_0_.refs_3_), channel_id=1, source_target_pairs={{0,2},{2,4},{4,6},{1,3},{3,5},{5,7},{8,10},{10,12},{12,14},{9,11},... | collective-permute-start | bytes 1572872 | tf_op jit(solution)/shard_map/ppermute | solution.py:268
  15.9 4.8 %collective-permute-done.6.refs_0_.refs_15_.refs_21_ = bf16[512,256]{1,0:T(8,128)(2,1)S(1)} collective-permute-done((bf16[512,256]{1,0:T(8,128)(2,1)}, bf16[512,256]{1,0:T(8,128)(2,1)S(1)}, u32[]{:S(2)}, u32[]{:S(2)}) %collective-permute-start.6) | collective-permute-done | bytes 262176 | tf_op jit(solution)/shard_map/ppermute | solution.py:18
  21.0 4.1 %collective-permute-done.2.refs_2_.refs_5_ = bf16[512,512]{1,0:T(8,128)(2,1)S(1)} collective-permute-done((bf16[512,512]{1,0:T(8,128)(2,1)S(1)}, bf16[512,512]{1,0:T(8,128)(2,1)S(1)}, u32[]{:S(2)}, u32[]{:S(2)}) %collective-permute-start.2) | collective-permute-done | bytes 524320 | tf_op jit(solution)/shard_map/ppermute | solution.py:269
  32.4 8.4 %collective-permute-done.4.refs_5_.refs_2_ = bf16[256,512]{1,0:T(8,128)(2,1)S(1)} collective-permute-done((bf16[256,512]{1,0:T(8,128)(2,1)}, bf16[256,512]{1,0:T(8,128)(2,1)S(1)}, u32[]{:S(2)}, u32[]{:S(2)}) %collective-permute-start.4) | collective-permute-done | bytes 262176 | tf_op jit(solution)/shard_map/ppermute | solution.py:269
  43.6 5.2 %collective-permute-start.3 = (bf16[256,512]{1,0:T(8,128)(2,1)}, bf16[256,512]{1,0:T(8,128)(2,1)}, u32[]{:S(2)}, u32[]{:S(2)}) collective-permute-start(bf16[256,512]{1,0:T(8,128)(2,1)} %sent_chunk.2.refs_3_.refs_0_), channel_id=1, source_target_pairs={{0,2},{2,4},{4,6},{1,3},{3,5},{5,7},{8,10},{10,12},{12,14},{9,11},... | collective-permute-start | bytes 786440 | tf_op jit(solution)/shard_map/ppermute | solution.py:268
  52.4 4.3 %collective-permute-start.13 = (bf16[256,512]{1,0:T(8,128)(2,1)}, bf16[256,512]{1,0:T(8,128)(2,1)}, u32[]{:S(2)}, u32[]{:S(2)}) collective-permute-start(bf16[256,512]{1,0:T(8,128)(2,1)} %sent_chunk.3.refs_3_.refs_0_), channel_id=1, source_target_pairs={{0,2},{2,4},{4,6},{1,3},{3,5},{5,7},{8,10},{10,12},{12,14},{9,11},... | collective-permute-start | bytes 786440 | tf_op jit(solution)/shard_map/ppermute | solution.py:268
  70.9 5.6 %collective-permute-done.20.refs_7_ = bf16[256,512]{1,0:T(8,128)(2,1)S(1)} collective-permute-done((bf16[256,512]{1,0:T(8,128)(2,1)S(1)}, bf16[256,512]{1,0:T(8,128)(2,1)S(1)}, u32[]{:S(2)}, u32[]{:S(2)}) %collective-permute-start.20) | collective-permute-done | bytes 262176 | tf_op jit(solution)/shard_map/ppermute | solution.py:261
  103.8 4.1 %products.4 = (f32[4,256,512]{2,1,0:T(8,128)S(1)}, bf16[256,512]{1,0:T(8,128)(2,1)S(1)}, bf16[256,512]{1,0:T(8,128)(2,1)S(1)}) custom-call(bf16[512,512]{1,0:T(8,128)(2,1)S(1)} %copy-done.13, bf16[512,512]{1,0:T(8,128)(2,1)S(1)} %copy-done.6, bf16[512,512]{1,0:T(8,128)(2,1)S(1)} %copy-done.9, bf16[256,512]{1,0:T(8,128)(2,1)} %sent_chunk.2.refs_3_.refs_0_, ...), custom_call_target="tpu_custom_call" | custom-call | flops 1610612736 | bytes 9437184 | tf_op jit(solution)/shard_map/products/pallas_call | solution.py:181
  109.3 4.0 %products.5 = (f32[4,256,512]{2,1,0:T(8,128)S(1)}, bf16[256,512]{1,0:T(8,128)(2,1)S(1)}, bf16[256,512]{1,0:T(8,128)(2,1)S(1)}) custom-call(bf16[512,512]{1,0:T(8,128)(2,1)S(1)} %copy-done.14, bf16[512,512]{1,0:T(8,128)(2,1)S(1)} %copy-done.6, bf16[512,512]{1,0:T(8,128)(2,1)S(1)} %copy-done.10, bf16[256,512]{1,0:T(8,128)(2,1)} %sent_chunk.3.refs_3_.refs_0_, ...), custom_call_target="tpu_custom_call" | custom-call | flops 1610612736 | bytes 9437184 | tf_op jit(solution)/shard_map/products/pallas_call | solution.py:181
  116.5 5.3 %collective-permute-start.32 = (bf16[256,512]{1,0:T(8,128)(2,1)}, bf16[256,512]{1,0:T(8,128)(2,1)}, u32[]{:S(2)}, u32[]{:S(2)}) collective-permute-start(bf16[256,512]{1,0:T(8,128)(2,1)} %get-tuple-element.73), channel_id=1, source_target_pairs={{0,2},{2,4},{4,6},{1,3},{3,5},{5,7},{8,10},{10,12},{12,14},{9,11},... | collective-permute-start | bytes 786440 | tf_op jit(solution)/shard_map/ppermute | solution.py:293
  123.1 4.6 %collective-permute-start.23 = (bf16[256,512]{1,0:T(8,128)(2,1)}, bf16[256,512]{1,0:T(8,128)(2,1)S(1)}, u32[]{:S(2)}, u32[]{:S(2)}) collective-permute-start(bf16[256,512]{1,0:T(8,128)(2,1)} %get-tuple-element.74), channel_id=1, source_target_pairs={{0,2},{2,4},{4,6},{1,3},{3,5},{5,7},{8,10},{10,12},{12,14},{9,11},... | collective-permute-start | bytes 786440 | tf_op jit(solution)/shard_map/ppermute | solution.py:293
  129.3 4.0 %collective-permute-start.33 = (bf16[256,512]{1,0:T(8,128)(2,1)S(1)}, bf16[256,512]{1,0:T(8,128)(2,1)S(1)}, u32[]{:S(2)}, u32[]{:S(2)}) collective-permute-start(bf16[256,512]{1,0:T(8,128)(2,1)S(1)} %get-tuple-element.65), channel_id=1, source_target_pairs={{0,2},{2,4},{4,6},{1,3},{3,5},{5,7},{8,10},{10,12},{12,14},{9,11},... | collective-permute-start | bytes 786440 | tf_op jit(solution)/shard_map/ppermute | solution.py:293
  135.8 4.6 %collective-permute-start.25 = (bf16[256,512]{1,0:T(8,128)(2,1)S(1)}, bf16[256,512]{1,0:T(8,128)(2,1)S(1)}, u32[]{:S(2)}, u32[]{:S(2)}) collective-permute-start(bf16[256,512]{1,0:T(8,128)(2,1)S(1)} %get-tuple-element.70), channel_id=1, source_target_pairs={{0,2},{2,4},{4,6},{1,3},{3,5},{5,7},{8,10},{10,12},{12,14},{9,11},... | collective-permute-start | bytes 786440 | tf_op jit(solution)/shard_map/ppermute | solution.py:293
  142.7 4.1 %collective-permute-start.34 = (bf16[256,512]{1,0:T(8,128)(2,1)S(1)}, bf16[256,512]{1,0:T(8,128)(2,1)S(1)}, u32[]{:S(2)}, u32[]{:S(2)}) collective-permute-start(bf16[256,512]{1,0:T(8,128)(2,1)S(1)} %get-tuple-element.63), channel_id=1, source_target_pairs={{0,2},{2,4},{4,6},{1,3},{3,5},{5,7},{8,10},{10,12},{12,14},{9,11},... | collective-permute-start | bytes 786440 | tf_op jit(solution)/shard_map/ppermute | solution.py:293
  157.7 3.9 %collective-permute-done.28 = bf16[256,512]{1,0:T(8,128)(2,1)S(1)} collective-permute-done((bf16[256,512]{1,0:T(8,128)(2,1)S(1)}, bf16[256,512]{1,0:T(8,128)(2,1)S(1)}, u32[]{:S(2)}, u32[]{:S(2)}) %collective-permute-start.28) | collective-permute-done | bytes 262176 | tf_op jit(solution)/shard_map/ppermute | solution.py:294
  164.3 3.9 %collective-permute-done.30.refs_12_.refs_6_ = bf16[256,512]{1,0:T(8,128)(2,1)S(1)} collective-permute-done((bf16[256,512]{1,0:T(8,128)(2,1)S(1)}, bf16[256,512]{1,0:T(8,128)(2,1)S(1)}, u32[]{:S(2)}, u32[]{:S(2)}) %collective-permute-start.30) | collective-permute-done | bytes 262176 | tf_op jit(solution)/shard_map/ppermute | solution.py:18
  169.8 4.0 %products.7 = (f32[4,256,512]{2,1,0:T(8,128)S(1)}, bf16[256,512]{1,0:T(8,128)(2,1)S(1)}, bf16[256,512]{1,0:T(8,128)(2,1)S(1)}) custom-call(bf16[256,512]{1,0:T(8,128)(2,1)} %sent_chunk.3.refs_3_.refs_0_, bf16[256,512]{1,0:T(8,128)(2,1)} %collective-permute-done.13.refs_4_.refs_1_, bf16[256,512]{1,0:T(8,128)(2,1)} %collective-permute-done.14.refs_5_.refs_2_, ...), custom_call_target="tpu_custom_call" | custom-call | flops 1610612736 | bytes 9437184 | tf_op jit(solution)/shard_map/products/pallas_call | solution.py:181
  177.6 4.0 %products.6 = (f32[4,256,512]{2,1,0:T(8,128)S(1)}, bf16[256,512]{1,0:T(8,128)(2,1)S(1)}, bf16[256,512]{1,0:T(8,128)(2,1)S(1)}) custom-call(bf16[256,512]{1,0:T(8,128)(2,1)} %sent_chunk.2.refs_3_.refs_0_, bf16[256,512]{1,0:T(8,128)(2,1)} %collective-permute-done.3.refs_4_.refs_1_, bf16[256,512]{1,0:T(8,128)(2,1)S(1)} %copy-done.31, ...), custom_call_target="tpu_custom_call" | custom-call | flops 1610612736 | bytes 9437184 | tf_op jit(solution)/shard_map/products/pallas_call | solution.py:181
  183.7 4.4 %collective-permute-start.48 = (bf16[256,512]{1,0:T(8,128)(2,1)S(1)}, bf16[256,512]{1,0:T(8,128)(2,1)S(1)}, u32[]{:S(2)}, u32[]{:S(2)}) collective-permute-start(bf16[256,512]{1,0:T(8,128)(2,1)S(1)} %fusion.1), channel_id=1, source_target_pairs={{0,2},{2,4},{1,3},{3,5},{8,10},{10,12},{9,11},{11,13},{16,18},{18,... | collective-permute-start | bytes 786440 | tf_op jit(solution)/shard_map/ppermute | solution.py:293
  189.6 4.4 %collective-permute-start.42 = (bf16[256,512]{1,0:T(8,128)(2,1)S(1)}, bf16[256,512]{1,0:T(8,128)(2,1)S(1)}, u32[]{:S(2)}, u32[]{:S(2)}) collective-permute-start(bf16[256,512]{1,0:T(8,128)(2,1)S(1)} %fusion.7), channel_id=1, source_target_pairs={{0,2},{2,4},{1,3},{3,5},{8,10},{10,12},{9,11},{11,13},{16,18},{18,... | collective-permute-start | bytes 786440 | tf_op jit(solution)/shard_map/ppermute | solution.py:293
  196.0 4.2 %collective-permute-done.42 = bf16[256,512]{1,0:T(8,128)(2,1)S(1)} collective-permute-done((bf16[256,512]{1,0:T(8,128)(2,1)S(1)}, bf16[256,512]{1,0:T(8,128)(2,1)S(1)}, u32[]{:S(2)}, u32[]{:S(2)}) %collective-permute-start.42) | collective-permute-done | bytes 262176 | tf_op jit(solution)/shard_map/ppermute | solution.py:293
  201.1 5.0 %collective-permute-start.49 = (bf16[256,512]{1,0:T(8,128)(2,1)S(1)}, bf16[256,512]{1,0:T(8,128)(2,1)S(1)}, u32[]{:S(2)}, u32[]{:S(2)}) collective-permute-start(bf16[256,512]{1,0:T(8,128)(2,1)S(1)} %get-tuple-element.59), channel_id=1, source_target_pairs={{0,2},{2,4},{4,6},{1,3},{3,5},{5,7},{8,10},{10,12},{12,14},{9,11},... | collective-permute-start | bytes 786440 | tf_op jit(solution)/shard_map/ppermute | solution.py:293
  207.5 5.2 %collective-permute-start.43 = (bf16[256,512]{1,0:T(8,128)(2,1)S(1)}, bf16[256,512]{1,0:T(8,128)(2,1)S(1)}, u32[]{:S(2)}, u32[]{:S(2)}) collective-permute-start(bf16[256,512]{1,0:T(8,128)(2,1)S(1)} %get-tuple-element.61), channel_id=1, source_target_pairs={{0,2},{2,4},{4,6},{1,3},{3,5},{5,7},{8,10},{10,12},{12,14},{9,11},... | collective-permute-start | bytes 786440 | tf_op jit(solution)/shard_map/ppermute | solution.py:293
  223.6 5.0 %collective-permute-done.53.refs_2_ = bf16[256,512]{1,0:T(8,128)(2,1)S(1)} collective-permute-done((bf16[256,512]{1,0:T(8,128)(2,1)S(1)}, bf16[256,512]{1,0:T(8,128)(2,1)S(1)}, u32[]{:S(2)}, u32[]{:S(2)}) %collective-permute-start.53) | collective-permute-done | bytes 262176 | tf_op jit(solution)/shard_map/ppermute | solution.py:18
  (220 shorter events, 117.8 us)
Async XLA Ops:
  4.3 27.2 %collective-permute-start.12 = (bf16[1024,512]{1,0:T(8,128)(2,1)}, bf16[1024,512]{1,0:T(8,128)(2,1)}, u32[]{:S(2)}, u32[]{:S(2)}) collective-permute-start(bf16[1024,512]{1,0:T(8,128)(2,1)} %bitcast.103.refs_10_), channel_id=1, source_target_pairs={{0,1},{1,0},{2,3},{3,2},{4,5},{5,4},{6,7},{7,6},{8,9},{9,8},{10,11... | collective-permute-start | bytes 3145736 | tf_op jit(solution)/shard_map/ppermute | solution.py:18
  4.7 16.3 %collective-permute-start.1 = (bf16[512,512]{1,0:T(8,128)(2,1)S(1)}, bf16[512,512]{1,0:T(8,128)(2,1)S(1)}, u32[]{:S(2)}, u32[]{:S(2)}) collective-permute-start(bf16[512,512]{1,0:T(8,128)(2,1)S(1)} %own_panel.1.refs_0_.refs_3_), channel_id=1, source_target_pairs={{0,2},{2,4},{4,6},{1,3},{3,5},{5,7},{8,10},{10,12},{12,14},{9,11},... | collective-permute-start | bytes 1572872 | tf_op jit(solution)/shard_map/ppermute | solution.py:268
  9.2 15.9 %collective-permute-start.2 = (bf16[512,512]{1,0:T(8,128)(2,1)S(1)}, bf16[512,512]{1,0:T(8,128)(2,1)S(1)}, u32[]{:S(2)}, u32[]{:S(2)}) collective-permute-start(bf16[512,512]{1,0:T(8,128)(2,1)S(1)} %own_panel.1.refs_0_.refs_3_), channel_id=1, source_target_pairs={{2,0},{4,2},{6,4},{3,1},{5,3},{7,5},{10,8},{12,10},{14,12},{11,9},... | collective-permute-start | bytes 1572872 | tf_op jit(solution)/shard_map/ppermute | solution.py:269
  12.8 12.8 %collective-permute-start = (bf16[512,256]{1,0:T(8,128)(2,1)S(1)}, bf16[512,256]{1,0:T(8,128)(2,1)S(1)}, u32[]{:S(2)}, u32[]{:S(2)}) collective-permute-start(bf16[512,256]{1,0:T(8,128)(2,1)S(1)} %get-tuple-element.72), channel_id=1, source_target_pairs={{0,8},{8,0},{1,9},{9,1},{2,10},{10,2},{3,11},{11,3},{4,12},{12,4},... | collective-permute-start | bytes 786440 | tf_op jit(solution)/shard_map/ppermute | solution.py:18
  26.3 37.2 %collective-permute-start.10 = (bf16[512,1024]{1,0:T(8,128)(2,1)S(1)}, bf16[512,1024]{1,0:T(8,128)(2,1)}, u32[]{:S(2)}, u32[]{:S(2)}) collective-permute-start(bf16[512,1024]{1,0:T(8,128)(2,1)S(1)} %bitcast.105), channel_id=1, source_target_pairs={{0,1},{1,0},{2,3},{3,2},{4,5},{5,4},{6,7},{7,6},{8,9},{9,8},{10,11... | collective-permute-start | bytes 3145736 | tf_op jit(solution)/shard_map/ppermute | solution.py:18
  26.3 38.5 %collective-permute-start.11 = (bf16[512,1024]{1,0:T(8,128)(2,1)}, bf16[512,1024]{1,0:T(8,128)(2,1)}, u32[]{:S(2)}, u32[]{:S(2)}) collective-permute-start(bf16[512,1024]{1,0:T(8,128)(2,1)} %bitcast.3.refs_20_.refs_26_), channel_id=1, source_target_pairs={{0,1},{1,0},{2,3},{3,2},{4,5},{5,4},{6,7},{7,6},{8,9},{9,8},{10,11... | collective-permute-start | bytes 3145736 | tf_op jit(solution)/shard_map/ppermute | solution.py:18
  26.8 61.5 %collective-permute-start.17 = (bf16[512,1536]{1,0:T(8,128)(2,1)}, bf16[512,1536]{1,0:T(8,128)(2,1)S(1)}, u32[]{:S(2)}, u32[]{:S(2)}) collective-permute-start(bf16[512,1536]{1,0:T(8,128)(2,1)} %pad_maximum_fusion), channel_id=1, source_target_pairs={{0,8},{8,0},{1,9},{9,1},{2,10},{10,2},{3,11},{11,3},{4,12},{12,4},... | collective-permute-start | bytes 4718600 | tf_op jit(solution)/shard_map/ppermute | solution.py:18
  41.6 10.9 %collective-permute-start.14 = (bf16[256,512]{1,0:T(8,128)(2,1)}, bf16[256,512]{1,0:T(8,128)(2,1)}, u32[]{:S(2)}, u32[]{:S(2)}) collective-permute-start(bf16[256,512]{1,0:T(8,128)(2,1)} %sent_chunk.3.refs_3_.refs_0_), channel_id=1, source_target_pairs={{2,0},{4,2},{6,4},{3,1},{5,3},{7,5},{10,8},{12,10},{14,12},{11,9},... | collective-permute-start | bytes 786440 | tf_op jit(solution)/shard_map/ppermute | solution.py:269
  43.6 14.4 %collective-permute-start.3 = (bf16[256,512]{1,0:T(8,128)(2,1)}, bf16[256,512]{1,0:T(8,128)(2,1)}, u32[]{:S(2)}, u32[]{:S(2)}) collective-permute-start(bf16[256,512]{1,0:T(8,128)(2,1)} %sent_chunk.2.refs_3_.refs_0_), channel_id=1, source_target_pairs={{0,2},{2,4},{4,6},{1,3},{3,5},{5,7},{8,10},{10,12},{12,14},{9,11},... | collective-permute-start | bytes 786440 | tf_op jit(solution)/shard_map/ppermute | solution.py:268
  63.5 13.0 %collective-permute-start.20 = (bf16[256,512]{1,0:T(8,128)(2,1)S(1)}, bf16[256,512]{1,0:T(8,128)(2,1)S(1)}, u32[]{:S(2)}, u32[]{:S(2)}) collective-permute-start(bf16[256,512]{1,0:T(8,128)(2,1)S(1)} %get-tuple-element.45), channel_id=1, source_target_pairs={{2,0},{4,2},{3,1},{5,3},{10,8},{12,10},{11,9},{13,11},{18,16},{20,... | collective-permute-start | bytes 786440 | tf_op jit(solution)/shard_map/ppermute | solution.py:261
  64.9 13.7 %collective-permute-start.18 = (bf16[256,512]{1,0:T(8,128)(2,1)S(1)}, bf16[256,512]{1,0:T(8,128)(2,1)S(1)}, u32[]{:S(2)}, u32[]{:S(2)}) collective-permute-start(bf16[256,512]{1,0:T(8,128)(2,1)S(1)} %get-tuple-element.44), channel_id=1, source_target_pairs={{2,4},{4,6},{3,5},{5,7},{10,12},{12,14},{11,13},{13,15},{18,20},{2... | collective-permute-start | bytes 786440 | tf_op jit(solution)/shard_map/ppermute | solution.py:260
  67.5 15.7 %collective-permute-start.16 = (bf16[256,512]{1,0:T(8,128)(2,1)S(1)}, bf16[256,512]{1,0:T(8,128)(2,1)S(1)}, u32[]{:S(2)}, u32[]{:S(2)}) collective-permute-start(bf16[256,512]{1,0:T(8,128)(2,1)S(1)} %collective-permute-done.9.refs_7_), channel_id=1, source_target_pairs={{2,0},{3,1},{10,8},{11,9},{18,16},{19,17},{26,24},{27,25}} | collective-permute-start | bytes 786440 | tf_op jit(solution)/shard_map/ppermute | solution.py:261
  69.5 14.4 %collective-permute-start.15 = (bf16[256,512]{1,0:T(8,128)(2,1)S(1)}, bf16[256,512]{1,0:T(8,128)(2,1)S(1)}, u32[]{:S(2)}, u32[]{:S(2)}) collective-permute-start(bf16[256,512]{1,0:T(8,128)(2,1)S(1)} %collective-permute-done.8.refs_6_), channel_id=1, source_target_pairs={{4,6},{5,7},{12,14},{13,15},{20,22},{21,23},{28,30},{29,31}} | collective-permute-start | bytes 786440 | tf_op jit(solution)/shard_map/ppermute | solution.py:260
  114.3 13.4 %collective-permute-start.35 = (bf16[256,512]{1,0:T(8,128)(2,1)}, bf16[256,512]{1,0:T(8,128)(2,1)}, u32[]{:S(2)}, u32[]{:S(2)}) collective-permute-start(bf16[256,512]{1,0:T(8,128)(2,1)} %get-tuple-element.75), channel_id=1, source_target_pairs={{2,0},{4,2},{6,4},{3,1},{5,3},{7,5},{10,8},{12,10},{14,12},{11,9},... | collective-permute-start | bytes 786440 | tf_op jit(solution)/shard_map/ppermute | solution.py:294
  116.5 11.3 %collective-permute-start.32 = (bf16[256,512]{1,0:T(8,128)(2,1)}, bf16[256,512]{1,0:T(8,128)(2,1)}, u32[]{:S(2)}, u32[]{:S(2)}) collective-permute-start(bf16[256,512]{1,0:T(8,128)(2,1)} %get-tuple-element.73), channel_id=1, source_target_pairs={{0,2},{2,4},{4,6},{1,3},{3,5},{5,7},{8,10},{10,12},{12,14},{9,11},... | collective-permute-start | bytes 786440 | tf_op jit(solution)/shard_map/ppermute | solution.py:293
  121.7 12.8 %collective-permute-start.24 = (bf16[256,512]{1,0:T(8,128)(2,1)}, bf16[256,512]{1,0:T(8,128)(2,1)S(1)}, u32[]{:S(2)}, u32[]{:S(2)}) collective-permute-start(bf16[256,512]{1,0:T(8,128)(2,1)} %get-tuple-element.76), channel_id=1, source_target_pairs={{2,0},{4,2},{6,4},{3,1},{5,3},{7,5},{10,8},{12,10},{14,12},{11,9},... | collective-permute-start | bytes 786440 | tf_op jit(solution)/shard_map/ppermute | solution.py:294
  123.1 11.4 %collective-permute-start.23 = (bf16[256,512]{1,0:T(8,128)(2,1)}, bf16[256,512]{1,0:T(8,128)(2,1)S(1)}, u32[]{:S(2)}, u32[]{:S(2)}) collective-permute-start(bf16[256,512]{1,0:T(8,128)(2,1)} %get-tuple-element.74), channel_id=1, source_target_pairs={{0,2},{2,4},{4,6},{1,3},{3,5},{5,7},{8,10},{10,12},{12,14},{9,11},... | collective-permute-start | bytes 786440 | tf_op jit(solution)/shard_map/ppermute | solution.py:293
  129.3 12.3 %collective-permute-start.33 = (bf16[256,512]{1,0:T(8,128)(2,1)S(1)}, bf16[256,512]{1,0:T(8,128)(2,1)S(1)}, u32[]{:S(2)}, u32[]{:S(2)}) collective-permute-start(bf16[256,512]{1,0:T(8,128)(2,1)S(1)} %get-tuple-element.65), channel_id=1, source_target_pairs={{0,2},{2,4},{4,6},{1,3},{3,5},{5,7},{8,10},{10,12},{12,14},{9,11},... | collective-permute-start | bytes 786440 | tf_op jit(solution)/shard_map/ppermute | solution.py:293
  135.8 12.7 %collective-permute-start.25 = (bf16[256,512]{1,0:T(8,128)(2,1)S(1)}, bf16[256,512]{1,0:T(8,128)(2,1)S(1)}, u32[]{:S(2)}, u32[]{:S(2)}) collective-permute-start(bf16[256,512]{1,0:T(8,128)(2,1)S(1)} %get-tuple-element.70), channel_id=1, source_target_pairs={{0,2},{2,4},{4,6},{1,3},{3,5},{5,7},{8,10},{10,12},{12,14},{9,11},... | collective-permute-start | bytes 786440 | tf_op jit(solution)/shard_map/ppermute | solution.py:293
  142.7 11.9 %collective-permute-start.34 = (bf16[256,512]{1,0:T(8,128)(2,1)S(1)}, bf16[256,512]{1,0:T(8,128)(2,1)S(1)}, u32[]{:S(2)}, u32[]{:S(2)}) collective-permute-start(bf16[256,512]{1,0:T(8,128)(2,1)S(1)} %get-tuple-element.63), channel_id=1, source_target_pairs={{0,2},{2,4},{4,6},{1,3},{3,5},{5,7},{8,10},{10,12},{12,14},{9,11},... | collective-permute-start | bytes 786440 | tf_op jit(solution)/shard_map/ppermute | solution.py:293
  182.9 11.1 %collective-permute-start.50 = (bf16[256,512]{1,0:T(8,128)(2,1)S(1)}, bf16[256,512]{1,0:T(8,128)(2,1)S(1)}, u32[]{:S(2)}, u32[]{:S(2)}) collective-permute-start(bf16[256,512]{1,0:T(8,128)(2,1)S(1)} %get-tuple-element.58), channel_id=1, source_target_pairs={{6,4},{7,5},{14,12},{15,13},{22,20},{23,21},{30,28},{31,29}} | collective-permute-start | bytes 786440 | tf_op jit(solution)/shard_map/ppermute | solution.py:294
  183.7 11.5 %collective-permute-start.48 = (bf16[256,512]{1,0:T(8,128)(2,1)S(1)}, bf16[256,512]{1,0:T(8,128)(2,1)S(1)}, u32[]{:S(2)}, u32[]{:S(2)}) collective-permute-start(bf16[256,512]{1,0:T(8,128)(2,1)S(1)} %fusion.1), channel_id=1, source_target_pairs={{0,2},{2,4},{1,3},{3,5},{8,10},{10,12},{9,11},{11,13},{16,18},{18,... | collective-permute-start | bytes 786440 | tf_op jit(solution)/shard_map/ppermute | solution.py:293
  200.4 12.3 %collective-permute-start.45 = (bf16[256,512]{1,0:T(8,128)(2,1)S(1)}, bf16[256,512]{1,0:T(8,128)(2,1)S(1)}, u32[]{:S(2)}, u32[]{:S(2)}) collective-permute-start(bf16[256,512]{1,0:T(8,128)(2,1)S(1)} %get-tuple-element.62), channel_id=1, source_target_pairs={{4,2},{6,4},{5,3},{7,5},{12,10},{14,12},{13,11},{15,13},{20,18},{2... | collective-permute-start | bytes 786440 | tf_op jit(solution)/shard_map/ppermute | solution.py:294
  201.1 13.0 %collective-permute-start.49 = (bf16[256,512]{1,0:T(8,128)(2,1)S(1)}, bf16[256,512]{1,0:T(8,128)(2,1)S(1)}, u32[]{:S(2)}, u32[]{:S(2)}) collective-permute-start(bf16[256,512]{1,0:T(8,128)(2,1)S(1)} %get-tuple-element.59), channel_id=1, source_target_pairs={{0,2},{2,4},{4,6},{1,3},{3,5},{5,7},{8,10},{10,12},{12,14},{9,11},... | collective-permute-start | bytes 786440 | tf_op jit(solution)/shard_map/ppermute | solution.py:293
  (83 other events, 605.7 us)

commit v7 on v4

--- a/solution.py
+++ b/solution.py
@@ -10,7 +10,7 @@
 CHUNKS = 2
 ANY = pl.BlockSpec(memory_space=pl.ANY)
 VMEM = pl.BlockSpec(memory_space=pltpu.VMEM)
-PARAMS = pltpu.CompilerParams(vmem_limit_bytes=16 * 1024 * 1024)
+PARAMS = pltpu.CompilerParams(vmem_limit_bytes=12 * 1024 * 1024)
 
 
 def exchanged(value, axis, steps):
@@ -31,13 +31,14 @@
         self.per_tile = self.row // self.col
 
 
-def chosen_copies(sizes, step, tiles, target, sems):
+def chosen_copies(sizes, step, tiles, target, top, sems):
     sec_index, col_index = lax.axis_index("sec"), lax.axis_index("col")
     copies = []
     for kc in range(sizes.col):
-        place = lax.rem(col_index - kc + sizes.col, sizes.col)
+        begin = lax.rem(col_index - kc + sizes.col, sizes.col) * sizes.cols
+        place = target.at[top : top + sizes.rows, pl.ds(pl.multiple_of(begin, sizes.cols), sizes.cols)]
         for kx in range(sizes.sec):
-            copy = pltpu.make_async_copy(tiles[kx][kc], target.at[place], sems.at[kc])
+            copy = pltpu.make_async_copy(tiles[kx][kc], place, sems.at[kc])
             wanted = lax.rem(sec_index - kx + sizes.sec, sizes.sec) == step
             copies.append((wanted, copy))
     return copies
@@ -45,12 +46,12 @@
 
 def start_all(copies):
     for wanted, copy in copies:
-        pl.when(wanted)(copy.start)
+        copy.start() if wanted is True else pl.when(wanted)(copy.start)
 
 
 def wait_all(copies):
     for wanted, copy in copies:
-        pl.when(wanted)(copy.wait)
+        copy.wait() if wanted is True else pl.when(wanted)(copy.wait)
 
 
 def nested(refs, sizes):
@@ -83,7 +84,7 @@
     return pl.pallas_call(
         functools.partial(panel_kernel, sizes, step, offset),
         out_shape=jax.ShapeDtypeStruct((count, sizes.rows), jnp.bfloat16),
-        in_specs=[ANY] * (1 + len(flat)),
+        in_specs=[ANY] + [VMEM] * len(flat),
         out_specs=VMEM,
         scratch_shapes=[
             pltpu.VMEM((sizes.rows, count), jnp.bfloat16),
@@ -101,51 +102,46 @@
     tiles, refs = nested(refs[:n_tiles], sizes), refs[n_tiles:]
     inverse_tiles, refs = nested(refs[:n_tiles], sizes), refs[n_tiles:]
     out, up_first, down_first, *refs = refs
-    state, rows, inverses, product, tile_sems, inverse_sems, state_sems = refs
+    panel, state, rows, left, block_sems, state_sems, tile_sems = refs
     row_index, sec_index, col_index = (lax.axis_index(a) for a in ("row", "sec", "col"))
-
-    state_copies = []
+    count = sizes.chunk
+
+    first_copies = []
     for number, (kx, kc, offset) in enumerate(state_places):
         first = lax.rem(col_index - kc + sizes.col, sizes.col) * sizes.cols + offset
         if kx is not None:
             first = first + lax.rem(sec_index - kx + sizes.sec, sizes.sec) * sizes.width
         height = states[number].shape[0]
         place = state.at[pl.ds(pl.multiple_of(first, height), height)]
-        state_copies.append(pltpu.make_async_copy(states[number], place, state_sems.at[number]))
-    for copy in state_copies:
-        copy.start()
-    tile_copies = chosen_copies(sizes, step, tiles, rows, tile_sems)
+        copy = pltpu.make_async_copy(states[number], place, state_sems.at[number])
+        first_copies.append((True, copy))
+    for number, (ref, row_of) in enumerate(zip(blocks, block_rows)):
+        q, low, high = row_of(row_index)
+        wanted = (q >= low) & (q <= high)
+        source = ref if ref.shape[0] == count else ref.at[part * count : (part + 1) * count]
+        begin = pl.multiple_of(jnp.clip(q, 0, sizes.row - 1) * sizes.rows, sizes.rows)
+        place = panel.at[:, pl.ds(begin, sizes.rows)]
+        first_copies.append((wanted, pltpu.make_async_copy(source, place, block_sems.at[number])))
+    start_all(first_copies)
+    tile_copies = []
+    for number, array in enumerate((tiles, inverse_tiles)):
+        tile_copies += chosen_copies(sizes, step, array, rows, number * sizes.rows, tile_sems.at[number])
     start_all(tile_copies)
-    inverse_copies = chosen_copies(sizes, step, inverse_tiles, inverses, inverse_sems)
-    start_all(inverse_copies)
-    for copy in state_copies:
-        copy.wait()
-
-    product[...] = jnp.zeros((sizes.chunk, sizes.rows), jnp.float32)
-
-    def accumulate(ref, q):
-        first = pl.multiple_of(q * sizes.rows, sizes.rows)
-        count = sizes.chunk
-        block = ref[...] if ref.shape[0] == count else ref[part * count : (part + 1) * count]
-        product[...] += jnp.dot(
-            block, state[pl.ds(first, sizes.rows)], preferred_element_type=jnp.float32
-        )
-
-    for ref, row_of in zip(blocks, block_rows):
-        q, low, high = row_of(row_index)
-        pl.when((q >= low) & (q <= high))(functools.partial(accumulate, ref, q))
-    image = product[...].astype(jnp.bfloat16)
+
+    wait_all(first_copies)
+    image = jnp.dot(panel[...], state[...], preferred_element_type=jnp.float32)
+    left[:, : sizes.rows] = image.astype(jnp.bfloat16)
     wait_all(tile_copies)
-    wait_all(inverse_copies)
-    begin = pl.multiple_of(sec_index * sizes.width + part * sizes.chunk, sizes.chunk)
-    left = inverses[col_index, :, pl.ds(begin, sizes.chunk)].T
+    begin = col_index * sizes.cols + sec_index * sizes.width + part * count
+    inverse_panel = rows[sizes.rows :, pl.ds(pl.multiple_of(begin, count), count)]
+    left[:, sizes.rows :] = inverse_panel.T
     for d in range(sizes.row):
-        h, i = divmod(d, sizes.per_tile)
-        block = slice(i * sizes.rows, (i + 1) * sizes.rows)
         place = lax.rem(d - row_index + sizes.row, sizes.row)
         out[place] = jnp.dot(
-            image, rows[h, :, block], preferred_element_type=jnp.float32
-        ) + jnp.dot(left, inverses[h, :, block], preferred_element_type=jnp.float32)
+            left[...],
+            rows[:, d * sizes.rows : (d + 1) * sizes.rows],
+            preferred_element_type=jnp.float32,
+        )
     up_first[...] = out[sizes.row - 1].astype(jnp.bfloat16)
     down_first[...] = out[1].astype(jnp.bfloat16)
 
@@ -162,18 +158,18 @@
         in_specs=[VMEM] * len(blocks) + [ANY] * (len(states) + len(flat)),
         out_specs=[VMEM] * 3,
         scratch_shapes=[
+            pltpu.VMEM((sizes.chunk, sizes.order), jnp.bfloat16),
             pltpu.VMEM((sizes.order, sizes.rows), jnp.bfloat16),
-            pltpu.VMEM((sizes.col, sizes.rows, sizes.cols), jnp.bfloat16),
-            pltpu.VMEM((sizes.col, sizes.rows, sizes.cols), jnp.bfloat16),
-            pltpu.VMEM(shape[1:], jnp.float32),
-            pltpu.SemaphoreType.DMA((sizes.col,)),
-            pltpu.SemaphoreType.DMA((sizes.col,)),
+            pltpu.VMEM((2 * sizes.rows, sizes.order), jnp.bfloat16),
+            pltpu.VMEM((sizes.chunk, 2 * sizes.rows), jnp.bfloat16),
+            pltpu.SemaphoreType.DMA((len(blocks),)),
             pltpu.SemaphoreType.DMA((len(states),)),
+            pltpu.SemaphoreType.DMA((2, sizes.col)),
         ],
         compiler_params=PARAMS,
         cost_estimate=pl.CostEstimate(
             flops=6 * sizes.rows * sizes.chunk * sizes.order,
-            bytes_accessed=4 * sizes.rows * sizes.order + 10 * sizes.chunk * sizes.order,
+            bytes_accessed=6 * sizes.rows * sizes.order + 6 * sizes.chunk * sizes.order,
             transcendentals=0,
         ),
         name="products",

time: 205 us -> 204 us (level)
  waiting for transfers between devices: 56.3 us -> 59.6 us
  starting transfers between devices: 108 us -> 105 us
    ppermute x17, starting transfers between devices: 13.9 us -> 10.7 us  [exchanged(): lax.ppermute(value, axis, [(i, (i + steps) % count) for i in range(count)])]
  transfers between devices with their start and end apart: 57 -> 57, of which waited for: 21 -> 22; matrix products, arithmetic and copies ran while one was open for 3% -> 3% of each run, Pallas kernels for 8% -> 8%
where the time goes in v7:
time: 204 us; the launch traced here: 202 us
  starting transfers between devices  105 us (51%)
  waiting for transfers between devices  59.6 us (29%)
  Pallas kernels  21.9 us (11%)
  local copies, waits for them, and re-layouts  11.2 us (5%)
  other arithmetic  3.77 us (2%)
    ppermute x12, starting transfers between devices, scattered_sum(): up = lax.ppermute(up_block, 'row', [(i, i + 1) for i in range(low + 1)])  47.5 us
    ppermute x17, waiting for transfers between devices, exchanged(): lax.ppermute(value, axis, [(i, (i + steps) % count) for i in range(count)])  19.4 us
    pallas_call x4, Pallas kernels, products(): pl.pallas_call(functools.partial(products_kernel, sizes, step, part, [b[0...  18.8 us
    ppermute x12, waiting for transfers between devices, scattered_sum(): lax.ppermute(down_block, 'row', [(i, i - 1) for i in range(last - low, la...  16.8 us
    ppermute x6, waiting for transfers between devices, neighbours_gathered(): lax.ppermute(down, 'row', [(i, i - 1) for i in range(1, sizes.row - slot)])  16.1 us
    ppermute x6, starting transfers between devices, neighbours_gathered(): up = lax.ppermute(up, 'row', [(i, i + 1) for i in range(slot, last)])  14.3 us
    ppermute x12, starting transfers between devices, scattered_sum(): lax.ppermute(down_block, 'row', [(i, i - 1) for i in range(last - low, la...  13 us
    ppermute x17, starting transfers between devices, exchanged(): lax.ppermute(value, axis, [(i, (i + steps) % count) for i in range(count)])  10.7 us
  transfers between devices with their start and end apart: 57, of which 22 were waited for; matrix products, arithmetic and copies ran while one was open for 3% of the time, Pallas kernels for 8%

profile of v7, /device:TPU:0, one launch (start us, length us, event | category | flops | bytes accessed | tf_op | source)
XLA Modules:
  0.0 202.5 jit_solution(6626516167993025459)
XLA Ops:
  4.2 7.1 %collective-permute-done.7.refs_0_ = bf16[512,256]{1,0:T(8,128)(2,1)S(1)} collective-permute-done((bf16[512,256]{1,0:T(8,128)(2,1)S(1)}, bf16[512,256]{1,0:T(8,128)(2,1)S(1)}, u32[]{:S(2)}, u32[]{:S(2)}) %collective-permute-start.7) | collective-permute-done | bytes 262176 | tf_op jit(solution)/shard_map/ppermute | solution.py:18
  12.8 4.2 %collective-permute-start.8 = (bf16[256,512]{1,0:T(8,128)(2,1)S(1)}, bf16[256,512]{1,0:T(8,128)(2,1)S(1)}, u32[]{:S(2)}, u32[]{:S(2)}) collective-permute-start(bf16[256,512]{1,0:T(8,128)(2,1)S(1)} %panel.6.refs_0_), channel_id=1, source_target_pairs={{0,2},{2,4},{4,6},{1,3},{3,5},{5,7},{8,10},{10,12},{12,14},{9,11},... | collective-permute-start | bytes 786440 | tf_op jit(solution)/shard_map/ppermute | solution.py:215
  20.6 4.6 %collective-permute-start.1 = (bf16[256,512]{1,0:T(8,128)(2,1)S(1)}, bf16[256,512]{1,0:T(8,128)(2,1)S(1)}, u32[]{:S(2)}, u32[]{:S(2)}) collective-permute-start(bf16[256,512]{1,0:T(8,128)(2,1)S(1)} %panel.5.refs_0_), channel_id=1, source_target_pairs={{0,2},{2,4},{4,6},{1,3},{3,5},{5,7},{8,10},{10,12},{12,14},{9,11},... | collective-permute-start | bytes 786440 | tf_op jit(solution)/shard_map/ppermute | solution.py:215
  43.5 8.0 %collective-permute-done.5.refs_4_ = bf16[256,512]{1,0:T(8,128)(2,1)} collective-permute-done((bf16[256,512]{1,0:T(8,128)(2,1)S(1)}, bf16[256,512]{1,0:T(8,128)(2,1)}, u32[]{:S(2)}, u32[]{:S(2)}) %collective-permute-start.5) | collective-permute-done | bytes 262176 | tf_op jit(solution)/shard_map/ppermute | solution.py:216
  64.0 4.7 %collective-permute-start.32 = (bf16[256,512]{1,0:T(8,128)(2,1)}, bf16[256,512]{1,0:T(8,128)(2,1)S(1)}, u32[]{:S(2)}, u32[]{:S(2)}) collective-permute-start(bf16[256,512]{1,0:T(8,128)(2,1)} %panel.7.refs_0_), channel_id=1, source_target_pairs={{0,2},{2,4},{4,6},{1,3},{3,5},{5,7},{8,10},{10,12},{12,14},{9,11},... | collective-permute-start | bytes 786440 | tf_op jit(solution)/shard_map/ppermute | solution.py:224
  70.0 4.6 %collective-permute-start.14 = (bf16[256,512]{1,0:T(8,128)(2,1)S(1)}, bf16[256,512]{1,0:T(8,128)(2,1)S(1)}, u32[]{:S(2)}, u32[]{:S(2)}) collective-permute-start(bf16[256,512]{1,0:T(8,128)(2,1)S(1)} %panel.4.refs_0_), channel_id=1, source_target_pairs={{0,2},{2,4},{4,6},{1,3},{3,5},{5,7},{8,10},{10,12},{12,14},{9,11},... | collective-permute-start | bytes 786440 | tf_op jit(solution)/shard_map/ppermute | solution.py:224
  77.5 5.3 %products.5 = (f32[4,256,512]{2,1,0:T(8,128)S(1)}, bf16[256,512]{1,0:T(8,128)(2,1)S(1)}, bf16[256,512]{1,0:T(8,128)(2,1)S(1)}) custom-call(bf16[256,512]{1,0:T(8,128)(2,1)S(1)} %copy-done.10, bf16[256,512]{1,0:T(8,128)(2,1)S(1)} %copy-done.14, bf16[256,512]{1,0:T(8,128)(2,1)S(1)} %copy-done.18, bf16[256,512]{1,0:T(8,128)(2,1)} %collective-permute-done.9.refs_3_, ...), custom_call_target="tpu_custom_call" | custom-call | flops 1610612736 | bytes 9437184 | tf_op jit(solution)/shard_map/products/pallas_call | solution.py:152
  85.1 4.6 %collective-permute-start.33 = (bf16[256,512]{1,0:T(8,128)(2,1)S(1)}, bf16[256,512]{1,0:T(8,128)(2,1)S(1)}, u32[]{:S(2)}, u32[]{:S(2)}) collective-permute-start(bf16[256,512]{1,0:T(8,128)(2,1)S(1)} %broadcast_select_fusion.2), channel_id=1, source_target_pairs={{0,2},{2,4},{4,6},{1,3},{3,5},{5,7},{8,10},{10,12},{12,14},{9,11},... | collective-permute-start | bytes 786440 | tf_op jit(solution)/shard_map/ppermute | solution.py:249
  89.7 5.3 %products.4 = (f32[4,256,512]{2,1,0:T(8,128)S(1)}, bf16[256,512]{1,0:T(8,128)(2,1)S(1)}, bf16[256,512]{1,0:T(8,128)(2,1)S(1)}) custom-call(bf16[256,512]{1,0:T(8,128)(2,1)S(1)} %copy-done.8, bf16[256,512]{1,0:T(8,128)(2,1)S(1)} %copy-done.12, bf16[256,512]{1,0:T(8,128)(2,1)S(1)} %copy-done.16, bf16[256,512]{1,0:T(8,128)(2,1)} %collective-permute-done.2.refs_3_, ...), custom_call_target="tpu_custom_call" | custom-call | flops 1610612736 | bytes 9437184 | tf_op jit(solution)/shard_map/products/pallas_call | solution.py:152
  96.3 4.6 %collective-permute-start.23 = (bf16[256,512]{1,0:T(8,128)(2,1)S(1)}, bf16[256,512]{1,0:T(8,128)(2,1)S(1)}, u32[]{:S(2)}, u32[]{:S(2)}) collective-permute-start(bf16[256,512]{1,0:T(8,128)(2,1)S(1)} %broadcast_select_fusion.3), channel_id=1, source_target_pairs={{0,2},{2,4},{4,6},{1,3},{3,5},{5,7},{8,10},{10,12},{12,14},{9,11},... | collective-permute-start | bytes 786440 | tf_op jit(solution)/shard_map/ppermute | solution.py:249
  101.1 3.7 %collective-permute-start.34 = (bf16[256,512]{1,0:T(8,128)(2,1)S(1)}, bf16[256,512]{1,0:T(8,128)(2,1)S(1)}, u32[]{:S(2)}, u32[]{:S(2)}) collective-permute-start(bf16[256,512]{1,0:T(8,128)(2,1)S(1)} %get-tuple-element.43), channel_id=1, source_target_pairs={{0,2},{2,4},{4,6},{1,3},{3,5},{5,7},{8,10},{10,12},{12,14},{9,11},... | collective-permute-start | bytes 786440 | tf_op jit(solution)/shard_map/ppermute | solution.py:249
  107.1 4.4 %collective-permute-start.25 = (bf16[256,512]{1,0:T(8,128)(2,1)S(1)}, bf16[256,512]{1,0:T(8,128)(2,1)S(1)}, u32[]{:S(2)}, u32[]{:S(2)}) collective-permute-start(bf16[256,512]{1,0:T(8,128)(2,1)S(1)} %get-tuple-element.48), channel_id=1, source_target_pairs={{0,2},{2,4},{4,6},{1,3},{3,5},{5,7},{8,10},{10,12},{12,14},{9,11},... | collective-permute-start | bytes 786440 | tf_op jit(solution)/shard_map/ppermute | solution.py:249
  113.8 4.2 %collective-permute-start.35 = (bf16[256,512]{1,0:T(8,128)(2,1)S(1)}, bf16[256,512]{1,0:T(8,128)(2,1)S(1)}, u32[]{:S(2)}, u32[]{:S(2)}) collective-permute-start(bf16[256,512]{1,0:T(8,128)(2,1)S(1)} %get-tuple-element.41), channel_id=1, source_target_pairs={{0,2},{2,4},{4,6},{1,3},{3,5},{5,7},{8,10},{10,12},{12,14},{9,11},... | collective-permute-start | bytes 786440 | tf_op jit(solution)/shard_map/ppermute | solution.py:249
  130.0 4.1 %collective-permute-done.28 = bf16[256,512]{1,0:T(8,128)(2,1)S(1)} collective-permute-done((bf16[256,512]{1,0:T(8,128)(2,1)S(1)}, bf16[256,512]{1,0:T(8,128)(2,1)S(1)}, u32[]{:S(2)}, u32[]{:S(2)}) %collective-permute-start.28) | collective-permute-done | bytes 262176 | tf_op jit(solution)/shard_map/ppermute | solution.py:250
  137.3 3.4 %collective-permute-done.30.refs_9_.refs_6_ = bf16[256,512]{1,0:T(8,128)(2,1)S(1)} collective-permute-done((bf16[256,512]{1,0:T(8,128)(2,1)S(1)}, bf16[256,512]{1,0:T(8,128)(2,1)S(1)}, u32[]{:S(2)}, u32[]{:S(2)}) %collective-permute-start.30) | collective-permute-done | bytes 262176 | tf_op jit(solution)/shard_map/ppermute | solution.py:18
  142.2 4.6 %products.7 = (f32[4,256,512]{2,1,0:T(8,128)S(1)}, bf16[256,512]{1,0:T(8,128)(2,1)S(1)}, bf16[256,512]{1,0:T(8,128)(2,1)S(1)}) custom-call(bf16[256,512]{1,0:T(8,128)(2,1)} %panel.7.refs_0_, bf16[256,512]{1,0:T(8,128)(2,1)S(1)} %collective-permute-done.32.refs_1_, bf16[256,512]{1,0:T(8,128)(2,1)} %collective-permute-done.36.refs_2_, ...), custom_call_target="tpu_custom_call" | custom-call | flops 1610612736 | bytes 9437184 | tf_op jit(solution)/shard_map/products/pallas_call | solution.py:152
  149.6 3.7 %products.6 = (f32[4,256,512]{2,1,0:T(8,128)S(1)}, bf16[256,512]{1,0:T(8,128)(2,1)S(1)}, bf16[256,512]{1,0:T(8,128)(2,1)S(1)}) custom-call(bf16[256,512]{1,0:T(8,128)(2,1)S(1)} %panel.4.refs_0_, bf16[256,512]{1,0:T(8,128)(2,1)S(1)} %collective-permute-done.14.refs_1_, bf16[256,512]{1,0:T(8,128)(2,1)S(1)} %collective-permute-done.15.refs_2_, ...), custom_call_target="tpu_custom_call" | custom-call | flops 1610612736 | bytes 9437184 | tf_op jit(solution)/shard_map/products/pallas_call | solution.py:152
  155.7 4.4 %collective-permute-start.50 = (bf16[256,512]{1,0:T(8,128)(2,1)S(1)}, bf16[256,512]{1,0:T(8,128)(2,1)S(1)}, u32[]{:S(2)}, u32[]{:S(2)}) collective-permute-start(bf16[256,512]{1,0:T(8,128)(2,1)S(1)} %fusion.1), channel_id=1, source_target_pairs={{0,2},{2,4},{1,3},{3,5},{8,10},{10,12},{9,11},{11,13},{16,18},{18,... | collective-permute-start | bytes 786440 | tf_op jit(solution)/shard_map/ppermute | solution.py:249
  161.4 4.4 %collective-permute-start.44 = (bf16[256,512]{1,0:T(8,128)(2,1)S(1)}, bf16[256,512]{1,0:T(8,128)(2,1)S(1)}, u32[]{:S(2)}, u32[]{:S(2)}) collective-permute-start(bf16[256,512]{1,0:T(8,128)(2,1)S(1)} %fusion.7), channel_id=1, source_target_pairs={{0,2},{2,4},{1,3},{3,5},{8,10},{10,12},{9,11},{11,13},{16,18},{18,... | collective-permute-start | bytes 786440 | tf_op jit(solution)/shard_map/ppermute | solution.py:249
  167.8 4.4 %collective-permute-done.44 = bf16[256,512]{1,0:T(8,128)(2,1)S(1)} collective-permute-done((bf16[256,512]{1,0:T(8,128)(2,1)S(1)}, bf16[256,512]{1,0:T(8,128)(2,1)S(1)}, u32[]{:S(2)}, u32[]{:S(2)}) %collective-permute-start.44) | collective-permute-done | bytes 262176 | tf_op jit(solution)/shard_map/ppermute | solution.py:249
  173.0 5.0 %collective-permute-start.51 = (bf16[256,512]{1,0:T(8,128)(2,1)S(1)}, bf16[256,512]{1,0:T(8,128)(2,1)S(1)}, u32[]{:S(2)}, u32[]{:S(2)}) collective-permute-start(bf16[256,512]{1,0:T(8,128)(2,1)S(1)} %get-tuple-element.37), channel_id=1, source_target_pairs={{0,2},{2,4},{4,6},{1,3},{3,5},{5,7},{8,10},{10,12},{12,14},{9,11},... | collective-permute-start | bytes 786440 | tf_op jit(solution)/shard_map/ppermute | solution.py:249
  179.4 5.2 %collective-permute-start.45 = (bf16[256,512]{1,0:T(8,128)(2,1)S(1)}, bf16[256,512]{1,0:T(8,128)(2,1)S(1)}, u32[]{:S(2)}, u32[]{:S(2)}) collective-permute-start(bf16[256,512]{1,0:T(8,128)(2,1)S(1)} %get-tuple-element.39), channel_id=1, source_target_pairs={{0,2},{2,4},{4,6},{1,3},{3,5},{5,7},{8,10},{10,12},{12,14},{9,11},... | collective-permute-start | bytes 786440 | tf_op jit(solution)/shard_map/ppermute | solution.py:249
  189.4 4.4 %collective-permute-done.48 = bf16[256,512]{1,0:T(8,128)(2,1)S(1)} collective-permute-done((bf16[256,512]{1,0:T(8,128)(2,1)S(1)}, bf16[256,512]{1,0:T(8,128)(2,1)S(1)}, u32[]{:S(2)}, u32[]{:S(2)}) %collective-permute-start.48) | collective-permute-done | bytes 262176 | tf_op jit(solution)/shard_map/ppermute | solution.py:250
  195.4 5.3 %collective-permute-done.55.refs_2_ = bf16[256,512]{1,0:T(8,128)(2,1)S(1)} collective-permute-done((bf16[256,512]{1,0:T(8,128)(2,1)S(1)}, bf16[256,512]{1,0:T(8,128)(2,1)S(1)}, u32[]{:S(2)}, u32[]{:S(2)}) %collective-permute-start.55) | collective-permute-done | bytes 262176 | tf_op jit(solution)/shard_map/ppermute | solution.py:18
  (165 shorter events, 87.7 us)
Async XLA Ops:
  4.2 12.9 %collective-permute-start = (bf16[512,256]{1,0:T(8,128)(2,1)S(1)}, bf16[512,256]{1,0:T(8,128)(2,1)S(1)}, u32[]{:S(2)}, u32[]{:S(2)}) collective-permute-start(bf16[512,256]{1,0:T(8,128)(2,1)S(1)} %get-tuple-element.50), channel_id=1, source_target_pairs={{0,8},{8,0},{1,9},{9,1},{2,10},{10,2},{3,11},{11,3},{4,12},{12,4},... | collective-permute-start | bytes 786440 | tf_op jit(solution)/shard_map/ppermute | solution.py:18
  12.8 12.4 %collective-permute-start.8 = (bf16[256,512]{1,0:T(8,128)(2,1)S(1)}, bf16[256,512]{1,0:T(8,128)(2,1)S(1)}, u32[]{:S(2)}, u32[]{:S(2)}) collective-permute-start(bf16[256,512]{1,0:T(8,128)(2,1)S(1)} %panel.6.refs_0_), channel_id=1, source_target_pairs={{0,2},{2,4},{4,6},{1,3},{3,5},{5,7},{8,10},{10,12},{12,14},{9,11},... | collective-permute-start | bytes 786440 | tf_op jit(solution)/shard_map/ppermute | solution.py:215
  17.1 17.9 %collective-permute-start.18 = (bf16[512,512]{1,0:T(8,128)(2,1)S(1)}, bf16[512,512]{1,0:T(8,128)(2,1)S(1)}, u32[]{:S(2)}, u32[]{:S(2)}) collective-permute-start(bf16[512,512]{1,0:T(8,128)(2,1)S(1)} %dynamic-slice_bitcast_fusion), channel_id=1, source_target_pairs={{0,8},{8,0},{1,9},{9,1},{2,10},{10,2},{3,11},{11,3},{4,12},{12,4},... | collective-permute-start | bytes 1572872 | tf_op jit(solution)/shard_map/ppermute | solution.py:18
  18.6 41.4 %collective-permute-start.21 = (bf16[512,1024]{1,0:T(8,128)(2,1)S(1)}, bf16[512,1024]{1,0:T(8,128)(2,1)}, u32[]{:S(2)}, u32[]{:S(2)}) collective-permute-start(bf16[512,1024]{1,0:T(8,128)(2,1)S(1)} %bitcast.113), channel_id=1, source_target_pairs={{0,8},{8,0},{1,9},{9,1},{2,10},{10,2},{3,11},{11,3},{4,12},{12,4},... | collective-permute-start | bytes 3145736 | tf_op jit(solution)/shard_map/ppermute | solution.py:18
  35.0 16.5 %collective-permute-start.5 = (bf16[256,512]{1,0:T(8,128)(2,1)S(1)}, bf16[256,512]{1,0:T(8,128)(2,1)}, u32[]{:S(2)}, u32[]{:S(2)}) collective-permute-start(bf16[256,512]{1,0:T(8,128)(2,1)S(1)} %collective-permute-done.4.refs_2_), channel_id=1, source_target_pairs={{2,0},{4,2},{3,1},{5,3},{10,8},{12,10},{11,9},{13,11},{18,16},{20,... | collective-permute-start | bytes 786440 | tf_op jit(solution)/shard_map/ppermute | solution.py:216
  37.0 19.6 %collective-permute-start.10 = (bf16[256,512]{1,0:T(8,128)(2,1)}, bf16[256,512]{1,0:T(8,128)(2,1)}, u32[]{:S(2)}, u32[]{:S(2)}) collective-permute-start(bf16[256,512]{1,0:T(8,128)(2,1)} %collective-permute-done.9.refs_3_), channel_id=1, source_target_pairs={{4,6},{5,7},{12,14},{13,15},{20,22},{21,23},{28,30},{29,31}} | collective-permute-start | bytes 786440 | tf_op jit(solution)/shard_map/ppermute | solution.py:215
  40.8 15.9 %collective-permute-start.13 = (bf16[256,512]{1,0:T(8,128)(2,1)}, bf16[256,512]{1,0:T(8,128)(2,1)}, u32[]{:S(2)}, u32[]{:S(2)}) collective-permute-start(bf16[256,512]{1,0:T(8,128)(2,1)} %collective-permute-done.12.refs_4_), channel_id=1, source_target_pairs={{2,0},{3,1},{10,8},{11,9},{18,16},{19,17},{26,24},{27,25}} | collective-permute-start | bytes 786440 | tf_op jit(solution)/shard_map/ppermute | solution.py:216
  42.1 15.1 %collective-permute-start.3 = (bf16[256,512]{1,0:T(8,128)(2,1)}, bf16[256,512]{1,0:T(8,128)(2,1)}, u32[]{:S(2)}, u32[]{:S(2)}) collective-permute-start(bf16[256,512]{1,0:T(8,128)(2,1)} %collective-permute-done.2.refs_3_), channel_id=1, source_target_pairs={{4,6},{5,7},{12,14},{13,15},{20,22},{21,23},{28,30},{29,31}} | collective-permute-start | bytes 786440 | tf_op jit(solution)/shard_map/ppermute | solution.py:215
  57.2 11.5 %collective-permute-start.16 = (bf16[1024,512]{1,0:T(8,128)(2,1)}, bf16[1024,512]{1,0:T(8,128)(2,1)}, u32[]{:S(2)}, u32[]{:S(2)}) collective-permute-start(bf16[1024,512]{1,0:T(8,128)(2,1)} %bitcast.103.refs_7_), channel_id=1, source_target_pairs={{0,1},{1,0},{2,3},{3,2},{4,5},{5,4},{6,7},{7,6},{8,9},{9,8},{10,11... | collective-permute-start | bytes 3145736 | tf_op jit(solution)/shard_map/ppermute | solution.py:18
  60.1 14.5 %collective-permute-start.22 = (bf16[512,1024]{1,0:T(8,128)(2,1)}, bf16[512,1024]{1,0:T(8,128)(2,1)}, u32[]{:S(2)}, u32[]{:S(2)}) collective-permute-start(bf16[512,1024]{1,0:T(8,128)(2,1)} %collective-permute-done.21.refs_15_.refs_21_), channel_id=1, source_target_pairs={{0,1},{1,0},{2,3},{3,2},{4,5},{5,4},{6,7},{7,6},{8,9},{9,8},{10,11... | collective-permute-start | bytes 3145736 | tf_op jit(solution)/shard_map/ppermute | solution.py:18
  62.5 20.3 %collective-permute-start.36 = (bf16[256,512]{1,0:T(8,128)(2,1)}, bf16[256,512]{1,0:T(8,128)(2,1)}, u32[]{:S(2)}, u32[]{:S(2)}) collective-permute-start(bf16[256,512]{1,0:T(8,128)(2,1)} %panel.7.refs_0_), channel_id=1, source_target_pairs={{2,0},{4,2},{6,4},{3,1},{5,3},{7,5},{10,8},{12,10},{14,12},{11,9},... | collective-permute-start | bytes 786440 | tf_op jit(solution)/shard_map/ppermute | solution.py:225
  64.0 21.0 %collective-permute-start.32 = (bf16[256,512]{1,0:T(8,128)(2,1)}, bf16[256,512]{1,0:T(8,128)(2,1)S(1)}, u32[]{:S(2)}, u32[]{:S(2)}) collective-permute-start(bf16[256,512]{1,0:T(8,128)(2,1)} %panel.7.refs_0_), channel_id=1, source_target_pairs={{0,2},{2,4},{4,6},{1,3},{3,5},{5,7},{8,10},{10,12},{12,14},{9,11},... | collective-permute-start | bytes 786440 | tf_op jit(solution)/shard_map/ppermute | solution.py:224
  68.7 26.2 %collective-permute-start.15 = (bf16[256,512]{1,0:T(8,128)(2,1)S(1)}, bf16[256,512]{1,0:T(8,128)(2,1)S(1)}, u32[]{:S(2)}, u32[]{:S(2)}) collective-permute-start(bf16[256,512]{1,0:T(8,128)(2,1)S(1)} %panel.4.refs_0_), channel_id=1, source_target_pairs={{2,0},{4,2},{6,4},{3,1},{5,3},{7,5},{10,8},{12,10},{14,12},{11,9},... | collective-permute-start | bytes 786440 | tf_op jit(solution)/shard_map/ppermute | solution.py:225
  70.0 26.3 %collective-permute-start.14 = (bf16[256,512]{1,0:T(8,128)(2,1)S(1)}, bf16[256,512]{1,0:T(8,128)(2,1)S(1)}, u32[]{:S(2)}, u32[]{:S(2)}) collective-permute-start(bf16[256,512]{1,0:T(8,128)(2,1)S(1)} %panel.4.refs_0_), channel_id=1, source_target_pairs={{0,2},{2,4},{4,6},{1,3},{3,5},{5,7},{8,10},{10,12},{12,14},{9,11},... | collective-permute-start | bytes 786440 | tf_op jit(solution)/shard_map/ppermute | solution.py:224
  83.7 17.2 %collective-permute-start.37 = (bf16[256,512]{1,0:T(8,128)(2,1)S(1)}, bf16[256,512]{1,0:T(8,128)(2,1)S(1)}, u32[]{:S(2)}, u32[]{:S(2)}) collective-permute-start(bf16[256,512]{1,0:T(8,128)(2,1)S(1)} %broadcast_select_fusion), channel_id=1, source_target_pairs={{2,0},{4,2},{6,4},{3,1},{5,3},{7,5},{10,8},{12,10},{14,12},{11,9},... | collective-permute-start | bytes 786440 | tf_op jit(solution)/shard_map/ppermute | solution.py:250
  85.1 15.8 %collective-permute-start.33 = (bf16[256,512]{1,0:T(8,128)(2,1)S(1)}, bf16[256,512]{1,0:T(8,128)(2,1)S(1)}, u32[]{:S(2)}, u32[]{:S(2)}) collective-permute-start(bf16[256,512]{1,0:T(8,128)(2,1)S(1)} %broadcast_select_fusion.2), channel_id=1, source_target_pairs={{0,2},{2,4},{4,6},{1,3},{3,5},{5,7},{8,10},{10,12},{12,14},{9,11},... | collective-permute-start | bytes 786440 | tf_op jit(solution)/shard_map/ppermute | solution.py:249
  101.1 11.8 %collective-permute-start.34 = (bf16[256,512]{1,0:T(8,128)(2,1)S(1)}, bf16[256,512]{1,0:T(8,128)(2,1)S(1)}, u32[]{:S(2)}, u32[]{:S(2)}) collective-permute-start(bf16[256,512]{1,0:T(8,128)(2,1)S(1)} %get-tuple-element.43), channel_id=1, source_target_pairs={{0,2},{2,4},{4,6},{1,3},{3,5},{5,7},{8,10},{10,12},{12,14},{9,11},... | collective-permute-start | bytes 786440 | tf_op jit(solution)/shard_map/ppermute | solution.py:249
  107.1 12.1 %collective-permute-start.25 = (bf16[256,512]{1,0:T(8,128)(2,1)S(1)}, bf16[256,512]{1,0:T(8,128)(2,1)S(1)}, u32[]{:S(2)}, u32[]{:S(2)}) collective-permute-start(bf16[256,512]{1,0:T(8,128)(2,1)S(1)} %get-tuple-element.48), channel_id=1, source_target_pairs={{0,2},{2,4},{4,6},{1,3},{3,5},{5,7},{8,10},{10,12},{12,14},{9,11},... | collective-permute-start | bytes 786440 | tf_op jit(solution)/shard_map/ppermute | solution.py:249
  111.5 11.1 %collective-permute-start.26 = (bf16[256,512]{1,0:T(8,128)(2,1)S(1)}, bf16[256,512]{1,0:T(8,128)(2,1)S(1)}, u32[]{:S(2)}, u32[]{:S(2)}) collective-permute-start(bf16[256,512]{1,0:T(8,128)(2,1)S(1)} %get-tuple-element.47), channel_id=1, source_target_pairs={{2,0},{4,2},{6,4},{3,1},{5,3},{7,5},{10,8},{12,10},{14,12},{11,9},... | collective-permute-start | bytes 786440 | tf_op jit(solution)/shard_map/ppermute | solution.py:250
  113.8 13.4 %collective-permute-start.35 = (bf16[256,512]{1,0:T(8,128)(2,1)S(1)}, bf16[256,512]{1,0:T(8,128)(2,1)S(1)}, u32[]{:S(2)}, u32[]{:S(2)}) collective-permute-start(bf16[256,512]{1,0:T(8,128)(2,1)S(1)} %get-tuple-element.41), channel_id=1, source_target_pairs={{0,2},{2,4},{4,6},{1,3},{3,5},{5,7},{8,10},{10,12},{12,14},{9,11},... | collective-permute-start | bytes 786440 | tf_op jit(solution)/shard_map/ppermute | solution.py:249
  154.6 11.2 %collective-permute-start.52 = (bf16[256,512]{1,0:T(8,128)(2,1)S(1)}, bf16[256,512]{1,0:T(8,128)(2,1)S(1)}, u32[]{:S(2)}, u32[]{:S(2)}) collective-permute-start(bf16[256,512]{1,0:T(8,128)(2,1)S(1)} %get-tuple-element.36), channel_id=1, source_target_pairs={{6,4},{7,5},{14,12},{15,13},{22,20},{23,21},{30,28},{31,29}} | collective-permute-start | bytes 786440 | tf_op jit(solution)/shard_map/ppermute | solution.py:250
  155.7 11.2 %collective-permute-start.50 = (bf16[256,512]{1,0:T(8,128)(2,1)S(1)}, bf16[256,512]{1,0:T(8,128)(2,1)S(1)}, u32[]{:S(2)}, u32[]{:S(2)}) collective-permute-start(bf16[256,512]{1,0:T(8,128)(2,1)S(1)} %fusion.1), channel_id=1, source_target_pairs={{0,2},{2,4},{1,3},{3,5},{8,10},{10,12},{9,11},{11,13},{16,18},{18,... | collective-permute-start | bytes 786440 | tf_op jit(solution)/shard_map/ppermute | solution.py:249
  172.3 12.3 %collective-permute-start.47 = (bf16[256,512]{1,0:T(8,128)(2,1)S(1)}, bf16[256,512]{1,0:T(8,128)(2,1)S(1)}, u32[]{:S(2)}, u32[]{:S(2)}) collective-permute-start(bf16[256,512]{1,0:T(8,128)(2,1)S(1)} %get-tuple-element.40), channel_id=1, source_target_pairs={{4,2},{6,4},{5,3},{7,5},{12,10},{14,12},{13,11},{15,13},{20,18},{2... | collective-permute-start | bytes 786440 | tf_op jit(solution)/shard_map/ppermute | solution.py:250
  173.0 13.0 %collective-permute-start.51 = (bf16[256,512]{1,0:T(8,128)(2,1)S(1)}, bf16[256,512]{1,0:T(8,128)(2,1)S(1)}, u32[]{:S(2)}, u32[]{:S(2)}) collective-permute-start(bf16[256,512]{1,0:T(8,128)(2,1)S(1)} %get-tuple-element.37), channel_id=1, source_target_pairs={{0,2},{2,4},{4,6},{1,3},{3,5},{5,7},{8,10},{10,12},{12,14},{9,11},... | collective-permute-start | bytes 786440 | tf_op jit(solution)/shard_map/ppermute | solution.py:249
  (54 other events, 526.9 us)

commit v8 on v7

--- a/solution.py
+++ b/solution.py
@@ -316,20 +316,19 @@
 
     results = {}
     for step in reversed(range(sec_size)):
-        trailing = []
-        if step:
-            earlier = [array for k in range(CHUNKS) for _, array in factor_blocks[step, k][-2:]]
-            for part in range(CHUNKS):
+        next_pieces = []
+        for part in range(CHUNKS):
+            if step:
+                earlier = [array for k in range(CHUNKS) for _, array in factor_blocks[step, k][-2:]]
+                if part:
+                    earlier += partials[1:]
                 sent = [[chunks[part]] for chunks in arrived_chunks[1:]]
                 block = after(transposed_panel(sizes, step - 1, factor, sent, part), *earlier)
-                trailing.append((block, first_slot(sizes, block)))
-        next_pieces = []
-        for part in range(CHUNKS):
+                up, down = first_slot(sizes, block)
             partials = products(
                 sizes, step, part, factor_blocks[step, part], state_pieces, factor_tiles, inverse_tiles
             )
             if step:
-                block, (up, down) = trailing[part]
                 total, found = scattered_sum(sizes, partials, (up, down))
                 edge = sizes.row - 1
                 factor_blocks[step - 1, part] = [

time: 204 us -> 201 us (0.985)
    ppermute x12, starting transfers between devices: 47.5 us -> 45.4 us  [scattered_sum(): up = lax.ppermute(up_block, 'row', [(i, i + 1) for i in range(low + 1)])]
    unnamed x43 -> x41, local copies, waits for them, and re-layouts: 9.84 us -> 8.5 us
  transfers between devices with their start and end apart: 57 -> 57, of which waited for: 22 -> 20; matrix products, arithmetic and copies ran while one was open for 3% -> 4% of each run, Pallas kernels for 8% -> 8%
where the time goes in v8:
time: 201 us; the launch traced here: 200 us
  starting transfers between devices  104 us (52%)
  waiting for transfers between devices  58.7 us (29%)
  Pallas kernels  21.9 us (11%)
  local copies, waits for them, and re-layouts  11 us (5%)
  other arithmetic  3.77 us (2%)
    ppermute x12, starting transfers between devices, scattered_sum(): up = lax.ppermute(up_block, 'row', [(i, i + 1) for i in range(low + 1)])  45.4 us
    pallas_call x4, Pallas kernels, products(): pl.pallas_call(functools.partial(products_kernel, sizes, step, part, [b[0...  18.8 us
    ppermute x17, waiting for transfers between devices, exchanged(): lax.ppermute(value, axis, [(i, (i + steps) % count) for i in range(count)])  18.2 us
    ppermute x6, waiting for transfers between devices, neighbours_gathered(): lax.ppermute(down, 'row', [(i, i - 1) for i in range(1, sizes.row - slot)])  16.1 us
    ppermute x12, waiting for transfers between devices, scattered_sum(): lax.ppermute(down_block, 'row', [(i, i - 1) for i in range(last - low, la...  15.5 us
    ppermute x6, starting transfers between devices, neighbours_gathered(): up = lax.ppermute(up, 'row', [(i, i + 1) for i in range(slot, last)])  14.1 us
    ppermute x12, starting transfers between devices, scattered_sum(): lax.ppermute(down_block, 'row', [(i, i - 1) for i in range(last - low, la...  13 us
    ppermute x17, starting transfers between devices, exchanged(): lax.ppermute(value, axis, [(i, (i + steps) % count) for i in range(count)])  11.5 us
  transfers between devices with their start and end apart: 57, of which 20 were waited for; matrix products, arithmetic and copies ran while one was open for 4% of the time, Pallas kernels for 8%

profile of v8, /device:TPU:0, one launch (start us, length us, event | category | flops | bytes accessed | tf_op | source)
XLA Modules:
  0.0 199.8 jit_solution(14794336215979760223)
XLA Ops:
  5.4 6.0 %collective-permute-done.refs_0_ = bf16[512,256]{1,0:T(8,128)(2,1)S(1)} collective-permute-done((bf16[512,256]{1,0:T(8,128)(2,1)S(1)}, bf16[512,256]{1,0:T(8,128)(2,1)S(1)}, u32[]{:S(2)}, u32[]{:S(2)}) %collective-permute-start) | collective-permute-done | bytes 262176 | tf_op jit(solution)/shard_map/ppermute | solution.py:18
  11.5 4.1 %collective-permute-start.1 = (bf16[256,512]{1,0:T(8,128)(2,1)S(1)}, bf16[256,512]{1,0:T(8,128)(2,1)S(1)}, u32[]{:S(2)}, u32[]{:S(2)}) collective-permute-start(bf16[256,512]{1,0:T(8,128)(2,1)S(1)} %panel.5.refs_0_), channel_id=1, source_target_pairs={{0,2},{2,4},{4,6},{1,3},{3,5},{5,7},{8,10},{10,12},{12,14},{9,11},... | collective-permute-start | bytes 786440 | tf_op jit(solution)/shard_map/ppermute | solution.py:215
  19.7 4.6 %collective-permute-start.8 = (bf16[256,512]{1,0:T(8,128)(2,1)S(1)}, bf16[256,512]{1,0:T(8,128)(2,1)S(1)}, u32[]{:S(2)}, u32[]{:S(2)}) collective-permute-start(bf16[256,512]{1,0:T(8,128)(2,1)S(1)} %panel.6.refs_0_), channel_id=1, source_target_pairs={{0,2},{2,4},{4,6},{1,3},{3,5},{5,7},{8,10},{10,12},{12,14},{9,11},... | collective-permute-start | bytes 786440 | tf_op jit(solution)/shard_map/ppermute | solution.py:215
  42.4 8.1 %collective-permute-done.12.refs_4_ = bf16[256,512]{1,0:T(8,128)(2,1)} collective-permute-done((bf16[256,512]{1,0:T(8,128)(2,1)S(1)}, bf16[256,512]{1,0:T(8,128)(2,1)}, u32[]{:S(2)}, u32[]{:S(2)}) %collective-permute-start.12) | collective-permute-done | bytes 262176 | tf_op jit(solution)/shard_map/ppermute | solution.py:216
  63.0 4.7 %collective-permute-start.14 = (bf16[256,512]{1,0:T(8,128)(2,1)}, bf16[256,512]{1,0:T(8,128)(2,1)S(1)}, u32[]{:S(2)}, u32[]{:S(2)}) collective-permute-start(bf16[256,512]{1,0:T(8,128)(2,1)} %panel.4.refs_0_), channel_id=1, source_target_pairs={{0,2},{2,4},{4,6},{1,3},{3,5},{5,7},{8,10},{10,12},{12,14},{9,11},... | collective-permute-start | bytes 786440 | tf_op jit(solution)/shard_map/ppermute | solution.py:224
  70.6 5.2 %products.4 = (f32[4,256,512]{2,1,0:T(8,128)S(1)}, bf16[256,512]{1,0:T(8,128)(2,1)S(1)}, bf16[256,512]{1,0:T(8,128)(2,1)S(1)}) custom-call(bf16[256,512]{1,0:T(8,128)(2,1)S(1)} %copy-done.9, bf16[256,512]{1,0:T(8,128)(2,1)S(1)} %copy-done.15, bf16[256,512]{1,0:T(8,128)(2,1)S(1)} %copy-done.17, bf16[256,512]{1,0:T(8,128)(2,1)} %collective-permute-done.2.refs_3_, ...), custom_call_target="tpu_custom_call" | custom-call | flops 1610612736 | bytes 9437184 | tf_op jit(solution)/shard_map/products/pallas_call | solution.py:152
  77.2 4.6 %collective-permute-start.32 = (bf16[256,512]{1,0:T(8,128)(2,1)S(1)}, bf16[256,512]{1,0:T(8,128)(2,1)S(1)}, u32[]{:S(2)}, u32[]{:S(2)}) collective-permute-start(bf16[256,512]{1,0:T(8,128)(2,1)S(1)} %panel.7.refs_0_), channel_id=1, source_target_pairs={{0,2},{2,4},{4,6},{1,3},{3,5},{5,7},{8,10},{10,12},{12,14},{9,11},... | collective-permute-start | bytes 786440 | tf_op jit(solution)/shard_map/ppermute | solution.py:224
  84.1 4.6 %collective-permute-start.23 = (bf16[256,512]{1,0:T(8,128)(2,1)S(1)}, bf16[256,512]{1,0:T(8,128)(2,1)S(1)}, u32[]{:S(2)}, u32[]{:S(2)}) collective-permute-start(bf16[256,512]{1,0:T(8,128)(2,1)S(1)} %broadcast_select_fusion.3), channel_id=1, source_target_pairs={{0,2},{2,4},{4,6},{1,3},{3,5},{5,7},{8,10},{10,12},{12,14},{9,11},... | collective-permute-start | bytes 786440 | tf_op jit(solution)/shard_map/ppermute | solution.py:249
  88.7 5.3 %products.5 = (f32[4,256,512]{2,1,0:T(8,128)S(1)}, bf16[256,512]{1,0:T(8,128)(2,1)S(1)}, bf16[256,512]{1,0:T(8,128)(2,1)S(1)}) custom-call(bf16[256,512]{1,0:T(8,128)(2,1)S(1)} %copy-done.7, bf16[256,512]{1,0:T(8,128)(2,1)S(1)} %copy-done.11, bf16[256,512]{1,0:T(8,128)(2,1)S(1)} %copy-done.13, bf16[256,512]{1,0:T(8,128)(2,1)} %collective-permute-done.9.refs_3_, ...), custom_call_target="tpu_custom_call" | custom-call | flops 1610612736 | bytes 9437184 | tf_op jit(solution)/shard_map/products/pallas_call | solution.py:152
  95.4 4.6 %collective-permute-start.33 = (bf16[256,512]{1,0:T(8,128)(2,1)S(1)}, bf16[256,512]{1,0:T(8,128)(2,1)S(1)}, u32[]{:S(2)}, u32[]{:S(2)}) collective-permute-start(bf16[256,512]{1,0:T(8,128)(2,1)S(1)} %broadcast_select_fusion.2), channel_id=1, source_target_pairs={{0,2},{2,4},{4,6},{1,3},{3,5},{5,7},{8,10},{10,12},{12,14},{9,11},... | collective-permute-start | bytes 786440 | tf_op jit(solution)/shard_map/ppermute | solution.py:249
  106.6 4.4 %collective-permute-start.34 = (bf16[256,512]{1,0:T(8,128)(2,1)S(1)}, bf16[256,512]{1,0:T(8,128)(2,1)S(1)}, u32[]{:S(2)}, u32[]{:S(2)}) collective-permute-start(bf16[256,512]{1,0:T(8,128)(2,1)S(1)} %get-tuple-element.43), channel_id=1, source_target_pairs={{0,2},{2,4},{4,6},{1,3},{3,5},{5,7},{8,10},{10,12},{12,14},{9,11},... | collective-permute-start | bytes 786440 | tf_op jit(solution)/shard_map/ppermute | solution.py:249
  112.5 4.6 %collective-permute-start.27 = (bf16[256,512]{1,0:T(8,128)(2,1)S(1)}, bf16[256,512]{1,0:T(8,128)(2,1)S(1)}, u32[]{:S(2)}, u32[]{:S(2)}) collective-permute-start(bf16[256,512]{1,0:T(8,128)(2,1)S(1)} %get-tuple-element.45), channel_id=1, source_target_pairs={{0,2},{2,4},{4,6},{1,3},{3,5},{5,7},{8,10},{10,12},{12,14},{9,11},... | collective-permute-start | bytes 786440 | tf_op jit(solution)/shard_map/ppermute | solution.py:249
  118.3 3.6 %collective-permute-done.38.refs_6_ = bf16[256,512]{1,0:T(8,128)(2,1)S(1)} collective-permute-done((bf16[256,512]{1,0:T(8,128)(2,1)S(1)}, bf16[256,512]{1,0:T(8,128)(2,1)S(1)}, u32[]{:S(2)}, u32[]{:S(2)}) %collective-permute-start.38) | collective-permute-done | bytes 262176 | tf_op jit(solution)/shard_map/ppermute | solution.py:250
  128.5 4.1 %collective-permute-done.39 = bf16[256,512]{1,0:T(8,128)(2,1)S(1)} collective-permute-done((bf16[256,512]{1,0:T(8,128)(2,1)S(1)}, bf16[256,512]{1,0:T(8,128)(2,1)S(1)}, u32[]{:S(2)}, u32[]{:S(2)}) %collective-permute-start.39) | collective-permute-done | bytes 262176 | tf_op jit(solution)/shard_map/ppermute | solution.py:250
  135.4 3.7 %collective-permute-done.41.refs_13_.refs_7_ = bf16[256,512]{1,0:T(8,128)(2,1)S(1)} collective-permute-done((bf16[256,512]{1,0:T(8,128)(2,1)S(1)}, bf16[256,512]{1,0:T(8,128)(2,1)S(1)}, u32[]{:S(2)}, u32[]{:S(2)}) %collective-permute-start.41) | collective-permute-done | bytes 262176 | tf_op jit(solution)/shard_map/ppermute | solution.py:18
  140.7 3.6 %products.7 = (f32[4,256,512]{2,1,0:T(8,128)S(1)}, bf16[256,512]{1,0:T(8,128)(2,1)S(1)}, bf16[256,512]{1,0:T(8,128)(2,1)S(1)}) custom-call(bf16[256,512]{1,0:T(8,128)(2,1)S(1)} %panel.7.refs_0_, bf16[256,512]{1,0:T(8,128)(2,1)S(1)} %collective-permute-done.32.refs_1_, bf16[256,512]{1,0:T(8,128)(2,1)S(1)} %collective-permute-done.36.refs_2_, ...), custom_call_target="tpu_custom_call" | custom-call | flops 1610612736 | bytes 9437184 | tf_op jit(solution)/shard_map/products/pallas_call | solution.py:152
  147.0 4.7 %products.6 = (f32[4,256,512]{2,1,0:T(8,128)S(1)}, bf16[256,512]{1,0:T(8,128)(2,1)S(1)}, bf16[256,512]{1,0:T(8,128)(2,1)S(1)}) custom-call(bf16[256,512]{1,0:T(8,128)(2,1)} %panel.4.refs_0_, bf16[256,512]{1,0:T(8,128)(2,1)S(1)} %collective-permute-done.14.refs_1_, bf16[256,512]{1,0:T(8,128)(2,1)} %collective-permute-done.15.refs_2_, ...), custom_call_target="tpu_custom_call" | custom-call | flops 1610612736 | bytes 9437184 | tf_op jit(solution)/shard_map/products/pallas_call | solution.py:152
  153.8 3.4 %collective-permute-start.50 = (bf16[256,512]{1,0:T(8,128)(2,1)S(1)}, bf16[256,512]{1,0:T(8,128)(2,1)S(1)}, u32[]{:S(2)}, u32[]{:S(2)}) collective-permute-start(bf16[256,512]{1,0:T(8,128)(2,1)S(1)} %fusion.1), channel_id=1, source_target_pairs={{0,2},{2,4},{1,3},{3,5},{8,10},{10,12},{9,11},{11,13},{16,18},{18,... | collective-permute-start | bytes 786440 | tf_op jit(solution)/shard_map/ppermute | solution.py:249
  159.7 4.4 %collective-permute-start.44 = (bf16[256,512]{1,0:T(8,128)(2,1)S(1)}, bf16[256,512]{1,0:T(8,128)(2,1)S(1)}, u32[]{:S(2)}, u32[]{:S(2)}) collective-permute-start(bf16[256,512]{1,0:T(8,128)(2,1)S(1)} %fusion.7), channel_id=1, source_target_pairs={{0,2},{2,4},{1,3},{3,5},{8,10},{10,12},{9,11},{11,13},{16,18},{18,... | collective-permute-start | bytes 786440 | tf_op jit(solution)/shard_map/ppermute | solution.py:249
  166.1 4.0 %collective-permute-done.44 = bf16[256,512]{1,0:T(8,128)(2,1)S(1)} collective-permute-done((bf16[256,512]{1,0:T(8,128)(2,1)S(1)}, bf16[256,512]{1,0:T(8,128)(2,1)S(1)}, u32[]{:S(2)}, u32[]{:S(2)}) %collective-permute-start.44) | collective-permute-done | bytes 262176 | tf_op jit(solution)/shard_map/ppermute | solution.py:249
  170.9 5.0 %collective-permute-start.51 = (bf16[256,512]{1,0:T(8,128)(2,1)S(1)}, bf16[256,512]{1,0:T(8,128)(2,1)S(1)}, u32[]{:S(2)}, u32[]{:S(2)}) collective-permute-start(bf16[256,512]{1,0:T(8,128)(2,1)S(1)} %get-tuple-element.37), channel_id=1, source_target_pairs={{0,2},{2,4},{4,6},{1,3},{3,5},{5,7},{8,10},{10,12},{12,14},{9,11},... | collective-permute-start | bytes 786440 | tf_op jit(solution)/shard_map/ppermute | solution.py:249
  177.3 5.2 %collective-permute-start.45 = (bf16[256,512]{1,0:T(8,128)(2,1)S(1)}, bf16[256,512]{1,0:T(8,128)(2,1)S(1)}, u32[]{:S(2)}, u32[]{:S(2)}) collective-permute-start(bf16[256,512]{1,0:T(8,128)(2,1)S(1)} %get-tuple-element.39), channel_id=1, source_target_pairs={{0,2},{2,4},{4,6},{1,3},{3,5},{5,7},{8,10},{10,12},{12,14},{9,11},... | collective-permute-start | bytes 786440 | tf_op jit(solution)/shard_map/ppermute | solution.py:249
  187.4 4.0 %collective-permute-done.48 = bf16[256,512]{1,0:T(8,128)(2,1)S(1)} collective-permute-done((bf16[256,512]{1,0:T(8,128)(2,1)S(1)}, bf16[256,512]{1,0:T(8,128)(2,1)S(1)}, u32[]{:S(2)}, u32[]{:S(2)}) %collective-permute-start.48) | collective-permute-done | bytes 262176 | tf_op jit(solution)/shard_map/ppermute | solution.py:250
  192.9 5.2 %collective-permute-done.55.refs_2_ = bf16[256,512]{1,0:T(8,128)(2,1)S(1)} collective-permute-done((bf16[256,512]{1,0:T(8,128)(2,1)S(1)}, bf16[256,512]{1,0:T(8,128)(2,1)S(1)}, u32[]{:S(2)}, u32[]{:S(2)}) %collective-permute-start.55) | collective-permute-done | bytes 262176 | tf_op jit(solution)/shard_map/ppermute | solution.py:18
  (163 shorter events, 87.7 us)
Async XLA Ops:
  4.2 11.9 %collective-permute-start.7 = (bf16[512,256]{1,0:T(8,128)(2,1)S(1)}, bf16[512,256]{1,0:T(8,128)(2,1)S(1)}, u32[]{:S(2)}, u32[]{:S(2)}) collective-permute-start(bf16[512,256]{1,0:T(8,128)(2,1)S(1)} %get-tuple-element.49), channel_id=1, source_target_pairs={{0,8},{8,0},{1,9},{9,1},{2,10},{10,2},{3,11},{11,3},{4,12},{12,4},... | collective-permute-start | bytes 786440 | tf_op jit(solution)/shard_map/ppermute | solution.py:18
  11.5 12.7 %collective-permute-start.1 = (bf16[256,512]{1,0:T(8,128)(2,1)S(1)}, bf16[256,512]{1,0:T(8,128)(2,1)S(1)}, u32[]{:S(2)}, u32[]{:S(2)}) collective-permute-start(bf16[256,512]{1,0:T(8,128)(2,1)S(1)} %panel.5.refs_0_), channel_id=1, source_target_pairs={{0,2},{2,4},{4,6},{1,3},{3,5},{5,7},{8,10},{10,12},{12,14},{9,11},... | collective-permute-start | bytes 786440 | tf_op jit(solution)/shard_map/ppermute | solution.py:215
  16.2 17.9 %collective-permute-start.18 = (bf16[512,512]{1,0:T(8,128)(2,1)S(1)}, bf16[512,512]{1,0:T(8,128)(2,1)S(1)}, u32[]{:S(2)}, u32[]{:S(2)}) collective-permute-start(bf16[512,512]{1,0:T(8,128)(2,1)S(1)} %dynamic-slice_bitcast_fusion), channel_id=1, source_target_pairs={{0,8},{8,0},{1,9},{9,1},{2,10},{10,2},{3,11},{11,3},{4,12},{12,4},... | collective-permute-start | bytes 1572872 | tf_op jit(solution)/shard_map/ppermute | solution.py:18
  17.9 41.2 %collective-permute-start.21 = (bf16[512,1024]{1,0:T(8,128)(2,1)S(1)}, bf16[512,1024]{1,0:T(8,128)(2,1)}, u32[]{:S(2)}, u32[]{:S(2)}) collective-permute-start(bf16[512,1024]{1,0:T(8,128)(2,1)S(1)} %bitcast.113), channel_id=1, source_target_pairs={{0,8},{8,0},{1,9},{9,1},{2,10},{10,2},{3,11},{11,3},{4,12},{12,4},... | collective-permute-start | bytes 3145736 | tf_op jit(solution)/shard_map/ppermute | solution.py:18
  34.0 16.5 %collective-permute-start.12 = (bf16[256,512]{1,0:T(8,128)(2,1)S(1)}, bf16[256,512]{1,0:T(8,128)(2,1)}, u32[]{:S(2)}, u32[]{:S(2)}) collective-permute-start(bf16[256,512]{1,0:T(8,128)(2,1)S(1)} %collective-permute-done.11.refs_2_), channel_id=1, source_target_pairs={{2,0},{4,2},{3,1},{5,3},{10,8},{12,10},{11,9},{13,11},{18,16},{20,... | collective-permute-start | bytes 786440 | tf_op jit(solution)/shard_map/ppermute | solution.py:216
  36.0 19.6 %collective-permute-start.3 = (bf16[256,512]{1,0:T(8,128)(2,1)}, bf16[256,512]{1,0:T(8,128)(2,1)}, u32[]{:S(2)}, u32[]{:S(2)}) collective-permute-start(bf16[256,512]{1,0:T(8,128)(2,1)} %collective-permute-done.2.refs_3_), channel_id=1, source_target_pairs={{4,6},{5,7},{12,14},{13,15},{20,22},{21,23},{28,30},{29,31}} | collective-permute-start | bytes 786440 | tf_op jit(solution)/shard_map/ppermute | solution.py:215
  39.8 16.0 %collective-permute-start.6 = (bf16[256,512]{1,0:T(8,128)(2,1)}, bf16[256,512]{1,0:T(8,128)(2,1)}, u32[]{:S(2)}, u32[]{:S(2)}) collective-permute-start(bf16[256,512]{1,0:T(8,128)(2,1)} %collective-permute-done.5.refs_4_), channel_id=1, source_target_pairs={{2,0},{3,1},{10,8},{11,9},{18,16},{19,17},{26,24},{27,25}} | collective-permute-start | bytes 786440 | tf_op jit(solution)/shard_map/ppermute | solution.py:216
  41.1 15.3 %collective-permute-start.10 = (bf16[256,512]{1,0:T(8,128)(2,1)}, bf16[256,512]{1,0:T(8,128)(2,1)}, u32[]{:S(2)}, u32[]{:S(2)}) collective-permute-start(bf16[256,512]{1,0:T(8,128)(2,1)} %collective-permute-done.9.refs_3_), channel_id=1, source_target_pairs={{4,6},{5,7},{12,14},{13,15},{20,22},{21,23},{28,30},{29,31}} | collective-permute-start | bytes 786440 | tf_op jit(solution)/shard_map/ppermute | solution.py:215
  56.4 11.3 %collective-permute-start.16 = (bf16[1024,512]{1,0:T(8,128)(2,1)}, bf16[1024,512]{1,0:T(8,128)(2,1)}, u32[]{:S(2)}, u32[]{:S(2)}) collective-permute-start(bf16[1024,512]{1,0:T(8,128)(2,1)} %bitcast.103.refs_7_), channel_id=1, source_target_pairs={{0,1},{1,0},{2,3},{3,2},{4,5},{5,4},{6,7},{7,6},{8,9},{9,8},{10,11... | collective-permute-start | bytes 3145736 | tf_op jit(solution)/shard_map/ppermute | solution.py:18
  61.5 20.3 %collective-permute-start.15 = (bf16[256,512]{1,0:T(8,128)(2,1)}, bf16[256,512]{1,0:T(8,128)(2,1)}, u32[]{:S(2)}, u32[]{:S(2)}) collective-permute-start(bf16[256,512]{1,0:T(8,128)(2,1)} %panel.4.refs_0_), channel_id=1, source_target_pairs={{2,0},{4,2},{6,4},{3,1},{5,3},{7,5},{10,8},{12,10},{14,12},{11,9},... | collective-permute-start | bytes 786440 | tf_op jit(solution)/shard_map/ppermute | solution.py:225
  63.0 21.0 %collective-permute-start.14 = (bf16[256,512]{1,0:T(8,128)(2,1)}, bf16[256,512]{1,0:T(8,128)(2,1)S(1)}, u32[]{:S(2)}, u32[]{:S(2)}) collective-permute-start(bf16[256,512]{1,0:T(8,128)(2,1)} %panel.4.refs_0_), channel_id=1, source_target_pairs={{0,2},{2,4},{4,6},{1,3},{3,5},{5,7},{8,10},{10,12},{12,14},{9,11},... | collective-permute-start | bytes 786440 | tf_op jit(solution)/shard_map/ppermute | solution.py:224
  75.9 18.1 %collective-permute-start.36 = (bf16[256,512]{1,0:T(8,128)(2,1)S(1)}, bf16[256,512]{1,0:T(8,128)(2,1)S(1)}, u32[]{:S(2)}, u32[]{:S(2)}) collective-permute-start(bf16[256,512]{1,0:T(8,128)(2,1)S(1)} %panel.7.refs_0_), channel_id=1, source_target_pairs={{2,0},{4,2},{6,4},{3,1},{5,3},{7,5},{10,8},{12,10},{14,12},{11,9},... | collective-permute-start | bytes 786440 | tf_op jit(solution)/shard_map/ppermute | solution.py:225
  77.2 18.1 %collective-permute-start.32 = (bf16[256,512]{1,0:T(8,128)(2,1)S(1)}, bf16[256,512]{1,0:T(8,128)(2,1)S(1)}, u32[]{:S(2)}, u32[]{:S(2)}) collective-permute-start(bf16[256,512]{1,0:T(8,128)(2,1)S(1)} %panel.7.refs_0_), channel_id=1, source_target_pairs={{0,2},{2,4},{4,6},{1,3},{3,5},{5,7},{8,10},{10,12},{12,14},{9,11},... | collective-permute-start | bytes 786440 | tf_op jit(solution)/shard_map/ppermute | solution.py:224
  82.7 17.2 %collective-permute-start.24 = (bf16[256,512]{1,0:T(8,128)(2,1)S(1)}, bf16[256,512]{1,0:T(8,128)(2,1)S(1)}, u32[]{:S(2)}, u32[]{:S(2)}) collective-permute-start(bf16[256,512]{1,0:T(8,128)(2,1)S(1)} %broadcast_select_fusion.1), channel_id=1, source_target_pairs={{2,0},{4,2},{6,4},{3,1},{5,3},{7,5},{10,8},{12,10},{14,12},{11,9},... | collective-permute-start | bytes 786440 | tf_op jit(solution)/shard_map/ppermute | solution.py:250
  84.1 15.9 %collective-permute-start.23 = (bf16[256,512]{1,0:T(8,128)(2,1)S(1)}, bf16[256,512]{1,0:T(8,128)(2,1)S(1)}, u32[]{:S(2)}, u32[]{:S(2)}) collective-permute-start(bf16[256,512]{1,0:T(8,128)(2,1)S(1)} %broadcast_select_fusion.3), channel_id=1, source_target_pairs={{0,2},{2,4},{4,6},{1,3},{3,5},{5,7},{8,10},{10,12},{12,14},{9,11},... | collective-permute-start | bytes 786440 | tf_op jit(solution)/shard_map/ppermute | solution.py:249
  95.4 11.1 %collective-permute-start.33 = (bf16[256,512]{1,0:T(8,128)(2,1)S(1)}, bf16[256,512]{1,0:T(8,128)(2,1)S(1)}, u32[]{:S(2)}, u32[]{:S(2)}) collective-permute-start(bf16[256,512]{1,0:T(8,128)(2,1)S(1)} %broadcast_select_fusion.2), channel_id=1, source_target_pairs={{0,2},{2,4},{4,6},{1,3},{3,5},{5,7},{8,10},{10,12},{12,14},{9,11},... | collective-permute-start | bytes 786440 | tf_op jit(solution)/shard_map/ppermute | solution.py:249
  100.1 12.2 %collective-permute-start.25 = (bf16[256,512]{1,0:T(8,128)(2,1)S(1)}, bf16[256,512]{1,0:T(8,128)(2,1)S(1)}, u32[]{:S(2)}, u32[]{:S(2)}) collective-permute-start(bf16[256,512]{1,0:T(8,128)(2,1)S(1)} %get-tuple-element.48), channel_id=1, source_target_pairs={{0,2},{2,4},{4,6},{1,3},{3,5},{5,7},{8,10},{10,12},{12,14},{9,11},... | collective-permute-start | bytes 786440 | tf_op jit(solution)/shard_map/ppermute | solution.py:249
  106.6 11.8 %collective-permute-start.34 = (bf16[256,512]{1,0:T(8,128)(2,1)S(1)}, bf16[256,512]{1,0:T(8,128)(2,1)S(1)}, u32[]{:S(2)}, u32[]{:S(2)}) collective-permute-start(bf16[256,512]{1,0:T(8,128)(2,1)S(1)} %get-tuple-element.43), channel_id=1, source_target_pairs={{0,2},{2,4},{4,6},{1,3},{3,5},{5,7},{8,10},{10,12},{12,14},{9,11},... | collective-permute-start | bytes 786440 | tf_op jit(solution)/shard_map/ppermute | solution.py:249
  111.0 10.9 %collective-permute-start.38 = (bf16[256,512]{1,0:T(8,128)(2,1)S(1)}, bf16[256,512]{1,0:T(8,128)(2,1)S(1)}, u32[]{:S(2)}, u32[]{:S(2)}) collective-permute-start(bf16[256,512]{1,0:T(8,128)(2,1)S(1)} %get-tuple-element.44), channel_id=1, source_target_pairs={{2,0},{4,2},{6,4},{3,1},{5,3},{7,5},{10,8},{12,10},{14,12},{11,9},... | collective-permute-start | bytes 786440 | tf_op jit(solution)/shard_map/ppermute | solution.py:250
  112.5 13.2 %collective-permute-start.27 = (bf16[256,512]{1,0:T(8,128)(2,1)S(1)}, bf16[256,512]{1,0:T(8,128)(2,1)S(1)}, u32[]{:S(2)}, u32[]{:S(2)}) collective-permute-start(bf16[256,512]{1,0:T(8,128)(2,1)S(1)} %get-tuple-element.45), channel_id=1, source_target_pairs={{0,2},{2,4},{4,6},{1,3},{3,5},{5,7},{8,10},{10,12},{12,14},{9,11},... | collective-permute-start | bytes 786440 | tf_op jit(solution)/shard_map/ppermute | solution.py:249
  153.0 11.1 %collective-permute-start.52 = (bf16[256,512]{1,0:T(8,128)(2,1)S(1)}, bf16[256,512]{1,0:T(8,128)(2,1)S(1)}, u32[]{:S(2)}, u32[]{:S(2)}) collective-permute-start(bf16[256,512]{1,0:T(8,128)(2,1)S(1)} %get-tuple-element.36), channel_id=1, source_target_pairs={{6,4},{7,5},{14,12},{15,13},{22,20},{23,21},{30,28},{31,29}} | collective-permute-start | bytes 786440 | tf_op jit(solution)/shard_map/ppermute | solution.py:250
  153.8 11.5 %collective-permute-start.50 = (bf16[256,512]{1,0:T(8,128)(2,1)S(1)}, bf16[256,512]{1,0:T(8,128)(2,1)S(1)}, u32[]{:S(2)}, u32[]{:S(2)}) collective-permute-start(bf16[256,512]{1,0:T(8,128)(2,1)S(1)} %fusion.1), channel_id=1, source_target_pairs={{0,2},{2,4},{1,3},{3,5},{8,10},{10,12},{9,11},{11,13},{16,18},{18,... | collective-permute-start | bytes 786440 | tf_op jit(solution)/shard_map/ppermute | solution.py:249
  170.2 12.3 %collective-permute-start.47 = (bf16[256,512]{1,0:T(8,128)(2,1)S(1)}, bf16[256,512]{1,0:T(8,128)(2,1)S(1)}, u32[]{:S(2)}, u32[]{:S(2)}) collective-permute-start(bf16[256,512]{1,0:T(8,128)(2,1)S(1)} %get-tuple-element.40), channel_id=1, source_target_pairs={{4,2},{6,4},{5,3},{7,5},{12,10},{14,12},{13,11},{15,13},{20,18},{2... | collective-permute-start | bytes 786440 | tf_op jit(solution)/shard_map/ppermute | solution.py:250
  170.9 13.0 %collective-permute-start.51 = (bf16[256,512]{1,0:T(8,128)(2,1)S(1)}, bf16[256,512]{1,0:T(8,128)(2,1)S(1)}, u32[]{:S(2)}, u32[]{:S(2)}) collective-permute-start(bf16[256,512]{1,0:T(8,128)(2,1)S(1)} %get-tuple-element.37), channel_id=1, source_target_pairs={{0,2},{2,4},{4,6},{1,3},{3,5},{5,7},{8,10},{10,12},{12,14},{9,11},... | collective-permute-start | bytes 786440 | tf_op jit(solution)/shard_map/ppermute | solution.py:249
  (53 other events, 554.1 us)

commit v9 on v8

--- a/solution.py
+++ b/solution.py
@@ -155,7 +155,7 @@
         ),
         out_shape=[jax.ShapeDtypeStruct(shape, jnp.float32)]
         + [jax.ShapeDtypeStruct(shape[1:], jnp.bfloat16)] * 2,
-        in_specs=[VMEM] * len(blocks) + [ANY] * (len(states) + len(flat)),
+        in_specs=[ANY] * (len(blocks) + len(states) + len(flat)),
         out_specs=[VMEM] * 3,
         scratch_shapes=[
             pltpu.VMEM((sizes.chunk, sizes.order), jnp.bfloat16),

time: 201 us -> 199 us (0.990)
  Pallas kernels: 21.9 us -> 18.8 us
    pallas_call x4, Pallas kernels: 18.8 us -> 15.7 us  [products(): pl.pallas_call(functools.partial(products_kernel, sizes, step, part, [b[0...]
  transfers between devices with their start and end apart: 57 -> 57, of which waited for: 20 -> 22; matrix products, arithmetic and copies ran while one was open for 4% -> 4% of each run, Pallas kernels for 8% -> 7%
where the time goes in v9:
time: 199 us; the launch traced here: 198 us
  starting transfers between devices  103 us (52%)
  waiting for transfers between devices  59.8 us (30%)
  Pallas kernels  18.8 us (9%)
  local copies, waits for them, and re-layouts  11 us (6%)
  other arithmetic  3.77 us (2%)
    ppermute x12, starting transfers between devices, scattered_sum(): up = lax.ppermute(up_block, 'row', [(i, i + 1) for i in range(low + 1)])  46.2 us
    ppermute x17, waiting for transfers between devices, exchanged(): lax.ppermute(value, axis, [(i, (i + steps) % count) for i in range(count)])  19 us
    ppermute x6, waiting for transfers between devices, neighbours_gathered(): lax.ppermute(down, 'row', [(i, i - 1) for i in range(1, sizes.row - slot)])  16.1 us
    ppermute x12, waiting for transfers between devices, scattered_sum(): lax.ppermute(down_block, 'row', [(i, i - 1) for i in range(last - low, la...  16.1 us
    pallas_call x4, Pallas kernels, products(): pl.pallas_call(functools.partial(products_kernel, sizes, step, part, [b[0...  15.7 us
    ppermute x6, starting transfers between devices, neighbours_gathered(): up = lax.ppermute(up, 'row', [(i, i + 1) for i in range(slot, last)])  14.1 us
    ppermute x12, starting transfers between devices, scattered_sum(): lax.ppermute(down_block, 'row', [(i, i - 1) for i in range(last - low, la...  13 us
    ppermute x17, starting transfers between devices, exchanged(): lax.ppermute(value, axis, [(i, (i + steps) % count) for i in range(count)])  10.4 us
  transfers between devices with their start and end apart: 57, of which 22 were waited for; matrix products, arithmetic and copies ran while one was open for 4% of the time, Pallas kernels for 7%

profile of v9, /device:TPU:0, one launch (start us, length us, event | category | flops | bytes accessed | tf_op | source)
XLA Modules:
  0.0 197.6 jit_solution(10884335660438481768)
XLA Ops:
  5.4 6.0 %collective-permute-done.refs_0_ = bf16[512,256]{1,0:T(8,128)(2,1)S(1)} collective-permute-done((bf16[512,256]{1,0:T(8,128)(2,1)S(1)}, bf16[512,256]{1,0:T(8,128)(2,1)S(1)}, u32[]{:S(2)}, u32[]{:S(2)}) %collective-permute-start) | collective-permute-done | bytes 262176 | tf_op jit(solution)/shard_map/ppermute | solution.py:18
  11.5 4.1 %collective-permute-start.1 = (bf16[256,512]{1,0:T(8,128)(2,1)S(1)}, bf16[256,512]{1,0:T(8,128)(2,1)S(1)}, u32[]{:S(2)}, u32[]{:S(2)}) collective-permute-start(bf16[256,512]{1,0:T(8,128)(2,1)S(1)} %panel.5.refs_0_), channel_id=1, source_target_pairs={{0,2},{2,4},{4,6},{1,3},{3,5},{5,7},{8,10},{10,12},{12,14},{9,11},... | collective-permute-start | bytes 786440 | tf_op jit(solution)/shard_map/ppermute | solution.py:215
  19.7 4.6 %collective-permute-start.8 = (bf16[256,512]{1,0:T(8,128)(2,1)S(1)}, bf16[256,512]{1,0:T(8,128)(2,1)S(1)}, u32[]{:S(2)}, u32[]{:S(2)}) collective-permute-start(bf16[256,512]{1,0:T(8,128)(2,1)S(1)} %panel.6.refs_0_), channel_id=1, source_target_pairs={{0,2},{2,4},{4,6},{1,3},{3,5},{5,7},{8,10},{10,12},{12,14},{9,11},... | collective-permute-start | bytes 786440 | tf_op jit(solution)/shard_map/ppermute | solution.py:215
  42.4 8.1 %collective-permute-done.12.refs_4_ = bf16[256,512]{1,0:T(8,128)(2,1)} collective-permute-done((bf16[256,512]{1,0:T(8,128)(2,1)S(1)}, bf16[256,512]{1,0:T(8,128)(2,1)}, u32[]{:S(2)}, u32[]{:S(2)}) %collective-permute-start.12) | collective-permute-done | bytes 262176 | tf_op jit(solution)/shard_map/ppermute | solution.py:216
  63.0 4.7 %collective-permute-start.14 = (bf16[256,512]{1,0:T(8,128)(2,1)}, bf16[256,512]{1,0:T(8,128)(2,1)S(1)}, u32[]{:S(2)}, u32[]{:S(2)}) collective-permute-start(bf16[256,512]{1,0:T(8,128)(2,1)} %panel.4.refs_0_), channel_id=1, source_target_pairs={{0,2},{2,4},{4,6},{1,3},{3,5},{5,7},{8,10},{10,12},{12,14},{9,11},... | collective-permute-start | bytes 786440 | tf_op jit(solution)/shard_map/ppermute | solution.py:224
  70.6 4.2 %products.4 = (f32[4,256,512]{2,1,0:T(8,128)S(1)}, bf16[256,512]{1,0:T(8,128)(2,1)S(1)}, bf16[256,512]{1,0:T(8,128)(2,1)S(1)}) custom-call(bf16[256,512]{1,0:T(8,128)(2,1)S(1)} %copy-done.9, bf16[256,512]{1,0:T(8,128)(2,1)S(1)} %copy-done.15, bf16[256,512]{1,0:T(8,128)(2,1)S(1)} %copy-done.17, bf16[256,512]{1,0:T(8,128)(2,1)} %collective-permute-done.2.refs_3_, ...), custom_call_target="tpu_custom_call" | custom-call | flops 1610612736 | bytes 9437184 | tf_op jit(solution)/shard_map/products/pallas_call | solution.py:152
  76.1 4.6 %collective-permute-start.32 = (bf16[256,512]{1,0:T(8,128)(2,1)S(1)}, bf16[256,512]{1,0:T(8,128)(2,1)S(1)}, u32[]{:S(2)}, u32[]{:S(2)}) collective-permute-start(bf16[256,512]{1,0:T(8,128)(2,1)S(1)} %panel.7.refs_0_), channel_id=1, source_target_pairs={{0,2},{2,4},{4,6},{1,3},{3,5},{5,7},{8,10},{10,12},{12,14},{9,11},... | collective-permute-start | bytes 786440 | tf_op jit(solution)/shard_map/ppermute | solution.py:224
  83.0 4.6 %collective-permute-start.23 = (bf16[256,512]{1,0:T(8,128)(2,1)S(1)}, bf16[256,512]{1,0:T(8,128)(2,1)S(1)}, u32[]{:S(2)}, u32[]{:S(2)}) collective-permute-start(bf16[256,512]{1,0:T(8,128)(2,1)S(1)} %broadcast_select_fusion.3), channel_id=1, source_target_pairs={{0,2},{2,4},{4,6},{1,3},{3,5},{5,7},{8,10},{10,12},{12,14},{9,11},... | collective-permute-start | bytes 786440 | tf_op jit(solution)/shard_map/ppermute | solution.py:249
  87.6 4.2 %products.5 = (f32[4,256,512]{2,1,0:T(8,128)S(1)}, bf16[256,512]{1,0:T(8,128)(2,1)S(1)}, bf16[256,512]{1,0:T(8,128)(2,1)S(1)}) custom-call(bf16[256,512]{1,0:T(8,128)(2,1)S(1)} %copy-done.7, bf16[256,512]{1,0:T(8,128)(2,1)S(1)} %copy-done.11, bf16[256,512]{1,0:T(8,128)(2,1)S(1)} %copy-done.13, bf16[256,512]{1,0:T(8,128)(2,1)} %collective-permute-done.9.refs_3_, ...), custom_call_target="tpu_custom_call" | custom-call | flops 1610612736 | bytes 9437184 | tf_op jit(solution)/shard_map/products/pallas_call | solution.py:152
  93.3 4.6 %collective-permute-start.33 = (bf16[256,512]{1,0:T(8,128)(2,1)S(1)}, bf16[256,512]{1,0:T(8,128)(2,1)S(1)}, u32[]{:S(2)}, u32[]{:S(2)}) collective-permute-start(bf16[256,512]{1,0:T(8,128)(2,1)S(1)} %broadcast_select_fusion.2), channel_id=1, source_target_pairs={{0,2},{2,4},{4,6},{1,3},{3,5},{5,7},{8,10},{10,12},{12,14},{9,11},... | collective-permute-start | bytes 786440 | tf_op jit(solution)/shard_map/ppermute | solution.py:249
  104.6 4.4 %collective-permute-start.34 = (bf16[256,512]{1,0:T(8,128)(2,1)S(1)}, bf16[256,512]{1,0:T(8,128)(2,1)S(1)}, u32[]{:S(2)}, u32[]{:S(2)}) collective-permute-start(bf16[256,512]{1,0:T(8,128)(2,1)S(1)} %get-tuple-element.43), channel_id=1, source_target_pairs={{0,2},{2,4},{4,6},{1,3},{3,5},{5,7},{8,10},{10,12},{12,14},{9,11},... | collective-permute-start | bytes 786440 | tf_op jit(solution)/shard_map/ppermute | solution.py:249
  110.6 4.6 %collective-permute-start.27 = (bf16[256,512]{1,0:T(8,128)(2,1)S(1)}, bf16[256,512]{1,0:T(8,128)(2,1)S(1)}, u32[]{:S(2)}, u32[]{:S(2)}) collective-permute-start(bf16[256,512]{1,0:T(8,128)(2,1)S(1)} %get-tuple-element.45), channel_id=1, source_target_pairs={{0,2},{2,4},{4,6},{1,3},{3,5},{5,7},{8,10},{10,12},{12,14},{9,11},... | collective-permute-start | bytes 786440 | tf_op jit(solution)/shard_map/ppermute | solution.py:249
  116.4 3.3 %collective-permute-done.38.refs_6_ = bf16[256,512]{1,0:T(8,128)(2,1)S(1)} collective-permute-done((bf16[256,512]{1,0:T(8,128)(2,1)S(1)}, bf16[256,512]{1,0:T(8,128)(2,1)S(1)}, u32[]{:S(2)}, u32[]{:S(2)}) %collective-permute-start.38) | collective-permute-done | bytes 262176 | tf_op jit(solution)/shard_map/ppermute | solution.py:250
  126.3 4.1 %collective-permute-done.39 = bf16[256,512]{1,0:T(8,128)(2,1)S(1)} collective-permute-done((bf16[256,512]{1,0:T(8,128)(2,1)S(1)}, bf16[256,512]{1,0:T(8,128)(2,1)S(1)}, u32[]{:S(2)}, u32[]{:S(2)}) %collective-permute-start.39) | collective-permute-done | bytes 262176 | tf_op jit(solution)/shard_map/ppermute | solution.py:250
  132.9 4.1 %collective-permute-done.41.refs_13_.refs_7_ = bf16[256,512]{1,0:T(8,128)(2,1)S(1)} collective-permute-done((bf16[256,512]{1,0:T(8,128)(2,1)S(1)}, bf16[256,512]{1,0:T(8,128)(2,1)S(1)}, u32[]{:S(2)}, u32[]{:S(2)}) %collective-permute-start.41) | collective-permute-done | bytes 262176 | tf_op jit(solution)/shard_map/ppermute | solution.py:18
  138.5 3.6 %products.7 = (f32[4,256,512]{2,1,0:T(8,128)S(1)}, bf16[256,512]{1,0:T(8,128)(2,1)S(1)}, bf16[256,512]{1,0:T(8,128)(2,1)S(1)}) custom-call(bf16[256,512]{1,0:T(8,128)(2,1)S(1)} %panel.7.refs_0_, bf16[256,512]{1,0:T(8,128)(2,1)S(1)} %collective-permute-done.32.refs_1_, bf16[256,512]{1,0:T(8,128)(2,1)S(1)} %collective-permute-done.36.refs_2_, ...), custom_call_target="tpu_custom_call" | custom-call | flops 1610612736 | bytes 9437184 | tf_op jit(solution)/shard_map/products/pallas_call | solution.py:152
  144.8 3.7 %products.6 = (f32[4,256,512]{2,1,0:T(8,128)S(1)}, bf16[256,512]{1,0:T(8,128)(2,1)S(1)}, bf16[256,512]{1,0:T(8,128)(2,1)S(1)}) custom-call(bf16[256,512]{1,0:T(8,128)(2,1)} %panel.4.refs_0_, bf16[256,512]{1,0:T(8,128)(2,1)S(1)} %collective-permute-done.14.refs_1_, bf16[256,512]{1,0:T(8,128)(2,1)} %collective-permute-done.15.refs_2_, ...), custom_call_target="tpu_custom_call" | custom-call | flops 1610612736 | bytes 9437184 | tf_op jit(solution)/shard_map/products/pallas_call | solution.py:152
  150.9 4.4 %collective-permute-start.50 = (bf16[256,512]{1,0:T(8,128)(2,1)S(1)}, bf16[256,512]{1,0:T(8,128)(2,1)S(1)}, u32[]{:S(2)}, u32[]{:S(2)}) collective-permute-start(bf16[256,512]{1,0:T(8,128)(2,1)S(1)} %fusion.1), channel_id=1, source_target_pairs={{0,2},{2,4},{1,3},{3,5},{8,10},{10,12},{9,11},{11,13},{16,18},{18,... | collective-permute-start | bytes 786440 | tf_op jit(solution)/shard_map/ppermute | solution.py:249
  156.5 4.4 %collective-permute-start.44 = (bf16[256,512]{1,0:T(8,128)(2,1)S(1)}, bf16[256,512]{1,0:T(8,128)(2,1)S(1)}, u32[]{:S(2)}, u32[]{:S(2)}) collective-permute-start(bf16[256,512]{1,0:T(8,128)(2,1)S(1)} %fusion.7), channel_id=1, source_target_pairs={{0,2},{2,4},{1,3},{3,5},{8,10},{10,12},{9,11},{11,13},{16,18},{18,... | collective-permute-start | bytes 786440 | tf_op jit(solution)/shard_map/ppermute | solution.py:249
  162.9 4.4 %collective-permute-done.44 = bf16[256,512]{1,0:T(8,128)(2,1)S(1)} collective-permute-done((bf16[256,512]{1,0:T(8,128)(2,1)S(1)}, bf16[256,512]{1,0:T(8,128)(2,1)S(1)}, u32[]{:S(2)}, u32[]{:S(2)}) %collective-permute-start.44) | collective-permute-done | bytes 262176 | tf_op jit(solution)/shard_map/ppermute | solution.py:249
  168.1 5.0 %collective-permute-start.51 = (bf16[256,512]{1,0:T(8,128)(2,1)S(1)}, bf16[256,512]{1,0:T(8,128)(2,1)S(1)}, u32[]{:S(2)}, u32[]{:S(2)}) collective-permute-start(bf16[256,512]{1,0:T(8,128)(2,1)S(1)} %get-tuple-element.37), channel_id=1, source_target_pairs={{0,2},{2,4},{4,6},{1,3},{3,5},{5,7},{8,10},{10,12},{12,14},{9,11},... | collective-permute-start | bytes 786440 | tf_op jit(solution)/shard_map/ppermute | solution.py:249
  174.6 5.2 %collective-permute-start.45 = (bf16[256,512]{1,0:T(8,128)(2,1)S(1)}, bf16[256,512]{1,0:T(8,128)(2,1)S(1)}, u32[]{:S(2)}, u32[]{:S(2)}) collective-permute-start(bf16[256,512]{1,0:T(8,128)(2,1)S(1)} %get-tuple-element.39), channel_id=1, source_target_pairs={{0,2},{2,4},{4,6},{1,3},{3,5},{5,7},{8,10},{10,12},{12,14},{9,11},... | collective-permute-start | bytes 786440 | tf_op jit(solution)/shard_map/ppermute | solution.py:249
  184.6 4.4 %collective-permute-done.48 = bf16[256,512]{1,0:T(8,128)(2,1)S(1)} collective-permute-done((bf16[256,512]{1,0:T(8,128)(2,1)S(1)}, bf16[256,512]{1,0:T(8,128)(2,1)S(1)}, u32[]{:S(2)}, u32[]{:S(2)}) %collective-permute-start.48) | collective-permute-done | bytes 262176 | tf_op jit(solution)/shard_map/ppermute | solution.py:250
  190.6 5.3 %collective-permute-done.55.refs_2_ = bf16[256,512]{1,0:T(8,128)(2,1)S(1)} collective-permute-done((bf16[256,512]{1,0:T(8,128)(2,1)S(1)}, bf16[256,512]{1,0:T(8,128)(2,1)S(1)}, u32[]{:S(2)}, u32[]{:S(2)}) %collective-permute-start.55) | collective-permute-done | bytes 262176 | tf_op jit(solution)/shard_map/ppermute | solution.py:18
  (163 shorter events, 86.4 us)
Async XLA Ops:
  4.2 11.9 %collective-permute-start.7 = (bf16[512,256]{1,0:T(8,128)(2,1)S(1)}, bf16[512,256]{1,0:T(8,128)(2,1)S(1)}, u32[]{:S(2)}, u32[]{:S(2)}) collective-permute-start(bf16[512,256]{1,0:T(8,128)(2,1)S(1)} %get-tuple-element.49), channel_id=1, source_target_pairs={{0,8},{8,0},{1,9},{9,1},{2,10},{10,2},{3,11},{11,3},{4,12},{12,4},... | collective-permute-start | bytes 786440 | tf_op jit(solution)/shard_map/ppermute | solution.py:18
  11.5 12.7 %collective-permute-start.1 = (bf16[256,512]{1,0:T(8,128)(2,1)S(1)}, bf16[256,512]{1,0:T(8,128)(2,1)S(1)}, u32[]{:S(2)}, u32[]{:S(2)}) collective-permute-start(bf16[256,512]{1,0:T(8,128)(2,1)S(1)} %panel.5.refs_0_), channel_id=1, source_target_pairs={{0,2},{2,4},{4,6},{1,3},{3,5},{5,7},{8,10},{10,12},{12,14},{9,11},... | collective-permute-start | bytes 786440 | tf_op jit(solution)/shard_map/ppermute | solution.py:215
  16.2 17.9 %collective-permute-start.18 = (bf16[512,512]{1,0:T(8,128)(2,1)S(1)}, bf16[512,512]{1,0:T(8,128)(2,1)S(1)}, u32[]{:S(2)}, u32[]{:S(2)}) collective-permute-start(bf16[512,512]{1,0:T(8,128)(2,1)S(1)} %dynamic-slice_bitcast_fusion), channel_id=1, source_target_pairs={{0,8},{8,0},{1,9},{9,1},{2,10},{10,2},{3,11},{11,3},{4,12},{12,4},... | collective-permute-start | bytes 1572872 | tf_op jit(solution)/shard_map/ppermute | solution.py:18
  17.9 41.2 %collective-permute-start.21 = (bf16[512,1024]{1,0:T(8,128)(2,1)S(1)}, bf16[512,1024]{1,0:T(8,128)(2,1)}, u32[]{:S(2)}, u32[]{:S(2)}) collective-permute-start(bf16[512,1024]{1,0:T(8,128)(2,1)S(1)} %bitcast.113), channel_id=1, source_target_pairs={{0,8},{8,0},{1,9},{9,1},{2,10},{10,2},{3,11},{11,3},{4,12},{12,4},... | collective-permute-start | bytes 3145736 | tf_op jit(solution)/shard_map/ppermute | solution.py:18
  34.0 16.5 %collective-permute-start.12 = (bf16[256,512]{1,0:T(8,128)(2,1)S(1)}, bf16[256,512]{1,0:T(8,128)(2,1)}, u32[]{:S(2)}, u32[]{:S(2)}) collective-permute-start(bf16[256,512]{1,0:T(8,128)(2,1)S(1)} %collective-permute-done.11.refs_2_), channel_id=1, source_target_pairs={{2,0},{4,2},{3,1},{5,3},{10,8},{12,10},{11,9},{13,11},{18,16},{20,... | collective-permute-start | bytes 786440 | tf_op jit(solution)/shard_map/ppermute | solution.py:216
  36.0 19.6 %collective-permute-start.3 = (bf16[256,512]{1,0:T(8,128)(2,1)}, bf16[256,512]{1,0:T(8,128)(2,1)}, u32[]{:S(2)}, u32[]{:S(2)}) collective-permute-start(bf16[256,512]{1,0:T(8,128)(2,1)} %collective-permute-done.2.refs_3_), channel_id=1, source_target_pairs={{4,6},{5,7},{12,14},{13,15},{20,22},{21,23},{28,30},{29,31}} | collective-permute-start | bytes 786440 | tf_op jit(solution)/shard_map/ppermute | solution.py:215
  39.8 16.0 %collective-permute-start.6 = (bf16[256,512]{1,0:T(8,128)(2,1)}, bf16[256,512]{1,0:T(8,128)(2,1)}, u32[]{:S(2)}, u32[]{:S(2)}) collective-permute-start(bf16[256,512]{1,0:T(8,128)(2,1)} %collective-permute-done.5.refs_4_), channel_id=1, source_target_pairs={{2,0},{3,1},{10,8},{11,9},{18,16},{19,17},{26,24},{27,25}} | collective-permute-start | bytes 786440 | tf_op jit(solution)/shard_map/ppermute | solution.py:216
  41.1 15.3 %collective-permute-start.10 = (bf16[256,512]{1,0:T(8,128)(2,1)}, bf16[256,512]{1,0:T(8,128)(2,1)}, u32[]{:S(2)}, u32[]{:S(2)}) collective-permute-start(bf16[256,512]{1,0:T(8,128)(2,1)} %collective-permute-done.9.refs_3_), channel_id=1, source_target_pairs={{4,6},{5,7},{12,14},{13,15},{20,22},{21,23},{28,30},{29,31}} | collective-permute-start | bytes 786440 | tf_op jit(solution)/shard_map/ppermute | solution.py:215
  56.4 11.3 %collective-permute-start.16 = (bf16[1024,512]{1,0:T(8,128)(2,1)}, bf16[1024,512]{1,0:T(8,128)(2,1)}, u32[]{:S(2)}, u32[]{:S(2)}) collective-permute-start(bf16[1024,512]{1,0:T(8,128)(2,1)} %bitcast.103.refs_7_), channel_id=1, source_target_pairs={{0,1},{1,0},{2,3},{3,2},{4,5},{5,4},{6,7},{7,6},{8,9},{9,8},{10,11... | collective-permute-start | bytes 3145736 | tf_op jit(solution)/shard_map/ppermute | solution.py:18
  61.5 19.2 %collective-permute-start.15 = (bf16[256,512]{1,0:T(8,128)(2,1)}, bf16[256,512]{1,0:T(8,128)(2,1)}, u32[]{:S(2)}, u32[]{:S(2)}) collective-permute-start(bf16[256,512]{1,0:T(8,128)(2,1)} %panel.4.refs_0_), channel_id=1, source_target_pairs={{2,0},{4,2},{6,4},{3,1},{5,3},{7,5},{10,8},{12,10},{14,12},{11,9},... | collective-permute-start | bytes 786440 | tf_op jit(solution)/shard_map/ppermute | solution.py:225
  63.0 20.0 %collective-permute-start.14 = (bf16[256,512]{1,0:T(8,128)(2,1)}, bf16[256,512]{1,0:T(8,128)(2,1)S(1)}, u32[]{:S(2)}, u32[]{:S(2)}) collective-permute-start(bf16[256,512]{1,0:T(8,128)(2,1)} %panel.4.refs_0_), channel_id=1, source_target_pairs={{0,2},{2,4},{4,6},{1,3},{3,5},{5,7},{8,10},{10,12},{12,14},{9,11},... | collective-permute-start | bytes 786440 | tf_op jit(solution)/shard_map/ppermute | solution.py:224
  74.8 17.1 %collective-permute-start.36 = (bf16[256,512]{1,0:T(8,128)(2,1)S(1)}, bf16[256,512]{1,0:T(8,128)(2,1)S(1)}, u32[]{:S(2)}, u32[]{:S(2)}) collective-permute-start(bf16[256,512]{1,0:T(8,128)(2,1)S(1)} %panel.7.refs_0_), channel_id=1, source_target_pairs={{2,0},{4,2},{6,4},{3,1},{5,3},{7,5},{10,8},{12,10},{14,12},{11,9},... | collective-permute-start | bytes 786440 | tf_op jit(solution)/shard_map/ppermute | solution.py:225
  76.1 17.1 %collective-permute-start.32 = (bf16[256,512]{1,0:T(8,128)(2,1)S(1)}, bf16[256,512]{1,0:T(8,128)(2,1)S(1)}, u32[]{:S(2)}, u32[]{:S(2)}) collective-permute-start(bf16[256,512]{1,0:T(8,128)(2,1)S(1)} %panel.7.refs_0_), channel_id=1, source_target_pairs={{0,2},{2,4},{4,6},{1,3},{3,5},{5,7},{8,10},{10,12},{12,14},{9,11},... | collective-permute-start | bytes 786440 | tf_op jit(solution)/shard_map/ppermute | solution.py:224
  81.7 16.2 %collective-permute-start.24 = (bf16[256,512]{1,0:T(8,128)(2,1)S(1)}, bf16[256,512]{1,0:T(8,128)(2,1)S(1)}, u32[]{:S(2)}, u32[]{:S(2)}) collective-permute-start(bf16[256,512]{1,0:T(8,128)(2,1)S(1)} %broadcast_select_fusion.1), channel_id=1, source_target_pairs={{2,0},{4,2},{6,4},{3,1},{5,3},{7,5},{10,8},{12,10},{14,12},{11,9},... | collective-permute-start | bytes 786440 | tf_op jit(solution)/shard_map/ppermute | solution.py:250
  83.0 14.8 %collective-permute-start.23 = (bf16[256,512]{1,0:T(8,128)(2,1)S(1)}, bf16[256,512]{1,0:T(8,128)(2,1)S(1)}, u32[]{:S(2)}, u32[]{:S(2)}) collective-permute-start(bf16[256,512]{1,0:T(8,128)(2,1)S(1)} %broadcast_select_fusion.3), channel_id=1, source_target_pairs={{0,2},{2,4},{4,6},{1,3},{3,5},{5,7},{8,10},{10,12},{12,14},{9,11},... | collective-permute-start | bytes 786440 | tf_op jit(solution)/shard_map/ppermute | solution.py:249
  93.3 11.2 %collective-permute-start.33 = (bf16[256,512]{1,0:T(8,128)(2,1)S(1)}, bf16[256,512]{1,0:T(8,128)(2,1)S(1)}, u32[]{:S(2)}, u32[]{:S(2)}) collective-permute-start(bf16[256,512]{1,0:T(8,128)(2,1)S(1)} %broadcast_select_fusion.2), channel_id=1, source_target_pairs={{0,2},{2,4},{4,6},{1,3},{3,5},{5,7},{8,10},{10,12},{12,14},{9,11},... | collective-permute-start | bytes 786440 | tf_op jit(solution)/shard_map/ppermute | solution.py:249
  98.0 12.3 %collective-permute-start.25 = (bf16[256,512]{1,0:T(8,128)(2,1)S(1)}, bf16[256,512]{1,0:T(8,128)(2,1)S(1)}, u32[]{:S(2)}, u32[]{:S(2)}) collective-permute-start(bf16[256,512]{1,0:T(8,128)(2,1)S(1)} %get-tuple-element.48), channel_id=1, source_target_pairs={{0,2},{2,4},{4,6},{1,3},{3,5},{5,7},{8,10},{10,12},{12,14},{9,11},... | collective-permute-start | bytes 786440 | tf_op jit(solution)/shard_map/ppermute | solution.py:249
  104.6 11.8 %collective-permute-start.34 = (bf16[256,512]{1,0:T(8,128)(2,1)S(1)}, bf16[256,512]{1,0:T(8,128)(2,1)S(1)}, u32[]{:S(2)}, u32[]{:S(2)}) collective-permute-start(bf16[256,512]{1,0:T(8,128)(2,1)S(1)} %get-tuple-element.43), channel_id=1, source_target_pairs={{0,2},{2,4},{4,6},{1,3},{3,5},{5,7},{8,10},{10,12},{12,14},{9,11},... | collective-permute-start | bytes 786440 | tf_op jit(solution)/shard_map/ppermute | solution.py:249
  110.6 12.9 %collective-permute-start.27 = (bf16[256,512]{1,0:T(8,128)(2,1)S(1)}, bf16[256,512]{1,0:T(8,128)(2,1)S(1)}, u32[]{:S(2)}, u32[]{:S(2)}) collective-permute-start(bf16[256,512]{1,0:T(8,128)(2,1)S(1)} %get-tuple-element.45), channel_id=1, source_target_pairs={{0,2},{2,4},{4,6},{1,3},{3,5},{5,7},{8,10},{10,12},{12,14},{9,11},... | collective-permute-start | bytes 786440 | tf_op jit(solution)/shard_map/ppermute | solution.py:249
  149.8 11.2 %collective-permute-start.52 = (bf16[256,512]{1,0:T(8,128)(2,1)S(1)}, bf16[256,512]{1,0:T(8,128)(2,1)S(1)}, u32[]{:S(2)}, u32[]{:S(2)}) collective-permute-start(bf16[256,512]{1,0:T(8,128)(2,1)S(1)} %get-tuple-element.36), channel_id=1, source_target_pairs={{6,4},{7,5},{14,12},{15,13},{22,20},{23,21},{30,28},{31,29}} | collective-permute-start | bytes 786440 | tf_op jit(solution)/shard_map/ppermute | solution.py:250
  150.9 11.2 %collective-permute-start.50 = (bf16[256,512]{1,0:T(8,128)(2,1)S(1)}, bf16[256,512]{1,0:T(8,128)(2,1)S(1)}, u32[]{:S(2)}, u32[]{:S(2)}) collective-permute-start(bf16[256,512]{1,0:T(8,128)(2,1)S(1)} %fusion.1), channel_id=1, source_target_pairs={{0,2},{2,4},{1,3},{3,5},{8,10},{10,12},{9,11},{11,13},{16,18},{18,... | collective-permute-start | bytes 786440 | tf_op jit(solution)/shard_map/ppermute | solution.py:249
  162.2 10.9 %collective-permute-start.53 = (bf16[256,512]{1,0:T(8,128)(2,1)S(1)}, bf16[256,512]{1,0:T(8,128)(2,1)S(1)}, u32[]{:S(2)}, u32[]{:S(2)}) collective-permute-start(bf16[256,512]{1,0:T(8,128)(2,1)S(1)} %get-tuple-element.38), channel_id=1, source_target_pairs={{4,2},{6,4},{5,3},{7,5},{12,10},{14,12},{13,11},{15,13},{20,18},{2... | collective-permute-start | bytes 786440 | tf_op jit(solution)/shard_map/ppermute | solution.py:250
  167.5 12.3 %collective-permute-start.47 = (bf16[256,512]{1,0:T(8,128)(2,1)S(1)}, bf16[256,512]{1,0:T(8,128)(2,1)S(1)}, u32[]{:S(2)}, u32[]{:S(2)}) collective-permute-start(bf16[256,512]{1,0:T(8,128)(2,1)S(1)} %get-tuple-element.40), channel_id=1, source_target_pairs={{4,2},{6,4},{5,3},{7,5},{12,10},{14,12},{13,11},{15,13},{20,18},{2... | collective-permute-start | bytes 786440 | tf_op jit(solution)/shard_map/ppermute | solution.py:250
  168.1 13.0 %collective-permute-start.51 = (bf16[256,512]{1,0:T(8,128)(2,1)S(1)}, bf16[256,512]{1,0:T(8,128)(2,1)S(1)}, u32[]{:S(2)}, u32[]{:S(2)}) collective-permute-start(bf16[256,512]{1,0:T(8,128)(2,1)S(1)} %get-tuple-element.37), channel_id=1, source_target_pairs={{0,2},{2,4},{4,6},{1,3},{3,5},{5,7},{8,10},{10,12},{12,14},{9,11},... | collective-permute-start | bytes 786440 | tf_op jit(solution)/shard_map/ppermute | solution.py:249
  (53 other events, 550.4 us)

commit v10 on v9

--- a/solution.py
+++ b/solution.py
@@ -84,7 +84,7 @@
     return pl.pallas_call(
         functools.partial(panel_kernel, sizes, step, offset),
         out_shape=jax.ShapeDtypeStruct((count, sizes.rows), jnp.bfloat16),
-        in_specs=[ANY] + [VMEM] * len(flat),
+        in_specs=[pl.BlockSpec(memory_space=pltpu.HBM)] + [VMEM] * len(flat),
         out_specs=VMEM,
         scratch_shapes=[
             pltpu.VMEM((sizes.rows, count), jnp.bfloat16),

time: 199 us -> 199 us (level)
  no operation moved by 1% of the time
where the time goes in v10:
time: 199 us; the launch traced here: 198 us
  starting transfers between devices  103 us (52%)
  waiting for transfers between devices  59.8 us (30%)
  Pallas kernels  18.8 us (9%)
  local copies, waits for them, and re-layouts  11 us (6%)
  other arithmetic  3.77 us (2%)
    ppermute x12, starting transfers between devices, scattered_sum(): up = lax.ppermute(up_block, 'row', [(i, i + 1) for i in range(low + 1)])  46.2 us
    ppermute x17, waiting for transfers between devices, exchanged(): lax.ppermute(value, axis, [(i, (i + steps) % count) for i in range(count)])  19 us
    ppermute x6, waiting for transfers between devices, neighbours_gathered(): lax.ppermute(down, 'row', [(i, i - 1) for i in range(1, sizes.row - slot)])  16.1 us
    ppermute x12, waiting for transfers between devices, scattered_sum(): lax.ppermute(down_block, 'row', [(i, i - 1) for i in range(last - low, la...  16.1 us
    pallas_call x4, Pallas kernels, products(): pl.pallas_call(functools.partial(products_kernel, sizes, step, part, [b[0...  15.7 us
    ppermute x6, starting transfers between devices, neighbours_gathered(): up = lax.ppermute(up, 'row', [(i, i + 1) for i in range(slot, last)])  14.1 us
    ppermute x12, starting transfers between devices, scattered_sum(): lax.ppermute(down_block, 'row', [(i, i - 1) for i in range(last - low, la...  13 us
    ppermute x17, starting transfers between devices, exchanged(): lax.ppermute(value, axis, [(i, (i + steps) % count) for i in range(count)])  10.4 us
  transfers between devices with their start and end apart: 57, of which 22 were waited for; matrix products, arithmetic and copies ran while one was open for 4% of the time, Pallas kernels for 7%

profile of v10, /device:TPU:0, one launch (start us, length us, event | category | flops | bytes accessed | tf_op | source)
XLA Modules:
  0.0 197.6 jit_solution(10884335660438481768)
XLA Ops:
  5.4 6.0 %collective-permute-done.refs_0_ = bf16[512,256]{1,0:T(8,128)(2,1)S(1)} collective-permute-done((bf16[512,256]{1,0:T(8,128)(2,1)S(1)}, bf16[512,256]{1,0:T(8,128)(2,1)S(1)}, u32[]{:S(2)}, u32[]{:S(2)}) %collective-permute-start) | collective-permute-done | bytes 262176 | tf_op jit(solution)/shard_map/ppermute | solution.py:18
  11.5 4.1 %collective-permute-start.1 = (bf16[256,512]{1,0:T(8,128)(2,1)S(1)}, bf16[256,512]{1,0:T(8,128)(2,1)S(1)}, u32[]{:S(2)}, u32[]{:S(2)}) collective-permute-start(bf16[256,512]{1,0:T(8,128)(2,1)S(1)} %panel.5.refs_0_), channel_id=1, source_target_pairs={{0,2},{2,4},{4,6},{1,3},{3,5},{5,7},{8,10},{10,12},{12,14},{9,11},... | collective-permute-start | bytes 786440 | tf_op jit(solution)/shard_map/ppermute | solution.py:215
  19.7 4.6 %collective-permute-start.8 = (bf16[256,512]{1,0:T(8,128)(2,1)S(1)}, bf16[256,512]{1,0:T(8,128)(2,1)S(1)}, u32[]{:S(2)}, u32[]{:S(2)}) collective-permute-start(bf16[256,512]{1,0:T(8,128)(2,1)S(1)} %panel.6.refs_0_), channel_id=1, source_target_pairs={{0,2},{2,4},{4,6},{1,3},{3,5},{5,7},{8,10},{10,12},{12,14},{9,11},... | collective-permute-start | bytes 786440 | tf_op jit(solution)/shard_map/ppermute | solution.py:215
  42.4 8.1 %collective-permute-done.12.refs_4_ = bf16[256,512]{1,0:T(8,128)(2,1)} collective-permute-done((bf16[256,512]{1,0:T(8,128)(2,1)S(1)}, bf16[256,512]{1,0:T(8,128)(2,1)}, u32[]{:S(2)}, u32[]{:S(2)}) %collective-permute-start.12) | collective-permute-done | bytes 262176 | tf_op jit(solution)/shard_map/ppermute | solution.py:216
  63.0 4.7 %collective-permute-start.14 = (bf16[256,512]{1,0:T(8,128)(2,1)}, bf16[256,512]{1,0:T(8,128)(2,1)S(1)}, u32[]{:S(2)}, u32[]{:S(2)}) collective-permute-start(bf16[256,512]{1,0:T(8,128)(2,1)} %panel.4.refs_0_), channel_id=1, source_target_pairs={{0,2},{2,4},{4,6},{1,3},{3,5},{5,7},{8,10},{10,12},{12,14},{9,11},... | collective-permute-start | bytes 786440 | tf_op jit(solution)/shard_map/ppermute | solution.py:224
  70.6 4.2 %products.4 = (f32[4,256,512]{2,1,0:T(8,128)S(1)}, bf16[256,512]{1,0:T(8,128)(2,1)S(1)}, bf16[256,512]{1,0:T(8,128)(2,1)S(1)}) custom-call(bf16[256,512]{1,0:T(8,128)(2,1)S(1)} %copy-done.9, bf16[256,512]{1,0:T(8,128)(2,1)S(1)} %copy-done.15, bf16[256,512]{1,0:T(8,128)(2,1)S(1)} %copy-done.17, bf16[256,512]{1,0:T(8,128)(2,1)} %collective-permute-done.2.refs_3_, ...), custom_call_target="tpu_custom_call" | custom-call | flops 1610612736 | bytes 9437184 | tf_op jit(solution)/shard_map/products/pallas_call | solution.py:152
  76.1 4.6 %collective-permute-start.32 = (bf16[256,512]{1,0:T(8,128)(2,1)S(1)}, bf16[256,512]{1,0:T(8,128)(2,1)S(1)}, u32[]{:S(2)}, u32[]{:S(2)}) collective-permute-start(bf16[256,512]{1,0:T(8,128)(2,1)S(1)} %panel.7.refs_0_), channel_id=1, source_target_pairs={{0,2},{2,4},{4,6},{1,3},{3,5},{5,7},{8,10},{10,12},{12,14},{9,11},... | collective-permute-start | bytes 786440 | tf_op jit(solution)/shard_map/ppermute | solution.py:224
  83.0 4.6 %collective-permute-start.23 = (bf16[256,512]{1,0:T(8,128)(2,1)S(1)}, bf16[256,512]{1,0:T(8,128)(2,1)S(1)}, u32[]{:S(2)}, u32[]{:S(2)}) collective-permute-start(bf16[256,512]{1,0:T(8,128)(2,1)S(1)} %broadcast_select_fusion.3), channel_id=1, source_target_pairs={{0,2},{2,4},{4,6},{1,3},{3,5},{5,7},{8,10},{10,12},{12,14},{9,11},... | collective-permute-start | bytes 786440 | tf_op jit(solution)/shard_map/ppermute | solution.py:249
  87.6 4.2 %products.5 = (f32[4,256,512]{2,1,0:T(8,128)S(1)}, bf16[256,512]{1,0:T(8,128)(2,1)S(1)}, bf16[256,512]{1,0:T(8,128)(2,1)S(1)}) custom-call(bf16[256,512]{1,0:T(8,128)(2,1)S(1)} %copy-done.7, bf16[256,512]{1,0:T(8,128)(2,1)S(1)} %copy-done.11, bf16[256,512]{1,0:T(8,128)(2,1)S(1)} %copy-done.13, bf16[256,512]{1,0:T(8,128)(2,1)} %collective-permute-done.9.refs_3_, ...), custom_call_target="tpu_custom_call" | custom-call | flops 1610612736 | bytes 9437184 | tf_op jit(solution)/shard_map/products/pallas_call | solution.py:152
  93.3 4.6 %collective-permute-start.33 = (bf16[256,512]{1,0:T(8,128)(2,1)S(1)}, bf16[256,512]{1,0:T(8,128)(2,1)S(1)}, u32[]{:S(2)}, u32[]{:S(2)}) collective-permute-start(bf16[256,512]{1,0:T(8,128)(2,1)S(1)} %broadcast_select_fusion.2), channel_id=1, source_target_pairs={{0,2},{2,4},{4,6},{1,3},{3,5},{5,7},{8,10},{10,12},{12,14},{9,11},... | collective-permute-start | bytes 786440 | tf_op jit(solution)/shard_map/ppermute | solution.py:249
  104.6 4.4 %collective-permute-start.34 = (bf16[256,512]{1,0:T(8,128)(2,1)S(1)}, bf16[256,512]{1,0:T(8,128)(2,1)S(1)}, u32[]{:S(2)}, u32[]{:S(2)}) collective-permute-start(bf16[256,512]{1,0:T(8,128)(2,1)S(1)} %get-tuple-element.43), channel_id=1, source_target_pairs={{0,2},{2,4},{4,6},{1,3},{3,5},{5,7},{8,10},{10,12},{12,14},{9,11},... | collective-permute-start | bytes 786440 | tf_op jit(solution)/shard_map/ppermute | solution.py:249
  110.6 4.6 %collective-permute-start.27 = (bf16[256,512]{1,0:T(8,128)(2,1)S(1)}, bf16[256,512]{1,0:T(8,128)(2,1)S(1)}, u32[]{:S(2)}, u32[]{:S(2)}) collective-permute-start(bf16[256,512]{1,0:T(8,128)(2,1)S(1)} %get-tuple-element.45), channel_id=1, source_target_pairs={{0,2},{2,4},{4,6},{1,3},{3,5},{5,7},{8,10},{10,12},{12,14},{9,11},... | collective-permute-start | bytes 786440 | tf_op jit(solution)/shard_map/ppermute | solution.py:249
  116.4 3.3 %collective-permute-done.38.refs_6_ = bf16[256,512]{1,0:T(8,128)(2,1)S(1)} collective-permute-done((bf16[256,512]{1,0:T(8,128)(2,1)S(1)}, bf16[256,512]{1,0:T(8,128)(2,1)S(1)}, u32[]{:S(2)}, u32[]{:S(2)}) %collective-permute-start.38) | collective-permute-done | bytes 262176 | tf_op jit(solution)/shard_map/ppermute | solution.py:250
  126.3 4.1 %collective-permute-done.39 = bf16[256,512]{1,0:T(8,128)(2,1)S(1)} collective-permute-done((bf16[256,512]{1,0:T(8,128)(2,1)S(1)}, bf16[256,512]{1,0:T(8,128)(2,1)S(1)}, u32[]{:S(2)}, u32[]{:S(2)}) %collective-permute-start.39) | collective-permute-done | bytes 262176 | tf_op jit(solution)/shard_map/ppermute | solution.py:250
  132.9 4.1 %collective-permute-done.41.refs_13_.refs_7_ = bf16[256,512]{1,0:T(8,128)(2,1)S(1)} collective-permute-done((bf16[256,512]{1,0:T(8,128)(2,1)S(1)}, bf16[256,512]{1,0:T(8,128)(2,1)S(1)}, u32[]{:S(2)}, u32[]{:S(2)}) %collective-permute-start.41) | collective-permute-done | bytes 262176 | tf_op jit(solution)/shard_map/ppermute | solution.py:18
  138.5 3.6 %products.7 = (f32[4,256,512]{2,1,0:T(8,128)S(1)}, bf16[256,512]{1,0:T(8,128)(2,1)S(1)}, bf16[256,512]{1,0:T(8,128)(2,1)S(1)}) custom-call(bf16[256,512]{1,0:T(8,128)(2,1)S(1)} %panel.7.refs_0_, bf16[256,512]{1,0:T(8,128)(2,1)S(1)} %collective-permute-done.32.refs_1_, bf16[256,512]{1,0:T(8,128)(2,1)S(1)} %collective-permute-done.36.refs_2_, ...), custom_call_target="tpu_custom_call" | custom-call | flops 1610612736 | bytes 9437184 | tf_op jit(solution)/shard_map/products/pallas_call | solution.py:152
  144.8 3.7 %products.6 = (f32[4,256,512]{2,1,0:T(8,128)S(1)}, bf16[256,512]{1,0:T(8,128)(2,1)S(1)}, bf16[256,512]{1,0:T(8,128)(2,1)S(1)}) custom-call(bf16[256,512]{1,0:T(8,128)(2,1)} %panel.4.refs_0_, bf16[256,512]{1,0:T(8,128)(2,1)S(1)} %collective-permute-done.14.refs_1_, bf16[256,512]{1,0:T(8,128)(2,1)} %collective-permute-done.15.refs_2_, ...), custom_call_target="tpu_custom_call" | custom-call | flops 1610612736 | bytes 9437184 | tf_op jit(solution)/shard_map/products/pallas_call | solution.py:152
  150.9 4.4 %collective-permute-start.50 = (bf16[256,512]{1,0:T(8,128)(2,1)S(1)}, bf16[256,512]{1,0:T(8,128)(2,1)S(1)}, u32[]{:S(2)}, u32[]{:S(2)}) collective-permute-start(bf16[256,512]{1,0:T(8,128)(2,1)S(1)} %fusion.1), channel_id=1, source_target_pairs={{0,2},{2,4},{1,3},{3,5},{8,10},{10,12},{9,11},{11,13},{16,18},{18,... | collective-permute-start | bytes 786440 | tf_op jit(solution)/shard_map/ppermute | solution.py:249
  156.5 4.4 %collective-permute-start.44 = (bf16[256,512]{1,0:T(8,128)(2,1)S(1)}, bf16[256,512]{1,0:T(8,128)(2,1)S(1)}, u32[]{:S(2)}, u32[]{:S(2)}) collective-permute-start(bf16[256,512]{1,0:T(8,128)(2,1)S(1)} %fusion.7), channel_id=1, source_target_pairs={{0,2},{2,4},{1,3},{3,5},{8,10},{10,12},{9,11},{11,13},{16,18},{18,... | collective-permute-start | bytes 786440 | tf_op jit(solution)/shard_map/ppermute | solution.py:249
  162.9 4.4 %collective-permute-done.44 = bf16[256,512]{1,0:T(8,128)(2,1)S(1)} collective-permute-done((bf16[256,512]{1,0:T(8,128)(2,1)S(1)}, bf16[256,512]{1,0:T(8,128)(2,1)S(1)}, u32[]{:S(2)}, u32[]{:S(2)}) %collective-permute-start.44) | collective-permute-done | bytes 262176 | tf_op jit(solution)/shard_map/ppermute | solution.py:249
  168.1 5.0 %collective-permute-start.51 = (bf16[256,512]{1,0:T(8,128)(2,1)S(1)}, bf16[256,512]{1,0:T(8,128)(2,1)S(1)}, u32[]{:S(2)}, u32[]{:S(2)}) collective-permute-start(bf16[256,512]{1,0:T(8,128)(2,1)S(1)} %get-tuple-element.37), channel_id=1, source_target_pairs={{0,2},{2,4},{4,6},{1,3},{3,5},{5,7},{8,10},{10,12},{12,14},{9,11},... | collective-permute-start | bytes 786440 | tf_op jit(solution)/shard_map/ppermute | solution.py:249
  174.6 5.2 %collective-permute-start.45 = (bf16[256,512]{1,0:T(8,128)(2,1)S(1)}, bf16[256,512]{1,0:T(8,128)(2,1)S(1)}, u32[]{:S(2)}, u32[]{:S(2)}) collective-permute-start(bf16[256,512]{1,0:T(8,128)(2,1)S(1)} %get-tuple-element.39), channel_id=1, source_target_pairs={{0,2},{2,4},{4,6},{1,3},{3,5},{5,7},{8,10},{10,12},{12,14},{9,11},... | collective-permute-start | bytes 786440 | tf_op jit(solution)/shard_map/ppermute | solution.py:249
  184.6 4.4 %collective-permute-done.48 = bf16[256,512]{1,0:T(8,128)(2,1)S(1)} collective-permute-done((bf16[256,512]{1,0:T(8,128)(2,1)S(1)}, bf16[256,512]{1,0:T(8,128)(2,1)S(1)}, u32[]{:S(2)}, u32[]{:S(2)}) %collective-permute-start.48) | collective-permute-done | bytes 262176 | tf_op jit(solution)/shard_map/ppermute | solution.py:250
  190.6 5.3 %collective-permute-done.55.refs_2_ = bf16[256,512]{1,0:T(8,128)(2,1)S(1)} collective-permute-done((bf16[256,512]{1,0:T(8,128)(2,1)S(1)}, bf16[256,512]{1,0:T(8,128)(2,1)S(1)}, u32[]{:S(2)}, u32[]{:S(2)}) %collective-permute-start.55) | collective-permute-done | bytes 262176 | tf_op jit(solution)/shard_map/ppermute | solution.py:18
  (163 shorter events, 86.4 us)
Async XLA Ops:
  4.2 11.9 %collective-permute-start.7 = (bf16[512,256]{1,0:T(8,128)(2,1)S(1)}, bf16[512,256]{1,0:T(8,128)(2,1)S(1)}, u32[]{:S(2)}, u32[]{:S(2)}) collective-permute-start(bf16[512,256]{1,0:T(8,128)(2,1)S(1)} %get-tuple-element.49), channel_id=1, source_target_pairs={{0,8},{8,0},{1,9},{9,1},{2,10},{10,2},{3,11},{11,3},{4,12},{12,4},... | collective-permute-start | bytes 786440 | tf_op jit(solution)/shard_map/ppermute | solution.py:18
  11.5 12.7 %collective-permute-start.1 = (bf16[256,512]{1,0:T(8,128)(2,1)S(1)}, bf16[256,512]{1,0:T(8,128)(2,1)S(1)}, u32[]{:S(2)}, u32[]{:S(2)}) collective-permute-start(bf16[256,512]{1,0:T(8,128)(2,1)S(1)} %panel.5.refs_0_), channel_id=1, source_target_pairs={{0,2},{2,4},{4,6},{1,3},{3,5},{5,7},{8,10},{10,12},{12,14},{9,11},... | collective-permute-start | bytes 786440 | tf_op jit(solution)/shard_map/ppermute | solution.py:215
  16.2 17.9 %collective-permute-start.18 = (bf16[512,512]{1,0:T(8,128)(2,1)S(1)}, bf16[512,512]{1,0:T(8,128)(2,1)S(1)}, u32[]{:S(2)}, u32[]{:S(2)}) collective-permute-start(bf16[512,512]{1,0:T(8,128)(2,1)S(1)} %dynamic-slice_bitcast_fusion), channel_id=1, source_target_pairs={{0,8},{8,0},{1,9},{9,1},{2,10},{10,2},{3,11},{11,3},{4,12},{12,4},... | collective-permute-start | bytes 1572872 | tf_op jit(solution)/shard_map/ppermute | solution.py:18
  17.9 41.2 %collective-permute-start.21 = (bf16[512,1024]{1,0:T(8,128)(2,1)S(1)}, bf16[512,1024]{1,0:T(8,128)(2,1)}, u32[]{:S(2)}, u32[]{:S(2)}) collective-permute-start(bf16[512,1024]{1,0:T(8,128)(2,1)S(1)} %bitcast.113), channel_id=1, source_target_pairs={{0,8},{8,0},{1,9},{9,1},{2,10},{10,2},{3,11},{11,3},{4,12},{12,4},... | collective-permute-start | bytes 3145736 | tf_op jit(solution)/shard_map/ppermute | solution.py:18
  34.0 16.5 %collective-permute-start.12 = (bf16[256,512]{1,0:T(8,128)(2,1)S(1)}, bf16[256,512]{1,0:T(8,128)(2,1)}, u32[]{:S(2)}, u32[]{:S(2)}) collective-permute-start(bf16[256,512]{1,0:T(8,128)(2,1)S(1)} %collective-permute-done.11.refs_2_), channel_id=1, source_target_pairs={{2,0},{4,2},{3,1},{5,3},{10,8},{12,10},{11,9},{13,11},{18,16},{20,... | collective-permute-start | bytes 786440 | tf_op jit(solution)/shard_map/ppermute | solution.py:216
  36.0 19.6 %collective-permute-start.3 = (bf16[256,512]{1,0:T(8,128)(2,1)}, bf16[256,512]{1,0:T(8,128)(2,1)}, u32[]{:S(2)}, u32[]{:S(2)}) collective-permute-start(bf16[256,512]{1,0:T(8,128)(2,1)} %collective-permute-done.2.refs_3_), channel_id=1, source_target_pairs={{4,6},{5,7},{12,14},{13,15},{20,22},{21,23},{28,30},{29,31}} | collective-permute-start | bytes 786440 | tf_op jit(solution)/shard_map/ppermute | solution.py:215
  39.8 16.0 %collective-permute-start.6 = (bf16[256,512]{1,0:T(8,128)(2,1)}, bf16[256,512]{1,0:T(8,128)(2,1)}, u32[]{:S(2)}, u32[]{:S(2)}) collective-permute-start(bf16[256,512]{1,0:T(8,128)(2,1)} %collective-permute-done.5.refs_4_), channel_id=1, source_target_pairs={{2,0},{3,1},{10,8},{11,9},{18,16},{19,17},{26,24},{27,25}} | collective-permute-start | bytes 786440 | tf_op jit(solution)/shard_map/ppermute | solution.py:216
  41.1 15.3 %collective-permute-start.10 = (bf16[256,512]{1,0:T(8,128)(2,1)}, bf16[256,512]{1,0:T(8,128)(2,1)}, u32[]{:S(2)}, u32[]{:S(2)}) collective-permute-start(bf16[256,512]{1,0:T(8,128)(2,1)} %collective-permute-done.9.refs_3_), channel_id=1, source_target_pairs={{4,6},{5,7},{12,14},{13,15},{20,22},{21,23},{28,30},{29,31}} | collective-permute-start | bytes 786440 | tf_op jit(solution)/shard_map/ppermute | solution.py:215
  56.4 11.3 %collective-permute-start.16 = (bf16[1024,512]{1,0:T(8,128)(2,1)}, bf16[1024,512]{1,0:T(8,128)(2,1)}, u32[]{:S(2)}, u32[]{:S(2)}) collective-permute-start(bf16[1024,512]{1,0:T(8,128)(2,1)} %bitcast.103.refs_7_), channel_id=1, source_target_pairs={{0,1},{1,0},{2,3},{3,2},{4,5},{5,4},{6,7},{7,6},{8,9},{9,8},{10,11... | collective-permute-start | bytes 3145736 | tf_op jit(solution)/shard_map/ppermute | solution.py:18
  61.5 19.2 %collective-permute-start.15 = (bf16[256,512]{1,0:T(8,128)(2,1)}, bf16[256,512]{1,0:T(8,128)(2,1)}, u32[]{:S(2)}, u32[]{:S(2)}) collective-permute-start(bf16[256,512]{1,0:T(8,128)(2,1)} %panel.4.refs_0_), channel_id=1, source_target_pairs={{2,0},{4,2},{6,4},{3,1},{5,3},{7,5},{10,8},{12,10},{14,12},{11,9},... | collective-permute-start | bytes 786440 | tf_op jit(solution)/shard_map/ppermute | solution.py:225
  63.0 20.0 %collective-permute-start.14 = (bf16[256,512]{1,0:T(8,128)(2,1)}, bf16[256,512]{1,0:T(8,128)(2,1)S(1)}, u32[]{:S(2)}, u32[]{:S(2)}) collective-permute-start(bf16[256,512]{1,0:T(8,128)(2,1)} %panel.4.refs_0_), channel_id=1, source_target_pairs={{0,2},{2,4},{4,6},{1,3},{3,5},{5,7},{8,10},{10,12},{12,14},{9,11},... | collective-permute-start | bytes 786440 | tf_op jit(solution)/shard_map/ppermute | solution.py:224
  74.8 17.1 %collective-permute-start.36 = (bf16[256,512]{1,0:T(8,128)(2,1)S(1)}, bf16[256,512]{1,0:T(8,128)(2,1)S(1)}, u32[]{:S(2)}, u32[]{:S(2)}) collective-permute-start(bf16[256,512]{1,0:T(8,128)(2,1)S(1)} %panel.7.refs_0_), channel_id=1, source_target_pairs={{2,0},{4,2},{6,4},{3,1},{5,3},{7,5},{10,8},{12,10},{14,12},{11,9},... | collective-permute-start | bytes 786440 | tf_op jit(solution)/shard_map/ppermute | solution.py:225
  76.1 17.1 %collective-permute-start.32 = (bf16[256,512]{1,0:T(8,128)(2,1)S(1)}, bf16[256,512]{1,0:T(8,128)(2,1)S(1)}, u32[]{:S(2)}, u32[]{:S(2)}) collective-permute-start(bf16[256,512]{1,0:T(8,128)(2,1)S(1)} %panel.7.refs_0_), channel_id=1, source_target_pairs={{0,2},{2,4},{4,6},{1,3},{3,5},{5,7},{8,10},{10,12},{12,14},{9,11},... | collective-permute-start | bytes 786440 | tf_op jit(solution)/shard_map/ppermute | solution.py:224
  81.7 16.2 %collective-permute-start.24 = (bf16[256,512]{1,0:T(8,128)(2,1)S(1)}, bf16[256,512]{1,0:T(8,128)(2,1)S(1)}, u32[]{:S(2)}, u32[]{:S(2)}) collective-permute-start(bf16[256,512]{1,0:T(8,128)(2,1)S(1)} %broadcast_select_fusion.1), channel_id=1, source_target_pairs={{2,0},{4,2},{6,4},{3,1},{5,3},{7,5},{10,8},{12,10},{14,12},{11,9},... | collective-permute-start | bytes 786440 | tf_op jit(solution)/shard_map/ppermute | solution.py:250
  83.0 14.8 %collective-permute-start.23 = (bf16[256,512]{1,0:T(8,128)(2,1)S(1)}, bf16[256,512]{1,0:T(8,128)(2,1)S(1)}, u32[]{:S(2)}, u32[]{:S(2)}) collective-permute-start(bf16[256,512]{1,0:T(8,128)(2,1)S(1)} %broadcast_select_fusion.3), channel_id=1, source_target_pairs={{0,2},{2,4},{4,6},{1,3},{3,5},{5,7},{8,10},{10,12},{12,14},{9,11},... | collective-permute-start | bytes 786440 | tf_op jit(solution)/shard_map/ppermute | solution.py:249
  93.3 11.2 %collective-permute-start.33 = (bf16[256,512]{1,0:T(8,128)(2,1)S(1)}, bf16[256,512]{1,0:T(8,128)(2,1)S(1)}, u32[]{:S(2)}, u32[]{:S(2)}) collective-permute-start(bf16[256,512]{1,0:T(8,128)(2,1)S(1)} %broadcast_select_fusion.2), channel_id=1, source_target_pairs={{0,2},{2,4},{4,6},{1,3},{3,5},{5,7},{8,10},{10,12},{12,14},{9,11},... | collective-permute-start | bytes 786440 | tf_op jit(solution)/shard_map/ppermute | solution.py:249
  98.0 12.3 %collective-permute-start.25 = (bf16[256,512]{1,0:T(8,128)(2,1)S(1)}, bf16[256,512]{1,0:T(8,128)(2,1)S(1)}, u32[]{:S(2)}, u32[]{:S(2)}) collective-permute-start(bf16[256,512]{1,0:T(8,128)(2,1)S(1)} %get-tuple-element.48), channel_id=1, source_target_pairs={{0,2},{2,4},{4,6},{1,3},{3,5},{5,7},{8,10},{10,12},{12,14},{9,11},... | collective-permute-start | bytes 786440 | tf_op jit(solution)/shard_map/ppermute | solution.py:249
  104.6 11.8 %collective-permute-start.34 = (bf16[256,512]{1,0:T(8,128)(2,1)S(1)}, bf16[256,512]{1,0:T(8,128)(2,1)S(1)}, u32[]{:S(2)}, u32[]{:S(2)}) collective-permute-start(bf16[256,512]{1,0:T(8,128)(2,1)S(1)} %get-tuple-element.43), channel_id=1, source_target_pairs={{0,2},{2,4},{4,6},{1,3},{3,5},{5,7},{8,10},{10,12},{12,14},{9,11},... | collective-permute-start | bytes 786440 | tf_op jit(solution)/shard_map/ppermute | solution.py:249
  110.6 12.9 %collective-permute-start.27 = (bf16[256,512]{1,0:T(8,128)(2,1)S(1)}, bf16[256,512]{1,0:T(8,128)(2,1)S(1)}, u32[]{:S(2)}, u32[]{:S(2)}) collective-permute-start(bf16[256,512]{1,0:T(8,128)(2,1)S(1)} %get-tuple-element.45), channel_id=1, source_target_pairs={{0,2},{2,4},{4,6},{1,3},{3,5},{5,7},{8,10},{10,12},{12,14},{9,11},... | collective-permute-start | bytes 786440 | tf_op jit(solution)/shard_map/ppermute | solution.py:249
  149.8 11.2 %collective-permute-start.52 = (bf16[256,512]{1,0:T(8,128)(2,1)S(1)}, bf16[256,512]{1,0:T(8,128)(2,1)S(1)}, u32[]{:S(2)}, u32[]{:S(2)}) collective-permute-start(bf16[256,512]{1,0:T(8,128)(2,1)S(1)} %get-tuple-element.36), channel_id=1, source_target_pairs={{6,4},{7,5},{14,12},{15,13},{22,20},{23,21},{30,28},{31,29}} | collective-permute-start | bytes 786440 | tf_op jit(solution)/shard_map/ppermute | solution.py:250
  150.9 11.2 %collective-permute-start.50 = (bf16[256,512]{1,0:T(8,128)(2,1)S(1)}, bf16[256,512]{1,0:T(8,128)(2,1)S(1)}, u32[]{:S(2)}, u32[]{:S(2)}) collective-permute-start(bf16[256,512]{1,0:T(8,128)(2,1)S(1)} %fusion.1), channel_id=1, source_target_pairs={{0,2},{2,4},{1,3},{3,5},{8,10},{10,12},{9,11},{11,13},{16,18},{18,... | collective-permute-start | bytes 786440 | tf_op jit(solution)/shard_map/ppermute | solution.py:249
  162.2 10.9 %collective-permute-start.53 = (bf16[256,512]{1,0:T(8,128)(2,1)S(1)}, bf16[256,512]{1,0:T(8,128)(2,1)S(1)}, u32[]{:S(2)}, u32[]{:S(2)}) collective-permute-start(bf16[256,512]{1,0:T(8,128)(2,1)S(1)} %get-tuple-element.38), channel_id=1, source_target_pairs={{4,2},{6,4},{5,3},{7,5},{12,10},{14,12},{13,11},{15,13},{20,18},{2... | collective-permute-start | bytes 786440 | tf_op jit(solution)/shard_map/ppermute | solution.py:250
  167.5 12.3 %collective-permute-start.47 = (bf16[256,512]{1,0:T(8,128)(2,1)S(1)}, bf16[256,512]{1,0:T(8,128)(2,1)S(1)}, u32[]{:S(2)}, u32[]{:S(2)}) collective-permute-start(bf16[256,512]{1,0:T(8,128)(2,1)S(1)} %get-tuple-element.40), channel_id=1, source_target_pairs={{4,2},{6,4},{5,3},{7,5},{12,10},{14,12},{13,11},{15,13},{20,18},{2... | collective-permute-start | bytes 786440 | tf_op jit(solution)/shard_map/ppermute | solution.py:250
  168.1 13.0 %collective-permute-start.51 = (bf16[256,512]{1,0:T(8,128)(2,1)S(1)}, bf16[256,512]{1,0:T(8,128)(2,1)S(1)}, u32[]{:S(2)}, u32[]{:S(2)}) collective-permute-start(bf16[256,512]{1,0:T(8,128)(2,1)S(1)} %get-tuple-element.37), channel_id=1, source_target_pairs={{0,2},{2,4},{4,6},{1,3},{3,5},{5,7},{8,10},{10,12},{12,14},{9,11},... | collective-permute-start | bytes 786440 | tf_op jit(solution)/shard_map/ppermute | solution.py:249
  (53 other events, 550.4 us)
